TPU v7x, 32 devices: a whole 2x2x4 slice. The times are simulated.
32 devices in a mesh: dp: 16 (over z, x, core), tensor: 2 (over y).
Axes of the slice: x: 2, y: 2, z: 4, core: 2. Of those that a mesh axis runs over, the one named last changes fastest.
Arguments:
- layer_in: bfloat16 [8192, 1536], P('dp'), may hold values from -6 to 6
- norm1_gain: float32 [1536], replicated, may hold values from 0.1 to 1.9
- w_query: bfloat16 [1536, 1536], P(None, 'tensor'), may hold values from -0.3125 to 0.3125
- w_key: bfloat16 [1536, 512], P(None, 'tensor'), may hold values from -0.15625 to 0.15625
- w_value: bfloat16 [1536, 512], P(None, 'tensor'), may hold values from -0.15625 to 0.15625
- w_out: bfloat16 [1536, 1536], P('tensor'), may hold values from -0.75 to 0.75
- norm2_gain: float32 [1536], replicated, may hold values from 0.1 to 1.9
- router: bfloat16 [1536, 16], replicated, may hold values from -0.10986328 to 0.10986328
- w_gate: bfloat16 [16, 1536, 1024], P(None, None, 'tensor'), may hold values from -0.15625 to 0.15625
- w_up: bfloat16 [16, 1536, 1024], P(None, None, 'tensor'), may hold values from -0.15625 to 0.15625
- w_down: bfloat16 [16, 1024, 1536], P(None, 'tensor'), may hold values from -0.375 to 0.375
- segments: int32 [8192], replicated, may hold values from 0 to 7, never falling along the last dimension, each value on 1 to 4096 neighbouring positions
- routes: int32 [8192, 2], P('dp'), may hold values from 0 to 15, all different within a row; in each aligned block of 512 rows (0 to 511, 512 to 1023, ...) at most 128 rows name the same one
- out_grad: bfloat16 [8192, 1536], P('dp'), may hold values from -6 to 6
Outputs:
- layer_out: bfloat16 [8192, 1536], P(('dp', 'tensor'))
- input_grad: float32 [8192, 1536], P(('dp', 'tensor'))
- norm1_gain_grad: float32 [1536], replicated
- w_query_grad: float32 [1536, 1536], P('dp', 'tensor')
- w_key_grad: float32 [1536, 512], P('dp', 'tensor')
- w_value_grad: float32 [1536, 512], P('dp', 'tensor')
- w_out_grad: float32 [1536, 1536], P('tensor', 'dp')
- norm2_gain_grad: float32 [1536], replicated
- router_grad: float32 [1536, 16], replicated
- w_gate_grad: float32 [16, 1536, 1024], P('dp', None, 'tensor')
- w_up_grad: float32 [16, 1536, 1024], P('dp', None, 'tensor')
- w_down_grad: float32 [16, 1024, 1536], P('dp', 'tensor')
Inputs may be any that keep to these rules, and one draw needn't show every extreme that they name: `segments`: document numbers never fall along the tokens; each document has 1 to 4096 tokens, and one has exactly 4096. `routes`: each token names 2 different experts; among the tokens of one index of dp no expert is named more than 128 times, and in every draw some expert is named exactly 128 times there.
All inputs are finite; a program needn't handle non-finite values.
Results may differ from a plain program's by a relative error of at most 0.02.
The roundings to bfloat16 on the way count: a program that leaves them out, or rounds other values in their place, can miss the bound.
Values may be sent and summed in bfloat16 or wider, within the bound.
No kernel may reach another device: no remote copies, remote signals or barrier semaphores. Data moves between devices by JAX's collectives and lax.ppermute only.
A program may use at most 448 MiB of HBM per device.

v0:
```python
import jax
import jax.numpy as jnp
from jax import lax
from jax.sharding import PartitionSpec as P

HD = 64
TOP = 2
SEQ_LEN = 4096
CAP = 128


EPS = 1e-05
HIGH = lax.Precision.HIGHEST


def from_behind(block, axis, distance):
    devices = range(lax.axis_size(axis))
    route = [(i - distance, i) for i in devices if i - distance in devices]
    return lax.ppermute(block, axis, route)


def norm_factor(value):
    return lax.rsqrt(jnp.mean(value * value, axis=-1, keepdims=True) + EPS)


def norm_back(unit, factor, gain, grad):
    inner = gain * grad
    return factor * (inner - unit * jnp.mean(unit * inner, axis=-1, keepdims=True))


def shards(
    layer_in,
    norm1_gain,
    w_query,
    w_key,
    w_value,
    w_out,
    norm2_gain,
    router,
    w_gate,
    w_up,
    w_down,
    segments,
    routes,
    out_grad,
):
    rows = layer_in.shape[0]
    kv_cols = w_key.shape[1]
    kv_heads = kv_cols // HD
    q_heads = w_query.shape[1] // HD
    group = q_heads // kv_heads
    experts = w_gate.shape[0]
    reach = (SEQ_LEN + rows - 2) // rows
    block = min(rows, 256)
    blocks = rows // block
    place = lax.axis_index("dp")
    tensor_size = lax.axis_size("tensor")
    part = rows // tensor_size
    first = lax.axis_index("tensor") * part
    in_float = layer_in.astype(jnp.float32)
    factor_one = norm_factor(in_float)
    unit_one = in_float * factor_one
    normed_in = (unit_one * norm1_gain).astype(jnp.bfloat16)
    query = jnp.dot(normed_in, w_query, preferred_element_type=jnp.float32).astype(jnp.bfloat16)
    kv_local = jnp.concatenate(
        [
            jnp.dot(normed_in, w_key, preferred_element_type=jnp.float32),
            jnp.dot(normed_in, w_value, preferred_element_type=jnp.float32),
        ],
        1,
    ).astype(jnp.bfloat16)
    earlier = []
    for back in range(reach, 0, -1):
        earlier.append(from_behind(kv_local, "dp", back))
    kv_all = jnp.concatenate(earlier + [kv_local], 0)
    span = kv_all.shape[0]
    keys = kv_all[:, :kv_cols].reshape(span, kv_heads, HD)
    values = kv_all[:, kv_cols:].reshape(span, kv_heads, HD)
    backs = jnp.arange(reach, -1, -1, dtype=jnp.int32)
    owners = place - backs
    seg_rows = jax.vmap(lambda start_row: lax.dynamic_slice_in_dim(segments, start_row, rows, 0))(
        jnp.maximum(owners, 0) * rows
    )
    seg_keys = jnp.where(owners[:, None] >= 0, seg_rows, -1).reshape(-1)
    pos_keys = (owners[:, None] * rows + jnp.arange(rows, dtype=jnp.int32)[None, :]).reshape(-1)
    seg_query = lax.dynamic_slice_in_dim(segments, place * rows, rows, 0).reshape(blocks, block)
    pos_query = (place * rows + jnp.arange(rows, dtype=jnp.int32)).reshape(blocks, block)
    q_blocks = query.reshape(blocks, block, kv_heads, group, HD)

    def masked_scores(q_blk, seg_blk, pos_blk):
        scores = (
            jnp.einsum("qkgd,skd->kgqs", q_blk, keys, preferred_element_type=jnp.float32) * 0.125
        )
        visible = (seg_blk[:, None] == seg_keys[None, :]) & (pos_keys[None, :] <= pos_blk[:, None])
        return jnp.where(visible[None, None], scores, -1000000000.0)

    def attend(inputs):
        q_blk, seg_blk, pos_blk = inputs
        scores = masked_scores(q_blk, seg_blk, pos_blk)
        row_max = jnp.max(scores, axis=-1, keepdims=True)
        expo = jnp.exp(scores - row_max)
        row_total = jnp.sum(expo, axis=-1, keepdims=True)
        probs = (expo / row_total).astype(jnp.bfloat16)
        result = jnp.einsum("kgqs,skd->qkgd", probs, values, preferred_element_type=jnp.float32)
        return (
            result.reshape(block, q_heads * HD).astype(jnp.bfloat16),
            row_max + jnp.log(row_total),
        )

    mixed, log_total = lax.map(attend, (q_blocks, seg_query, pos_query))
    mixed = mixed.reshape(rows, q_heads * HD)
    attn_term = jnp.dot(mixed, w_out, preferred_element_type=jnp.float32)
    attn = lax.psum(attn_term, "tensor")
    hidden = in_float + attn
    factor_two = norm_factor(hidden)
    unit_two = hidden * factor_two
    normed_mid = (unit_two * norm2_gain).astype(jnp.bfloat16)
    hidden_rows = lax.dynamic_slice_in_dim(hidden, first, part, 0)
    logits = jnp.dot(normed_mid, router, preferred_element_type=jnp.float32)
    picks = (routes[:, :, None] == jnp.arange(experts, dtype=jnp.int32)[None, None, :]).astype(
        jnp.float32
    )
    chosen = jnp.sum(picks * logits[:, None, :], axis=-1)
    gates = jax.nn.softmax(chosen, axis=-1)
    flat_routes = routes.reshape(-1)
    onehot = (flat_routes[:, None] == jnp.arange(experts, dtype=jnp.int32)[None, :]).astype(
        jnp.int32
    )
    before = jnp.cumsum(onehot, axis=0) - onehot
    slot = jnp.sum(before * onehot, axis=1)
    dest = flat_routes * CAP + slot
    owner_tok = (
        jnp.zeros((experts * CAP,), jnp.int32)
        .at[dest]
        .set(jnp.arange(rows * TOP, dtype=jnp.int32) // TOP)
    )
    slot_gate = jnp.zeros((experts * CAP,), jnp.float32).at[dest].set(gates.reshape(-1))
    expert_in = jnp.take(normed_mid, owner_tok, axis=0).reshape(experts, CAP, -1)
    gate_pre = jnp.einsum("ecd,edf->ecf", expert_in, w_gate, preferred_element_type=jnp.float32)
    up_pre = jnp.einsum("ecd,edf->ecf", expert_in, w_up, preferred_element_type=jnp.float32)
    sigma = jax.nn.sigmoid(gate_pre)
    silu_gate = gate_pre * sigma
    act = (silu_gate * up_pre).astype(jnp.bfloat16)
    expert_out = jnp.einsum(
        "ecf,efd->ecd", act, w_down, preferred_element_type=jnp.float32
    ).reshape(experts * CAP, -1)
    picked = jnp.take(expert_out, dest, axis=0).reshape(rows, TOP, -1)
    moe_part = jnp.sum(gates[:, :, None] * picked, axis=1)
    moe_rows = lax.psum_scatter(
        moe_part.astype(jnp.bfloat16), "tensor", scatter_dimension=0, tiled=True
    ).astype(jnp.float32)
    layer_out = (hidden_rows + moe_rows).astype(jnp.bfloat16)
    grad_out = out_grad.astype(jnp.float32)
    grad_gates = jnp.sum(picked * grad_out[:, None, :], axis=-1)
    grad_chosen = gates * (grad_gates - jnp.sum(gates * grad_gates, axis=-1, keepdims=True))
    grad_logits = jnp.sum(picks * grad_chosen[:, :, None], axis=1)
    router_part = jnp.einsum(
        "td,te->de", normed_mid, grad_logits, precision=HIGH, preferred_element_type=jnp.float32
    )
    grad_expert = (
        (slot_gate[:, None] * jnp.take(grad_out, owner_tok, axis=0))
        .astype(jnp.bfloat16)
        .reshape(experts, CAP, -1)
    )
    down_grad = jnp.einsum("ecf,ecd->efd", act, grad_expert, preferred_element_type=jnp.float32)
    grad_act = jnp.einsum("ecd,efd->ecf", grad_expert, w_down, preferred_element_type=jnp.float32)
    grad_gate = (grad_act * up_pre * sigma * (1.0 + gate_pre * (1.0 - sigma))).astype(jnp.bfloat16)
    grad_up = (grad_act * silu_gate).astype(jnp.bfloat16)
    gate_grad = jnp.einsum("ecd,ecf->edf", expert_in, grad_gate, preferred_element_type=jnp.float32)
    up_grad = jnp.einsum("ecd,ecf->edf", expert_in, grad_up, preferred_element_type=jnp.float32)
    grad_slots = (
        jnp.einsum("ecf,edf->ecd", grad_gate, w_gate, preferred_element_type=jnp.float32)
        + jnp.einsum("ecf,edf->ecd", grad_up, w_up, preferred_element_type=jnp.float32)
    ).reshape(experts * CAP, -1)
    grad_mid_part = jnp.sum(jnp.take(grad_slots, dest, axis=0).reshape(rows, TOP, -1), axis=1)
    grad_mid_part = grad_mid_part + jnp.einsum(
        "te,de->td", grad_logits, router, precision=HIGH, preferred_element_type=jnp.float32
    )
    grad_mid = lax.psum(grad_mid_part, "tensor")
    gain_two_part = jnp.sum(lax.dynamic_slice_in_dim(grad_mid * unit_two, first, part, 0), axis=0)
    grad_hidden = grad_out + norm_back(unit_two, factor_two, norm2_gain, grad_mid)
    hidden_grad_rows = lax.dynamic_slice_in_dim(grad_hidden, first, part, 0)
    grad_hidden_low = grad_hidden.astype(jnp.bfloat16)
    proj_grad = jnp.einsum("tc,td->cd", mixed, grad_hidden_low, preferred_element_type=jnp.float32)
    grad_mixed = jnp.einsum(
        "td,cd->tc", grad_hidden_low, w_out, preferred_element_type=jnp.float32
    ).astype(jnp.bfloat16)

    def attend_back(carry, inputs):
        key_grad, value_grad = carry
        q_blk, grad_blk, total_blk, seg_blk, pos_blk = inputs
        scores = masked_scores(q_blk, seg_blk, pos_blk)
        probs = jnp.exp(scores - total_blk)
        grad_heads = grad_blk.reshape(block, kv_heads, group, HD)
        grad_probs = jnp.einsum(
            "qkgd,skd->kgqs", grad_heads, values, preferred_element_type=jnp.float32
        )
        grad_scores = (
            probs * (grad_probs - jnp.sum(probs * grad_probs, axis=-1, keepdims=True))
        ).astype(jnp.bfloat16)
        grad_query = (
            jnp.einsum("kgqs,skd->qkgd", grad_scores, keys, preferred_element_type=jnp.float32)
            * 0.125
        )
        key_grad = (
            key_grad
            + jnp.einsum("kgqs,qkgd->skd", grad_scores, q_blk, preferred_element_type=jnp.float32)
            * 0.125
        )
        value_grad = value_grad + jnp.einsum(
            "kgqs,qkgd->skd",
            probs.astype(jnp.bfloat16),
            grad_heads,
            preferred_element_type=jnp.float32,
        )
        return (
            (key_grad, value_grad),
            grad_query.reshape(block, q_heads * HD).astype(jnp.bfloat16),
        )

    start_grads = (
        jnp.zeros((span, kv_heads, HD), jnp.float32),
        jnp.zeros((span, kv_heads, HD), jnp.float32),
    )
    (key_grad, value_grad), grad_query = lax.scan(
        attend_back,
        start_grads,
        (
            q_blocks,
            grad_mixed.reshape(blocks, block, q_heads * HD),
            log_total,
            seg_query,
            pos_query,
        ),
    )
    grad_query = grad_query.reshape(rows, q_heads * HD)
    kv_grad_all = jnp.concatenate(
        [key_grad.reshape(reach + 1, rows, kv_cols), value_grad.reshape(reach + 1, rows, kv_cols)],
        2,
    )
    kv_grad_mine = kv_grad_all[reach]
    for back in range(1, reach + 1):
        kv_grad_mine = kv_grad_mine + from_behind(
            kv_grad_all[reach - back].astype(jnp.bfloat16), "dp", -back
        ).astype(jnp.float32)
    grad_key = kv_grad_mine[:, :kv_cols].astype(jnp.bfloat16)
    grad_value = kv_grad_mine[:, kv_cols:].astype(jnp.bfloat16)
    query_grad = jnp.einsum("td,tc->dc", normed_in, grad_query, preferred_element_type=jnp.float32)
    key_weight_grad = jnp.einsum(
        "td,tc->dc", normed_in, grad_key, preferred_element_type=jnp.float32
    )
    value_weight_grad = jnp.einsum(
        "td,tc->dc", normed_in, grad_value, preferred_element_type=jnp.float32
    )
    grad_in_part = (
        jnp.einsum("tc,dc->td", grad_query, w_query, preferred_element_type=jnp.float32)
        + jnp.einsum("tc,dc->td", grad_key, w_key, preferred_element_type=jnp.float32)
        + jnp.einsum("tc,dc->td", grad_value, w_value, preferred_element_type=jnp.float32)
    )
    grad_in_rows = lax.psum_scatter(
        grad_in_part.astype(jnp.bfloat16), "tensor", scatter_dimension=0, tiled=True
    ).astype(jnp.float32)
    unit_rows = lax.dynamic_slice_in_dim(unit_one, first, part, 0)
    factor_rows = lax.dynamic_slice_in_dim(factor_one, first, part, 0)
    input_grad = hidden_grad_rows + norm_back(unit_rows, factor_rows, norm1_gain, grad_in_rows)
    gain_one_part = jnp.sum(grad_in_rows * unit_rows, axis=0)
    gain_one_grad, gain_two_grad, router_grad = lax.psum(
        (gain_one_part, gain_two_part, router_part), ("dp", "tensor")
    )
    query_out, key_out, value_out, proj_out, gate_out, up_out, down_out = (
        lax.psum_scatter(
            query_grad.astype(jnp.bfloat16), "dp", scatter_dimension=0, tiled=True
        ).astype(jnp.float32),
        lax.psum_scatter(
            key_weight_grad.astype(jnp.bfloat16), "dp", scatter_dimension=0, tiled=True
        ).astype(jnp.float32),
        lax.psum_scatter(
            value_weight_grad.astype(jnp.bfloat16), "dp", scatter_dimension=0, tiled=True
        ).astype(jnp.float32),
        lax.psum_scatter(
            proj_grad.astype(jnp.bfloat16), "dp", scatter_dimension=1, tiled=True
        ).astype(jnp.float32),
        lax.psum_scatter(
            gate_grad.astype(jnp.bfloat16), "dp", scatter_dimension=0, tiled=True
        ).astype(jnp.float32),
        lax.psum_scatter(
            up_grad.astype(jnp.bfloat16), "dp", scatter_dimension=0, tiled=True
        ).astype(jnp.float32),
        lax.psum_scatter(
            down_grad.astype(jnp.bfloat16), "dp", scatter_dimension=0, tiled=True
        ).astype(jnp.float32),
    )
    return (
        layer_out,
        input_grad,
        gain_one_grad,
        query_out,
        key_out,
        value_out,
        proj_out,
        gain_two_grad,
        router_grad,
        gate_out,
        up_out,
        down_out,
    )


def solution(mesh):
    in_specs = (
        P("dp", None),
        P(),
        P(None, "tensor"),
        P(None, "tensor"),
        P(None, "tensor"),
        P("tensor", None),
        P(),
        P(),
        P(None, None, "tensor"),
        P(None, None, "tensor"),
        P(None, "tensor", None),
        P(),
        P("dp", None),
        P("dp", None),
    )
    out_specs = (
        P(("dp", "tensor"), None),
        P(("dp", "tensor"), None),
        P(),
        P("dp", "tensor"),
        P("dp", "tensor"),
        P("dp", "tensor"),
        P("tensor", "dp"),
        P(),
        P(),
        P("dp", None, "tensor"),
        P("dp", None, "tensor"),
        P("dp", "tensor", None),
    )
    return jax.shard_map(shards, mesh=mesh, in_specs=in_specs, out_specs=out_specs, check_vma=False)
```

profile of v0, /device:TPU:0, one launch (start us, length us, event | category | flops | bytes accessed | tf_op | source)
XLA Modules:
  0.0 2350.6 jit_solution(16200550390509747110)
XLA Ops:
  31.0 18.5 while.31
  61.9 13.5 collective-permute-done
  78.5 20.3 collective-permute-start.6
  99.8 25.9 %collective-permute-start.7 = (bf16[512,512]{0,1:T(8,128)(2,1)}, bf16[512,512]{0,1:T(8,128)(2,1)S(1)}, u32[]{:S(2)}, u32[]{:S(2)}) collective-permute-start(bf16[512,512]{0,1:T(8,128)(2,1)} %pad_maximum_fusion), channel_id=1, source_target_pairs={{0,2},{2,4},{4,6},{6,8},{8,10},{10,12},{12,14},{14,16},{16,18},{18... | collective-permute-start | bytes 1572872 | tf_op jit(solution)/shard_map/ppermute | solution.py:19
  132.6 142.6 %while.32 = (s32[]{:T(128)}, bf16[2,256,768]{2,1,0:T(8,128)(2,1)}, f32[2,4,3,256,1]{3,2,1,4,0:T(4,128)}, s32[2,256]{1,0:T(2,128)}, s32[9,512]{1,0:T(8,128)}, /*i...) while((s32[]{:T(128)}, bf16[2,256,768]{2,1,0:T(8,128)(2,1)}, ...), condition=%wide.wide.region_4.5_spmd.clone, body=%wide.wide.region_1.4_spmd.clone.sunk | while | flops 3797485056 | bytes 182120720 | solution.py:110
  136.4 22.2 bitcast_reduce_fusion.3
  158.6 19.1 fusion.186
  177.7 23.6 %fusion.187 = bf16[4,3,256,64]{2,3,1,0:T(8,128)(2,1)} fusion(bf16[4608,4,64]{0,2,1:T(8,128)(2,1)} %get-tuple-element.878, f32[4,256,3,4608]{3,1,2,0:T(8,128)} %get-tuple-element.808, f32[4,3,256]{2,1,0:T(4,128)} %fusion.186, f32[4,3,256]{2,1,0:T(4,128)S(1)} %get-tuple-element.809, pred[256,4608]{1,0:T(8,128)(4,1)S(1)} %compare_and_fusion.7), kind=kOutput, calls=%fused_computation.20.clone.clone.1 | convolution fusion | flops 1882914816 | bytes 60579840 | tf_op jit(solution)/shard_map/while/body/eval_jaxpr/kgqs,skd->qkgd/dot_general | solution.py:104
  207.7 22.2 bitcast_reduce_fusion.3
  229.9 19.1 fusion.186
  249.0 23.6 %fusion.187 = bf16[4,3,256,64]{2,3,1,0:T(8,128)(2,1)} fusion(bf16[4608,4,64]{0,2,1:T(8,128)(2,1)} %get-tuple-element.878, f32[4,256,3,4608]{3,1,2,0:T(8,128)} %get-tuple-element.808, f32[4,3,256]{2,1,0:T(4,128)} %fusion.186, f32[4,3,256]{2,1,0:T(4,128)S(1)} %get-tuple-element.809, pred[256,4608]{1,0:T(8,128)(4,1)S(1)} %compare_and_fusion.7), kind=kOutput, calls=%fused_computation.20.clone.clone.1 | convolution fusion | flops 1882914816 | bytes 60579840 | tf_op jit(solution)/shard_map/while/body/eval_jaxpr/kgqs,skd->qkgd/dot_general | solution.py:104
  293.5 8.4 mul.298
  306.4 16.2 gather_fusion.1
  322.6 59.1 %all-reduce.5.cloned.1.call-done = f32[512,1536]{1,0:T(8,128)} async-done(((f32[512,1536]{1,0:T(8,128)}), f32[512,1536]{1,0:T(8,128)}) %all-reduce.5.cloned.1.call-update) | async-done | bytes 3145744 | tf_op jit(solution)/shard_map/psum | solution.py:113
  390.5 15.3 gather_fusion
  407.8 16.0 fusion.57
  423.8 17.1 multiply_convert_fusion.3
  441.0 17.0 fusion.111
  458.0 12.3 gather_fusion.2
  470.3 7.6 multiply_reduce_fusion
  483.0 18.6 multiply_convert_fusion.1
  501.6 18.3 fusion.112
  519.9 20.8 convolution_add_fusion
  540.7 12.3 gather_fusion.3
  553.1 5.9 broadcast_select_fusion.5
  558.9 8.5 reshape.517
  567.4 12.0 reduce_sum.155
  584.6 8.5 reshape.515
  593.0 12.0 multiply_reduce_fusion.1
  605.1 65.3 %all-reduce.7.cloned.1.call-done = f32[512,1536]{1,0:T(8,128)} async-done(((f32[512,1536]{1,0:T(8,128)}), f32[512,1536]{1,0:T(8,128)}) %all-reduce.7.cloned.1.call-update) | async-done | bytes 3145744 | tf_op jit(solution)/shard_map/psum | solution.py:179
  680.6 344.4 %while.33 = (s32[]{:T(128)}, f32[4608,4,64]{0,2,1:T(8,128)}, f32[4608,4,64]{0,2,1:T(8,128)}, bf16[2,256,768]{2,1,0:T(8,128)(2,1)}, bf16[2,256,4,3,64]{1,4,3,2,0:...) while((s32[]{:T(128)}, f32[4608,4,64]{0,2,1:T(8,128)}, ...), condition=%wide.wide.region_25.27_spmd.clone, body=%wide.wide.region_23.26_spmd.clone.sunk | while | flops 9281865728 | bytes 467079488 | solution.py:225
  685.1 22.2 fusion.197
  707.3 25.6 %fusion.201 = f32[4608,4,64]{0,2,1:T(8,128)} fusion(bf16[256,4,3,64]{0,3,2,1:T(8,128)(2,1)S(1)} %bitcast.342, f32[4,256,3,4608]{3,1,2,0:T(8,128)} %fusion.197, f32[4,3,256]{2,1,0:T(4,128)S(1)} %dynamic-slice_bitcast_fusion.3, pred[256,4608]{1,0:T(8,128)(4,1)S(1)} %compare_and_fusion.8, f32[4608,4,64]{0,2,1:T(8,128)} %get-tuple-element.900, ...), kind=kOutput, calls=%fused_computation.42.clone.clone.1 | convolution fusion | flops 1870921728 | bytes 67645440 | tf_op jit(solution)/shard_map/while/body/eval_jaxpr/kgqs,qkgd->skd/dot_general | solution.py:210
  732.9 41.9 %fusion.198 = (f32[4,3,256]{2,1,0:T(4,128)S(1)}, f32[4,256,3,4608]{3,1,2,0:T(8,128)}) fusion(f32[4,256,3,4608]{3,1,2,0:T(8,128)} %fusion.197, f32[4,3,256]{2,1,0:T(4,128)S(1)} %dynamic-slice_bitcast_fusion.3, pred[256,4608]{1,0:T(8,128)(4,1)S(1)} %compare_and_fusion.8, bf16[256,4,3,64]{0,3,2,1:T(8,128)(2,1)S(1)} %bitcast.343, ...), kind=kOutput, calls=%fused_computation.33.clone.clone.1 | convolution fusion | flops 1882715136 | bytes 117202944 | tf_op jit(solution)/shard_map/while/body/eval_jaxpr/qkgd,skd->kgqs/dot_general | solution.py:195
  774.8 44.7 %fusion.199 = bf16[4,3,256,4608]{3,2,1,0:T(8,128)(2,1)} fusion(f32[4,256,3,4608]{3,1,2,0:T(8,128)} %get-tuple-element.826, f32[4,256,3,4608]{3,1,2,0:T(8,128)} %fusion.197, f32[4,3,256]{2,1,0:T(4,128)S(1)} %get-tuple-element.827, f32[4,3,256]{2,1,0:T(4,128)S(1)} %dynamic-slice_bitcast_fusion.3, pred[256,4608]{1,0:T(8,128)(4,1)S(1)} %compare_and_fusion.8), kind=kLoop, calls=%fused_computation.35.clone.clone.1 | loop fusion | flops 84934656 | bytes 142761984 | tf_op jit(solution)/shard_map/while/body/eval_jaxpr/convert_element_type | solution.py:200
  819.5 14.2 fusion.202
  833.7 16.4 fusion.200
  855.6 22.0 fusion.197
  877.6 27.1 %fusion.201 = f32[4608,4,64]{0,2,1:T(8,128)} fusion(bf16[256,4,3,64]{0,3,2,1:T(8,128)(2,1)S(1)} %bitcast.342, f32[4,256,3,4608]{3,1,2,0:T(8,128)} %fusion.197, f32[4,3,256]{2,1,0:T(4,128)S(1)} %dynamic-slice_bitcast_fusion.3, pred[256,4608]{1,0:T(8,128)(4,1)S(1)} %compare_and_fusion.8, f32[4608,4,64]{0,2,1:T(8,128)} %get-tuple-element.900, ...), kind=kOutput, calls=%fused_computation.42.clone.clone.1 | convolution fusion | flops 1870921728 | bytes 67645440 | tf_op jit(solution)/shard_map/while/body/eval_jaxpr/kgqs,qkgd->skd/dot_general | solution.py:210
  904.8 41.9 %fusion.198 = (f32[4,3,256]{2,1,0:T(4,128)S(1)}, f32[4,256,3,4608]{3,1,2,0:T(8,128)}) fusion(f32[4,256,3,4608]{3,1,2,0:T(8,128)} %fusion.197, f32[4,3,256]{2,1,0:T(4,128)S(1)} %dynamic-slice_bitcast_fusion.3, pred[256,4608]{1,0:T(8,128)(4,1)S(1)} %compare_and_fusion.8, bf16[256,4,3,64]{0,3,2,1:T(8,128)(2,1)S(1)} %bitcast.343, ...), kind=kOutput, calls=%fused_computation.33.clone.clone.1 | convolution fusion | flops 1882715136 | bytes 117202944 | tf_op jit(solution)/shard_map/while/body/eval_jaxpr/qkgd,skd->kgqs/dot_general | solution.py:195
  946.7 44.7 %fusion.199 = bf16[4,3,256,4608]{3,2,1,0:T(8,128)(2,1)} fusion(f32[4,256,3,4608]{3,1,2,0:T(8,128)} %get-tuple-element.826, f32[4,256,3,4608]{3,1,2,0:T(8,128)} %fusion.197, f32[4,3,256]{2,1,0:T(4,128)S(1)} %get-tuple-element.827, f32[4,3,256]{2,1,0:T(4,128)S(1)} %dynamic-slice_bitcast_fusion.3, pred[256,4608]{1,0:T(8,128)(4,1)S(1)} %compare_and_fusion.8), kind=kLoop, calls=%fused_computation.35.clone.clone.1 | loop fusion | flops 84934656 | bytes 142761984 | tf_op jit(solution)/shard_map/while/body/eval_jaxpr/convert_element_type | solution.py:200
  991.4 14.2 fusion.202
  1005.6 17.8 fusion.200
  1024.9 6.9 reshape.520
  1031.8 8.5 constant_dynamic-update-slice_fusion.12
  1040.4 6.9 reshape.521
  1047.3 8.5 constant_dynamic-update-slice_fusion.11
  1055.8 6.6 convert.22
  1062.4 7.6 fusion.107
  1077.7 9.3 collective-permute-done.9
  1092.8 17.6 collective-permute-done.11
  1124.5 70.0 %collective-permute-done.15 = bf16[512,512]{0,1:T(8,128)(2,1)S(1)} collective-permute-done((bf16[512,512]{0,1:T(8,128)(2,1)S(1)}, bf16[512,512]{0,1:T(8,128)(2,1)S(1)}, u32[]{:S(2)}, u32[]{:S(2)}) %collective-permute-start.15) | collective-permute-done | bytes 524320 | tf_op jit(solution)/shard_map/ppermute | solution.py:19
  1213.2 18.5 convolution_convert_fusion
  1233.3 14.7 convolution_convert_fusion.1
  1249.6 14.7 convolution_convert_fusion.2
  1273.5 41.3 %reduce-scatter.18.cloned.1.call-done = bf16[96,256]{1,0:T(8,128)(2,1)} async-done(((bf16[1536,256]{1,0:T(8,128)(2,1)}), bf16[96,256]{1,0:T(8,128)(2,1)}) %reduce-scatter.18.cloned.1.call-update) | async-done | bytes 49168 | tf_op jit(solution)/shard_map/reduce_scatter | solution.py:277
  1316.2 64.6 %reduce-scatter.20.cloned.1.call-done = bf16[768,96]{0,1:T(8,128)(2,1)} async-done(((bf16[768,1536]{0,1:T(8,128)(2,1)}), bf16[768,96]{0,1:T(8,128)(2,1)}) %reduce-scatter.20.cloned.1.call-update) | async-done | bytes 147472 | tf_op jit(solution)/shard_map/reduce_scatter | solution.py:280
  1382.5 64.1 %reduce-scatter.14.cloned.1.call-done = bf16[96,768]{1,0:T(8,128)(2,1)} async-done(((bf16[1536,768]{1,0:T(8,128)(2,1)}), bf16[96,768]{1,0:T(8,128)(2,1)}) %reduce-scatter.14.cloned.1.call-update) | async-done | bytes 147472 | tf_op jit(solution)/shard_map/reduce_scatter | solution.py:271
  1448.2 25.8 %reduce-scatter.12.cloned.1.call-done = bf16[256,1536]{1,0:T(8,128)(2,1)} async-done(((bf16[512,1536]{1,0:T(8,128)(2,1)}), bf16[256,1536]{1,0:T(8,128)(2,1)}) %reduce-scatter.12.cloned.1.call-update) | async-done | bytes 786448 | tf_op jit(solution)/shard_map/reduce_scatter | solution.py:260
  1479.8 39.5 %all-reduce = (f32[1536]{0:T(1024)}, f32[1536]{0:T(1024)}) all-reduce(f32[1536]{0:T(1024)S(1)} %get-tuple-element.446, f32[1536]{0:T(1024)S(1)} %fusion.71), channel_id=1, replica_groups=mesh['dp'=16,'tensor'=2] {'dp','tensor'}, use_global_device_ids=true, to_apply=%region_29.31 | all-reduce | flops 3072 | bytes 24576 | tf_op jit(solution)/shard_map/psum | solution.py:267
  1519.3 202.8 %reduce-scatter.26.cloned.1.call-done = bf16[1,512,1536]{2,1,0:T(8,128)(2,1)} async-done(((bf16[16,512,1536]{2,1,0:T(8,128)(2,1)}), bf16[1,512,1536]{2,1,0:T(8,128)(2,1)}) %reduce-scatter.26.cloned.1.call-update) | async-done | bytes 1572880 | tf_op jit(solution)/shard_map/reduce_scatter | solution.py:289
  1725.8 243.3 %reduce-scatter.24.cloned.1.call-done = bf16[1,1536,512]{2,1,0:T(8,128)(2,1)} async-done(((bf16[16,1536,512]{2,1,0:T(8,128)(2,1)}), bf16[1,1536,512]{2,1,0:T(8,128)(2,1)}) %reduce-scatter.24.cloned.1.call-update) | async-done | bytes 1572880 | tf_op jit(solution)/shard_map/reduce_scatter | solution.py:286
  1972.6 243.6 %reduce-scatter.22.cloned.1.call-done = bf16[1,1536,512]{2,1,0:T(8,128)(2,1)} async-done(((bf16[16,1536,512]{2,1,0:T(8,128)(2,1)}), bf16[1,1536,512]{2,1,0:T(8,128)(2,1)}) %reduce-scatter.22.cloned.1.call-update) | async-done | bytes 1572880 | tf_op jit(solution)/shard_map/reduce_scatter | solution.py:283
  2219.8 122.2 %all-reduce.9.cloned.1.call-done = f32[1536,16]{0,1:T(8,128)} async-done(((f32[1536,16]{0,1:T(8,128)}), f32[1536,16]{0,1:T(8,128)}) %all-reduce.9.cloned.1.call-update) | async-done | bytes 98320 | tf_op jit(solution)/shard_map/psum | solution.py:267
  (332 shorter events, 223.7 us)
Async XLA Ops:
  7.2 268.0 %copy-start = (bf16[768,1536]{1,0:T(8,128)(2,1)S(1)}, bf16[768,1536]{1,0:T(8,128)(2,1)}, u32[]{:S(2)}) copy-start(bf16[768,1536]{1,0:T(8,128)(2,1)} %param.25) | copy-start | bytes 7077892
  7.2 4.4 copy-start.41
  7.2 4.4 copy-start.23
  7.2 374.4 %all-reduce.5.cloned.1.call-start = ((), (), s32[]{:S(2)}) async-start(), calls=%async_computation.9 | async-start | bytes 6291456 | tf_op jit(solution)/shard_map/psum | solution.py:113
  7.3 4.4 copy-start.14
  9.2 40.3 %copy-start.45 = (f32[512]{0:T(512)}, f32[512]{0:T(512)S(1)}, u32[]{:S(2)}) copy-start(f32[512]{0:T(512)S(1)} %add_rsqrt_fusion.1) | copy-start | bytes 6148
  14.0 113.9 %collective-permute-start.4 = (bf16[512,512]{0,1:T(8,128)(2,1)}, bf16[512,512]{0,1:T(8,128)(2,1)}, u32[]{:S(2)}, u32[]{:S(2)}) collective-permute-start(bf16[512,512]{0,1:T(8,128)(2,1)} %pad_maximum_fusion), channel_id=1, source_target_pairs={{0,8},{2,10},{4,12},{6,14},{8,16},{10,18},{12,20},{14,22},{16,24},... | collective-permute-start | bytes 1572872 | tf_op jit(solution)/shard_map/ppermute | solution.py:19
  19.7 107.1 %collective-permute-start.3 = (bf16[512,512]{0,1:T(8,128)(2,1)}, bf16[512,512]{0,1:T(8,128)(2,1)}, u32[]{:S(2)}, u32[]{:S(2)}) collective-permute-start(bf16[512,512]{0,1:T(8,128)(2,1)} %pad_maximum_fusion), channel_id=1, source_target_pairs={{0,10},{2,12},{4,14},{6,16},{8,18},{10,20},{12,22},{14,24},{16,26}... | collective-permute-start | bytes 1572872 | tf_op jit(solution)/shard_map/ppermute | solution.py:19
  22.4 77.5 %collective-permute-start.2 = (bf16[512,512]{0,1:T(8,128)(2,1)}, bf16[512,512]{0,1:T(8,128)(2,1)}, u32[]{:S(2)}, u32[]{:S(2)}) collective-permute-start(bf16[512,512]{0,1:T(8,128)(2,1)} %pad_maximum_fusion), channel_id=1, source_target_pairs={{0,12},{2,14},{4,16},{6,18},{8,20},{10,22},{12,24},{14,26},{16,28}... | collective-permute-start | bytes 1572872 | tf_op jit(solution)/shard_map/ppermute | solution.py:19
  26.8 51.6 %collective-permute-start.1 = (bf16[512,512]{0,1:T(8,128)(2,1)}, bf16[512,512]{0,1:T(8,128)(2,1)}, u32[]{:S(2)}, u32[]{:S(2)}) collective-permute-start(bf16[512,512]{0,1:T(8,128)(2,1)} %pad_maximum_fusion), channel_id=1, source_target_pairs={{0,14},{2,16},{4,18},{6,20},{8,22},{10,24},{12,26},{14,28},{16,30}... | collective-permute-start | bytes 1572872 | tf_op jit(solution)/shard_map/ppermute | solution.py:19
  28.9 46.5 %collective-permute-start = (bf16[512,512]{0,1:T(8,128)(2,1)}, bf16[512,512]{0,1:T(8,128)(2,1)}, u32[]{:S(2)}, u32[]{:S(2)}) collective-permute-start(bf16[512,512]{0,1:T(8,128)(2,1)} %pad_maximum_fusion), channel_id=1, source_target_pairs={{0,16},{2,18},{4,20},{6,22},{8,24},{10,26},{12,28},{14,30},{1,17},... | collective-permute-start | bytes 1572872 | tf_op jit(solution)/shard_map/ppermute | solution.py:19
  61.9 67.3 %copy-start.18 = (bf16[512,256]{0,1:T(8,128)(2,1)S(1)}, bf16[512,256]{0,1:T(8,128)(2,1)}, u32[]{:S(2)}) copy-start(bf16[512,256]{0,1:T(8,128)(2,1)} %copy-done.17) | copy-start | bytes 786436
  75.4 53.6 %collective-permute-start.5 = (bf16[512,512]{0,1:T(8,128)(2,1)}, bf16[512,512]{0,1:T(8,128)(2,1)S(1)}, u32[]{:S(2)}, u32[]{:S(2)}) collective-permute-start(bf16[512,512]{0,1:T(8,128)(2,1)} %pad_maximum_fusion), channel_id=1, source_target_pairs={{0,6},{2,8},{4,10},{6,12},{8,14},{10,16},{12,18},{14,20},{16,22},{... | collective-permute-start | bytes 1572872 | tf_op jit(solution)/shard_map/ppermute | solution.py:19
  78.5 50.6 %collective-permute-start.6 = (bf16[512,512]{0,1:T(8,128)(2,1)}, bf16[512,512]{0,1:T(8,128)(2,1)S(1)}, u32[]{:S(2)}, u32[]{:S(2)}) collective-permute-start(bf16[512,512]{0,1:T(8,128)(2,1)} %pad_maximum_fusion), channel_id=1, source_target_pairs={{0,4},{2,6},{4,8},{6,10},{8,12},{10,14},{12,16},{14,18},{16,20},{1... | collective-permute-start | bytes 1572872 | tf_op jit(solution)/shard_map/ppermute | solution.py:19
  99.8 29.3 %collective-permute-start.7 = (bf16[512,512]{0,1:T(8,128)(2,1)}, bf16[512,512]{0,1:T(8,128)(2,1)S(1)}, u32[]{:S(2)}, u32[]{:S(2)}) collective-permute-start(bf16[512,512]{0,1:T(8,128)(2,1)} %pad_maximum_fusion), channel_id=1, source_target_pairs={{0,2},{2,4},{4,6},{6,8},{8,10},{10,12},{12,14},{14,16},{16,18},{18... | collective-permute-start | bytes 1572872 | tf_op jit(solution)/shard_map/ppermute | solution.py:19
  177.7 23.6 %copy-start.16 = (f32[4,3,256]{2,1,0:T(4,128)S(1)}, f32[4,3,256]{2,1,0:T(4,128)}, u32[]{:S(2)}) copy-start(f32[4,3,256]{2,1,0:T(4,128)} %fusion.186) | copy-start | bytes 36868 | tf_op jit(solution)/shard_map/while
  177.7 23.6 %copy-start.31 = (f32[2,4,3,256,1]{3,2,1,4,0:T(4,128)S(1)}, f32[2,4,3,256,1]{3,2,1,4,0:T(4,128)}, u32[]{:S(2)}) copy-start(f32[2,4,3,256,1]{3,2,1,4,0:T(4,128)} %get-tuple-element.860) | copy-start | bytes 73732 | tf_op jit(solution)/shard_map/while
  249.0 23.6 %copy-start.16 = (f32[4,3,256]{2,1,0:T(4,128)S(1)}, f32[4,3,256]{2,1,0:T(4,128)}, u32[]{:S(2)}) copy-start(f32[4,3,256]{2,1,0:T(4,128)} %fusion.186) | copy-start | bytes 36868 | tf_op jit(solution)/shard_map/while
  249.0 23.6 %copy-start.31 = (f32[2,4,3,256,1]{3,2,1,4,0:T(4,128)S(1)}, f32[2,4,3,256,1]{3,2,1,4,0:T(4,128)}, u32[]{:S(2)}) copy-start(f32[2,4,3,256,1]{3,2,1,4,0:T(4,128)} %get-tuple-element.860) | copy-start | bytes 73732 | tf_op jit(solution)/shard_map/while
  275.2 4.5 copy-start.40
  279.4 390.9 %all-reduce.7.cloned.1.call-start = ((), (), s32[]{:S(2)}) async-start(), calls=%async_computation.11 | async-start | bytes 6291456 | tf_op jit(solution)/shard_map/psum | solution.py:179
  306.3 75.3 %copy-start.46 = (f32[512]{0:T(512)S(1)}, f32[512]{0:T(512)}, u32[]{:S(2)}) copy-start(f32[512]{0:T(512)} %copy-done.45) | copy-start | bytes 6148
  322.5 160.5 %copy-start.38 = (pred[16,128]{1,0:T(8,128)(4,1)}, pred[16,128]{1,0:T(8,128)(4,1)S(1)}, u32[]{:S(2)}) copy-start(pred[16,128]{1,0:T(8,128)(4,1)S(1)} %and_bitcast_fusion) | copy-start | bytes 6148
  322.6 65.3 %copy-start.36 = (f32[1536]{0:T(1024)S(1)}, f32[1536]{0:T(1024)}, u32[]{:S(2)}) copy-start(f32[1536]{0:T(1024)} %param.26) | copy-start | bytes 18436
  386.2 19.6 copy-start.43
  390.5 15.3 copy-start.33
  441.0 17.0 copy-start.8
  478.5 100.9 %copy-start.27 = (f32[512,16]{0,1:T(8,128)}, f32[512,16]{0,1:T(8,128)S(1)}, u32[]{:S(2)}) copy-start(f32[512,16]{0,1:T(8,128)S(1)} %select_reduce_fusion) | copy-start | bytes 98308
  483.0 18.6 copy-start.34
  501.6 18.3 copy-start.11
  579.4 5.1 copy-start.30
  584.5 684.8 %reduce-scatter.10.cloned.1.call-start = ((), (), s32[]{:S(2)}) async-start(), calls=%async_computation.10 | async-start | bytes 2359296 | tf_op jit(solution)/shard_map/reduce_scatter | solution.py:149
  593.0 77.4 %copy-start.37 = (f32[1536]{0:T(1024)S(1)}, f32[1536]{0:T(1024)}, u32[]{:S(2)}) copy-start(f32[1536]{0:T(1024)} %param.26) | copy-start | bytes 18436
  605.0 68.7 %copy-start.44 = (f32[512]{0:T(512)S(1)}, f32[512]{0:T(512)}, u32[]{:S(2)}) copy-start(f32[512]{0:T(512)} %copy-done.43) | copy-start | bytes 6148
  605.1 666.9 %reduce-scatter.16.cloned.1.call-start = ((), (), s32[]{:S(2)}) async-start(), calls=%async_computation.14 | async-start | bytes 835584 | tf_op jit(solution)/shard_map/reduce_scatter | solution.py:274
  670.4 3.7 copy-start.4
  670.4 4.7 copy-start.6
  680.7 26.6 %copy-start.25 = (s32[4608]{0:T(1024)}, s32[4608]{0:T(1024)S(1)}, u32[]{:S(2)}) copy-start(s32[4608]{0:T(1024)S(1)} %get-tuple-element.927) | copy-start | bytes 55300 | tf_op jit(solution)/shard_map/while
  833.7 16.6 copy-start.20
  833.7 17.5 copy-start.26
  851.2 26.4 %copy-start.25 = (s32[4608]{0:T(1024)}, s32[4608]{0:T(1024)S(1)}, u32[]{:S(2)}) copy-start(s32[4608]{0:T(1024)S(1)} %get-tuple-element.927) | copy-start | bytes 55300 | tf_op jit(solution)/shard_map/while
  1005.6 18.0 copy-start.20
  1005.6 19.0 copy-start.26
  1070.3 16.7 collective-permute-start.9
  1071.6 19.9 collective-permute-start.10
  1073.0 37.3 %collective-permute-start.11 = (bf16[512,512]{0,1:T(8,128)(2,1)S(1)}, bf16[512,512]{0,1:T(8,128)(2,1)S(1)}, u32[]{:S(2)}, u32[]{:S(2)}) collective-permute-start(bf16[512,512]{0,1:T(8,128)(2,1)S(1)} %bitcast.363), channel_id=1, source_target_pairs={{8,0},{10,2},{12,4},{14,6},{16,8},{18,10},{20,12},{22,14},{24,16},... | collective-permute-start | bytes 1572872 | tf_op jit(solution)/shard_map/ppermute | solution.py:19
  1075.0 120.1 %copy-start.15 = (bf16[512,1536]{1,0:T(8,128)(2,1)S(1)}, bf16[512,1536]{1,0:T(8,128)(2,1)}, u32[]{:S(2)}) copy-start(bf16[512,1536]{1,0:T(8,128)(2,1)} %param.20) | copy-start | bytes 4718596
  1075.0 120.1 %copy-start.42 = (f32[1536]{0:T(1024)S(1)}, f32[1536]{0:T(1024)}, u32[]{:S(2)}) copy-start(f32[1536]{0:T(1024)} %param.21) | copy-start | bytes 18436
  1075.0 120.1 %copy-start.47 = (f32[512]{0:T(512)S(1)}, f32[512]{0:T(512)}, u32[]{:S(2)}) copy-start(f32[512]{0:T(512)} %copy-done.45) | copy-start | bytes 6148
  1075.0 42.3 %collective-permute-start.12 = (bf16[512,512]{0,1:T(8,128)(2,1)S(1)}, bf16[512,512]{0,1:T(8,128)(2,1)S(1)}, u32[]{:S(2)}, u32[]{:S(2)}) collective-permute-start(bf16[512,512]{0,1:T(8,128)(2,1)S(1)} %bitcast.364), channel_id=1, source_target_pairs={{10,0},{12,2},{14,4},{16,6},{18,8},{20,10},{22,12},{24,14},{26,16}... | collective-permute-start | bytes 1572872 | tf_op jit(solution)/shard_map/ppermute | solution.py:19
  1076.4 44.2 %collective-permute-start.13 = (bf16[512,512]{0,1:T(8,128)(2,1)S(1)}, bf16[512,512]{0,1:T(8,128)(2,1)S(1)}, u32[]{:S(2)}, u32[]{:S(2)}) collective-permute-start(bf16[512,512]{0,1:T(8,128)(2,1)S(1)} %bitcast.362), channel_id=1, source_target_pairs={{12,0},{14,2},{16,4},{18,6},{20,8},{22,10},{24,12},{26,14},{28,16}... | collective-permute-start | bytes 1572872 | tf_op jit(solution)/shard_map/ppermute | solution.py:19
  1087.0 37.5 %collective-permute-start.14 = (bf16[512,512]{0,1:T(8,128)(2,1)S(1)}, bf16[512,512]{0,1:T(8,128)(2,1)S(1)}, u32[]{:S(2)}, u32[]{:S(2)}) collective-permute-start(bf16[512,512]{0,1:T(8,128)(2,1)S(1)} %bitcast.360), channel_id=1, source_target_pairs={{14,0},{16,2},{18,4},{20,6},{22,8},{24,10},{26,12},{28,14},{30,16}... | collective-permute-start | bytes 1572872 | tf_op jit(solution)/shard_map/ppermute | solution.py:19
  1091.5 102.9 %collective-permute-start.15 = (bf16[512,512]{0,1:T(8,128)(2,1)S(1)}, bf16[512,512]{0,1:T(8,128)(2,1)S(1)}, u32[]{:S(2)}, u32[]{:S(2)}) collective-permute-start(bf16[512,512]{0,1:T(8,128)(2,1)S(1)} %bitcast.359), channel_id=1, source_target_pairs={{16,0},{18,2},{20,4},{22,6},{24,8},{26,10},{28,12},{30,14},{17,1},... | collective-permute-start | bytes 1572872 | tf_op jit(solution)/shard_map/ppermute | solution.py:19
  1110.4 84.0 %collective-permute-start.8 = (bf16[512,512]{0,1:T(8,128)(2,1)S(1)}, bf16[512,512]{0,1:T(8,128)(2,1)S(1)}, u32[]{:S(2)}, u32[]{:S(2)}) collective-permute-start(bf16[512,512]{0,1:T(8,128)(2,1)S(1)} %bitcast.358), channel_id=1, source_target_pairs={{2,0},{4,2},{6,4},{8,6},{10,8},{12,10},{14,12},{16,14},{18,16},{20... | collective-permute-start | bytes 1572872 | tf_op jit(solution)/shard_map/ppermute | solution.py:19
  1196.8 117.9 %reduce-scatter.18.cloned.1.call-start = ((), (), s32[]{:S(2)}) async-start(), calls=%async_computation.15 | async-start | bytes 835584 | tf_op jit(solution)/shard_map/reduce_scatter | solution.py:277
  1198.6 5.3 copy-start.22
  1198.6 182.3 %reduce-scatter.20.cloned.1.call-start = ((), (), s32[]{:S(2)}) async-start(), calls=%async_computation.16 | async-start | bytes 2506752 | tf_op jit(solution)/shard_map/reduce_scatter | solution.py:280
  1203.7 242.9 %reduce-scatter.14.cloned.1.call-start = ((), (), s32[]{:S(2)}) async-start(), calls=%async_computation.13 | async-start | bytes 2506752 | tf_op jit(solution)/shard_map/reduce_scatter | solution.py:271
  1206.9 267.1 %reduce-scatter.12.cloned.1.call-start = ((), (), s32[]{:S(2)}) async-start(), calls=%async_computation.12 | async-start | bytes 2359296 | tf_op jit(solution)/shard_map/reduce_scatter | solution.py:260
  1213.2 509.0 %reduce-scatter.26.cloned.1.call-start = ((), (), s32[]{:S(2)}) async-start(), calls=%async_computation.20 | async-start | bytes 26738688 | tf_op jit(solution)/shard_map/reduce_scatter | solution.py:289
  1231.7 737.3 %reduce-scatter.24.cloned.1.call-start = ((), (), s32[]{:S(2)}) async-start(), calls=%async_computation.19 | async-start | bytes 26738688 | tf_op jit(solution)/shard_map/reduce_scatter | solution.py:286
  1248.1 968.2 %reduce-scatter.22.cloned.1.call-start = ((), (), s32[]{:S(2)}) async-start(), calls=%async_computation.18 | async-start | bytes 26738688 | tf_op jit(solution)/shard_map/reduce_scatter | solution.py:283
  1264.3 1077.6 %all-reduce.9.cloned.1.call-start = ((), (), s32[]{:S(2)}) async-start(), calls=%async_computation.17 | async-start | bytes 196608 | tf_op jit(solution)/shard_map/psum | solution.py:267
  1722.1 621.4 %copy-start.1 = (bf16[768,1536]{1,0:T(8,128)(2,1)S(1)}, bf16[768,1536]{1,0:T(8,128)(2,1)}, u32[]{:S(2)}) copy-start(bf16[768,1536]{1,0:T(8,128)(2,1)} %param.25) | copy-start | bytes 7077892
  (19 other events, 33.2 us)
Sparse Core Ops, SparseCore 0:
  279.6 102.0 all-reduce.4
  584.6 85.7 all-reduce.6
  672.6 26.0 reduce-scatter.9
  1196.9 58.8 reduce-scatter.15
  1259.3 55.4 reduce-scatter.17
  1318.9 61.9 reduce-scatter.19
  1384.6 61.9 reduce-scatter.13
  1448.9 25.0 reduce-scatter.11
  1478.2 243.9 reduce-scatter.25
  1726.1 242.9 reduce-scatter.23
  1973.2 242.9 reduce-scatter.21
  2222.2 119.6 all-reduce.8
where the time goes:
time: 2360 us; the launch traced here: 2350 us
  waiting for transfers between devices  1250 us (53%)
  matrix products  530 us (22%)
  other arithmetic  233 us (10%)
  local copies, waits for them, and re-layouts  200 us (8%)
  starting transfers between devices  76.5 us (3%)
  blocking collectives  39.5 us (2%)
    reduce_scatter x1, waiting for transfers between devices, shards(): lax.psum_scatter(gate_grad.astype(jnp.bfloat16), 'dp', scatter_dimension=...  244 us
    reduce_scatter x1, waiting for transfers between devices, shards(): lax.psum_scatter(up_grad.astype(jnp.bfloat16), 'dp', scatter_dimension=0,...  243 us
    reduce_scatter x1, waiting for transfers between devices, shards(): lax.psum_scatter(down_grad.astype(jnp.bfloat16), 'dp', scatter_dimension=...  203 us
    psum x1, waiting for transfers between devices, shards(): lax.psum((gain_one_part, gain_two_part, router_part), ('dp', 'tensor'))  122 us
    ppermute x16, waiting for transfers between devices, from_behind(): return lax.ppermute(block, axis, route)  122 us
    convert_element_type x2, other arithmetic, attend_back(): grad_scores = (probs * (grad_probs - jnp.sum(probs * grad_probs, axis=-1,...  89.3 us
    dot_general x4, matrix products, masked_scores(): jnp.einsum('qkgd,skd->kgqs', q_blk, keys, preferred_element_type=jnp.floa...  88.7 us
    dot_general x2, matrix products, attend_back(): jnp.einsum('qkgd,skd->kgqs', grad_heads, values, preferred_element_type=j...  83.8 us
  transfers between devices with their start and end apart: 28, of which 18 were waited for; matrix products, arithmetic and copies ran while one was open for 25% of the time, Pallas kernels for 0%

commit v1 on v0

v1 whole, which is shorter than its diff:
```python
import functools

import jax
import jax.numpy as jnp
from jax import lax
from jax.experimental import pallas as pl
from jax.experimental.pallas import tpu as pltpu
from jax.sharding import PartitionSpec as P

HD = 64
PAIR = 2 * HD
CAP = 128
EPS = 1e-05
HIGH = lax.Precision.HIGHEST
NEG = -1000000000.0
BF = jnp.bfloat16
F32 = jnp.float32

NT = (((1,), (1,)), ((), ()))
TN = (((0,), (0,)), ((), ()))


def dot(a, b, dims=None):
    if dims is None:
        return jnp.dot(a, b, preferred_element_type=F32)
    return lax.dot_general(a, b, dims, preferred_element_type=F32)


def across(x, axis, mask):
    n = lax.axis_size(axis)
    return lax.ppermute(x, axis, [(i, i ^ mask) for i in range(n)])


def bits_of(n):
    return [1 << k for k in range(n.bit_length() - 1)]


def after(x, y):
    return lax.optimization_barrier((x, y))


def to_owner(x):
    return lax.all_to_all(x, "dp", 0, 0, tiled=True)


def norm_factor(value):
    return lax.rsqrt(jnp.mean(value * value, axis=-1, keepdims=True) + EPS)


def norm_back(unit, factor, gain, grad):
    inner = gain * grad
    return factor * (inner - unit * jnp.mean(unit * inner, axis=-1, keepdims=True))


def total(x):
    for axis in ("dp", "tensor"):
        for bit in bits_of(lax.axis_size(axis)):
            x = x + across(x, axis, bit)
    return x


def scatter_tensor(x):
    n = lax.axis_size("tensor")
    if n != 2:
        return lax.psum_scatter(x.astype(BF), "tensor", scatter_dimension=0, tiled=True).astype(F32)
    me = lax.axis_index("tensor")
    part = x.shape[0] // 2
    sent = lax.dynamic_slice_in_dim(x, (1 - me) * part, part, 0).astype(BF)
    own = lax.dynamic_slice_in_dim(x, me * part, part, 0)
    return own.astype(F32) + across(sent, "tensor", 1).astype(F32)


def gather_tensor(x, dim):
    n = lax.axis_size("tensor")
    if n != 2:
        return lax.all_gather(x, "tensor", axis=dim, tiled=True)
    other = across(x, "tensor", 1)
    low = lax.axis_index("tensor") == 0
    return jnp.concatenate([jnp.where(low, x, other), jnp.where(low, other, x)], dim)


def xor_blocks(blocks, index):
    for bit in bits_of(len(blocks)):
        crossed = (index & bit) != 0
        blocks = [jnp.where(crossed, blocks[s ^ bit], block) for s, block in enumerate(blocks)]
    return blocks


def columns_of(x, count):
    size = x.shape[1] // count
    return [x[:, s * size : (s + 1) * size] for s in range(count)]


def scatter_rows(x):
    n = lax.axis_size("dp")
    at = lax.axis_index("dp")
    bits = bits_of(n)
    x = x.astype(BF)
    if not bits:
        return x.astype(F32)
    x = halve_first(x, at, n)
    half = x.shape[1] // 2
    outs = []
    for piece, order in ((x[:, :half], bits[1:]), (x[:, half:], bits[2:] + bits[1:2])):
        outs.append(halve_rest(piece, at, order))
    return jnp.concatenate(outs, 1).astype(F32)


def halve_first(x, at, n):
    size = x.shape[0] // n
    view = x.reshape(n // 2, 2, size, x.shape[1])
    mine = at % 2

    def pick(which):
        return lax.dynamic_index_in_dim(view, which, 1, keepdims=False)

    return (pick(mine) + across(pick(1 - mine), "dp", 1)).reshape(-1, x.shape[1])


def halve_rest(x, at, order):
    left = sorted(order)
    for bit in order:
        high = 1
        for other in left:
            if other > bit:
                high *= 2
        view = x.reshape(high, 2, -1, x.shape[1])
        mine = (at // bit) % 2
        kept = lax.dynamic_index_in_dim(view, mine, 1, keepdims=False)
        sent = lax.dynamic_index_in_dim(view, 1 - mine, 1, keepdims=False)
        x = (kept + across(sent, "dp", bit)).reshape(-1, x.shape[1])
        left.remove(bit)
    return x


def join_heads(x):
    lines, heads, rows, size = x.shape
    return x.transpose(0, 2, 1, 3).reshape(lines, rows, heads * size)


def attend_kernel(
    heads, rows, lines, stride, meta, q_ref, kv_ref, start_ref, raw_ref, log_ref, m_s, l_s, acc_s
):
    slot = pl.program_id(0)
    place = meta[0]
    own = meta[1 + slot]
    low = meta[1 + lines + slot]
    clear = meta[1 + 2 * lines + slot]
    m_s[...] = jnp.full_like(m_s, -3e38)
    l_s[...] = jnp.zeros_like(l_s)
    acc_s[...] = jnp.zeros_like(acc_s)

    def step(blk, masked):
        x = blk ^ place
        kv = kv_ref[(x % stride) * lines + x // stride]
        if masked:
            shape = (rows, rows)
            key_pos = lax.broadcasted_iota(jnp.int32, shape, 0) + blk * rows
            q_pos = lax.broadcasted_iota(jnp.int32, shape, 1) + own * rows
            seen = (key_pos >= start_ref[0]) & (key_pos <= q_pos)
        for h in range(heads):
            s = dot(kv, q_ref[0, h], NT)
            if masked:
                s = jnp.where(seen, s, NEG)
            m_old = m_s[h : h + 1, :]
            m_new = jnp.maximum(m_old, jnp.max(s, axis=0, keepdims=True))
            p = jnp.exp(s - m_new)
            alpha = jnp.exp(m_old - m_new)
            l_s[h : h + 1, :] = l_s[h : h + 1, :] * alpha + jnp.sum(p, axis=0, keepdims=True)
            acc_s[h] = acc_s[h] * alpha + dot(kv, p.astype(BF), TN)
            m_s[h : h + 1, :] = m_new

    def body(blk, carry):
        full = (blk >= clear) & (blk < own)

        @pl.when(full)
        def _():
            step(blk, False)

        @pl.when(jnp.logical_not(full))
        def _():
            step(blk, True)

        return carry

    lax.fori_loop(low, own + 1, body, 0)
    for h in range(heads):
        raw_ref[0, h] = (acc_s[h] / l_s[h : h + 1, :]).T
    log_ref[0] = m_s[...] + jnp.log(l_s[...])


def attend(meta, qz, kv, start_row, stride):
    lines, heads, rows, _ = qz.shape
    blocks = kv.shape[0]
    grid_spec = pltpu.PrefetchScalarGridSpec(
        num_scalar_prefetch=1,
        grid=(lines,),
        in_specs=[
            pl.BlockSpec((1, heads, rows, PAIR), lambda i, m: (i, 0, 0, 0)),
            pl.BlockSpec((blocks, rows, PAIR), lambda i, m: (0, 0, 0)),
            pl.BlockSpec((1, 1, rows), lambda i, m: (i, 0, 0)),
        ],
        out_specs=[
            pl.BlockSpec((1, heads, rows, PAIR), lambda i, m: (i, 0, 0, 0)),
            pl.BlockSpec((1, 8, rows), lambda i, m: (i, 0, 0)),
        ],
        scratch_shapes=[
            pltpu.VMEM((8, rows), F32),
            pltpu.VMEM((8, rows), F32),
            pltpu.VMEM((heads, PAIR, rows), F32),
        ],
    )
    return pl.pallas_call(
        functools.partial(attend_kernel, heads, rows, lines, stride),
        grid_spec=grid_spec,
        out_shape=[
            jax.ShapeDtypeStruct((lines, heads, rows, PAIR), F32),
            jax.ShapeDtypeStruct((lines, 8, rows), F32),
        ],
        compiler_params=pltpu.CompilerParams(vmem_limit_bytes=48 * 1024 * 1024),
        cost_estimate=pl.CostEstimate(
            flops=36 * 4 * rows * rows * PAIR * 2, bytes_accessed=8 << 20, transcendentals=36 * rows * rows
        ),
        name="attend",
    )(meta, qz, kv, start_row)


def attend_back_kernel(
    heads, rows, lines, stride, meta, q_ref, g_ref, raw_ref, log_ref, start_ref, kv_ref,
    dq_ref, dkv_ref, dq_s, dkv_s, delta_s,
):
    slot = pl.program_id(0)
    place = meta[0]
    own = meta[1 + slot]
    low = meta[1 + lines + slot]
    clear = meta[1 + 2 * lines + slot]

    @pl.when(slot == 0)
    def _():
        dkv_s[...] = jnp.zeros_like(dkv_s)

    dq_s[...] = jnp.zeros_like(dq_s)
    for h in range(heads):
        prod = raw_ref[0, h] * g_ref[0, h].astype(F32)
        delta_s[h : h + 1, :] = jnp.sum(prod.T, axis=0, keepdims=True)

    def step(blk, masked):
        x = blk ^ place
        index = (x % stride) * lines + x // stride
        kv = kv_ref[index]
        if masked:
            shape = (rows, rows)
            key_pos = lax.broadcasted_iota(jnp.int32, shape, 0) + blk * rows
            q_pos = lax.broadcasted_iota(jnp.int32, shape, 1) + own * rows
            seen = (key_pos >= start_ref[0]) & (key_pos <= q_pos)
        for h in range(heads):
            q = q_ref[0, h]
            g = g_ref[0, h]
            s = dot(kv, q, NT)
            if masked:
                s = jnp.where(seen, s, NEG)
            p = jnp.exp(s - log_ref[0, h : h + 1, :])
            gp = dot(kv, g, NT)
            gs = (p * (gp - delta_s[h : h + 1, :])).astype(BF)
            part = dot(gs, q) + dot(p.astype(BF), g)
            dkv_s[index] += part
            dq_s[h] += dot(gs, kv, TN)

    def body(blk, carry):
        full = (blk >= clear) & (blk < own)

        @pl.when(full)
        def _():
            step(blk, False)

        @pl.when(jnp.logical_not(full))
        def _():
            step(blk, True)

        return carry

    lax.fori_loop(low, own + 1, body, 0)
    dq_ref[0] = (dq_s[...] * 0.125).astype(BF)

    @pl.when(slot == lines - 1)
    def _():
        dkv_ref[...] = dkv_s[...].astype(BF)


def attend_back(meta, qz, gz, raw, logs, start_row, kv, stride):
    lines, heads, rows, _ = qz.shape
    blocks = kv.shape[0]
    wide = pl.BlockSpec((1, heads, rows, PAIR), lambda i, m: (i, 0, 0, 0))
    whole = pl.BlockSpec((blocks, rows, PAIR), lambda i, m: (0, 0, 0))
    grid_spec = pltpu.PrefetchScalarGridSpec(
        num_scalar_prefetch=1,
        grid=(lines,),
        in_specs=[
            wide,
            wide,
            wide,
            pl.BlockSpec((1, 8, rows), lambda i, m: (i, 0, 0)),
            pl.BlockSpec((1, 1, rows), lambda i, m: (i, 0, 0)),
            whole,
        ],
        out_specs=[wide, whole],
        scratch_shapes=[
            pltpu.VMEM((heads, rows, PAIR), F32),
            pltpu.VMEM((blocks, rows, PAIR), F32),
            pltpu.VMEM((8, rows), F32),
        ],
    )
    return pl.pallas_call(
        functools.partial(attend_back_kernel, heads, rows, lines, stride),
        grid_spec=grid_spec,
        out_shape=[
            jax.ShapeDtypeStruct((lines, heads, rows, PAIR), BF),
            jax.ShapeDtypeStruct((blocks, rows, PAIR), BF),
        ],
        compiler_params=pltpu.CompilerParams(vmem_limit_bytes=56 * 1024 * 1024),
        cost_estimate=pl.CostEstimate(
            flops=36 * 10 * rows * rows * PAIR * 2, bytes_accessed=10 << 20, transcendentals=36 * rows * rows
        ),
        name="attend_back",
    )(meta, qz, gz, raw, logs, start_row, kv)


def experts_kernel(x_ref, g_ref, gate_ref, wg_ref, wu_ref, wd_ref, out_ref, back_ref, inner_ref):
    x = x_ref[0]
    g = g_ref[0]
    gate = gate_ref[0]
    gate_pre = dot(x, wg_ref[0])
    up_pre = dot(x, wu_ref[0])
    sigma = jax.nn.sigmoid(gate_pre)
    silu = gate_pre * sigma
    act = (silu * up_pre).astype(BF)
    out = dot(act, wd_ref[0])
    g_float = g.astype(F32)
    inner = jnp.sum(out * g_float, axis=-1, keepdims=True)
    inner_ref[0] = jnp.broadcast_to(inner, (x.shape[0], 128)).T[:8]
    out_ref[0] = (gate * out).astype(BF)
    grad_expert = (gate * g_float).astype(BF)
    grad_act = dot(grad_expert, wd_ref[0], NT)
    grad_gate = (grad_act * up_pre * sigma * (1.0 + gate_pre * (1.0 - sigma))).astype(BF)
    grad_up = (grad_act * silu).astype(BF)
    back_ref[0] = (dot(grad_gate, wg_ref[0], NT) + dot(grad_up, wu_ref[0], NT)).astype(BF)


def run_experts(x, g, gate, w_gate, w_up, w_down):
    experts, cap, width = x.shape
    hidden = w_gate.shape[2]

    def of(*shape):
        return pl.BlockSpec((1,) + shape, lambda e: (e, 0, 0))

    return pl.pallas_call(
        experts_kernel,
        grid=(experts,),
        in_specs=[
            of(cap, width),
            of(cap, width),
            of(cap, 1),
            of(width, hidden),
            of(width, hidden),
            of(hidden, width),
        ],
        out_specs=[of(cap, width), of(cap, width), of(8, cap)],
        out_shape=[
            jax.ShapeDtypeStruct((experts, cap, width), BF),
            jax.ShapeDtypeStruct((experts, cap, width), BF),
            jax.ShapeDtypeStruct((experts, 8, cap), F32),
        ],
        compiler_params=pltpu.CompilerParams(vmem_limit_bytes=48 * 1024 * 1024),
        cost_estimate=pl.CostEstimate(
            flops=experts * cap * width * hidden * 12,
            bytes_accessed=experts * width * (hidden * 6 + cap * 8),
            transcendentals=experts * cap * hidden,
        ),
        name="experts",
    )(x, g, gate, w_gate, w_up, w_down)


def shards(
    layer_in,
    norm1_gain,
    w_query,
    w_key,
    w_value,
    w_out,
    norm2_gain,
    router,
    w_gate,
    w_up,
    w_down,
    segments,
    routes,
    out_grad,
):
    rows, width = layer_in.shape
    kv_heads = w_key.shape[1] // HD
    group = w_query.shape[1] // HD // kv_heads
    q_cols = group * HD
    experts = w_gate.shape[0]
    dp = lax.axis_size("dp")
    place = lax.axis_index("dp")
    tensor_size = lax.axis_size("tensor")
    tensor_at = lax.axis_index("tensor")
    lines = kv_heads
    stride = dp // lines
    line = place // stride
    part = rows // tensor_size
    first = tensor_at * part
    cols = width // tensor_size

    names = jnp.arange(experts, dtype=jnp.int32)
    named = jnp.any(routes[:, :, None] == names[None, None, :], axis=1)
    earlier = jnp.tril(jnp.ones((rows, rows), BF), -1)
    slots = jnp.where(named, dot(earlier, named.astype(BF)).astype(jnp.int32), -1)
    in_slot = slots.T[:, None, :] == jnp.arange(CAP, dtype=jnp.int32)[None, :, None]
    to_slots = in_slot.astype(BF).reshape(experts * CAP, rows)
    from_slots = (
        (slots[:, :, None] == jnp.arange(CAP, dtype=jnp.int32)[None, None, :])
        .astype(BF)
        .reshape(rows, experts * CAP)
    )

    def halves(x):
        own = lax.dynamic_slice_in_dim(x, tensor_at * cols, cols, 2)
        return own[..., : cols // 2], own[..., cols // 2 :]

    def whole_columns(one, two):
        size = one.shape[2] // tensor_size
        pieces = []
        for t in range(tensor_size):
            pieces += [one[..., t * size : (t + 1) * size], two[..., t * size : (t + 1) * size]]
        return jnp.concatenate(pieces, 2)

    q_blocks = place ^ (jnp.arange(lines, dtype=jnp.int32) * stride)
    seg_query = jnp.stack(
        [lax.dynamic_slice_in_dim(segments, q_blocks[s] * rows, rows, 0) for s in range(lines)]
    )
    starts = jnp.sum(
        (segments[None, None, :] < seg_query[:, :, None]).astype(jnp.int32), axis=-1
    )
    meta = jnp.concatenate(
        [place[None], q_blocks, starts[:, 0] // rows, (starts[:, -1] + rows - 1) // rows]
    ).astype(jnp.int32)

    lined = [xor_blocks(columns_of(w, lines), line) for w in (w_key, w_value, w_query)]
    w_kv = jnp.concatenate([w for pair in zip(*lined[:2]) for w in pair], 1)
    w_q = jnp.concatenate(lined[2], 1)
    w_o = jnp.concatenate(
        xor_blocks([w_out[s * q_cols : (s + 1) * q_cols] for s in range(lines)], line), 0
    )

    in_float = layer_in.astype(F32)
    factor_one = norm_factor(in_float)
    unit_one = in_float * factor_one
    normed_in = (unit_one * norm1_gain).astype(BF)
    kv_mine = dot(normed_in, w_kv).astype(BF)
    kv_mine, normed_late = after(kv_mine, normed_in)
    q_mine = dot(normed_late, w_q).astype(BF)

    def to_lines(x, size):
        return jnp.stack(
            [
                x[:, s * size : (s + 1) * size]
                if s == 0
                else across(x[:, s * size : (s + 1) * size], "dp", s * stride)
                for s in range(lines)
            ]
        )

    kv = to_lines(kv_mine, PAIR)
    kv = kv.reshape((1,) + kv.shape)
    for bit in reversed(bits_of(stride)):
        kv = jnp.stack([kv, across(kv, "dp", bit)], 1).reshape((-1,) + kv.shape[1:])
    kv = kv.reshape(dp, rows, PAIR)
    q = to_lines(q_mine, q_cols) * jnp.asarray(0.125, BF)
    q_heads = q.reshape(lines, rows, group, HD).transpose(0, 2, 1, 3)
    nothing = jnp.zeros_like(q_heads)
    q_wide = jnp.concatenate([q_heads, nothing], 3)
    g_slots = dot(to_slots, out_grad).astype(BF).reshape(experts, CAP, width)
    g_sent, kv = after(halves(g_slots), kv)
    g_first = to_owner(g_sent[0])
    raw, logs = attend(meta, q_wide, kv, starts[:, None, :], stride)
    raw, g_first = after(raw, g_first)
    mixed_far = join_heads(raw[..., HD:].astype(BF))

    def from_lines(x):
        return [x[s] if s == 0 else across(x[s], "dp", s * stride) for s in range(lines)]

    mixed = jnp.concatenate(from_lines(mixed_far), 1)
    g_late, mixed = after(g_sent[1], mixed)
    g_second = to_owner(g_late)
    attn = scatter_tensor(dot(mixed, w_o))
    hidden = lax.dynamic_slice_in_dim(layer_in, first, part, 0).astype(F32) + attn
    factor_two = norm_factor(hidden)
    unit_two = hidden * factor_two
    normed_mid = gather_tensor((unit_two * norm2_gain).astype(BF), 0)

    logits = dot(normed_mid, router)
    peak = jnp.max(jnp.where(named, logits, -jnp.inf), axis=1, keepdims=True)
    expo = jnp.where(named, jnp.exp(jnp.where(named, logits - peak, 0.0)), 0.0)
    gates = expo / jnp.sum(expo, axis=1, keepdims=True)
    slot_gate = jnp.sum(jnp.where(in_slot, gates.T[:, None, :], 0.0), axis=-1)

    x_slots = dot(to_slots, normed_mid).astype(BF).reshape(experts, CAP, width)
    x_sent = halves(x_slots)
    x_early, g_second = after(x_sent[0], g_second)
    x_first = to_owner(x_early)
    gate_owned = to_owner(slot_gate)
    g_first, x_slots = after(g_first, x_slots)
    g_first = gather_tensor(g_first, 2)

    out_slots, back_slots, inner_slots = run_experts(
        x_slots, g_slots, slot_gate[:, :, None], w_gate, w_up, w_down
    )
    back_slots, (x_first, g_first) = after(back_slots, (x_first, g_first))
    x_late, back_slots = after(x_sent[1], back_slots)
    x_second = to_owner(x_late)
    moe_part = dot(from_slots, out_slots.reshape(experts * CAP, width))
    grad_gates = jnp.sum(
        jnp.where(
            slots[:, :, None] == jnp.arange(CAP, dtype=jnp.int32)[None, None, :],
            inner_slots[None, :, 0, :],
            0.0,
        ),
        axis=-1,
    )
    grad_logits = gates * (grad_gates - jnp.sum(gates * grad_gates, axis=-1, keepdims=True))
    router_part = lax.dot_general(
        grad_logits, normed_mid.astype(F32), TN, precision=HIGH, preferred_element_type=F32
    )
    grad_mid_part = dot(from_slots, back_slots.reshape(experts * CAP, width)) + lax.dot_general(
        grad_logits, router.astype(F32), NT, precision=HIGH, preferred_element_type=F32
    )
    grad_mid = scatter_tensor(grad_mid_part)
    moe_part, grad_mid = after(moe_part, grad_mid)
    layer_out = (hidden + scatter_tensor(moe_part)).astype(BF)
    gain_two_part = jnp.sum(grad_mid * unit_two, axis=0)
    grad_rows = lax.dynamic_slice_in_dim(out_grad, first, part, 0).astype(F32)
    grad_hidden = grad_rows + norm_back(unit_two, factor_two, norm2_gain, grad_mid)
    hidden_low = gather_tensor(grad_hidden.astype(BF), 0)
    (x_first, g_second), hidden_low = after((x_first, g_second), hidden_low)
    x_first = gather_tensor(x_first, 2)
    g_second = gather_tensor(g_second, 2)
    g_owned = whole_columns(g_first, g_second)
    grad_mixed = dot(hidden_low, w_o, NT).astype(BF)
    small = total(jnp.concatenate([router_part, gain_two_part[None]], 0))

    g = to_lines(grad_mixed, q_cols)
    g_heads = g.reshape(lines, rows, group, HD).transpose(0, 2, 1, 3)
    g_wide = jnp.concatenate([nothing, g_heads], 3)
    dq_far, dkv = attend_back(meta, q_wide, g_wide, raw, logs, starts[:, None, :], kv, stride)

    dkv, x_second = after(dkv, x_second)
    x_owned = whole_columns(x_first, gather_tensor(x_second, 2))

    def reduce_back(x):
        for bit in bits_of(stride):
            view = x.reshape((x.shape[0] // 2, 2) + x.shape[1:])
            x = view[:, 0] + across(view[:, 1], "dp", bit)
        return x[0]

    mixed_true = jnp.concatenate(xor_blocks(columns_of(mixed, lines), line), 1)
    proj_out = scatter_rows(dot(hidden_low, mixed_true, TN)).T

    dkv = from_lines(reduce_back(dkv.reshape(stride, lines, rows, PAIR)))
    dq = from_lines(join_heads(dq_far[..., :HD]))
    dkv = jnp.concatenate(dkv, 1)
    dq = jnp.concatenate(dq, 1)
    grad_in_part = dot(dq, w_q, NT) + dot(dkv, w_kv, NT)
    grad_in_rows = scatter_tensor(grad_in_part)
    dqkv = jnp.concatenate(
        xor_blocks(columns_of(dkv, lines), line) + xor_blocks(columns_of(dq, lines), line), 1
    )
    dqkv, (x_owned, g_owned) = after(dqkv, (x_owned, g_owned))
    weight_grad = scatter_rows(dot(normed_in, dqkv, TN))
    kv_grad = weight_grad[:, : lines * PAIR].reshape(-1, lines, 2, HD)
    key_out = kv_grad[:, :, 0].reshape(-1, lines * HD)
    value_out = kv_grad[:, :, 1].reshape(-1, lines * HD)
    query_out = weight_grad[:, lines * PAIR :]

    factor_rows = lax.dynamic_slice_in_dim(factor_one, first, part, 0)
    unit_rows = lax.dynamic_slice_in_dim(in_float, first, part, 0) * factor_rows
    input_grad = grad_hidden + norm_back(unit_rows, factor_rows, norm1_gain, grad_in_rows)
    gain_one_grad = total(jnp.sum(grad_in_rows * unit_rows, axis=0)[None])[0]
    gain_two_grad = small[experts]
    router_grad = small[:experts].T

    held = experts // dp
    wg = lax.dynamic_slice_in_dim(w_gate, place * held, held, 0)
    wu = lax.dynamic_slice_in_dim(w_up, place * held, held, 0)
    wd = lax.dynamic_slice_in_dim(w_down, place * held, held, 0)
    grad_outs = []
    for e in range(held):
        x = x_owned.reshape(dp, held, CAP, width)[:, e].reshape(dp * CAP, width)
        gx = g_owned.reshape(dp, held, CAP, width)[:, e].reshape(dp * CAP, width)
        gate = gate_owned.reshape(dp, held, CAP)[:, e].reshape(dp * CAP, 1)
        gate_pre = dot(x, wg[e])
        up_pre = dot(x, wu[e])
        sigma = jax.nn.sigmoid(gate_pre)
        silu = gate_pre * sigma
        act = (silu * up_pre).astype(BF)
        grad_expert = (gate * gx.astype(F32)).astype(BF)
        grad_act = dot(grad_expert, wd[e], NT)
        grad_gate = (grad_act * up_pre * sigma * (1.0 + gate_pre * (1.0 - sigma))).astype(BF)
        grad_up = (grad_act * silu).astype(BF)
        grad_outs.append((dot(x, grad_gate, TN), dot(x, grad_up, TN), dot(act, grad_expert, TN)))
    gate_out, up_out, down_out = (jnp.stack(each) for each in zip(*grad_outs))
    return (
        layer_out,
        input_grad,
        gain_one_grad,
        query_out,
        key_out,
        value_out,
        proj_out,
        gain_two_grad,
        router_grad,
        gate_out,
        up_out,
        down_out,
    )


def solution(mesh):
    in_specs = (
        P("dp", None),
        P(),
        P(None, "tensor"),
        P(None, "tensor"),
        P(None, "tensor"),
        P("tensor", None),
        P(),
        P(),
        P(None, None, "tensor"),
        P(None, None, "tensor"),
        P(None, "tensor", None),
        P(),
        P("dp", None),
        P("dp", None),
    )
    out_specs = (
        P(("dp", "tensor"), None),
        P(("dp", "tensor"), None),
        P(),
        P("dp", "tensor"),
        P("dp", "tensor"),
        P("dp", "tensor"),
        P("tensor", "dp"),
        P(),
        P(),
        P("dp", None, "tensor"),
        P("dp", None, "tensor"),
        P("dp", "tensor", None),
    )
    return jax.shard_map(shards, mesh=mesh, in_specs=in_specs, out_specs=out_specs, check_vma=False)
```

time: 2360 us -> 694 us (0.29)
  waiting for transfers between devices: 1250 us -> 205 us
  matrix products: 530 us -> 89.6 us
  other arithmetic: 233 us -> 77.5 us
  local copies, waits for them, and re-layouts: 200 us -> 68.6 us
  Pallas kernels: 0 us -> 101 us
  starting transfers between devices: 76.5 us -> 144 us
  blocking collectives: 39.5 us -> 0 us
    reduce_scatter x9 -> x0, waiting for transfers between devices: 886 us -> none  [the longest x1 244 us: shards(): lax.psum_scatter(gate_grad.astype(jnp.bfloat16), 'dp', scatter_dimension=...]
    dot_general x38 -> x22, matrix products: 530 us -> 89.6 us  [the longest x9 44.5 us: dot(): return lax.dot_general(a, b, dims, preferred_element_type=F32)]
    psum x3 -> x0, waiting for transfers between devices: 247 us -> none  [the longest x1 122 us: shards(): lax.psum((gain_one_part, gain_two_part, router_part), ('dp', 'tensor'))]
    pallas_call x0 -> x3, Pallas kernels: none -> 101 us  [the longest x1 45.4 us: run_experts(): pl.pallas_call(experts_kernel, grid=(experts,), in_specs=[of(cap, width),...]
    convert_element_type x13 -> x7, other arithmetic: 115 us -> 14.6 us  [the longest x2 7.53 us: shards(): grad_expert = (gate * gx.astype(F32)).astype(BF)]
    ppermute x16 -> x56, waiting for transfers between devices: 122 us -> 205 us  [across(): return lax.ppermute(x, axis, [(i, i ^ mask) for i in range(n)])]
    gather x31 -> x0, local copies, waits for them, and re-layouts: 74.5 us -> none
    reduce_sum x12 -> x6, other arithmetic: 77.4 us -> 14.3 us  [the longest x1 9.47 us: shards(): jnp.sum((segments[None, None, :] < seg_query[:, :, None]).astype(jnp.int3...]
  transfers between devices with their start and end apart: 28 -> 61, of which waited for: 18 -> 28; matrix products, arithmetic and copies ran while one was open for 25% -> 27% of each run, Pallas kernels for 0% -> 15%
where the time goes in v1:
time: 694 us; the launch traced here: 690 us
  waiting for transfers between devices  205 us (30%)
  starting transfers between devices  144 us (21%)
  Pallas kernels  101 us (15%)
  matrix products  89.6 us (13%)
  other arithmetic  77.5 us (11%)
  local copies, waits for them, and re-layouts  68.6 us (10%)
    ppermute x56, waiting for transfers between devices, across(): return lax.ppermute(x, axis, [(i, i ^ mask) for i in range(n)])  205 us
    ppermute x56, starting transfers between devices, across(): return lax.ppermute(x, axis, [(i, i ^ mask) for i in range(n)])  94.1 us
    all_to_all x5, starting transfers between devices, to_owner(): return lax.all_to_all(x, 'dp', 0, 0, tiled=True)  49.5 us
    pallas_call x1, Pallas kernels, run_experts(): pl.pallas_call(experts_kernel, grid=(experts,), in_specs=[of(cap, width),...  45.4 us
    dot_general x9, matrix products, dot(): return lax.dot_general(a, b, dims, preferred_element_type=F32)  44.5 us
    dot_general x11, matrix products, dot(): return jnp.dot(a, b, preferred_element_type=F32)  42.9 us
    pallas_call x1, Pallas kernels, attend_back(): pl.pallas_call(functools.partial(attend_back_kernel, heads, rows, lines,...  32.2 us
    pallas_call x1, Pallas kernels, attend(): pl.pallas_call(functools.partial(attend_kernel, heads, rows, lines, strid...  23 us
  transfers between devices with their start and end apart: 61, of which 28 were waited for; matrix products, arithmetic and copies ran while one was open for 27% of the time, Pallas kernels for 15%

profile of v1, /device:TPU:0, one launch (start us, length us, event | category | flops | bytes accessed | tf_op | source)
XLA Modules:
  0.0 689.5 jit_solution(15249790470300572186)
XLA Ops:
  0.7 2.9 broadcast_select_fusion.36
  6.2 4.8 concatenate.59
  13.9 3.0 collective-permute-start
  17.0 2.6 collective-permute-start.1
  22.2 8.0 %collective-permute-done.1 = bf16[512,128]{1,0:T(8,128)(2,1)} collective-permute-done((bf16[512,128]{1,0:T(8,128)(2,1)}, bf16[512,128]{1,0:T(8,128)(2,1)}, u32[]{:S(2)}, u32[]{:S(2)}) %collective-permute-start.1) | collective-permute-done | bytes 131104 | tf_op jit(solution)/shard_map/ppermute | solution.py:31
  32.8 3.6 convolution_convert_fusion.2
  40.0 2.6 collective-permute-done.3
  46.3 7.4 %all-to-all-start = ((bf16[16,128,384]{2,1,0:T(8,128)(2,1)}), bf16[16,128,384]{2,1,0:T(8,128)(2,1)}, u32[]{:S(2)}, u32[]{:S(2)}) async-start(bf16[16,128,384]{2,1,0:T(8,128)(2,1)} %get-tuple-element.52), calls=%async_computation | async-start | bytes 3145728 | tf_op jit(solution)/shard_map/all_to_all | solution.py:43
  62.4 9.5 %convert_reduce_fusion = s32[4,512]{1,0:T(4,128)S(1)} fusion(s32[4,512]{1,0:T(4,128)S(1)} %pad_add_fusion, s32[8192]{0:T(1024)S(1)} %copy-done.74), kind=kLoop, calls=%fused_computation | loop fusion | flops 50329600 | bytes 49152 | tf_op jit(solution)/shard_map/reduce_sum | solution.py:442
  72.5 15.1 %collective-permute-done.5 = bf16[512,192]{1,0:T(8,128)(2,1)S(1)} collective-permute-done((bf16[512,192]{1,0:T(8,128)(2,1)}, bf16[512,192]{1,0:T(8,128)(2,1)S(1)}, u32[]{:S(2)}, u32[]{:S(2)}) %collective-permute-start.5) | collective-permute-done | bytes 196640 | tf_op jit(solution)/shard_map/ppermute | solution.py:31
  87.9 21.0 %collective-permute-done.6 = bf16[512,192]{1,0:T(8,128)(2,1)} collective-permute-done((bf16[512,192]{1,0:T(8,128)(2,1)}, bf16[512,192]{1,0:T(8,128)(2,1)}, u32[]{:S(2)}, u32[]{:S(2)}) %collective-permute-start.6) | collective-permute-done | bytes 196640 | tf_op jit(solution)/shard_map/ppermute | solution.py:31
  114.1 23.0 %attend.1 = (f32[4,3,512,128]{3,2,1,0:T(8,128)}, f32[4,8,512]{2,1,0:T(8,128)S(1)}) custom-call(s32[13]{0:T(128)S(1)} %pad_add_fusion.1.meta, bf16[4,3,512,128]{3,2,1,0:T(8,128)(2,1)S(1)} %concatenate.62.q_ref, bf16[16,512,128]{2,1,0:T(8,128)(2,1)S(1)} %bitcast.232, s32[4,1,512]{2,1,0:T(1,128)S(1)} %broadcast_in_dim.92.start_ref), custom_call_target="tpu_custom_call" | custom-call | flops 9663676416 | bytes 8388608 | tf_op jit(solution)/shard_map/attend/pallas_call | solution.py:213
  142.7 3.6 collective-permute-start.8
  148.0 2.6 broadcast_select_fusion.27
  151.6 9.4 %collective-permute-done.9 = bf16[512,192]{0,1:T(8,128)(2,1)S(1)} collective-permute-done((bf16[512,192]{0,1:T(8,128)(2,1)}, bf16[512,192]{0,1:T(8,128)(2,1)S(1)}, u32[]{:S(2)}, u32[]{:S(2)}) %collective-permute-start.9) | collective-permute-done | bytes 196640 | tf_op jit(solution)/shard_map/ppermute | solution.py:31
  162.7 2.5 fusion.52
  168.6 16.1 %all-to-all-start.1 = ((bf16[16,128,384]{2,1,0:T(8,128)(2,1)}), bf16[16,128,384]{2,1,0:T(8,128)(2,1)}, u32[]{:S(2)}, u32[]{:S(2)}) async-start(bf16[16,128,384]{2,1,0:T(8,128)(2,1)} %get-tuple-element.59), calls=%async_computation.1 | async-start | bytes 3145728 | tf_op jit(solution)/shard_map/all_to_all | solution.py:43
  191.8 3.5 convert_element_type.116
  195.9 14.1 %collective-permute-done.12 = bf16[256,1536]{1,0:T(8,128)(2,1)S(1)} collective-permute-done((bf16[256,1536]{1,0:T(8,128)(2,1)}, bf16[256,1536]{1,0:T(8,128)(2,1)S(1)}, u32[]{:S(2)}, u32[]{:S(2)}) %collective-permute-start.12) | collective-permute-done | bytes 786464 | tf_op jit(solution)/shard_map/ppermute | solution.py:31
  213.4 5.1 convolution_convert_fusion.1
  223.1 16.0 %all-to-all-start.2 = ((bf16[16,128,384]{2,1,0:T(8,128)(2,1)}), bf16[16,128,384]{2,1,0:T(8,128)(2,1)}, u32[]{:S(2)}, u32[]{:S(2)}) async-start(bf16[16,128,384]{2,1,0:T(8,128)(2,1)} %get-tuple-element.60), calls=%async_computation.2 | async-start | bytes 3145728 | tf_op jit(solution)/shard_map/all_to_all | solution.py:43
  239.2 45.4 %experts.1 = (bf16[16,128,1536]{2,1,0:T(8,128)(2,1)}, bf16[16,128,1536]{2,1,0:T(8,128)(2,1)}, f32[16,8,128]{2,1,0:T(8,128)S(1)}) custom-call(bf16[16,128,1536]{2,1,0:T(8,128)(2,1)} %bitcast.239, bf16[16,128,1536]{2,1,0:T(8,128)(2,1)} %bitcast.237, f32[16,128,1]{2,1,0:T(8,128)S(1)} %copy.153.gate_ref, bf16[16,1536,512]{2,1,0:T(8,128)(2,1)} %wg_ref.1, ...), custom_call_target="tpu_custom_call" | custom-call | flops 19327352832 | bytes 100663296 | tf_op jit(solution)/shard_map/experts/pallas_call | solution.py:356
  284.6 2.6 select_reduce_fusion
  292.2 6.2 fusion.5
  301.6 8.0 %fusion.4 = f32[512,1536]{1,0:T(8,128)} fusion(bf16[16,128,1536]{2,1,0:T(8,128)(2,1)} %get-tuple-element.57, s32[512,16]{0,1:T(8,128)S(1)} %copy-done.66), kind=kOutput, calls=%fused_computation.23 | convolution fusion | flops 3222274048 | bytes 9469952 | tf_op jit(solution)/shard_map/dot_general | solution.py:25
  309.6 10.4 %collective-permute-done.14 = bf16[256,1536]{1,0:T(8,128)(2,1)S(1)} collective-permute-done((bf16[256,1536]{1,0:T(8,128)(2,1)S(1)}, bf16[256,1536]{1,0:T(8,128)(2,1)S(1)}, u32[]{:S(2)}, u32[]{:S(2)}) %collective-permute-start.14) | collective-permute-done | bytes 786464 | tf_op jit(solution)/shard_map/ppermute | solution.py:31
  327.3 4.9 all-to-all-start.3
  334.3 27.4 %collective-permute-done.53 = f32[17,1536]{1,0:T(8,128)S(1)} collective-permute-done((f32[17,1536]{1,0:T(8,128)S(1)}, f32[17,1536]{1,0:T(8,128)S(1)}, u32[]{:S(2)}, u32[]{:S(2)}) %collective-permute-start.53) | collective-permute-done | bytes 104480 | tf_op jit(solution)/shard_map/ppermute | solution.py:31
  361.8 4.5 collective-permute-start.54
  369.9 6.4 collective-permute-done.54
  380.8 11.3 %collective-permute-done.55 = f32[17,1536]{1,0:T(8,128)S(1)} collective-permute-done((f32[17,1536]{1,0:T(8,128)S(1)}, f32[17,1536]{1,0:T(8,128)S(1)}, u32[]{:S(2)}, u32[]{:S(2)}) %collective-permute-start.55) | collective-permute-done | bytes 104480 | tf_op jit(solution)/shard_map/ppermute | solution.py:31
  398.7 3.4 collective-permute-start.19
  402.2 2.9 convolution_convert_fusion.3
  412.0 5.7 collective-permute-done.18
  420.6 32.2 %attend_back.1 = (bf16[4,3,512,128]{3,2,1,0:T(8,128)(2,1)}, bf16[16,512,128]{2,1,0:T(8,128)(2,1)}) custom-call(s32[13]{0:T(128)} %copy-done.5, bf16[4,3,512,128]{3,2,1,0:T(8,128)(2,1)} %copy-done.3, bf16[4,3,512,128]{3,2,1,0:T(8,128)(2,1)} %concatenate.68.g_ref, f32[4,3,512,128]{3,2,1,0:T(8,128)} %get-tuple-element.53.raw_ref, f32[4,8,512]{2,1,0:T(8,128)} %copy-done.6, ...), custom_call_target="tpu_custom_call" | custom-call | flops 24159191040 | bytes 10485760 | tf_op jit(solution)/shard_map/attend_back/pallas_call | solution.py:313
  455.2 3.1 collective-permute-start.20
  463.0 15.7 %collective-permute-start.45 = (bf16[4,96,384]{2,1,0:T(8,128)(2,1)S(1)}, bf16[4,96,384]{2,1,0:T(8,128)(2,1)S(1)}, u32[]{:S(2)}, u32[]{:S(2)}) collective-permute-start(bf16[4,96,384]{2,1,0:T(8,128)(2,1)S(1)} %dynamic-slice_bitcast_fusion.5), channel_id=1, source_target_pairs={{0,4},{2,6},{4,0},{6,2},{8,12},{10,14},{12,8},{14,10},{16,20},{18,... | collective-permute-start | bytes 884744 | tf_op jit(solution)/shard_map/ppermute | solution.py:31
  479.4 5.1 all-to-all-start.4
  484.5 3.1 fusion.88
  495.1 6.7 collective-permute-done.48
  506.2 3.1 pad_maximum_fusion.1
  517.7 6.4 collective-permute-done.49
  525.9 4.6 collective-permute-done.47
  532.8 8.1 %collective-permute-done.24 = bf16[1,4,512,128]{2,3,1,0:T(8,128)(2,1)S(1)} collective-permute-done((bf16[1,4,512,128]{2,3,1,0:T(8,128)(2,1)S(1)}, bf16[1,4,512,128]{2,3,1,0:T(8,128)(2,1)S(1)}, u32[]{:S(2)}, u32[]{:S(2)}) %collective-permute-start.24) | collective-permute-done | bytes 524320 | tf_op jit(solution)/shard_map/ppermute | solution.py:31
  541.0 2.9 collective-permute-start.25
  550.2 9.1 %collective-permute-done.26 = bf16[512,128]{0,1:T(8,128)(2,1)S(1)} collective-permute-done((bf16[512,128]{0,1:T(8,128)(2,1)S(1)}, bf16[512,128]{0,1:T(8,128)(2,1)S(1)}, u32[]{:S(2)}, u32[]{:S(2)}) %collective-permute-start.26) | collective-permute-done | bytes 131104 | tf_op jit(solution)/shard_map/ppermute | solution.py:31
  564.1 6.4 collective-permute-done.21
  573.6 6.3 fusion.10
  580.0 6.3 fusion.12
  586.3 3.9 multiply_convert_fusion
  590.2 7.0 %fusion.14 = f32[2048,512]{1,0:T(8,128)} fusion(bf16[2048,1536]{1,0:T(8,128)(2,1)S(1)} %bitcast.247, bf16[16,512,1536]{2,1,0:T(8,128)(2,1)} %wd_ref.1, s32[]{:T(128)S(6)} %select_n.619), kind=kOutput, calls=%fused_computation.50 | convolution fusion | flops 3221225472 | bytes 12058628 | tf_op jit(solution)/shard_map/dot_general | solution.py:26
  604.4 7.9 %convolution_bitcast_fusion.2 = f32[1,1536,512]{2,1,0:T(8,128)} fusion(bf16[2048,1536]{1,0:T(8,128)(2,1)S(1)} %bitcast.245, f32[2048,512]{1,0:T(8,128)S(1)} %copy-done.75, f32[2048,512]{1,0:T(8,128)} %fusion.14, f32[2048,512]{1,0:T(8,128)S(1)} %copy-done.76), kind=kOutput, calls=%fused_computation.27 | convolution fusion | flops 3231711232 | bytes 22020096 | tf_op jit(solution)/shard_map/dot_general | solution.py:26
  612.3 7.8 %convolution_bitcast_fusion.1 = f32[1,1536,512]{2,1,0:T(8,128)} fusion(bf16[2048,1536]{1,0:T(8,128)(2,1)S(1)} %bitcast.246, f32[2048,512]{1,0:T(8,128)} %fusion.14, f32[2048,512]{1,0:T(8,128)S(1)} %copy-done.75), kind=kOutput, calls=%fused_computation.26 | convolution fusion | flops 3227516928 | bytes 17825792 | tf_op jit(solution)/shard_map/dot_general | solution.py:26
  620.1 3.9 convolution_convert_fusion
  628.3 3.7 fusion
  632.0 3.7 collective-permute-start.31
  635.7 10.4 %convolution_bitcast_fusion = f32[1,512,1536]{2,1,0:T(8,128)} fusion(bf16[2048,1536]{1,0:T(8,128)(2,1)} %fusion, f32[2048,512]{1,0:T(8,128)} %fusion.12, f32[2048,512]{1,0:T(8,128)} %fusion.10), kind=kOutput, calls=%fused_computation.25 | convolution fusion | flops 3227516928 | bytes 17825792 | tf_op jit(solution)/shard_map/dot_general | solution.py:26
  646.3 4.4 collective-permute-done.32
  655.9 3.6 multiply_add_fusion
  660.2 5.0 collective-permute-done.38
  667.5 7.3 %collective-permute-done.39 = bf16[2,96,640]{2,1,0:T(8,128)(2,1)S(1)} collective-permute-done((bf16[2,96,640]{2,1,0:T(8,128)(2,1)S(1)}, bf16[2,96,640]{2,1,0:T(8,128)(2,1)S(1)}, u32[]{:S(2)}, u32[]{:S(2)}) %collective-permute-start.39) | collective-permute-done | bytes 245792 | tf_op jit(solution)/shard_map/ppermute | solution.py:31
  675.4 6.0 collective-permute-done.42
  681.5 2.5 collective-permute-start.43
  684.0 2.8 collective-permute-done.43
  (416 shorter events, 170.0 us)
Async XLA Ops:
  0.6 209.8 %copy-start = (bf16[1536,16]{0,1:T(8,128)(2,1)S(1)}, bf16[1536,16]{0,1:T(8,128)(2,1)}, u32[]{:S(2)}) copy-start(bf16[1536,16]{0,1:T(8,128)(2,1)} %param.21) | copy-start | bytes 147460
  13.9 8.3 %collective-permute-start = (bf16[512,128]{1,0:T(8,128)(2,1)}, bf16[512,128]{1,0:T(8,128)(2,1)S(1)}, u32[]{:S(2)}, u32[]{:S(2)}) collective-permute-start(bf16[512,128]{1,0:T(8,128)(2,1)} %get-tuple-element.211), channel_id=1, source_target_pairs={{0,8},{2,10},{4,12},{6,14},{8,0},{10,2},{12,4},{14,6},{16,24},{18,... | collective-permute-start | bytes 393224 | tf_op jit(solution)/shard_map/ppermute | solution.py:31
  17.0 13.2 %collective-permute-start.1 = (bf16[512,128]{1,0:T(8,128)(2,1)}, bf16[512,128]{1,0:T(8,128)(2,1)}, u32[]{:S(2)}, u32[]{:S(2)}) collective-permute-start(bf16[512,128]{1,0:T(8,128)(2,1)} %get-tuple-element.210), channel_id=1, source_target_pairs={{0,16},{2,18},{4,20},{6,22},{8,24},{10,26},{12,28},{14,30},{16,0},... | collective-permute-start | bytes 393224 | tf_op jit(solution)/shard_map/ppermute | solution.py:31
  19.6 10.7 %collective-permute-start.2 = (bf16[512,128]{1,0:T(8,128)(2,1)}, bf16[512,128]{1,0:T(8,128)(2,1)}, u32[]{:S(2)}, u32[]{:S(2)}) collective-permute-start(bf16[512,128]{1,0:T(8,128)(2,1)} %get-tuple-element.209), channel_id=1, source_target_pairs={{0,24},{2,26},{4,28},{6,30},{8,16},{10,18},{12,20},{14,22},{16,8},... | collective-permute-start | bytes 393224 | tf_op jit(solution)/shard_map/ppermute | solution.py:31
  31.3 11.3 %collective-permute-start.3 = (bf16[1,4,512,128]{3,2,1,0:T(8,128)(2,1)S(1)}, bf16[1,4,512,128]{3,2,1,0:T(8,128)(2,1)S(1)}, u32[]{:S(2)}, u32[]{:S(2)}) collective-permute-start(bf16[1,4,512,128]{3,2,1,0:T(8,128)(2,1)S(1)} %get-tuple-element.207), channel_id=1, source_target_pairs={{0,4},{2,6},{4,0},{6,2},{8,12},{10,14},{12,8},{14,10},{16,20},{18,... | collective-permute-start | bytes 1572872 | tf_op jit(solution)/shard_map/ppermute | solution.py:31
  42.7 3.2 collective-permute-start.4
  46.3 67.9 %copy-start.2 = (bf16[2,2,4,512,128]{4,3,2,1,0:T(8,128)(2,1)}, bf16[2,2,4,512,128]{4,3,2,1,0:T(8,128)(2,1)S(1)}, u32[]{:S(2)}) copy-start(bf16[2,2,4,512,128]{4,3,2,1,0:T(8,128)(2,1)S(1)} %copy.140) | copy-start | bytes 6291460
  46.3 92.0 %all-to-all-start = ((bf16[16,128,384]{2,1,0:T(8,128)(2,1)}), bf16[16,128,384]{2,1,0:T(8,128)(2,1)}, u32[]{:S(2)}, u32[]{:S(2)}) async-start(bf16[16,128,384]{2,1,0:T(8,128)(2,1)} %get-tuple-element.52), calls=%async_computation | async-start | bytes 3145728 | tf_op jit(solution)/shard_map/all_to_all | solution.py:43
  54.7 32.8 %collective-permute-start.5 = (bf16[512,192]{1,0:T(8,128)(2,1)}, bf16[512,192]{1,0:T(8,128)(2,1)S(1)}, u32[]{:S(2)}, u32[]{:S(2)}) collective-permute-start(bf16[512,192]{1,0:T(8,128)(2,1)} %get-tuple-element.193), channel_id=1, source_target_pairs={{0,8},{2,10},{4,12},{6,14},{8,0},{10,2},{12,4},{14,6},{16,24},{18,... | collective-permute-start | bytes 589832 | tf_op jit(solution)/shard_map/ppermute | solution.py:31
  56.8 52.2 %collective-permute-start.6 = (bf16[512,192]{1,0:T(8,128)(2,1)}, bf16[512,192]{1,0:T(8,128)(2,1)}, u32[]{:S(2)}, u32[]{:S(2)}) collective-permute-start(bf16[512,192]{1,0:T(8,128)(2,1)} %get-tuple-element.192), channel_id=1, source_target_pairs={{0,16},{2,18},{4,20},{6,22},{8,24},{10,26},{12,28},{14,30},{16,0},... | collective-permute-start | bytes 589832 | tf_op jit(solution)/shard_map/ppermute | solution.py:31
  59.1 51.1 %collective-permute-start.7 = (bf16[512,192]{1,0:T(8,128)(2,1)}, bf16[512,192]{1,0:T(8,128)(2,1)}, u32[]{:S(2)}, u32[]{:S(2)}) collective-permute-start(bf16[512,192]{1,0:T(8,128)(2,1)} %get-tuple-element.191), channel_id=1, source_target_pairs={{0,24},{2,26},{4,28},{6,30},{8,16},{10,18},{12,20},{14,22},{16,8},... | collective-permute-start | bytes 589832 | tf_op jit(solution)/shard_map/ppermute | solution.py:31
  141.0 9.8 %collective-permute-start.10 = (bf16[512,192]{0,1:T(8,128)(2,1)S(1)}, bf16[512,192]{0,1:T(8,128)(2,1)S(1)}, u32[]{:S(2)}, u32[]{:S(2)}) collective-permute-start(bf16[512,192]{0,1:T(8,128)(2,1)S(1)} %bitcast.292), channel_id=1, source_target_pairs={{0,24},{2,26},{4,28},{6,30},{8,16},{10,18},{12,20},{14,22},{16,8},... | collective-permute-start | bytes 589832 | tf_op jit(solution)/shard_map/ppermute | solution.py:31
  142.7 8.9 %collective-permute-start.8 = (bf16[512,192]{0,1:T(8,128)(2,1)S(1)}, bf16[512,192]{0,1:T(8,128)(2,1)S(1)}, u32[]{:S(2)}, u32[]{:S(2)}) collective-permute-start(bf16[512,192]{0,1:T(8,128)(2,1)S(1)} %bitcast.293), channel_id=1, source_target_pairs={{0,8},{2,10},{4,12},{6,14},{8,0},{10,2},{12,4},{14,6},{16,24},{18,... | collective-permute-start | bytes 589832 | tf_op jit(solution)/shard_map/ppermute | solution.py:31
  147.1 13.9 %collective-permute-start.9 = (bf16[512,192]{0,1:T(8,128)(2,1)}, bf16[512,192]{0,1:T(8,128)(2,1)S(1)}, u32[]{:S(2)}, u32[]{:S(2)}) collective-permute-start(bf16[512,192]{0,1:T(8,128)(2,1)} %bitcast.33), channel_id=1, source_target_pairs={{0,16},{2,18},{4,20},{6,22},{8,24},{10,26},{12,28},{14,30},{16,0},... | collective-permute-start | bytes 589832 | tf_op jit(solution)/shard_map/ppermute | solution.py:31
  167.0 19.3 %collective-permute-start.11 = (bf16[256,1536]{1,0:T(8,128)(2,1)S(1)}, bf16[256,1536]{1,0:T(8,128)(2,1)}, u32[]{:S(2)}, u32[]{:S(2)}) collective-permute-start(bf16[256,1536]{1,0:T(8,128)(2,1)S(1)} %dynamic-slice_convert_fusion.3), channel_id=1, source_target_pairs={{0,1},{1,0},{2,3},{3,2},{4,5},{5,4},{6,7},{7,6},{8,9},{9,8},{10,11... | collective-permute-start | bytes 2359304 | tf_op jit(solution)/shard_map/ppermute | solution.py:31
  168.6 54.5 %all-to-all-start.1 = ((bf16[16,128,384]{2,1,0:T(8,128)(2,1)}), bf16[16,128,384]{2,1,0:T(8,128)(2,1)}, u32[]{:S(2)}, u32[]{:S(2)}) async-start(bf16[16,128,384]{2,1,0:T(8,128)(2,1)} %get-tuple-element.59), calls=%async_computation.1 | async-start | bytes 3145728 | tf_op jit(solution)/shard_map/all_to_all | solution.py:43
  188.5 177.8 %copy-start.69 = (f32[256]{0:T(256)}, f32[256]{0:T(256)S(1)}, u32[]{:S(2)}) copy-start(f32[256]{0:T(256)S(1)} %add_rsqrt_fusion.1) | copy-start | bytes 3076
  189.6 20.4 %collective-permute-start.12 = (bf16[256,1536]{1,0:T(8,128)(2,1)}, bf16[256,1536]{1,0:T(8,128)(2,1)S(1)}, u32[]{:S(2)}, u32[]{:S(2)}) collective-permute-start(bf16[256,1536]{1,0:T(8,128)(2,1)} %multiply_convert_fusion.8), channel_id=1, source_target_pairs={{0,1},{1,0},{2,3},{3,2},{4,5},{5,4},{6,7},{7,6},{8,9},{9,8},{10,11... | collective-permute-start | bytes 2359304 | tf_op jit(solution)/shard_map/ppermute | solution.py:31
  218.5 69.5 %collective-permute-start.13 = (bf16[16,128,384]{2,1,0:T(8,128)(2,1)}, bf16[16,128,384]{2,1,0:T(8,128)(2,1)}, u32[]{:S(2)}, u32[]{:S(2)}) collective-permute-start(bf16[16,128,384]{2,1,0:T(8,128)(2,1)} %all-to-all-done), channel_id=1, source_target_pairs={{0,1},{1,0},{2,3},{3,2},{4,5},{5,4},{6,7},{7,6},{8,9},{9,8},{10,11... | collective-permute-start | bytes 4718600 | tf_op jit(solution)/shard_map/ppermute | solution.py:31
  223.1 69.0 %all-to-all-start.2 = ((bf16[16,128,384]{2,1,0:T(8,128)(2,1)}), bf16[16,128,384]{2,1,0:T(8,128)(2,1)}, u32[]{:S(2)}, u32[]{:S(2)}) async-start(bf16[16,128,384]{2,1,0:T(8,128)(2,1)} %get-tuple-element.60), calls=%async_computation.2 | async-start | bytes 3145728 | tf_op jit(solution)/shard_map/all_to_all | solution.py:43
  300.0 20.0 %collective-permute-start.14 = (bf16[256,1536]{1,0:T(8,128)(2,1)S(1)}, bf16[256,1536]{1,0:T(8,128)(2,1)S(1)}, u32[]{:S(2)}, u32[]{:S(2)}) collective-permute-start(bf16[256,1536]{1,0:T(8,128)(2,1)S(1)} %dynamic-slice_convert_fusion.2), channel_id=1, source_target_pairs={{0,1},{1,0},{2,3},{3,2},{4,5},{5,4},{6,7},{7,6},{8,9},{9,8},{10,11... | collective-permute-start | bytes 2359304 | tf_op jit(solution)/shard_map/ppermute | solution.py:31
  321.9 1.4 collective-permute-start.51
  323.3 8.9 %collective-permute-start.52 = (f32[17,1536]{1,0:T(8,128)S(1)}, f32[17,1536]{1,0:T(8,128)S(1)}, u32[]{:S(2)}, u32[]{:S(2)}) collective-permute-start(f32[17,1536]{1,0:T(8,128)S(1)} %fusion.83), channel_id=1, source_target_pairs={{0,4},{2,6},{4,0},{6,2},{8,12},{10,14},{12,8},{14,10},{16,20},{18,... | collective-permute-start | bytes 313352 | tf_op jit(solution)/shard_map/ppermute | solution.py:31
  327.3 152.1 %all-to-all-start.3 = ((bf16[16,128,384]{2,1,0:T(8,128)(2,1)}), bf16[16,128,384]{2,1,0:T(8,128)(2,1)}, u32[]{:S(2)}, u32[]{:S(2)}) async-start(bf16[16,128,384]{2,1,0:T(8,128)(2,1)} %get-tuple-element.73), calls=%async_computation.3 | async-start | bytes 3145728 | tf_op jit(solution)/shard_map/all_to_all | solution.py:43
  332.2 29.5 %collective-permute-start.53 = (f32[17,1536]{1,0:T(8,128)S(1)}, f32[17,1536]{1,0:T(8,128)S(1)}, u32[]{:S(2)}, u32[]{:S(2)}) collective-permute-start(f32[17,1536]{1,0:T(8,128)S(1)} %add.341), channel_id=1, source_target_pairs={{0,8},{2,10},{4,12},{6,14},{8,0},{10,2},{12,4},{14,6},{16,24},{18,... | collective-permute-start | bytes 313352 | tf_op jit(solution)/shard_map/ppermute | solution.py:31
  361.8 14.5 %collective-permute-start.54 = (f32[17,1536]{1,0:T(8,128)S(1)}, f32[17,1536]{1,0:T(8,128)S(1)}, u32[]{:S(2)}, u32[]{:S(2)}) collective-permute-start(f32[17,1536]{1,0:T(8,128)S(1)} %add.342), channel_id=1, source_target_pairs={{0,16},{2,18},{4,20},{6,22},{8,24},{10,26},{12,28},{14,30},{16,0},... | collective-permute-start | bytes 313352 | tf_op jit(solution)/shard_map/ppermute | solution.py:31
  368.3 25.0 %collective-permute-start.16 = (bf16[256,1536]{1,0:T(8,128)(2,1)S(1)}, bf16[256,1536]{1,0:T(8,128)(2,1)S(1)}, u32[]{:S(2)}, u32[]{:S(2)}) collective-permute-start(bf16[256,1536]{1,0:T(8,128)(2,1)S(1)} %fusion.86), channel_id=1, source_target_pairs={{0,1},{1,0},{2,3},{3,2},{4,5},{5,4},{6,7},{7,6},{8,9},{9,8},{10,11... | collective-permute-start | bytes 2359304 | tf_op jit(solution)/shard_map/ppermute | solution.py:31
  376.3 15.7 %collective-permute-start.55 = (f32[17,1536]{1,0:T(8,128)S(1)}, f32[17,1536]{1,0:T(8,128)S(1)}, u32[]{:S(2)}, u32[]{:S(2)}) collective-permute-start(f32[17,1536]{1,0:T(8,128)S(1)} %add.343), channel_id=1, source_target_pairs={{0,1},{1,0},{2,3},{3,2},{4,5},{5,4},{6,7},{7,6},{8,9},{9,8},{10,11... | collective-permute-start | bytes 313352 | tf_op jit(solution)/shard_map/ppermute | solution.py:31
  380.3 274.2 %collective-permute-start.15 = (bf16[256,1536]{1,0:T(8,128)(2,1)}, bf16[256,1536]{1,0:T(8,128)(2,1)}, u32[]{:S(2)}, u32[]{:S(2)}) collective-permute-start(bf16[256,1536]{1,0:T(8,128)(2,1)} %dynamic-slice_convert_fusion.1), channel_id=1, source_target_pairs={{0,1},{1,0},{2,3},{3,2},{4,5},{5,4},{6,7},{7,6},{8,9},{9,8},{10,11... | collective-permute-start | bytes 2359304 | tf_op jit(solution)/shard_map/ppermute | solution.py:31
  393.7 109.7 %collective-permute-start.36 = (bf16[16,128,384]{2,1,0:T(8,128)(2,1)}, bf16[16,128,384]{2,1,0:T(8,128)(2,1)}, u32[]{:S(2)}, u32[]{:S(2)}) collective-permute-start(bf16[16,128,384]{2,1,0:T(8,128)(2,1)} %all-to-all-done.1), channel_id=1, source_target_pairs={{0,1},{1,0},{2,3},{3,2},{4,5},{5,4},{6,7},{7,6},{8,9},{9,8},{10,11... | collective-permute-start | bytes 4718600 | tf_op jit(solution)/shard_map/ppermute | solution.py:31
  397.8 10.8 %collective-permute-start.17 = (bf16[512,192]{1,0:T(8,128)(2,1)}, bf16[512,192]{1,0:T(8,128)(2,1)S(1)}, u32[]{:S(2)}, u32[]{:S(2)}) collective-permute-start(bf16[512,192]{1,0:T(8,128)(2,1)} %get-tuple-element.189), channel_id=1, source_target_pairs={{0,8},{2,10},{4,12},{6,14},{8,0},{10,2},{12,4},{14,6},{16,24},{18,... | collective-permute-start | bytes 589832 | tf_op jit(solution)/shard_map/ppermute | solution.py:31
  397.8 19.9 %collective-permute-start.18 = (bf16[512,192]{1,0:T(8,128)(2,1)}, bf16[512,192]{1,0:T(8,128)(2,1)S(1)}, u32[]{:S(2)}, u32[]{:S(2)}) collective-permute-start(bf16[512,192]{1,0:T(8,128)(2,1)} %get-tuple-element.188), channel_id=1, source_target_pairs={{0,16},{2,18},{4,20},{6,22},{8,24},{10,26},{12,28},{14,30},{16,0},... | collective-permute-start | bytes 589832 | tf_op jit(solution)/shard_map/ppermute | solution.py:31
  398.7 19.3 %collective-permute-start.19 = (bf16[512,192]{1,0:T(8,128)(2,1)}, bf16[512,192]{1,0:T(8,128)(2,1)S(1)}, u32[]{:S(2)}, u32[]{:S(2)}) collective-permute-start(bf16[512,192]{1,0:T(8,128)(2,1)} %get-tuple-element.187), channel_id=1, source_target_pairs={{0,24},{2,26},{4,28},{6,30},{8,16},{10,18},{12,20},{14,22},{16,8},... | collective-permute-start | bytes 589832 | tf_op jit(solution)/shard_map/ppermute | solution.py:31
  409.3 100.1 %collective-permute-start.34 = (bf16[16,128,384]{2,1,0:T(8,128)(2,1)}, bf16[16,128,384]{2,1,0:T(8,128)(2,1)}, u32[]{:S(2)}, u32[]{:S(2)}) collective-permute-start(bf16[16,128,384]{2,1,0:T(8,128)(2,1)} %all-to-all-done.2), channel_id=1, source_target_pairs={{0,1},{1,0},{2,3},{3,2},{4,5},{5,4},{6,7},{7,6},{8,9},{9,8},{10,11... | collective-permute-start | bytes 4718600 | tf_op jit(solution)/shard_map/ppermute | solution.py:31
  417.7 42.5 %collective-permute-start.44 = (bf16[8,96,768]{2,1,0:T(8,128)(2,1)}, bf16[8,96,768]{2,1,0:T(8,128)(2,1)}, u32[]{:S(2)}, u32[]{:S(2)}) collective-permute-start(bf16[8,96,768]{2,1,0:T(8,128)(2,1)} %dynamic-slice_bitcast_fusion.1), channel_id=1, source_target_pairs={{0,2},{2,0},{4,6},{6,4},{8,10},{10,8},{12,14},{14,12},{16,18},{18,... | collective-permute-start | bytes 3538952 | tf_op jit(solution)/shard_map/ppermute | solution.py:31
  455.2 108.9 %collective-permute-start.20 = (bf16[512,192]{0,1:T(8,128)(2,1)}, bf16[512,192]{0,1:T(8,128)(2,1)S(1)}, u32[]{:S(2)}, u32[]{:S(2)}) collective-permute-start(bf16[512,192]{0,1:T(8,128)(2,1)} %bitcast.48), channel_id=1, source_target_pairs={{0,8},{2,10},{4,12},{6,14},{8,0},{10,2},{12,4},{14,6},{16,24},{18,... | collective-permute-start | bytes 589832 | tf_op jit(solution)/shard_map/ppermute | solution.py:31
  463.0 29.2 %collective-permute-start.45 = (bf16[4,96,384]{2,1,0:T(8,128)(2,1)S(1)}, bf16[4,96,384]{2,1,0:T(8,128)(2,1)S(1)}, u32[]{:S(2)}, u32[]{:S(2)}) collective-permute-start(bf16[4,96,384]{2,1,0:T(8,128)(2,1)S(1)} %dynamic-slice_bitcast_fusion.5), channel_id=1, source_target_pairs={{0,4},{2,6},{4,0},{6,2},{8,12},{10,14},{12,8},{14,10},{16,20},{18,... | collective-permute-start | bytes 884744 | tf_op jit(solution)/shard_map/ppermute | solution.py:31
  479.4 106.9 %all-to-all-start.4 = ((f32[16,1,128]{2,1,0:T(1,128)}), f32[16,1,128]{2,1,0:T(1,128)S(1)}, u32[]{:S(2)}, u32[]{:S(2)}) async-start(f32[16,1,128]{2,1,0:T(1,128)} %bitcast.104), calls=%async_computation.4 | async-start | bytes 16384 | tf_op jit(solution)/shard_map/all_to_all | solution.py:43
  492.1 9.6 %collective-permute-start.48 = (bf16[2,192,384]{2,1,0:T(8,128)(2,1)}, bf16[2,192,384]{2,1,0:T(8,128)(2,1)S(1)}, u32[]{:S(2)}, u32[]{:S(2)}) collective-permute-start(bf16[2,192,384]{2,1,0:T(8,128)(2,1)} %dynamic-slice_bitcast_fusion.4), channel_id=1, source_target_pairs={{0,8},{2,10},{4,12},{6,14},{8,0},{10,2},{12,4},{14,6},{16,24},{18,... | collective-permute-start | bytes 884744 | tf_op jit(solution)/shard_map/ppermute | solution.py:31
  501.8 44.2 %collective-permute-start.35 = (bf16[16,128,384]{2,1,0:T(8,128)(2,1)}, bf16[16,128,384]{2,1,0:T(8,128)(2,1)S(1)}, u32[]{:S(2)}, u32[]{:S(2)}) collective-permute-start(bf16[16,128,384]{2,1,0:T(8,128)(2,1)} %all-to-all-done.3), channel_id=1, source_target_pairs={{0,1},{1,0},{2,3},{3,2},{4,5},{5,4},{6,7},{7,6},{8,9},{9,8},{10,11... | collective-permute-start | bytes 4718600 | tf_op jit(solution)/shard_map/ppermute | solution.py:31
  503.4 20.7 %collective-permute-start.23 = (bf16[2,4,512,128]{2,3,1,0:T(8,128)(2,1)S(1)}, bf16[2,4,512,128]{2,3,1,0:T(8,128)(2,1)S(1)}, u32[]{:S(2)}, u32[]{:S(2)}) collective-permute-start(bf16[2,4,512,128]{2,3,1,0:T(8,128)(2,1)S(1)} %bitcast.272), channel_id=1, source_target_pairs={{0,2},{2,0},{4,6},{6,4},{8,10},{10,8},{12,14},{14,12},{16,18},{18,... | collective-permute-start | bytes 3145736 | tf_op jit(solution)/shard_map/ppermute | solution.py:31
  509.4 5.7 collective-permute-start.46
  515.1 9.0 %collective-permute-start.49 = (bf16[1,192,384]{2,1,0:T(8,128)(2,1)S(1)}, bf16[1,192,384]{2,1,0:T(8,128)(2,1)S(1)}, u32[]{:S(2)}, u32[]{:S(2)}) collective-permute-start(bf16[1,192,384]{2,1,0:T(8,128)(2,1)S(1)} %constant_dynamic-slice_fusion.2), channel_id=1, source_target_pairs={{0,16},{2,18},{4,20},{6,22},{8,24},{10,26},{12,28},{14,30},{16,0},... | collective-permute-start | bytes 442376 | tf_op jit(solution)/shard_map/ppermute | solution.py:31
  524.1 6.5 collective-permute-start.47
  524.2 7.9 %collective-permute-start.50 = (bf16[1,96,384]{2,1,0:T(8,128)(2,1)S(1)}, bf16[1,96,384]{2,1,0:T(8,128)(2,1)S(1)}, u32[]{:S(2)}, u32[]{:S(2)}) collective-permute-start(bf16[1,96,384]{2,1,0:T(8,128)(2,1)S(1)} %dynamic-slice_bitcast_fusion.9), channel_id=1, source_target_pairs={{0,4},{2,6},{4,0},{6,2},{8,12},{10,14},{12,8},{14,10},{16,20},{18,... | collective-permute-start | bytes 221192 | tf_op jit(solution)/shard_map/ppermute | solution.py:31
  530.5 10.3 %collective-permute-start.24 = (bf16[1,4,512,128]{2,3,1,0:T(8,128)(2,1)S(1)}, bf16[1,4,512,128]{2,3,1,0:T(8,128)(2,1)S(1)}, u32[]{:S(2)}, u32[]{:S(2)}) collective-permute-start(bf16[1,4,512,128]{2,3,1,0:T(8,128)(2,1)S(1)} %slice_bitcast_fusion.1), channel_id=1, source_target_pairs={{0,4},{2,6},{4,0},{6,2},{8,12},{10,14},{12,8},{14,10},{16,20},{18,... | collective-permute-start | bytes 1572872 | tf_op jit(solution)/shard_map/ppermute | solution.py:31
  541.0 7.8 %collective-permute-start.25 = (bf16[512,128]{0,1:T(8,128)(2,1)S(1)}, bf16[512,128]{0,1:T(8,128)(2,1)S(1)}, u32[]{:S(2)}, u32[]{:S(2)}) collective-permute-start(bf16[512,128]{0,1:T(8,128)(2,1)S(1)} %get-tuple-element.205), channel_id=1, source_target_pairs={{0,8},{2,10},{4,12},{6,14},{8,0},{10,2},{12,4},{14,6},{16,24},{18,... | collective-permute-start | bytes 393224 | tf_op jit(solution)/shard_map/ppermute | solution.py:31
  543.9 15.4 %collective-permute-start.26 = (bf16[512,128]{0,1:T(8,128)(2,1)S(1)}, bf16[512,128]{0,1:T(8,128)(2,1)S(1)}, u32[]{:S(2)}, u32[]{:S(2)}) collective-permute-start(bf16[512,128]{0,1:T(8,128)(2,1)S(1)} %get-tuple-element.204), channel_id=1, source_target_pairs={{0,16},{2,18},{4,20},{6,22},{8,24},{10,26},{12,28},{14,30},{16,0},... | collective-permute-start | bytes 393224 | tf_op jit(solution)/shard_map/ppermute | solution.py:31
  546.0 15.2 %collective-permute-start.27 = (bf16[512,128]{0,1:T(8,128)(2,1)S(1)}, bf16[512,128]{0,1:T(8,128)(2,1)S(1)}, u32[]{:S(2)}, u32[]{:S(2)}) collective-permute-start(bf16[512,128]{0,1:T(8,128)(2,1)S(1)} %get-tuple-element.203), channel_id=1, source_target_pairs={{0,24},{2,26},{4,28},{6,30},{8,16},{10,18},{12,20},{14,22},{16,8},... | collective-permute-start | bytes 393224 | tf_op jit(solution)/shard_map/ppermute | solution.py:31
  549.0 21.5 %collective-permute-start.21 = (bf16[512,192]{0,1:T(8,128)(2,1)S(1)}, bf16[512,192]{0,1:T(8,128)(2,1)S(1)}, u32[]{:S(2)}, u32[]{:S(2)}) collective-permute-start(bf16[512,192]{0,1:T(8,128)(2,1)S(1)} %bitcast.291), channel_id=1, source_target_pairs={{0,16},{2,18},{4,20},{6,22},{8,24},{10,26},{12,28},{14,30},{16,0},... | collective-permute-start | bytes 589832 | tf_op jit(solution)/shard_map/ppermute | solution.py:31
  559.3 11.2 %collective-permute-start.22 = (bf16[512,192]{0,1:T(8,128)(2,1)S(1)}, bf16[512,192]{0,1:T(8,128)(2,1)S(1)}, u32[]{:S(2)}, u32[]{:S(2)}) collective-permute-start(bf16[512,192]{0,1:T(8,128)(2,1)S(1)} %bitcast.290), channel_id=1, source_target_pairs={{0,24},{2,26},{4,28},{6,30},{8,16},{10,18},{12,20},{14,22},{16,8},... | collective-permute-start | bytes 589832 | tf_op jit(solution)/shard_map/ppermute | solution.py:31
  601.1 22.9 %collective-permute-start.28 = (bf16[256,1536]{1,0:T(8,128)(2,1)S(1)}, bf16[256,1536]{1,0:T(8,128)(2,1)S(1)}, u32[]{:S(2)}, u32[]{:S(2)}) collective-permute-start(bf16[256,1536]{1,0:T(8,128)(2,1)S(1)} %dynamic-slice_convert_fusion), channel_id=1, source_target_pairs={{0,1},{1,0},{2,3},{3,2},{4,5},{5,4},{6,7},{7,6},{8,9},{9,8},{10,11... | collective-permute-start | bytes 2359304 | tf_op jit(solution)/shard_map/ppermute | solution.py:31
  624.7 2.0 collective-permute-start.29
  626.6 24.7 %collective-permute-start.37 = (bf16[8,96,1280]{2,1,0:T(8,128)(2,1)}, bf16[8,96,1280]{2,1,0:T(8,128)(2,1)}, u32[]{:S(2)}, u32[]{:S(2)}) collective-permute-start(bf16[8,96,1280]{2,1,0:T(8,128)(2,1)} %dynamic-slice_bitcast_fusion), channel_id=1, source_target_pairs={{0,2},{2,0},{4,6},{6,4},{8,10},{10,8},{12,14},{14,12},{16,18},{18,... | collective-permute-start | bytes 5898248 | tf_op jit(solution)/shard_map/ppermute | solution.py:31
  626.7 5.2 collective-permute-start.30
  632.0 14.1 %collective-permute-start.31 = (f32[1,1536]{1,0:T(1,128)S(1)}, f32[1,1536]{1,0:T(1,128)S(1)}, u32[]{:S(2)}, u32[]{:S(2)}) collective-permute-start(f32[1,1536]{1,0:T(1,128)S(1)} %add.310), channel_id=1, source_target_pairs={{0,8},{2,10},{4,12},{6,14},{8,0},{10,2},{12,4},{14,6},{16,24},{18,... | collective-permute-start | bytes 18440 | tf_op jit(solution)/shard_map/ppermute | solution.py:31
  646.2 4.6 collective-permute-start.32
  650.8 8.8 %collective-permute-start.33 = (f32[1,1536]{1,0:T(1,128)S(1)}, f32[1,1536]{1,0:T(1,128)S(1)}, u32[]{:S(2)}, u32[]{:S(2)}) collective-permute-start(f32[1,1536]{1,0:T(1,128)S(1)} %add.312), channel_id=1, source_target_pairs={{0,1},{1,0},{2,3},{3,2},{4,5},{5,4},{6,7},{7,6},{8,9},{9,8},{10,11... | collective-permute-start | bytes 18440 | tf_op jit(solution)/shard_map/ppermute | solution.py:31
  653.6 11.6 %collective-permute-start.38 = (bf16[4,96,640]{2,1,0:T(8,128)(2,1)S(1)}, bf16[4,96,640]{2,1,0:T(8,128)(2,1)S(1)}, u32[]{:S(2)}, u32[]{:S(2)}) collective-permute-start(bf16[4,96,640]{2,1,0:T(8,128)(2,1)S(1)} %dynamic-slice_bitcast_fusion.3), channel_id=1, source_target_pairs={{0,4},{2,6},{4,0},{6,2},{8,12},{10,14},{12,8},{14,10},{16,20},{18,... | collective-permute-start | bytes 1474568 | tf_op jit(solution)/shard_map/ppermute | solution.py:31
  654.3 11.5 %collective-permute-start.41 = (bf16[2,192,640]{2,1,0:T(8,128)(2,1)S(1)}, bf16[2,192,640]{2,1,0:T(8,128)(2,1)S(1)}, u32[]{:S(2)}, u32[]{:S(2)}) collective-permute-start(bf16[2,192,640]{2,1,0:T(8,128)(2,1)S(1)} %dynamic-slice_bitcast_fusion.2), channel_id=1, source_target_pairs={{0,8},{2,10},{4,12},{6,14},{8,0},{10,2},{12,4},{14,6},{16,24},{18,... | collective-permute-start | bytes 1474568 | tf_op jit(solution)/shard_map/ppermute | solution.py:31
  665.3 9.5 %collective-permute-start.39 = (bf16[2,96,640]{2,1,0:T(8,128)(2,1)S(1)}, bf16[2,96,640]{2,1,0:T(8,128)(2,1)S(1)}, u32[]{:S(2)}, u32[]{:S(2)}) collective-permute-start(bf16[2,96,640]{2,1,0:T(8,128)(2,1)S(1)} %dynamic-slice_bitcast_fusion.6), channel_id=1, source_target_pairs={{0,8},{2,10},{4,12},{6,14},{8,0},{10,2},{12,4},{14,6},{16,24},{18,... | collective-permute-start | bytes 737288 | tf_op jit(solution)/shard_map/ppermute | solution.py:31
  665.9 15.5 %collective-permute-start.42 = (bf16[1,192,640]{2,1,0:T(8,128)(2,1)S(1)}, bf16[1,192,640]{2,1,0:T(8,128)(2,1)S(1)}, u32[]{:S(2)}, u32[]{:S(2)}) collective-permute-start(bf16[1,192,640]{2,1,0:T(8,128)(2,1)S(1)} %constant_dynamic-slice_fusion.4), channel_id=1, source_target_pairs={{0,16},{2,18},{4,20},{6,22},{8,24},{10,26},{12,28},{14,30},{16,0},... | collective-permute-start | bytes 737288 | tf_op jit(solution)/shard_map/ppermute | solution.py:31
  674.8 9.2 %collective-permute-start.40 = (bf16[1,96,640]{2,1,0:T(8,128)(2,1)S(1)}, bf16[1,96,640]{2,1,0:T(8,128)(2,1)S(1)}, u32[]{:S(2)}, u32[]{:S(2)}) collective-permute-start(bf16[1,96,640]{2,1,0:T(8,128)(2,1)S(1)} %constant_dynamic-slice_fusion.5), channel_id=1, source_target_pairs={{0,16},{2,18},{4,20},{6,22},{8,24},{10,26},{12,28},{14,30},{16,0},... | collective-permute-start | bytes 368648 | tf_op jit(solution)/shard_map/ppermute | solution.py:31
  681.5 5.4 collective-permute-start.43
  (78 other events, 703.5 us)

commit v2 on v1

v2 whole, which is shorter than its diff:
```python
import functools

import jax
import jax.numpy as jnp
from jax import lax
from jax.experimental import pallas as pl
from jax.experimental.pallas import tpu as pltpu
from jax.sharding import PartitionSpec as P

HD = 64
PAIR = 2 * HD
CAP = 128
DOCS = 8
EPS = 1e-05
HIGH = lax.Precision.HIGHEST
NEG = -1000000000.0
BF = jnp.bfloat16
F32 = jnp.float32

NT = (((1,), (1,)), ((), ()))
TN = (((0,), (0,)), ((), ()))


def dot(a, b, dims=None):
    if dims is None:
        return jnp.dot(a, b, preferred_element_type=F32)
    return lax.dot_general(a, b, dims, preferred_element_type=F32)


def across(x, axis, mask):
    n = lax.axis_size(axis)
    return lax.ppermute(x, axis, [(i, i ^ mask) for i in range(n)])


def bits_of(n):
    return [1 << k for k in range(n.bit_length() - 1)]


def after(x, y):
    return lax.optimization_barrier((x, y))


def to_owner(x):
    return lax.all_to_all(x, "dp", 0, 0, tiled=True)


def norm_factor(value):
    return lax.rsqrt(jnp.mean(value * value, axis=-1, keepdims=True) + EPS)


def norm_back(unit, factor, gain, grad):
    inner = gain * grad
    return factor * (inner - unit * jnp.mean(unit * inner, axis=-1, keepdims=True))


def total(x):
    for axis in ("dp", "tensor"):
        for bit in bits_of(lax.axis_size(axis)):
            x = x + across(x, axis, bit)
    return x


def scatter_tensor(x):
    n = lax.axis_size("tensor")
    if n != 2:
        return lax.psum_scatter(x.astype(BF), "tensor", scatter_dimension=0, tiled=True).astype(F32)
    me = lax.axis_index("tensor")
    part = x.shape[0] // 2
    sent = lax.dynamic_slice_in_dim(x, (1 - me) * part, part, 0).astype(BF)
    own = lax.dynamic_slice_in_dim(x, me * part, part, 0)
    return own.astype(F32) + across(sent, "tensor", 1).astype(F32)


def swap_tensor(x, dim):
    if lax.axis_size("tensor") != 2:
        return (lax.all_gather(x, "tensor", axis=dim, tiled=True),)
    return x, across(x, "tensor", 1)


def assemble(parts, dim):
    if len(parts) == 1:
        return parts[0]
    own, other = parts
    low = lax.axis_index("tensor") == 0
    return jnp.concatenate([jnp.where(low, own, other), jnp.where(low, other, own)], dim)


def gather_tensor(x, dim):
    return assemble(swap_tensor(x, dim), dim)


def xor_blocks(blocks, index):
    for bit in bits_of(len(blocks)):
        crossed = (index & bit) != 0
        blocks = [jnp.where(crossed, blocks[s ^ bit], block) for s, block in enumerate(blocks)]
    return blocks


def columns_of(x, count):
    size = x.shape[1] // count
    return [x[:, s * size : (s + 1) * size] for s in range(count)]


def scatter_rows(x, later):
    n = lax.axis_size("dp")
    at = lax.axis_index("dp")
    bits = bits_of(n)
    x = x.astype(BF)
    x = halve_first(x, at, n)
    half = x.shape[1] // 2
    orders = (bits[1:], bits[2:] + bits[1:2])
    pieces = [
        halve_rest(piece, at, order[:1], bits[1:])
        for piece, order in zip((x[:, :half], x[:, half:]), orders)
    ]
    pieces, later = after(pieces, later)
    outs = [
        halve_rest(piece, at, order[1:], [b for b in bits[1:] if b != order[0]])
        for piece, order in zip(pieces, orders)
    ]
    return jnp.concatenate(outs, 1).astype(F32), later


def halve_first(x, at, n):
    size = x.shape[0] // n
    view = x.reshape(n // 2, 2, size, x.shape[1])
    mine = at & 1

    def pick(which):
        return lax.dynamic_index_in_dim(view, which, 1, keepdims=False)

    return (pick(mine) + across(pick(1 - mine), "dp", 1)).reshape(-1, x.shape[1])


def halve_rest(x, at, order, left):
    left = sorted(left)
    for bit in order:
        high = 1
        for other in left:
            if other > bit:
                high *= 2
        view = x.reshape(high, 2, -1, x.shape[1])
        mine = (at >> (bit.bit_length() - 1)) & 1
        kept = lax.dynamic_index_in_dim(view, mine, 1, keepdims=False)
        sent = lax.dynamic_index_in_dim(view, 1 - mine, 1, keepdims=False)
        x = (kept + across(sent, "dp", bit)).reshape(-1, x.shape[1])
        left.remove(bit)
    return x


def project_kernel(lines, q_cols, at, x_ref, gain_ref, wq_ref, wk_ref, wv_ref, normed_ref, *rest):
    kv_refs, q_refs = rest[:lines], rest[lines : 2 * lines]
    kv_s, q_s = rest[2 * lines :]
    x = x_ref[...].astype(F32)
    scale = lax.rsqrt(jnp.mean(x * x, axis=-1, keepdims=True) + EPS)
    normed = (x * scale * gain_ref[...]).astype(BF)
    normed_ref[...] = normed
    key = dot(normed, wk_ref[...])
    value = dot(normed, wv_ref[...])
    query = dot(normed, wq_ref[...])
    for c in range(lines):
        pair = [key[:, c * HD : (c + 1) * HD], value[:, c * HD : (c + 1) * HD]]
        kv_s[c] = jnp.concatenate(pair, 1).astype(BF)
        q_s[c] = query[:, c * q_cols : (c + 1) * q_cols].astype(BF) * jnp.asarray(0.125, BF)
    for s in range(lines):
        kv_refs[s][...] = kv_s[s ^ at[0]]
        q_refs[s][...] = q_s[s ^ at[0]]


def project(line, x, gain, w_query, w_key, w_value, lines):
    rows, width = x.shape
    q_cols = w_query.shape[1] // lines

    def whole(*shape):
        return pl.BlockSpec(shape, lambda i, m: (0,) * len(shape))

    out = [(rows, width)] + [(rows, PAIR)] * lines + [(rows, q_cols)] * lines
    outs = pl.pallas_call(
        functools.partial(project_kernel, lines, q_cols),
        grid_spec=pltpu.PrefetchScalarGridSpec(
            num_scalar_prefetch=1,
            grid=(1,),
            in_specs=[
                whole(rows, width),
                whole(1, width),
                whole(*w_query.shape),
                whole(*w_key.shape),
                whole(*w_value.shape),
            ],
            out_specs=[whole(*shape) for shape in out],
            scratch_shapes=[
                pltpu.VMEM((lines, rows, PAIR), BF),
                pltpu.VMEM((lines, rows, q_cols), BF),
            ],
        ),
        out_shape=[jax.ShapeDtypeStruct(shape, BF) for shape in out],
        compiler_params=pltpu.CompilerParams(vmem_limit_bytes=48 * 1024 * 1024),
        cost_estimate=pl.CostEstimate(
            flops=2 * rows * width * (w_query.shape[1] + 2 * w_key.shape[1]),
            bytes_accessed=8 << 20,
            transcendentals=0,
        ),
        name="project",
    )(line[None], x, gain[None], w_query, w_key, w_value)
    return outs[0], outs[1 : 1 + lines], outs[1 + lines :]


def spread_heads(refs, out, heads, high):
    for s, ref in enumerate(refs):
        x = ref[...]
        zero = jnp.zeros((x.shape[0], HD), BF)
        for h in range(heads):
            one = x[:, h * HD : (h + 1) * HD]
            out[s, h] = jnp.concatenate([zero, one] if high else [one, zero], 1)


def gather_blocks(refs, out, lines):
    for m, ref in enumerate(refs):
        out[m * lines : (m + 1) * lines] = ref[...]


def position(meta, lines):
    slot = pl.program_id(0)
    return slot, meta[0], meta[1 + slot], meta[1 + lines + slot], meta[1 + 2 * lines + slot]


def walk(low, clear, own, step):
    def body(blk, carry):
        full = (blk >= clear) & (blk < own)

        @pl.when(full)
        def _():
            step(blk, False)

        @pl.when(jnp.logical_not(full))
        def _():
            step(blk, True)

        return carry

    lax.fori_loop(low, own + 1, body, 0)


def visible(blk, own, rows, start):
    key_pos = lax.broadcasted_iota(jnp.int32, (rows, rows), 0) + blk * rows
    q_pos = lax.broadcasted_iota(jnp.int32, (rows, rows), 1) + own * rows
    return (key_pos >= start) & (key_pos <= q_pos)


def attend_kernel(heads, rows, lines, stride, meta, *refs):
    q_refs, kv_refs, start_ref = refs[:lines], refs[lines : lines + stride], refs[lines + stride]
    outs = refs[lines + stride + 1 :]
    mixed_refs, (raw_ref, log_ref, q_s, kv_s, m_s, l_s, acc_s) = outs[:lines], outs[lines:]
    slot, place, own, low, clear = position(meta, lines)

    @pl.when(slot == 0)
    def _():
        spread_heads(q_refs, q_s, heads, False)
        gather_blocks(kv_refs, kv_s, lines)

    m_s[...] = jnp.full_like(m_s, -3e38)
    l_s[...] = jnp.zeros_like(l_s)
    acc_s[...] = jnp.zeros_like(acc_s)

    def step(blk, masked):
        x = blk ^ place
        kv = kv_s[(x % stride) * lines + x // stride]
        if masked:
            seen = visible(blk, own, rows, start_ref[0])
        for h in range(heads):
            s = dot(kv, q_s[slot, h], NT)
            if masked:
                s = jnp.where(seen, s, NEG)
            m_old = m_s[h : h + 1, :]
            m_new = jnp.maximum(m_old, jnp.max(s, axis=0, keepdims=True))
            p = jnp.exp(s - m_new)
            alpha = jnp.exp(m_old - m_new)
            l_s[h : h + 1, :] = l_s[h : h + 1, :] * alpha + jnp.sum(p, axis=0, keepdims=True)
            acc_s[h] = acc_s[h] * alpha + dot(kv, p.astype(BF), TN)
            m_s[h : h + 1, :] = m_new

    walk(low, clear, own, step)
    parts = []
    for h in range(heads):
        out = (acc_s[h] / l_s[h : h + 1, :]).T
        raw_ref[0, h] = out
        parts.append(out[:, HD:])
    log_ref[0] = m_s[...] + jnp.log(l_s[...])
    mixed = jnp.concatenate(parts, 1).astype(BF)
    for s in range(lines):

        @pl.when(slot == s)
        def _(s=s):
            mixed_refs[s][...] = mixed


def whole_block(shape):
    return pl.BlockSpec(shape, lambda i, m: (0,) * len(shape))


def attend(meta, q, kv, start_row, heads):
    lines, stride = len(q), len(kv)
    rows, q_cols = q[0].shape
    narrow = whole_block((rows, q_cols))
    return pl.pallas_call(
        functools.partial(attend_kernel, heads, rows, lines, stride),
        grid_spec=pltpu.PrefetchScalarGridSpec(
            num_scalar_prefetch=1,
            grid=(lines,),
            in_specs=[narrow] * lines
            + [whole_block((lines, rows, PAIR))] * stride
            + [pl.BlockSpec((1, 1, rows), lambda i, m: (i, 0, 0))],
            out_specs=[narrow] * lines
            + [
                pl.BlockSpec((1, heads, rows, PAIR), lambda i, m: (i, 0, 0, 0)),
                pl.BlockSpec((1, 8, rows), lambda i, m: (i, 0, 0)),
            ],
            scratch_shapes=[
                pltpu.VMEM((lines, heads, rows, PAIR), BF),
                pltpu.VMEM((stride * lines, rows, PAIR), BF),
                pltpu.VMEM((8, rows), F32),
                pltpu.VMEM((8, rows), F32),
                pltpu.VMEM((heads, PAIR, rows), F32),
            ],
        ),
        out_shape=[jax.ShapeDtypeStruct((rows, q_cols), BF)] * lines
        + [
            jax.ShapeDtypeStruct((lines, heads, rows, PAIR), F32),
            jax.ShapeDtypeStruct((lines, 8, rows), F32),
        ],
        compiler_params=pltpu.CompilerParams(vmem_limit_bytes=48 * 1024 * 1024),
        cost_estimate=pl.CostEstimate(
            flops=36 * 4 * rows * rows * PAIR * 2, bytes_accessed=8 << 20, transcendentals=36 * rows * rows
        ),
        name="attend",
    )(meta, *q, *kv, start_row)


def attend_back_kernel(heads, rows, lines, stride, meta, *refs):
    q_refs, g_refs, kv_refs = refs[:lines], refs[lines : 2 * lines], refs[2 * lines : 2 * lines + stride]
    raw_ref, log_ref, start_ref = refs[2 * lines + stride : 2 * lines + stride + 3]
    outs = refs[2 * lines + stride + 3 :]
    dq_refs, (keep_ref, send_ref, q_s, g_s, kv_s, dq_s, dkv_s, delta_s) = outs[:lines], outs[lines:]
    slot, place, own, low, clear = position(meta, lines)

    @pl.when(slot == 0)
    def _():
        spread_heads(q_refs, q_s, heads, False)
        spread_heads(g_refs, g_s, heads, True)
        gather_blocks(kv_refs, kv_s, lines)
        dkv_s[...] = jnp.zeros_like(dkv_s)

    dq_s[...] = jnp.zeros_like(dq_s)
    for h in range(heads):
        prod = raw_ref[0, h] * g_s[slot, h].astype(F32)
        delta_s[h : h + 1, :] = jnp.sum(prod.T, axis=0, keepdims=True)

    def step(blk, masked):
        x = blk ^ place
        index = (x % stride) * lines + x // stride
        kv = kv_s[index]
        if masked:
            seen = visible(blk, own, rows, start_ref[0])
        for h in range(heads):
            q = q_s[slot, h]
            g = g_s[slot, h]
            s = dot(kv, q, NT)
            if masked:
                s = jnp.where(seen, s, NEG)
            p = jnp.exp(s - log_ref[0, h : h + 1, :])
            gp = dot(kv, g, NT)
            gs = (p * (gp - delta_s[h : h + 1, :])).astype(BF)
            part = dot(gs, q) + dot(p.astype(BF), g)
            dkv_s[index] += part
            dq_s[h] += dot(gs, kv, TN)

    walk(low, clear, own, step)
    dq = jnp.concatenate([dq_s[h][:, :HD] * 0.125 for h in range(heads)], 1).astype(BF)
    for s in range(lines):

        @pl.when(slot == s)
        def _(s=s):
            dq_refs[s][...] = dq

    @pl.when(slot == lines - 1)
    def _():
        for m in range(stride):
            half = m // 2
            out = send_ref if m % 2 else keep_ref
            out[half * lines : (half + 1) * lines] = dkv_s[m * lines : (m + 1) * lines].astype(BF)


def attend_back(meta, q, g, kv, raw, logs, start_row, heads):
    lines, stride = len(q), len(kv)
    rows, q_cols = q[0].shape
    blocks = lines * stride
    narrow = whole_block((rows, q_cols))
    half = whole_block((blocks // 2, rows, PAIR))
    return pl.pallas_call(
        functools.partial(attend_back_kernel, heads, rows, lines, stride),
        grid_spec=pltpu.PrefetchScalarGridSpec(
            num_scalar_prefetch=1,
            grid=(lines,),
            in_specs=[narrow] * (2 * lines)
            + [whole_block((lines, rows, PAIR))] * stride
            + [
                pl.BlockSpec((1, heads, rows, PAIR), lambda i, m: (i, 0, 0, 0)),
                pl.BlockSpec((1, 8, rows), lambda i, m: (i, 0, 0)),
                pl.BlockSpec((1, 1, rows), lambda i, m: (i, 0, 0)),
            ],
            out_specs=[narrow] * lines + [half] * 2,
            scratch_shapes=[
                pltpu.VMEM((lines, heads, rows, PAIR), BF),
                pltpu.VMEM((lines, heads, rows, PAIR), BF),
                pltpu.VMEM((blocks, rows, PAIR), BF),
                pltpu.VMEM((heads, rows, PAIR), F32),
                pltpu.VMEM((blocks, rows, PAIR), F32),
                pltpu.VMEM((8, rows), F32),
            ],
        ),
        out_shape=[jax.ShapeDtypeStruct((rows, q_cols), BF)] * lines
        + [jax.ShapeDtypeStruct((blocks // 2, rows, PAIR), BF)] * 2,
        compiler_params=pltpu.CompilerParams(vmem_limit_bytes=56 * 1024 * 1024),
        cost_estimate=pl.CostEstimate(
            flops=36 * 10 * rows * rows * PAIR * 2, bytes_accessed=10 << 20, transcendentals=36 * rows * rows
        ),
        name="attend_back",
    )(meta, *q, *g, *kv, raw, logs, start_row)


def experts_kernel(x_ref, g_ref, gate_ref, wg_ref, wu_ref, wd_ref, out_ref, back_ref, inner_ref):
    x = x_ref[0]
    g = g_ref[0]
    gate = gate_ref[0]
    gate_pre = dot(x, wg_ref[0])
    up_pre = dot(x, wu_ref[0])
    sigma = jax.nn.sigmoid(gate_pre)
    silu = gate_pre * sigma
    act = (silu * up_pre).astype(BF)
    out = dot(act, wd_ref[0])
    g_float = g.astype(F32)
    inner = jnp.sum(out * g_float, axis=-1, keepdims=True)
    inner_ref[0] = jnp.broadcast_to(inner, (x.shape[0], 128)).T[:8]
    out_ref[0] = (gate * out).astype(BF)
    grad_expert = (gate * g_float).astype(BF)
    grad_act = dot(grad_expert, wd_ref[0], NT)
    grad_gate = (grad_act * up_pre * sigma * (1.0 + gate_pre * (1.0 - sigma))).astype(BF)
    grad_up = (grad_act * silu).astype(BF)
    back_ref[0] = (dot(grad_gate, wg_ref[0], NT) + dot(grad_up, wu_ref[0], NT)).astype(BF)


def run_experts(x, g, gate, w_gate, w_up, w_down):
    experts, cap, width = x.shape
    hidden = w_gate.shape[2]

    def of(*shape):
        return pl.BlockSpec((1,) + shape, lambda e: (e, 0, 0))

    return pl.pallas_call(
        experts_kernel,
        grid=(experts,),
        in_specs=[
            of(cap, width),
            of(cap, width),
            of(cap, 1),
            of(width, hidden),
            of(width, hidden),
            of(hidden, width),
        ],
        out_specs=[of(cap, width), of(cap, width), of(8, cap)],
        out_shape=[
            jax.ShapeDtypeStruct((experts, cap, width), BF),
            jax.ShapeDtypeStruct((experts, cap, width), BF),
            jax.ShapeDtypeStruct((experts, 8, cap), F32),
        ],
        compiler_params=pltpu.CompilerParams(vmem_limit_bytes=48 * 1024 * 1024),
        cost_estimate=pl.CostEstimate(
            flops=experts * cap * width * hidden * 12,
            bytes_accessed=experts * width * (hidden * 6 + cap * 8),
            transcendentals=experts * cap * hidden,
        ),
        name="experts",
    )(x, g, gate, w_gate, w_up, w_down)


def owner_forward(e, held, place, x_owned, g_owned, gate_owned, w_gate, w_up, w_down):
    dp, _, cap, width = x_owned.shape[0], held, x_owned.shape[1], x_owned.shape[2]

    def mine(x):
        return x.reshape((dp, held, cap) + x.shape[2:])[:, e].reshape((dp * cap,) + x.shape[2:])

    def weight(w):
        return lax.dynamic_index_in_dim(w, place * held + e, 0, keepdims=False)

    x = mine(x_owned)
    gate_pre = dot(x, weight(w_gate))
    up_pre = dot(x, weight(w_up))
    sigma = jax.nn.sigmoid(gate_pre)
    silu = gate_pre * sigma
    act = (silu * up_pre).astype(BF)
    grad_expert = (mine(gate_owned)[:, None] * mine(g_owned).astype(F32)).astype(BF)
    grad_act = dot(grad_expert, weight(w_down), NT)
    grad_gate = (grad_act * up_pre * sigma * (1.0 + gate_pre * (1.0 - sigma))).astype(BF)
    grad_up = (grad_act * silu).astype(BF)
    return x, act, grad_expert, grad_gate, grad_up


def shards(
    layer_in,
    norm1_gain,
    w_query,
    w_key,
    w_value,
    w_out,
    norm2_gain,
    router,
    w_gate,
    w_up,
    w_down,
    segments,
    routes,
    out_grad,
):
    rows, width = layer_in.shape
    kv_heads = w_key.shape[1] // HD
    group = w_query.shape[1] // HD // kv_heads
    q_cols = group * HD
    experts = w_gate.shape[0]
    dp = lax.axis_size("dp")
    place = lax.axis_index("dp")
    tensor_size = lax.axis_size("tensor")
    tensor_at = lax.axis_index("tensor")
    lines = kv_heads
    stride = dp // lines
    line = place >> (stride.bit_length() - 1)
    part = rows // tensor_size
    first = tensor_at * part
    held = experts // dp
    cols = width // tensor_size

    names = jnp.arange(experts, dtype=jnp.int32)
    named = jnp.any(routes[:, :, None] == names[None, None, :], axis=1)
    earlier = jnp.tril(jnp.ones((rows, rows), BF), -1)
    slots = jnp.where(named, dot(earlier, named.astype(BF)).astype(jnp.int32), -1)
    in_slot = slots.T[:, None, :] == jnp.arange(CAP, dtype=jnp.int32)[None, :, None]
    to_slots = in_slot.astype(BF).reshape(experts * CAP, rows)
    from_slots = (
        (slots[:, :, None] == jnp.arange(CAP, dtype=jnp.int32)[None, None, :])
        .astype(BF)
        .reshape(rows, experts * CAP)
    )

    def halves(x):
        own = lax.dynamic_slice_in_dim(x, tensor_at * cols, cols, 2)
        return own[..., : cols // 2], own[..., cols // 2 :]

    q_blocks = place ^ (jnp.arange(lines, dtype=jnp.int32) * stride)
    seg_query = jnp.stack(
        [lax.dynamic_slice_in_dim(segments, q_blocks[s] * rows, rows, 0) for s in range(lines)]
    )
    documents = jnp.arange(DOCS, dtype=jnp.int32)
    lengths_before = jnp.sum(
        (segments[None, :] < documents[:, None]).astype(jnp.int32), axis=1
    )
    starts = jnp.sum(
        jnp.where(seg_query[None] == documents[:, None, None], lengths_before[:, None, None], 0),
        axis=0,
    )
    shift = rows.bit_length() - 1
    meta = jnp.concatenate(
        [place[None], q_blocks, starts[:, 0] >> shift, (starts[:, -1] + rows - 1) >> shift]
    ).astype(jnp.int32)

    normed_in, kv_mine, q_mine = project(line, layer_in, norm1_gain, w_query, w_key, w_value, lines)

    def to_lines(blocks):
        return [b if s == 0 else across(b, "dp", s * stride) for s, b in enumerate(blocks)]

    kv = [jnp.stack(to_lines(kv_mine))]
    q = to_lines(q_mine)
    for bit in reversed(bits_of(stride)):
        kv = [piece for one in kv for piece in (one, across(one, "dp", bit))]
    g_slots = dot(to_slots, out_grad).astype(BF).reshape(experts, CAP, width)
    g_sent, (kv, q, starts, meta) = after(halves(g_slots), (kv, q, starts, meta))
    g_first = to_owner(g_sent[0])
    *mixed_far, raw, logs = attend(meta, q, kv, starts[:, None, :], group)
    mixed_far, g_first = after(mixed_far, g_first)

    def from_lines(blocks):
        return xor_blocks(to_lines(blocks), line)

    mixed = jnp.concatenate(from_lines(mixed_far), 1)
    g_late, mixed = after(g_sent[1], mixed)
    g_second = to_owner(g_late)
    attn = scatter_tensor(dot(mixed, w_out))
    hidden = lax.dynamic_slice_in_dim(layer_in, first, part, 0).astype(F32) + attn
    factor_two = norm_factor(hidden)
    unit_two = hidden * factor_two
    normed_mid = gather_tensor((unit_two * norm2_gain).astype(BF), 0)

    logits = dot(normed_mid, router)
    peak = jnp.max(jnp.where(named, logits, -jnp.inf), axis=1, keepdims=True)
    expo = jnp.where(named, jnp.exp(jnp.where(named, logits - peak, 0.0)), 0.0)
    gates = expo / jnp.sum(expo, axis=1, keepdims=True)
    slot_gate = jnp.sum(jnp.where(in_slot, gates.T[:, None, :], 0.0), axis=-1)

    x_slots = dot(to_slots, normed_mid).astype(BF).reshape(experts, CAP, width)
    x_early, x_late = halves(x_slots)
    x_early, g_second = after(x_early, g_second)
    x_first = to_owner(x_early)
    gate_high = lax.reduce_precision(slot_gate, 8, 7)
    gate_mid = lax.reduce_precision(slot_gate - gate_high, 8, 7)
    gate_pieces = jnp.stack([gate_high, gate_mid, slot_gate - gate_high - gate_mid], 2)
    x_late = jnp.concatenate(
        [x_late, jnp.pad(gate_pieces.astype(BF), ((0, 0), (0, 0), (0, 125)))], 2
    )
    g_first, x_slots = after(g_first, x_slots)
    g_first = swap_tensor(g_first, 2)

    out_slots, back_slots, inner_slots = run_experts(
        x_slots, g_slots, slot_gate[:, :, None], w_gate, w_up, w_down
    )
    back_slots, (x_first, g_first) = after(back_slots, (x_first, g_first))
    x_late, back_slots = after(x_late, back_slots)
    x_second = to_owner(x_late)
    moe_part = dot(from_slots, out_slots.reshape(experts * CAP, width))
    grad_gates = jnp.sum(
        jnp.where(
            slots[:, :, None] == jnp.arange(CAP, dtype=jnp.int32)[None, None, :],
            inner_slots[None, :, 0, :],
            0.0,
        ),
        axis=-1,
    )
    grad_logits = gates * (grad_gates - jnp.sum(gates * grad_gates, axis=-1, keepdims=True))
    router_part = lax.dot_general(
        grad_logits, normed_mid.astype(F32), TN, precision=HIGH, preferred_element_type=F32
    )
    grad_mid_part = dot(from_slots, back_slots.reshape(experts * CAP, width)) + lax.dot_general(
        grad_logits, router.astype(F32), NT, precision=HIGH, preferred_element_type=F32
    )
    grad_mid = scatter_tensor(grad_mid_part)
    gain_two_part = jnp.sum(grad_mid * unit_two, axis=0)
    grad_rows = lax.dynamic_slice_in_dim(out_grad, first, part, 0).astype(F32)
    grad_hidden = grad_rows + norm_back(unit_two, factor_two, norm2_gain, grad_mid)
    hidden_low = gather_tensor(grad_hidden.astype(BF), 0)
    (x_first, x_second, g_second), hidden_low = after((x_first, x_second, g_second), hidden_low)
    g_second = swap_tensor(g_second, 2)
    gate_owned = jnp.sum(x_second[..., cols // 2 : cols // 2 + 3].astype(F32), axis=2)
    x_owned = swap_tensor(jnp.concatenate([x_first, x_second[..., : cols // 2]], 2), 2)
    grad_mixed = dot(hidden_low, w_out, NT).astype(BF)
    g = to_lines(xor_blocks(columns_of(grad_mixed, lines), line))
    *dq_far, keep, send = attend_back(meta, q, g, kv, raw, logs, starts[:, None, :], group)

    dkv = (keep + across(send, "dp", 1)).reshape(stride // 2, lines, rows, PAIR)
    dkv, dq_far = after(dkv, dq_far)
    for bit in bits_of(stride)[1:]:
        view = dkv.reshape((dkv.shape[0] // 2, 2) + dkv.shape[1:])
        dkv = view[:, 0] + across(view[:, 1], "dp", bit)
    dkv, moe_part, x_owned, g_second = lax.optimization_barrier(
        (dkv[0], moe_part, x_owned, g_second)
    )
    x_owned = assemble(x_owned, 2)
    size = cols // 2
    g_pieces = [assemble(g_first, 2), assemble(g_second, 2)]
    g_owned = jnp.concatenate(
        [g[..., t * size : (t + 1) * size] for t in range(tensor_size) for g in g_pieces], 2
    )
    dq = from_lines(dq_far)
    layer_out = (hidden + scatter_tensor(moe_part)).astype(BF)
    dkv = from_lines([dkv[s] for s in range(lines)])
    owned = [
        owner_forward(e, held, place, x_owned, g_owned, gate_owned, w_gate, w_up, w_down)
        for e in range(held)
    ]
    w_all = jnp.concatenate([w_query, w_key, w_value], 1)
    dqkv = jnp.concatenate(dq + [b[:, :HD] for b in dkv] + [b[:, HD:] for b in dkv], 1)
    weight_part = jnp.concatenate(
        [dot(normed_in, dqkv, TN).astype(BF), dot(hidden_low, mixed, TN).astype(BF)], 1
    )
    dqkv, weight_part, owned = lax.optimization_barrier((dqkv, weight_part, owned))
    grad_in_part = dot(dqkv, w_all, NT)
    in_float = layer_in.astype(F32)
    factor_one = norm_factor(in_float)
    small_in = jnp.concatenate(
        [router_part, gain_two_part[None], jnp.sum(grad_in_part * (in_float * factor_one), axis=0)[None]], 0
    )
    weight_grad, small_in = scatter_rows(weight_part, small_in)
    grad_in_rows = scatter_tensor(grad_in_part)
    ends = [0]
    for size in (lines * q_cols, lines * HD, lines * HD, lines * q_cols):
        ends.append(ends[-1] + size)
    query_out, key_out, value_out, proj_out = (
        weight_grad[:, a:b] for a, b in zip(ends[:-1], ends[1:])
    )
    proj_out = proj_out.T

    factor_rows = lax.dynamic_slice_in_dim(factor_one, first, part, 0)
    unit_rows = lax.dynamic_slice_in_dim(in_float, first, part, 0) * factor_rows
    input_grad = grad_hidden + norm_back(unit_rows, factor_rows, norm1_gain, grad_in_rows)
    small = total(small_in)
    gain_one_grad = small[experts + 1]
    gain_two_grad = small[experts]
    router_grad = small[:experts].T

    grad_outs = [
        (dot(x, grad_gate, TN), dot(x, grad_up, TN), dot(act, grad_expert, TN))
        for x, act, grad_expert, grad_gate, grad_up in owned
    ]
    gate_out, up_out, down_out = (jnp.stack(each) for each in zip(*grad_outs))
    return (
        layer_out,
        input_grad,
        gain_one_grad,
        query_out,
        key_out,
        value_out,
        proj_out,
        gain_two_grad,
        router_grad,
        gate_out,
        up_out,
        down_out,
    )


def solution(mesh):
    in_specs = (
        P("dp", None),
        P(),
        P(None, "tensor"),
        P(None, "tensor"),
        P(None, "tensor"),
        P("tensor", None),
        P(),
        P(),
        P(None, None, "tensor"),
        P(None, None, "tensor"),
        P(None, "tensor", None),
        P(),
        P("dp", None),
        P("dp", None),
    )
    out_specs = (
        P(("dp", "tensor"), None),
        P(("dp", "tensor"), None),
        P(),
        P("dp", "tensor"),
        P("dp", "tensor"),
        P("dp", "tensor"),
        P("tensor", "dp"),
        P(),
        P(),
        P("dp", None, "tensor"),
        P("dp", None, "tensor"),
        P("dp", "tensor", None),
    )
    return jax.shard_map(shards, mesh=mesh, in_specs=in_specs, out_specs=out_specs, check_vma=False)
```

time: 694 us -> 590 us (0.85)
  waiting for transfers between devices: 205 us -> 154 us
  starting transfers between devices: 144 us -> 116 us
  other arithmetic: 77.5 us -> 51.7 us
  local copies, waits for them, and re-layouts: 68.6 us -> 48.8 us
  Pallas kernels: 101 us -> 118 us
    ppermute x56 -> x44, waiting for transfers between devices: 205 us -> 154 us  [across(): return lax.ppermute(x, axis, [(i, i ^ mask) for i in range(n)])]
    all_to_all x5 -> x4, starting transfers between devices: 49.5 us -> 33.6 us  [to_owner(): return lax.all_to_all(x, 'dp', 0, 0, tiled=True)]
    ppermute x56 -> x44, starting transfers between devices: 94.1 us -> 82.9 us  [across(): return lax.ppermute(x, axis, [(i, i ^ mask) for i in range(n)])]
    slice x21 -> x5, local copies, waits for them, and re-layouts: 13 us -> 3.61 us  [the longest x1 1.61 us: shards(): x_second[..., :cols // 2]]
    optimization_barrier x0 -> x1, local copies, waits for them, and re-layouts: none -> 8.61 us  [shards(): lax.optimization_barrier((dqkv, weight_part, owned))]
    reduce_sum x2 -> x4, other arithmetic: 10.1 us -> 1.99 us  [the longest x1 1.26 us: shards(): jnp.sum(x_second[..., cols // 2:cols // 2 + 3].astype(F32), axis=2)]
    unnamed x166 -> x148, local copies, waits for them, and re-layouts: 21.7 us -> 16.6 us
    dot_general x11 -> x9, matrix products: 42.9 us -> 41.2 us  [dot(): return jnp.dot(a, b, preferred_element_type=F32)]
  transfers between devices with their start and end apart: 61 -> 48, of which waited for: 28 -> 20; matrix products, arithmetic and copies ran while one was open for 27% -> 24% of each run, Pallas kernels for 15% -> 19%
where the time goes in v2:
time: 590 us; the launch traced here: 582 us
  waiting for transfers between devices  154 us (26%)
  Pallas kernels  118 us (20%)
  starting transfers between devices  116 us (20%)
  matrix products  88 us (15%)
  other arithmetic  51.7 us (9%)
  local copies, waits for them, and re-layouts  48.8 us (8%)
    ppermute x44, waiting for transfers between devices, across(): return lax.ppermute(x, axis, [(i, i ^ mask) for i in range(n)])  154 us
    ppermute x44, starting transfers between devices, across(): return lax.ppermute(x, axis, [(i, i ^ mask) for i in range(n)])  82.9 us
    pallas_call x1, Pallas kernels, run_experts(): pl.pallas_call(experts_kernel, grid=(experts,), in_specs=[of(cap, width),...  45.4 us
    dot_general x8, matrix products, dot(): return lax.dot_general(a, b, dims, preferred_element_type=F32)  44 us
    dot_general x9, matrix products, dot(): return jnp.dot(a, b, preferred_element_type=F32)  41.2 us
    pallas_call x1, Pallas kernels, attend_back(): pl.pallas_call(functools.partial(attend_back_kernel, heads, rows, lines,...  38.6 us
    all_to_all x4, starting transfers between devices, to_owner(): return lax.all_to_all(x, 'dp', 0, 0, tiled=True)  33.6 us
    pallas_call x1, Pallas kernels, attend(): pl.pallas_call(functools.partial(attend_kernel, heads, rows, lines, strid...  28.8 us
  transfers between devices with their start and end apart: 48, of which 20 were waited for; matrix products, arithmetic and copies ran while one was open for 24% of the time, Pallas kernels for 19%

profile of v2, /device:TPU:0, one launch (start us, length us, event | category | flops | bytes accessed | tf_op | source)
XLA Modules:
  0.0 582.0 jit_solution(8263167618090364903)
XLA Ops:
  3.8 5.7 project.1
  11.3 5.1 collective-permute-start.2
  18.4 2.9 collective-permute-start.7
  30.1 6.7 %convolution_convert_fusion.2 = bf16[2048,1536]{1,0:T(8,128)(2,1)} fusion(pred[2048,512]{1,0:T(32,128)(4,1)S(1)} %bitcast_compare_fusion, bf16[512,1536]{1,0:T(8,128)(2,1)} %param.27), kind=kOutput, calls=%fused_computation.5 | convolution fusion | flops 3224371200 | bytes 8912896 | tf_op jit(solution)/shard_map/dot_general | solution.py:26
  36.9 3.7 collective-permute-done.4.refs_6_.refs_10_
  40.9 4.1 constant_dynamic-slice_fusion.3
  45.4 8.6 %all-to-all-start = ((bf16[16,128,384]{2,1,0:T(8,128)(2,1)}), bf16[16,128,384]{2,1,0:T(8,128)(2,1)}, u32[]{:S(2)}, u32[]{:S(2)}) async-start(bf16[16,128,384]{2,1,0:T(8,128)(2,1)} %get-tuple-element.113), calls=%async_computation | async-start | bytes 3145728 | tf_op jit(solution)/shard_map/all_to_all | solution.py:44
  56.0 28.8 %attend.1 = (bf16[512,192]{1,0:T(8,128)(2,1)S(1)}, bf16[512,192]{1,0:T(8,128)(2,1)S(1)}, bf16[512,192]{1,0:T(8,128)(2,1)S(1)}, bf16[512,192]{1,0:T(8,128)(2,1)S(...) custom-call(s32[13]{0:T(128)S(1)} %pad_add_fusion.1.meta, bf16[512,192]{1,0:T(8,128)(2,1)S(1)} %copy-done.16, ...), custom_call_target="tpu_custom_call" | custom-call | flops 9663676416 | bytes 8388608 | tf_op jit(solution)/shard_map/attend/pallas_call | solution.py:305
  86.9 3.9 collective-permute-start.9
  90.8 2.5 collective-permute-start.10
  95.4 16.8 %collective-permute-done.10 = bf16[512,192]{1,0:T(8,128)(2,1)S(1)} collective-permute-done((bf16[512,192]{1,0:T(8,128)(2,1)}, bf16[512,192]{1,0:T(8,128)(2,1)S(1)}, u32[]{:S(2)}, u32[]{:S(2)}) %collective-permute-start.10) | collective-permute-done | bytes 196640 | tf_op jit(solution)/shard_map/ppermute | solution.py:32
  118.3 10.5 %all-to-all-start.1 = ((bf16[16,128,384]{2,1,0:T(8,128)(2,1)}), bf16[16,128,384]{2,1,0:T(8,128)(2,1)}, u32[]{:S(2)}, u32[]{:S(2)}) async-start(bf16[16,128,384]{2,1,0:T(8,128)(2,1)} %get-tuple-element.122), calls=%async_computation.1 | async-start | bytes 3145728 | tf_op jit(solution)/shard_map/all_to_all | solution.py:44
  128.8 6.7 %collective-permute-done.12 = bf16[256,1536]{1,0:T(8,128)(2,1)} collective-permute-done((bf16[256,1536]{1,0:T(8,128)(2,1)S(1)}, bf16[256,1536]{1,0:T(8,128)(2,1)}, u32[]{:S(2)}, u32[]{:S(2)}) %collective-permute-start.12) | collective-permute-done | bytes 786464 | tf_op jit(solution)/shard_map/ppermute | solution.py:32
  135.5 2.2 multiply_reduce_fusion.5
  141.5 18.2 %collective-permute-done.13 = bf16[256,1536]{1,0:T(8,128)(2,1)S(1)} collective-permute-done((bf16[256,1536]{1,0:T(8,128)(2,1)}, bf16[256,1536]{1,0:T(8,128)(2,1)S(1)}, u32[]{:S(2)}, u32[]{:S(2)}) %collective-permute-start.13) | collective-permute-done | bytes 786464 | tf_op jit(solution)/shard_map/ppermute | solution.py:32
  162.2 3.6 convolution_convert_fusion.1
  165.8 2.6 copy-done.21
  168.4 2.0 constant_dynamic-slice_fusion.2
  170.5 8.2 %all-to-all-start.2 = ((bf16[16,128,384]{2,1,0:T(8,128)(2,1)}), bf16[16,128,384]{2,1,0:T(8,128)(2,1)}, u32[]{:S(2)}, u32[]{:S(2)}) async-start(bf16[16,128,384]{2,1,0:T(8,128)(2,1)} %get-tuple-element.123), calls=%async_computation.2 | async-start | bytes 3145728 | tf_op jit(solution)/shard_map/all_to_all | solution.py:44
  182.2 45.4 %experts.1 = (bf16[16,128,1536]{2,1,0:T(8,128)(2,1)}, bf16[16,128,1536]{2,1,0:T(8,128)(2,1)}, f32[16,8,128]{2,1,0:T(8,128)S(1)}) custom-call(bf16[16,128,1536]{2,1,0:T(8,128)(2,1)} %bitcast.173, bf16[16,128,1536]{2,1,0:T(8,128)(2,1)} %bitcast.171, f32[16,128,1]{2,1,0:T(8,128)S(1)} %copy.36.gate_ref, bf16[16,1536,512]{2,1,0:T(8,128)(2,1)} %wg_ref.1, ...), custom_call_target="tpu_custom_call" | custom-call | flops 19327352832 | bytes 100663296 | tf_op jit(solution)/shard_map/experts/pallas_call | solution.py:459
  227.7 2.6 select_reduce_fusion
  231.9 6.3 %all-to-all-start.3 = ((bf16[16,128,512]{2,1,0:T(8,128)(2,1)}), bf16[16,128,512]{2,1,0:T(8,128)(2,1)}, u32[]{:S(2)}, u32[]{:S(2)}) async-start(bf16[16,128,512]{2,1,0:T(8,128)(2,1)} %fusion.22), calls=%async_computation.3 | async-start | bytes 4194304 | tf_op jit(solution)/shard_map/all_to_all | solution.py:44
  238.2 6.2 %fusion.20 = f32[512,1536]{1,0:T(8,128)S(1)} fusion(bf16[16,128,1536]{2,1,0:T(8,128)(2,1)} %get-tuple-element.129, s32[512,16]{0,1:T(8,128)S(1)} %broadcast_select_fusion.40), kind=kOutput, calls=%fused_computation.40 | convolution fusion | flops 3222274048 | bytes 9469952 | tf_op jit(solution)/shard_map/dot_general | solution.py:26
  246.7 19.4 %collective-permute-done.15 = bf16[256,1536]{1,0:T(8,128)(2,1)S(1)} collective-permute-done((bf16[256,1536]{1,0:T(8,128)(2,1)S(1)}, bf16[256,1536]{1,0:T(8,128)(2,1)S(1)}, u32[]{:S(2)}, u32[]{:S(2)}) %collective-permute-start.15) | collective-permute-done | bytes 786464 | tf_op jit(solution)/shard_map/ppermute | solution.py:32
  269.0 2.1 convert_element_type.124
  273.5 14.3 %collective-permute-done.16 = bf16[256,1536]{1,0:T(8,128)(2,1)} collective-permute-done((bf16[256,1536]{1,0:T(8,128)(2,1)S(1)}, bf16[256,1536]{1,0:T(8,128)(2,1)}, u32[]{:S(2)}, u32[]{:S(2)}) %collective-permute-start.16) | collective-permute-done | bytes 786464 | tf_op jit(solution)/shard_map/ppermute | solution.py:32
  290.4 2.9 convolution_convert_fusion.4
  295.5 2.2 collective-permute-start.18
  305.5 11.4 %collective-permute-done.18.refs_6_ = bf16[512,192]{1,0:T(8,128)(2,1)S(1)} collective-permute-done((bf16[512,192]{1,0:T(8,128)(2,1)S(1)}, bf16[512,192]{1,0:T(8,128)(2,1)S(1)}, u32[]{:S(2)}, u32[]{:S(2)}) %collective-permute-start.18) | collective-permute-done | bytes 196640 | tf_op jit(solution)/shard_map/ppermute | solution.py:32
  317.7 38.6 %attend_back.1 = (bf16[512,192]{1,0:T(8,128)(2,1)}, bf16[512,192]{1,0:T(8,128)(2,1)}, bf16[512,192]{1,0:T(8,128)(2,1)}, bf16[512,192]{1,0:T(8,128)(2,1)}, bf16[8...) custom-call(s32[13]{0:T(128)} %copy-done.4, bf16[512,192]{1,0:T(8,128)(2,1)} %copy-done.15, ...), custom_call_target="tpu_custom_call" | custom-call | flops 24159191040 | bytes 10485760 | tf_op jit(solution)/shard_map/attend_back/pallas_call | solution.py:399
  356.3 3.7 collective-permute-start.20
  360.0 7.9 %fusion.21 = f32[512,1536]{1,0:T(8,128)} fusion(bf16[16,128,1536]{2,1,0:T(8,128)(2,1)} %get-tuple-element.141, s32[512,16]{0,1:T(8,128)S(1)} %broadcast_select_fusion.40), kind=kOutput, calls=%fused_computation.41 | convolution fusion | flops 3222274048 | bytes 9469952 | tf_op jit(solution)/shard_map/dot_general | solution.py:26
  368.4 3.3 broadcast_select_fusion.5
  372.7 7.7 %collective-permute-start.26 = (bf16[512,192]{1,0:T(8,128)(2,1)S(1)}, bf16[512,192]{1,0:T(8,128)(2,1)S(1)}, u32[]{:S(2)}, u32[]{:S(2)}) collective-permute-start(bf16[512,192]{1,0:T(8,128)(2,1)S(1)} %copy-done.61), channel_id=1, source_target_pairs={{0,16},{2,18},{4,20},{6,22},{8,24},{10,26},{12,28},{14,30},{16,0},... | collective-permute-start | bytes 589832 | tf_op jit(solution)/shard_map/ppermute | solution.py:32
  380.4 10.9 %collective-permute-start.21 = (bf16[1,4,512,128]{3,2,1,0:T(8,128)(2,1)S(1)}, bf16[1,4,512,128]{3,2,1,0:T(8,128)(2,1)S(1)}, u32[]{:S(2)}, u32[]{:S(2)}) collective-permute-start(bf16[1,4,512,128]{3,2,1,0:T(8,128)(2,1)S(1)} %slice_bitcast_fusion), channel_id=1, source_target_pairs={{0,4},{2,6},{4,0},{6,2},{8,12},{10,14},{12,8},{14,10},{16,20},{18,... | collective-permute-start | bytes 1572872 | tf_op jit(solution)/shard_map/ppermute | solution.py:32
  392.8 2.8 convolution_convert_fusion.3
  396.9 5.4 collective-permute-done.25
  402.3 3.7 collective-permute-done.27
  407.4 4.0 broadcast_select_fusion.1
  411.4 2.4 pad_maximum_fusion.1
  413.8 7.5 %fusion.28 = f32[2048,512]{1,0:T(8,128)} fusion(bf16[2048,1536]{1,0:T(8,128)(2,1)S(1)} %bitcast.175, bf16[16,1536,512]{2,1,0:T(8,128)(2,1)} %wg_ref.1, s32[]{:T(128)S(6)} %select_n.368), kind=kOutput, calls=%fused_computation.60 | convolution fusion | flops 3221225472 | bytes 12058628 | tf_op jit(solution)/shard_map/dot_general | solution.py:26
  421.3 6.3 %fusion.26 = f32[2048,512]{1,0:T(8,128)} fusion(bf16[2048,1536]{1,0:T(8,128)(2,1)S(1)} %bitcast.176, bf16[16,1536,512]{2,1,0:T(8,128)(2,1)} %wu_ref.1, s32[]{:T(128)S(6)} %select_n.368), kind=kOutput, calls=%fused_computation.58 | convolution fusion | flops 3221225472 | bytes 12058628 | tf_op jit(solution)/shard_map/dot_general | solution.py:26
  427.7 2.5 dynamic-slice_convert_fusion.1
  431.6 5.0 collective-permute-start.29
  440.1 10.2 %multiply_convert_fusion.2 = (bf16[2048,512]{1,0:T(8,128)(2,1)}, bf16[2048,512]{1,0:T(8,128)(2,1)}, bf16[2048,512]{1,0:T(8,128)(2,1)}) fusion(f32[2048,512]{1,0:T(8,128)} %fusion.28, f32[2048,512]{1,0:T(8,128)} %fusion.26, bf16[16,512,1536]{2,1,0:T(8,128)(2,1)} %wd_ref.1, s32[]{:T(128)S(6)} %select_n.368, bf16[2048,384]{1,0:T(8,128)(2,1)S(1)} %bitcast.188, ...), kind=kOutput, calls=%fused_computation.20 | convolution fusion | flops 3268411392 | bytes 22552580 | tf_op jit(solution)/shard_map/dot_general | solution.py:27
  450.3 3.9 fusion
  455.2 3.5 concatenate.56
  458.7 3.7 convolution_convert_fusion
  462.4 3.1 pad_maximum_fusion
  465.5 6.0 %multiply_reduce_fusion = (f32[1536]{0:T(1024)S(1)}, f32[512,1536]{1,0:T(8,128)}) fusion(f32[512]{0:T(512)S(1)} %add_rsqrt_fusion, bf16[512,1536]{1,0:T(8,128)(2,1)S(1)} %copy-done.24, bf16[512,1280]{1,0:T(8,128)(2,1)} %concatenate.56, bf16[1536,256]{1,0:T(8,128)(2,1)S(1)} %copy-done.8, bf16[1536,256]{1,0:T(8,128)(2,1)S(1)} %copy-done.6, ...), kind=kOutput, calls=%fused_computation.47 | convolution fusion | flops 2028206592 | bytes 9969664 | tf_op jit(solution)/shard_map/dot_general | solution.py:27
  471.5 8.6 %copy.38 = bf16[1536,2048]{1,0:T(8,128)(2,1)} copy(bf16[1536,2048]{0,1:T(8,128)(2,1)} %pad_maximum_fusion) | data formatting | bytes 12582912 | tf_op jit(solution)/shard_map/optimization_barrier | solution.py:681
  480.1 2.5 dynamic-slice_bitcast_fusion
  484.7 8.1 %convolution_bitcast_fusion.2 = f32[1,1536,512]{2,1,0:T(8,128)} fusion(bf16[2048,1536]{1,0:T(8,128)(2,1)} %bitcast.177, bf16[2048,512]{1,0:T(8,128)(2,1)S(1)} %copy-done.67), kind=kOutput, calls=%fused_computation.44 | convolution fusion | flops 3221225472 | bytes 11534336 | tf_op jit(solution)/shard_map/dot_general | solution.py:27
  492.8 5.1 convolution_bitcast_fusion.1
  498.0 5.1 convolution_bitcast_fusion
  503.9 11.9 %collective-permute-start.33 = (bf16[4,96,1024]{2,1,0:T(8,128)(2,1)S(1)}, bf16[4,96,1024]{2,1,0:T(8,128)(2,1)S(1)}, u32[]{:S(2)}, u32[]{:S(2)}) collective-permute-start(bf16[4,96,1024]{2,1,0:T(8,128)(2,1)S(1)} %dynamic-slice_bitcast_fusion.2), channel_id=1, source_target_pairs={{0,4},{2,6},{4,0},{6,2},{8,12},{10,14},{12,8},{14,10},{16,20},{18,... | collective-permute-start | bytes 2359304 | tf_op jit(solution)/shard_map/ppermute | solution.py:32
  517.8 2.4 add_convert_fusion
  520.7 12.7 %collective-permute-done.33 = bf16[4,96,1024]{2,1,0:T(8,128)(2,1)S(1)} collective-permute-done((bf16[4,96,1024]{2,1,0:T(8,128)(2,1)S(1)}, bf16[4,96,1024]{2,1,0:T(8,128)(2,1)S(1)}, u32[]{:S(2)}, u32[]{:S(2)}) %collective-permute-start.33) | collective-permute-done | bytes 786464 | tf_op jit(solution)/shard_map/ppermute | solution.py:32
  535.4 2.7 collective-permute-start.42
  539.0 5.2 collective-permute-done.36
  546.2 13.7 %collective-permute-done.37 = f32[18,1536]{1,0:T(8,128)S(1)} collective-permute-done((f32[18,1536]{1,0:T(8,128)S(1)}, f32[18,1536]{1,0:T(8,128)S(1)}, u32[]{:S(2)}, u32[]{:S(2)}) %collective-permute-start.37) | collective-permute-done | bytes 110624 | tf_op jit(solution)/shard_map/ppermute | solution.py:32
  561.9 6.9 %collective-permute-done.38 = f32[18,1536]{1,0:T(8,128)S(1)} collective-permute-done((f32[18,1536]{1,0:T(8,128)S(1)}, f32[18,1536]{1,0:T(8,128)S(1)}, u32[]{:S(2)}, u32[]{:S(2)}) %collective-permute-start.38) | collective-permute-done | bytes 110624 | tf_op jit(solution)/shard_map/ppermute | solution.py:32
  569.5 4.6 collective-permute-done.39
  575.4 4.0 collective-permute-done.41
  (308 shorter events, 85.9 us)
Async XLA Ops:
  0.6 112.9 %copy-start = (bf16[768,1536]{1,0:T(8,128)(2,1)S(1)}, bf16[768,1536]{1,0:T(8,128)(2,1)}, u32[]{:S(2)}) copy-start(bf16[768,1536]{1,0:T(8,128)(2,1)} %param.19) | copy-start | bytes 7077892
  3.8 20.8 %copy-start.58 = (s32[512,2]{0,1:T(2,128)S(1)}, s32[512,2]{0,1:T(2,128)}, u32[]{:S(2)}) copy-start(s32[512,2]{0,1:T(2,128)} %param.26) | copy-start | bytes 12292
  3.8 21.7 %copy-start.53 = (s32[8192]{0:T(1024)S(1)}, s32[8192]{0:T(1024)}, u32[]{:S(2)}) copy-start(s32[8192]{0:T(1024)} %param.25) | copy-start | bytes 98308
  11.3 15.3 %collective-permute-start.2 = (bf16[512,128]{1,0:T(8,128)(2,1)S(1)}, bf16[512,128]{1,0:T(8,128)(2,1)S(1)}, u32[]{:S(2)}, u32[]{:S(2)}) collective-permute-start(bf16[512,128]{1,0:T(8,128)(2,1)S(1)} %get-tuple-element.93), channel_id=1, source_target_pairs={{0,24},{2,26},{4,28},{6,30},{8,16},{10,18},{12,20},{14,22},{16,8},... | collective-permute-start | bytes 393224 | tf_op jit(solution)/shard_map/ppermute | solution.py:32
  16.4 12.1 %collective-permute-start.1 = (bf16[512,128]{1,0:T(8,128)(2,1)S(1)}, bf16[512,128]{1,0:T(8,128)(2,1)S(1)}, u32[]{:S(2)}, u32[]{:S(2)}) collective-permute-start(bf16[512,128]{1,0:T(8,128)(2,1)S(1)} %get-tuple-element.92), channel_id=1, source_target_pairs={{0,16},{2,18},{4,20},{6,22},{8,24},{10,26},{12,28},{14,30},{16,0},... | collective-permute-start | bytes 393224 | tf_op jit(solution)/shard_map/ppermute | solution.py:32
  16.4 12.1 %collective-permute-start = (bf16[512,128]{1,0:T(8,128)(2,1)S(1)}, bf16[512,128]{1,0:T(8,128)(2,1)S(1)}, u32[]{:S(2)}, u32[]{:S(2)}) collective-permute-start(bf16[512,128]{1,0:T(8,128)(2,1)S(1)} %get-tuple-element.91), channel_id=1, source_target_pairs={{0,8},{2,10},{4,12},{6,14},{8,0},{10,2},{12,4},{14,6},{16,24},{18,... | collective-permute-start | bytes 393224 | tf_op jit(solution)/shard_map/ppermute | solution.py:32
  16.9 28.1 %collective-permute-start.6 = (bf16[512,192]{1,0:T(8,128)(2,1)}, bf16[512,192]{1,0:T(8,128)(2,1)}, u32[]{:S(2)}, u32[]{:S(2)}) collective-permute-start(bf16[512,192]{1,0:T(8,128)(2,1)} %get-tuple-element.95), channel_id=1, source_target_pairs={{0,8},{2,10},{4,12},{6,14},{8,0},{10,2},{12,4},{14,6},{16,24},{18,... | collective-permute-start | bytes 589832 | tf_op jit(solution)/shard_map/ppermute | solution.py:32
  18.4 27.0 %collective-permute-start.7 = (bf16[512,192]{1,0:T(8,128)(2,1)}, bf16[512,192]{1,0:T(8,128)(2,1)}, u32[]{:S(2)}, u32[]{:S(2)}) collective-permute-start(bf16[512,192]{1,0:T(8,128)(2,1)} %get-tuple-element.96), channel_id=1, source_target_pairs={{0,16},{2,18},{4,20},{6,22},{8,24},{10,26},{12,28},{14,30},{16,0},... | collective-permute-start | bytes 589832 | tf_op jit(solution)/shard_map/ppermute | solution.py:32
  26.6 18.8 %collective-permute-start.8 = (bf16[512,192]{1,0:T(8,128)(2,1)}, bf16[512,192]{1,0:T(8,128)(2,1)}, u32[]{:S(2)}, u32[]{:S(2)}) collective-permute-start(bf16[512,192]{1,0:T(8,128)(2,1)} %get-tuple-element.97), channel_id=1, source_target_pairs={{0,24},{2,26},{4,28},{6,30},{8,16},{10,18},{12,20},{14,22},{16,8},... | collective-permute-start | bytes 589832 | tf_op jit(solution)/shard_map/ppermute | solution.py:32
  28.6 25.5 %copy-start.2 = (bf16[4,512,128]{2,1,0:T(8,128)(2,1)}, bf16[4,512,128]{2,1,0:T(8,128)(2,1)S(1)}, u32[]{:S(2)}) copy-start(bf16[4,512,128]{2,1,0:T(8,128)(2,1)S(1)} %pad_maximum_fusion.7.refs_4_.refs_8_) | copy-start | bytes 1572868
  28.6 12.0 %collective-permute-start.4 = (bf16[4,512,128]{2,1,0:T(8,128)(2,1)S(1)}, bf16[4,512,128]{2,1,0:T(8,128)(2,1)S(1)}, u32[]{:S(2)}, u32[]{:S(2)}) collective-permute-start(bf16[4,512,128]{2,1,0:T(8,128)(2,1)S(1)} %pad_maximum_fusion.7.refs_4_.refs_8_), channel_id=1, source_target_pairs={{0,4},{2,6},{4,0},{6,2},{8,12},{10,14},{12,8},{14,10},{16,20},{18,... | collective-permute-start | bytes 1572872 | tf_op jit(solution)/shard_map/ppermute | solution.py:32
  36.9 8.5 %collective-permute-start.3 = (bf16[4,512,128]{2,1,0:T(8,128)(2,1)S(1)}, bf16[4,512,128]{2,1,0:T(8,128)(2,1)}, u32[]{:S(2)}, u32[]{:S(2)}) collective-permute-start(bf16[4,512,128]{2,1,0:T(8,128)(2,1)S(1)} %pad_maximum_fusion.7.refs_4_.refs_8_), channel_id=1, source_target_pairs={{0,2},{2,0},{4,6},{6,4},{8,10},{10,8},{12,14},{14,12},{16,18},{18,... | collective-permute-start | bytes 1572872 | tf_op jit(solution)/shard_map/ppermute | solution.py:32
  40.6 4.8 collective-permute-start.5
  45.4 41.5 %all-to-all-start = ((bf16[16,128,384]{2,1,0:T(8,128)(2,1)}), bf16[16,128,384]{2,1,0:T(8,128)(2,1)}, u32[]{:S(2)}, u32[]{:S(2)}) async-start(bf16[16,128,384]{2,1,0:T(8,128)(2,1)} %get-tuple-element.113), calls=%async_computation | async-start | bytes 3145728 | tf_op jit(solution)/shard_map/all_to_all | solution.py:44
  56.0 28.8 %copy-start.3 = (s32[4,1,512]{2,1,0:T(1,128)}, s32[4,1,512]{2,1,0:T(1,128)S(1)}, u32[]{:S(2)}) copy-start(s32[4,1,512]{2,1,0:T(1,128)S(1)} %broadcast_in_dim.115.refs_8_.refs_14_) | copy-start | bytes 24580
  86.9 8.5 %collective-permute-start.9 = (bf16[512,192]{1,0:T(8,128)(2,1)}, bf16[512,192]{1,0:T(8,128)(2,1)S(1)}, u32[]{:S(2)}, u32[]{:S(2)}) collective-permute-start(bf16[512,192]{1,0:T(8,128)(2,1)} %copy-done.12), channel_id=1, source_target_pairs={{0,24},{2,26},{4,28},{6,30},{8,16},{10,18},{12,20},{14,22},{16,8},... | collective-permute-start | bytes 589832 | tf_op jit(solution)/shard_map/ppermute | solution.py:32
  90.8 21.4 %collective-permute-start.10 = (bf16[512,192]{1,0:T(8,128)(2,1)}, bf16[512,192]{1,0:T(8,128)(2,1)S(1)}, u32[]{:S(2)}, u32[]{:S(2)}) collective-permute-start(bf16[512,192]{1,0:T(8,128)(2,1)} %copy-done.11), channel_id=1, source_target_pairs={{0,16},{2,18},{4,20},{6,22},{8,24},{10,26},{12,28},{14,30},{16,0},... | collective-permute-start | bytes 589832 | tf_op jit(solution)/shard_map/ppermute | solution.py:32
  93.3 18.9 %collective-permute-start.11 = (bf16[512,192]{1,0:T(8,128)(2,1)S(1)}, bf16[512,192]{1,0:T(8,128)(2,1)}, u32[]{:S(2)}, u32[]{:S(2)}) collective-permute-start(bf16[512,192]{1,0:T(8,128)(2,1)S(1)} %get-tuple-element.116), channel_id=1, source_target_pairs={{0,8},{2,10},{4,12},{6,14},{8,0},{10,2},{12,4},{14,6},{16,24},{18,... | collective-permute-start | bytes 589832 | tf_op jit(solution)/shard_map/ppermute | solution.py:32
  116.7 18.8 %collective-permute-start.12 = (bf16[256,1536]{1,0:T(8,128)(2,1)S(1)}, bf16[256,1536]{1,0:T(8,128)(2,1)}, u32[]{:S(2)}, u32[]{:S(2)}) collective-permute-start(bf16[256,1536]{1,0:T(8,128)(2,1)S(1)} %dynamic-slice_convert_fusion.3), channel_id=1, source_target_pairs={{0,1},{1,0},{2,3},{3,2},{4,5},{5,4},{6,7},{7,6},{8,9},{9,8},{10,11... | collective-permute-start | bytes 2359304 | tf_op jit(solution)/shard_map/ppermute | solution.py:32
  118.3 52.2 %all-to-all-start.1 = ((bf16[16,128,384]{2,1,0:T(8,128)(2,1)}), bf16[16,128,384]{2,1,0:T(8,128)(2,1)}, u32[]{:S(2)}, u32[]{:S(2)}) async-start(bf16[16,128,384]{2,1,0:T(8,128)(2,1)} %get-tuple-element.122), calls=%async_computation.1 | async-start | bytes 3145728 | tf_op jit(solution)/shard_map/all_to_all | solution.py:44
  138.9 22.7 %copy-start.54 = (bf16[1536,16]{0,1:T(8,128)(2,1)S(1)}, bf16[1536,16]{0,1:T(8,128)(2,1)}, u32[]{:S(2)}) copy-start(bf16[1536,16]{0,1:T(8,128)(2,1)} %param.21) | copy-start | bytes 147460
  140.0 19.7 %collective-permute-start.13 = (bf16[256,1536]{1,0:T(8,128)(2,1)}, bf16[256,1536]{1,0:T(8,128)(2,1)S(1)}, u32[]{:S(2)}, u32[]{:S(2)}) collective-permute-start(bf16[256,1536]{1,0:T(8,128)(2,1)} %multiply_convert_fusion.5), channel_id=1, source_target_pairs={{0,1},{1,0},{2,3},{3,2},{4,5},{5,4},{6,7},{7,6},{8,9},{9,8},{10,11... | collective-permute-start | bytes 2359304 | tf_op jit(solution)/shard_map/ppermute | solution.py:32
  141.5 20.6 %copy-start.39 = (pred[2048,512]{1,0:T(32,128)(4,1)S(1)}, pred[2048,512]{1,0:T(32,128)(4,1)}, u32[]{:S(2)}) copy-start(pred[2048,512]{1,0:T(32,128)(4,1)} %copy-done.38) | copy-start | bytes 3145732
  170.5 61.5 %all-to-all-start.2 = ((bf16[16,128,384]{2,1,0:T(8,128)(2,1)}), bf16[16,128,384]{2,1,0:T(8,128)(2,1)}, u32[]{:S(2)}, u32[]{:S(2)}) async-start(bf16[16,128,384]{2,1,0:T(8,128)(2,1)} %get-tuple-element.123), calls=%async_computation.2 | async-start | bytes 3145728 | tf_op jit(solution)/shard_map/all_to_all | solution.py:44
  179.5 52.4 %collective-permute-start.14 = (bf16[16,128,384]{2,1,0:T(8,128)(2,1)}, bf16[16,128,384]{2,1,0:T(8,128)(2,1)}, u32[]{:S(2)}, u32[]{:S(2)}) collective-permute-start(bf16[16,128,384]{2,1,0:T(8,128)(2,1)} %all-to-all-done), channel_id=1, source_target_pairs={{0,1},{1,0},{2,3},{3,2},{4,5},{5,4},{6,7},{7,6},{8,9},{9,8},{10,11... | collective-permute-start | bytes 4718600 | tf_op jit(solution)/shard_map/ppermute | solution.py:32
  182.2 48.1 %copy-start.28 = (bf16[16,128,384]{2,1,0:T(8,128)(2,1)S(1)}, bf16[16,128,384]{2,1,0:T(8,128)(2,1)}, u32[]{:S(2)}) copy-start(bf16[16,128,384]{2,1,0:T(8,128)(2,1)} %get-tuple-element.183) | copy-start | bytes 4718596
  182.2 48.1 %copy-start.31 = (bf16[16,128,3]{2,1,0:T(8,128)(2,1)S(1)}, bf16[16,128,3]{2,1,0:T(8,128)(2,1)}, u32[]{:S(2)}) copy-start(bf16[16,128,3]{2,1,0:T(8,128)(2,1)} %copy.37) | copy-start | bytes 36868
  231.9 58.4 %all-to-all-start.3 = ((bf16[16,128,512]{2,1,0:T(8,128)(2,1)}), bf16[16,128,512]{2,1,0:T(8,128)(2,1)}, u32[]{:S(2)}, u32[]{:S(2)}) async-start(bf16[16,128,512]{2,1,0:T(8,128)(2,1)} %fusion.22), calls=%async_computation.3 | async-start | bytes 4194304 | tf_op jit(solution)/shard_map/all_to_all | solution.py:44
  244.5 21.7 %copy-start.19 = (f32[256,1536]{1,0:T(8,128)S(1)}, f32[256,1536]{1,0:T(8,128)}, u32[]{:S(2)}) copy-start(f32[256,1536]{1,0:T(8,128)} %copy-done.18) | copy-start | bytes 4718596
  246.0 20.7 %copy-start.46 = (bf16[512,1536]{1,0:T(8,128)(2,1)S(1)}, bf16[512,1536]{1,0:T(8,128)(2,1)}, u32[]{:S(2)}) copy-start(bf16[512,1536]{1,0:T(8,128)(2,1)} %param.27) | copy-start | bytes 4718596
  246.2 20.0 %collective-permute-start.15 = (bf16[256,1536]{1,0:T(8,128)(2,1)S(1)}, bf16[256,1536]{1,0:T(8,128)(2,1)S(1)}, u32[]{:S(2)}, u32[]{:S(2)}) collective-permute-start(bf16[256,1536]{1,0:T(8,128)(2,1)S(1)} %dynamic-slice_convert_fusion.2), channel_id=1, source_target_pairs={{0,1},{1,0},{2,3},{3,2},{4,5},{5,4},{6,7},{7,6},{8,9},{9,8},{10,11... | collective-permute-start | bytes 2359304 | tf_op jit(solution)/shard_map/ppermute | solution.py:32
  268.5 19.4 %collective-permute-start.16 = (bf16[256,1536]{1,0:T(8,128)(2,1)S(1)}, bf16[256,1536]{1,0:T(8,128)(2,1)}, u32[]{:S(2)}, u32[]{:S(2)}) collective-permute-start(bf16[256,1536]{1,0:T(8,128)(2,1)S(1)} %get-tuple-element.174), channel_id=1, source_target_pairs={{0,1},{1,0},{2,3},{3,2},{4,5},{5,4},{6,7},{7,6},{8,9},{9,8},{10,11... | collective-permute-start | bytes 2359304 | tf_op jit(solution)/shard_map/ppermute | solution.py:32
  294.3 11.3 %collective-permute-start.17 = (bf16[512,192]{1,0:T(8,128)(2,1)S(1)}, bf16[512,192]{1,0:T(8,128)(2,1)S(1)}, u32[]{:S(2)}, u32[]{:S(2)}) collective-permute-start(bf16[512,192]{1,0:T(8,128)(2,1)S(1)} %get-tuple-element.211), channel_id=1, source_target_pairs={{0,8},{2,10},{4,12},{6,14},{8,0},{10,2},{12,4},{14,6},{16,24},{18,... | collective-permute-start | bytes 589832 | tf_op jit(solution)/shard_map/ppermute | solution.py:32
  295.5 21.4 %collective-permute-start.18 = (bf16[512,192]{1,0:T(8,128)(2,1)S(1)}, bf16[512,192]{1,0:T(8,128)(2,1)S(1)}, u32[]{:S(2)}, u32[]{:S(2)}) collective-permute-start(bf16[512,192]{1,0:T(8,128)(2,1)S(1)} %get-tuple-element.212), channel_id=1, source_target_pairs={{0,16},{2,18},{4,20},{6,22},{8,24},{10,26},{12,28},{14,30},{16,0},... | collective-permute-start | bytes 589832 | tf_op jit(solution)/shard_map/ppermute | solution.py:32
  297.8 19.1 %collective-permute-start.19 = (bf16[512,192]{1,0:T(8,128)(2,1)S(1)}, bf16[512,192]{1,0:T(8,128)(2,1)S(1)}, u32[]{:S(2)}, u32[]{:S(2)}) collective-permute-start(bf16[512,192]{1,0:T(8,128)(2,1)S(1)} %get-tuple-element.209), channel_id=1, source_target_pairs={{0,24},{2,26},{4,28},{6,30},{8,16},{10,18},{12,20},{14,22},{16,8},... | collective-permute-start | bytes 589832 | tf_op jit(solution)/shard_map/ppermute | solution.py:32
  303.4 104.1 %collective-permute-start.22 = (bf16[16,128,768]{2,1,0:T(8,128)(2,1)S(1)}, bf16[16,128,768]{2,1,0:T(8,128)(2,1)}, u32[]{:S(2)}, u32[]{:S(2)}) collective-permute-start(bf16[16,128,768]{2,1,0:T(8,128)(2,1)S(1)} %pad_maximum_fusion.3), channel_id=1, source_target_pairs={{0,1},{1,0},{2,3},{3,2},{4,5},{5,4},{6,7},{7,6},{8,9},{9,8},{10,11... | collective-permute-start | bytes 9437192 | tf_op jit(solution)/shard_map/ppermute | solution.py:32
  356.3 15.5 %collective-permute-start.20 = (bf16[8,512,128]{2,1,0:T(8,128)(2,1)}, bf16[8,512,128]{2,1,0:T(8,128)(2,1)S(1)}, u32[]{:S(2)}, u32[]{:S(2)}) collective-permute-start(bf16[8,512,128]{2,1,0:T(8,128)(2,1)} %get-tuple-element.135), channel_id=1, source_target_pairs={{0,2},{2,0},{4,6},{6,4},{8,10},{10,8},{12,14},{14,12},{16,18},{18,... | collective-permute-start | bytes 3145736 | tf_op jit(solution)/shard_map/ppermute | solution.py:32
  367.9 38.3 %collective-permute-start.23 = (bf16[16,128,384]{2,1,0:T(8,128)(2,1)}, bf16[16,128,384]{2,1,0:T(8,128)(2,1)S(1)}, u32[]{:S(2)}, u32[]{:S(2)}) collective-permute-start(bf16[16,128,384]{2,1,0:T(8,128)(2,1)} %all-to-all-done.1), channel_id=1, source_target_pairs={{0,1},{1,0},{2,3},{3,2},{4,5},{5,4},{6,7},{7,6},{8,9},{9,8},{10,11... | collective-permute-start | bytes 4718600 | tf_op jit(solution)/shard_map/ppermute | solution.py:32
  371.7 21.1 %copy-start.59 = (bf16[512,192]{1,0:T(8,128)(2,1)S(1)}, bf16[512,192]{1,0:T(8,128)(2,1)}, u32[]{:S(2)}) copy-start(bf16[512,192]{1,0:T(8,128)(2,1)} %get-tuple-element.148) | copy-start | bytes 589828
  371.7 21.1 %copy-start.34 = (bf16[512,1536]{1,0:T(8,128)(2,1)S(1)}, bf16[512,1536]{1,0:T(8,128)(2,1)}, u32[]{:S(2)}) copy-start(bf16[512,1536]{1,0:T(8,128)(2,1)} %pad_maximum_fusion.5) | copy-start | bytes 4718596
  371.8 21.1 %copy-start.41 = (bf16[512,768]{1,0:T(8,128)(2,1)S(1)}, bf16[512,768]{1,0:T(8,128)(2,1)}, u32[]{:S(2)}) copy-start(bf16[512,768]{1,0:T(8,128)(2,1)} %copy-done.40) | copy-start | bytes 2359300
  372.7 20.1 %collective-permute-start.26 = (bf16[512,192]{1,0:T(8,128)(2,1)S(1)}, bf16[512,192]{1,0:T(8,128)(2,1)S(1)}, u32[]{:S(2)}, u32[]{:S(2)}) collective-permute-start(bf16[512,192]{1,0:T(8,128)(2,1)S(1)} %copy-done.61), channel_id=1, source_target_pairs={{0,16},{2,18},{4,20},{6,22},{8,24},{10,26},{12,28},{14,30},{16,0},... | collective-permute-start | bytes 589832 | tf_op jit(solution)/shard_map/ppermute | solution.py:32
  380.4 25.7 %copy-start.47 = (bf16[512,192]{1,0:T(8,128)(2,1)S(1)}, bf16[512,192]{1,0:T(8,128)(2,1)}, u32[]{:S(2)}) copy-start(bf16[512,192]{1,0:T(8,128)(2,1)} %get-tuple-element.149) | copy-start | bytes 589828
  380.4 25.8 %collective-permute-start.21 = (bf16[1,4,512,128]{3,2,1,0:T(8,128)(2,1)S(1)}, bf16[1,4,512,128]{3,2,1,0:T(8,128)(2,1)S(1)}, u32[]{:S(2)}, u32[]{:S(2)}) collective-permute-start(bf16[1,4,512,128]{3,2,1,0:T(8,128)(2,1)S(1)} %slice_bitcast_fusion), channel_id=1, source_target_pairs={{0,4},{2,6},{4,0},{6,2},{8,12},{10,14},{12,8},{14,10},{16,20},{18,... | collective-permute-start | bytes 1572872 | tf_op jit(solution)/shard_map/ppermute | solution.py:32
  391.3 11.0 %collective-permute-start.25 = (bf16[512,192]{1,0:T(8,128)(2,1)S(1)}, bf16[512,192]{1,0:T(8,128)(2,1)S(1)}, u32[]{:S(2)}, u32[]{:S(2)}) collective-permute-start(bf16[512,192]{1,0:T(8,128)(2,1)S(1)} %copy-done.60), channel_id=1, source_target_pairs={{0,24},{2,26},{4,28},{6,30},{8,16},{10,18},{12,20},{14,22},{16,8},... | collective-permute-start | bytes 589832 | tf_op jit(solution)/shard_map/ppermute | solution.py:32
  392.8 13.3 %collective-permute-start.27 = (bf16[512,192]{1,0:T(8,128)(2,1)S(1)}, bf16[512,192]{1,0:T(8,128)(2,1)S(1)}, u32[]{:S(2)}, u32[]{:S(2)}) collective-permute-start(bf16[512,192]{1,0:T(8,128)(2,1)S(1)} %copy-done.59), channel_id=1, source_target_pairs={{0,8},{2,10},{4,12},{6,14},{8,0},{10,2},{12,4},{14,6},{16,24},{18,... | collective-permute-start | bytes 589832 | tf_op jit(solution)/shard_map/ppermute | solution.py:32
  430.2 87.6 %collective-permute-start.24 = (bf16[256,1536]{1,0:T(8,128)(2,1)}, bf16[256,1536]{1,0:T(8,128)(2,1)}, u32[]{:S(2)}, u32[]{:S(2)}) collective-permute-start(bf16[256,1536]{1,0:T(8,128)(2,1)} %dynamic-slice_convert_fusion.1), channel_id=1, source_target_pairs={{0,1},{1,0},{2,3},{3,2},{4,5},{5,4},{6,7},{7,6},{8,9},{9,8},{10,11... | collective-permute-start | bytes 2359304 | tf_op jit(solution)/shard_map/ppermute | solution.py:32
  431.6 22.6 %collective-permute-start.29 = (bf16[512,128]{1,0:T(8,128)(2,1)S(1)}, bf16[512,128]{1,0:T(8,128)(2,1)S(1)}, u32[]{:S(2)}, u32[]{:S(2)}) collective-permute-start(bf16[512,128]{1,0:T(8,128)(2,1)S(1)} %get-tuple-element.214), channel_id=1, source_target_pairs={{0,16},{2,18},{4,20},{6,22},{8,24},{10,26},{12,28},{14,30},{16,0},... | collective-permute-start | bytes 393224 | tf_op jit(solution)/shard_map/ppermute | solution.py:32
  436.6 17.6 %collective-permute-start.28 = (bf16[512,128]{1,0:T(8,128)(2,1)S(1)}, bf16[512,128]{1,0:T(8,128)(2,1)S(1)}, u32[]{:S(2)}, u32[]{:S(2)}) collective-permute-start(bf16[512,128]{1,0:T(8,128)(2,1)S(1)} %get-tuple-element.215), channel_id=1, source_target_pairs={{0,24},{2,26},{4,28},{6,30},{8,16},{10,18},{12,20},{14,22},{16,8},... | collective-permute-start | bytes 393224 | tf_op jit(solution)/shard_map/ppermute | solution.py:32
  437.6 16.6 %collective-permute-start.30 = (bf16[512,128]{1,0:T(8,128)(2,1)S(1)}, bf16[512,128]{1,0:T(8,128)(2,1)S(1)}, u32[]{:S(2)}, u32[]{:S(2)}) collective-permute-start(bf16[512,128]{1,0:T(8,128)(2,1)S(1)} %get-tuple-element.213), channel_id=1, source_target_pairs={{0,8},{2,10},{4,12},{6,14},{8,0},{10,2},{12,4},{14,6},{16,24},{18,... | collective-permute-start | bytes 393224 | tf_op jit(solution)/shard_map/ppermute | solution.py:32
  482.6 20.5 %collective-permute-start.32 = (bf16[8,96,2048]{2,1,0:T(8,128)(2,1)S(1)}, bf16[8,96,2048]{2,1,0:T(8,128)(2,1)S(1)}, u32[]{:S(2)}, u32[]{:S(2)}) collective-permute-start(bf16[8,96,2048]{2,1,0:T(8,128)(2,1)S(1)} %dynamic-slice_bitcast_fusion), channel_id=1, source_target_pairs={{0,2},{2,0},{4,6},{6,4},{8,10},{10,8},{12,14},{14,12},{16,18},{18,... | collective-permute-start | bytes 9437192 | tf_op jit(solution)/shard_map/ppermute | solution.py:32
  483.0 37.1 %collective-permute-start.31 = (bf16[256,1536]{1,0:T(8,128)(2,1)S(1)}, bf16[256,1536]{1,0:T(8,128)(2,1)S(1)}, u32[]{:S(2)}, u32[]{:S(2)}) collective-permute-start(bf16[256,1536]{1,0:T(8,128)(2,1)S(1)} %dynamic-slice_convert_fusion), channel_id=1, source_target_pairs={{0,1},{1,0},{2,3},{3,2},{4,5},{5,4},{6,7},{7,6},{8,9},{9,8},{10,11... | collective-permute-start | bytes 2359304 | tf_op jit(solution)/shard_map/ppermute | solution.py:32
  503.9 29.5 %collective-permute-start.33 = (bf16[4,96,1024]{2,1,0:T(8,128)(2,1)S(1)}, bf16[4,96,1024]{2,1,0:T(8,128)(2,1)S(1)}, u32[]{:S(2)}, u32[]{:S(2)}) collective-permute-start(bf16[4,96,1024]{2,1,0:T(8,128)(2,1)S(1)} %dynamic-slice_bitcast_fusion.2), channel_id=1, source_target_pairs={{0,4},{2,6},{4,0},{6,2},{8,12},{10,14},{12,8},{14,10},{16,20},{18,... | collective-permute-start | bytes 2359304 | tf_op jit(solution)/shard_map/ppermute | solution.py:32
  515.8 19.3 %collective-permute-start.34 = (bf16[2,192,1024]{2,1,0:T(8,128)(2,1)S(1)}, bf16[2,192,1024]{2,1,0:T(8,128)(2,1)S(1)}, u32[]{:S(2)}, u32[]{:S(2)}) collective-permute-start(bf16[2,192,1024]{2,1,0:T(8,128)(2,1)S(1)} %dynamic-slice_bitcast_fusion.1), channel_id=1, source_target_pairs={{0,8},{2,10},{4,12},{6,14},{8,0},{10,2},{12,4},{14,6},{16,24},{18,... | collective-permute-start | bytes 2359304 | tf_op jit(solution)/shard_map/ppermute | solution.py:32
  520.7 23.8 %copy-start.25 = (f32[256,1536]{1,0:T(8,128)S(1)}, f32[256,1536]{1,0:T(8,128)}, u32[]{:S(2)}) copy-start(f32[256,1536]{1,0:T(8,128)} %get-tuple-element.175) | copy-start | bytes 4718596
  535.3 2.8 collective-permute-start.35
  535.4 25.9 %collective-permute-start.42 = (bf16[1,192,1024]{2,1,0:T(8,128)(2,1)S(1)}, bf16[1,192,1024]{2,1,0:T(8,128)(2,1)S(1)}, u32[]{:S(2)}, u32[]{:S(2)}) collective-permute-start(bf16[1,192,1024]{2,1,0:T(8,128)(2,1)S(1)} %dynamic-slice_bitcast_fusion.3), channel_id=1, source_target_pairs={{0,16},{2,18},{4,20},{6,22},{8,24},{10,26},{12,28},{14,30},{16,0},... | collective-permute-start | bytes 1179656 | tf_op jit(solution)/shard_map/ppermute | solution.py:32
  538.1 6.0 %collective-permute-start.36 = (f32[18,1536]{1,0:T(8,128)S(1)}, f32[18,1536]{1,0:T(8,128)S(1)}, u32[]{:S(2)}, u32[]{:S(2)}) collective-permute-start(f32[18,1536]{1,0:T(8,128)S(1)} %add.233), channel_id=1, source_target_pairs={{0,4},{2,6},{4,0},{6,2},{8,12},{10,14},{12,8},{14,10},{16,20},{18,... | collective-permute-start | bytes 331784 | tf_op jit(solution)/shard_map/ppermute | solution.py:32
  538.6 23.3 %collective-permute-start.40 = (bf16[2,96,1024]{2,1,0:T(8,128)(2,1)S(1)}, bf16[2,96,1024]{2,1,0:T(8,128)(2,1)S(1)}, u32[]{:S(2)}, u32[]{:S(2)}) collective-permute-start(bf16[2,96,1024]{2,1,0:T(8,128)(2,1)S(1)} %dynamic-slice_bitcast_fusion.4), channel_id=1, source_target_pairs={{0,8},{2,10},{4,12},{6,14},{8,0},{10,2},{12,4},{14,6},{16,24},{18,... | collective-permute-start | bytes 1179656 | tf_op jit(solution)/shard_map/ppermute | solution.py:32
  544.2 15.7 %collective-permute-start.37 = (f32[18,1536]{1,0:T(8,128)S(1)}, f32[18,1536]{1,0:T(8,128)S(1)}, u32[]{:S(2)}, u32[]{:S(2)}) collective-permute-start(f32[18,1536]{1,0:T(8,128)S(1)} %add.234), channel_id=1, source_target_pairs={{0,8},{2,10},{4,12},{6,14},{8,0},{10,2},{12,4},{14,6},{16,24},{18,... | collective-permute-start | bytes 331784 | tf_op jit(solution)/shard_map/ppermute | solution.py:32
  559.9 8.9 %collective-permute-start.38 = (f32[18,1536]{1,0:T(8,128)S(1)}, f32[18,1536]{1,0:T(8,128)S(1)}, u32[]{:S(2)}, u32[]{:S(2)}) collective-permute-start(f32[18,1536]{1,0:T(8,128)S(1)} %add.235), channel_id=1, source_target_pairs={{0,16},{2,18},{4,20},{6,22},{8,24},{10,26},{12,28},{14,30},{16,0},... | collective-permute-start | bytes 331784 | tf_op jit(solution)/shard_map/ppermute | solution.py:32
  561.4 14.0 %collective-permute-start.43 = (bf16[1,96,1024]{2,1,0:T(8,128)(2,1)S(1)}, bf16[1,96,1024]{2,1,0:T(8,128)(2,1)S(1)}, u32[]{:S(2)}, u32[]{:S(2)}) collective-permute-start(bf16[1,96,1024]{2,1,0:T(8,128)(2,1)S(1)} %dynamic-slice_bitcast_fusion.5), channel_id=1, source_target_pairs={{0,4},{2,6},{4,0},{6,2},{8,12},{10,14},{12,8},{14,10},{16,20},{18,... | collective-permute-start | bytes 589832 | tf_op jit(solution)/shard_map/ppermute | solution.py:32
  568.9 5.2 collective-permute-start.39
  569.4 9.9 %collective-permute-start.41 = (bf16[1,96,1024]{2,1,0:T(8,128)(2,1)S(1)}, bf16[1,96,1024]{2,1,0:T(8,128)(2,1)S(1)}, u32[]{:S(2)}, u32[]{:S(2)}) collective-permute-start(bf16[1,96,1024]{2,1,0:T(8,128)(2,1)S(1)} %constant_dynamic-slice_fusion.1), channel_id=1, source_target_pairs={{0,16},{2,18},{4,20},{6,22},{8,24},{10,26},{12,28},{14,30},{16,0},... | collective-permute-start | bytes 589832 | tf_op jit(solution)/shard_map/ppermute | solution.py:32
  (58 other events, 340.4 us)

commit v3 on v2

--- a/solution.py
+++ b/solution.py
@@ -55,8 +55,15 @@
 
 def total(x):
     for axis in ("dp", "tensor"):
-        for bit in bits_of(lax.axis_size(axis)):
-            x = x + across(x, axis, bit)
+        bits = bits_of(lax.axis_size(axis))
+        while bits:
+            one, *bits = bits
+            if bits:
+                two, *bits = bits
+                far, both = across(x, axis, two), across(x, axis, one | two)
+                x = (x + across(x, axis, one)) + (far + both)
+            else:
+                x = x + across(x, axis, one)
     return x
 
 
@@ -101,51 +108,13 @@
     return [x[:, s * size : (s + 1) * size] for s in range(count)]
 
 
-def scatter_rows(x, later):
+def scatter_rows(keep, send, later):
     n = lax.axis_size("dp")
-    at = lax.axis_index("dp")
-    bits = bits_of(n)
-    x = x.astype(BF)
-    x = halve_first(x, at, n)
-    half = x.shape[1] // 2
-    orders = (bits[1:], bits[2:] + bits[1:2])
-    pieces = [
-        halve_rest(piece, at, order[:1], bits[1:])
-        for piece, order in zip((x[:, :half], x[:, half:]), orders)
-    ]
-    pieces, later = after(pieces, later)
-    outs = [
-        halve_rest(piece, at, order[1:], [b for b in bits[1:] if b != order[0]])
-        for piece, order in zip(pieces, orders)
-    ]
-    return jnp.concatenate(outs, 1).astype(F32), later
-
-
-def halve_first(x, at, n):
-    size = x.shape[0] // n
-    view = x.reshape(n // 2, 2, size, x.shape[1])
-    mine = at & 1
-
-    def pick(which):
-        return lax.dynamic_index_in_dim(view, which, 1, keepdims=False)
-
-    return (pick(mine) + across(pick(1 - mine), "dp", 1)).reshape(-1, x.shape[1])
-
-
-def halve_rest(x, at, order, left):
-    left = sorted(left)
-    for bit in order:
-        high = 1
-        for other in left:
-            if other > bit:
-                high *= 2
-        view = x.reshape(high, 2, -1, x.shape[1])
-        mine = (at >> (bit.bit_length() - 1)) & 1
-        kept = lax.dynamic_index_in_dim(view, mine, 1, keepdims=False)
-        sent = lax.dynamic_index_in_dim(view, 1 - mine, 1, keepdims=False)
-        x = (kept + across(sent, "dp", bit)).reshape(-1, x.shape[1])
-        left.remove(bit)
-    return x
+    x = keep + across(send, "dp", 1)
+    x, later = after(x, later)
+    groups = [list(range(first, n, 2)) for first in range(2)]
+    x = lax.all_to_all(x, "dp", 0, 0, tiled=True, axis_index_groups=groups)
+    return jnp.sum(x.astype(F32), axis=0), later
 
 
 def project_kernel(lines, q_cols, at, x_ref, gain_ref, wq_ref, wk_ref, wv_ref, normed_ref, *rest):
@@ -429,36 +398,39 @@
 
 
 def experts_kernel(x_ref, g_ref, gate_ref, wg_ref, wu_ref, wd_ref, out_ref, back_ref, inner_ref):
-    x = x_ref[0]
-    g = g_ref[0]
-    gate = gate_ref[0]
-    gate_pre = dot(x, wg_ref[0])
-    up_pre = dot(x, wu_ref[0])
-    sigma = jax.nn.sigmoid(gate_pre)
-    silu = gate_pre * sigma
-    act = (silu * up_pre).astype(BF)
-    out = dot(act, wd_ref[0])
-    g_float = g.astype(F32)
-    inner = jnp.sum(out * g_float, axis=-1, keepdims=True)
-    inner_ref[0] = jnp.broadcast_to(inner, (x.shape[0], 128)).T[:8]
-    out_ref[0] = (gate * out).astype(BF)
-    grad_expert = (gate * g_float).astype(BF)
-    grad_act = dot(grad_expert, wd_ref[0], NT)
-    grad_gate = (grad_act * up_pre * sigma * (1.0 + gate_pre * (1.0 - sigma))).astype(BF)
-    grad_up = (grad_act * silu).astype(BF)
-    back_ref[0] = (dot(grad_gate, wg_ref[0], NT) + dot(grad_up, wu_ref[0], NT)).astype(BF)
+    each = range(x_ref.shape[0])
+    cap = x_ref.shape[1]
+    gate_pre = [dot(x_ref[i], wg_ref[i]) for i in each]
+    grad_expert = [(gate_ref[i] * g_ref[i].astype(F32)).astype(BF) for i in each]
+    grad_act = [dot(grad_expert[i], wd_ref[i], NT) for i in each]
+    up_pre = [dot(x_ref[i], wu_ref[i]) for i in each]
+    sigma = [jax.nn.sigmoid(gate_pre[i]) for i in each]
+    silu = [gate_pre[i] * sigma[i] for i in each]
+    act = [(silu[i] * up_pre[i]).astype(BF) for i in each]
+    grad_gate = [
+        (grad_act[i] * up_pre[i] * sigma[i] * (1.0 + gate_pre[i] * (1.0 - sigma[i]))).astype(BF)
+        for i in each
+    ]
+    grad_up = [(grad_act[i] * silu[i]).astype(BF) for i in each]
+    for i in each:
+        out = dot(act[i], wd_ref[i])
+        inner = jnp.sum(out * g_ref[i].astype(F32), axis=-1, keepdims=True)
+        inner_ref[i] = jnp.broadcast_to(inner, (cap, 128)).T[:8]
+        out_ref[i] = (gate_ref[i] * out).astype(BF)
+        back_ref[i] = (dot(grad_gate[i], wg_ref[i], NT) + dot(grad_up[i], wu_ref[i], NT)).astype(BF)
 
 
 def run_experts(x, g, gate, w_gate, w_up, w_down):
     experts, cap, width = x.shape
     hidden = w_gate.shape[2]
+    at_once = 2 if experts % 2 == 0 else 1
 
     def of(*shape):
-        return pl.BlockSpec((1,) + shape, lambda e: (e, 0, 0))
+        return pl.BlockSpec((at_once,) + shape, lambda e: (e, 0, 0))
 
     return pl.pallas_call(
         experts_kernel,
-        grid=(experts,),
+        grid=(experts // at_once,),
         in_specs=[
             of(cap, width),
             of(cap, width),
@@ -473,7 +445,7 @@
             jax.ShapeDtypeStruct((experts, cap, width), BF),
             jax.ShapeDtypeStruct((experts, 8, cap), F32),
         ],
-        compiler_params=pltpu.CompilerParams(vmem_limit_bytes=48 * 1024 * 1024),
+        compiler_params=pltpu.CompilerParams(vmem_limit_bytes=56 * 1024 * 1024),
         cost_estimate=pl.CostEstimate(
             flops=experts * cap * width * hidden * 12,
             bytes_accessed=experts * width * (hidden * 6 + cap * 8),
@@ -483,26 +455,128 @@
     )(x, g, gate, w_gate, w_up, w_down)
 
 
-def owner_forward(e, held, place, x_owned, g_owned, gate_owned, w_gate, w_up, w_down):
-    dp, _, cap, width = x_owned.shape[0], held, x_owned.shape[1], x_owned.shape[2]
-
-    def mine(x):
-        return x.reshape((dp, held, cap) + x.shape[2:])[:, e].reshape((dp * cap,) + x.shape[2:])
-
-    def weight(w):
-        return lax.dynamic_index_in_dim(w, place * held + e, 0, keepdims=False)
-
-    x = mine(x_owned)
-    gate_pre = dot(x, weight(w_gate))
-    up_pre = dot(x, weight(w_up))
+def weights_kernel(dp, at, a_ref, b_ref, c_ref, d_ref, keep_ref, send_ref):
+    size = a_ref.shape[1] // dp
+    chunk = 4
+    split = b_ref.shape[1]
+    odd = at[0] != 0
+    for part in range(dp // chunk):
+        span = slice(part * chunk * size, (part + 1) * chunk * size)
+        for left, right, lanes in (
+            (a_ref, b_ref, slice(0, split)),
+            (c_ref, d_ref, slice(split, split + d_ref.shape[1])),
+        ):
+            block = dot(left[:, span], right[...], TN).astype(BF)
+            for pair in range(chunk // 2):
+                one = block[2 * pair * size : (2 * pair + 1) * size]
+                two = block[(2 * pair + 1) * size : (2 * pair + 2) * size]
+                at_pair = part * (chunk // 2) + pair
+                keep_ref[at_pair, :, lanes] = jnp.where(odd, two, one)
+                send_ref[at_pair, :, lanes] = jnp.where(odd, one, two)
+
+
+def weight_parts(bit, a, b, c, d, dp):
+    rows, width = a.shape
+    columns = b.shape[1] + d.shape[1]
+    out = (dp // 2, width // dp, columns)
+    return pl.pallas_call(
+        functools.partial(weights_kernel, dp),
+        grid_spec=pltpu.PrefetchScalarGridSpec(
+            num_scalar_prefetch=1,
+            grid=(1,),
+            in_specs=[whole_block(x.shape) for x in (a, b, c, d)],
+            out_specs=[whole_block(out)] * 2,
+        ),
+        out_shape=[jax.ShapeDtypeStruct(out, BF)] * 2,
+        compiler_params=pltpu.CompilerParams(vmem_limit_bytes=48 * 1024 * 1024),
+        cost_estimate=pl.CostEstimate(
+            flops=2 * rows * width * columns, bytes_accessed=12 << 20, transcendentals=0
+        ),
+        name="weights",
+    )(bit[None], a, b, c, d)
+
+
+def flat(x):
+    return x.reshape(x.shape[0] * x.shape[1], x.shape[2])
+
+
+def owner_forward_kernel(n_x, n_g, at, gate_ref, wg_ref, wu_ref, wd_ref, *refs):
+    x_refs, g_refs, outs = refs[:n_x], refs[n_x : n_x + n_g], refs[n_x + n_g :]
+    act_ref, grad_gate_ref, grad_up_ref = outs
+
+    def span(i, ref):
+        return pl.ds(pl.multiple_of(at[1 + i], ref.shape[2]), ref.shape[2])
+
+    gate_pre = sum(dot(flat(x[...]), wg_ref[0, span(i, x), :]) for i, x in enumerate(x_refs))
+    up_pre = sum(dot(flat(x[...]), wu_ref[0, span(i, x), :]) for i, x in enumerate(x_refs))
+    grad_act = sum(
+        dot(
+            (gate_ref[...] * flat(g[...]).astype(F32)).astype(BF),
+            wd_ref[0, :, span(n_x + i, g)],
+            NT,
+        )
+        for i, g in enumerate(g_refs)
+    )
     sigma = jax.nn.sigmoid(gate_pre)
     silu = gate_pre * sigma
-    act = (silu * up_pre).astype(BF)
-    grad_expert = (mine(gate_owned)[:, None] * mine(g_owned).astype(F32)).astype(BF)
-    grad_act = dot(grad_expert, weight(w_down), NT)
-    grad_gate = (grad_act * up_pre * sigma * (1.0 + gate_pre * (1.0 - sigma))).astype(BF)
-    grad_up = (grad_act * silu).astype(BF)
-    return x, act, grad_expert, grad_gate, grad_up
+    act_ref[...] = (silu * up_pre).astype(BF)
+    grad_gate_ref[...] = (
+        grad_act * up_pre * sigma * (1.0 + gate_pre * (1.0 - sigma))
+    ).astype(BF)
+    grad_up_ref[...] = (grad_act * silu).astype(BF)
+
+
+def owner_grads_kernel(n_x, n_g, at, gate_ref, act_ref, grad_gate_ref, grad_up_ref, *refs):
+    x_refs, g_refs, outs = refs[:n_x], refs[n_x : n_x + n_g], refs[n_x + n_g :]
+    gate_out, up_out, down_out = outs
+
+    def span(i, ref):
+        return pl.ds(pl.multiple_of(at[1 + i], ref.shape[2]), ref.shape[2])
+
+    @pl.when(pl.program_id(0) == 0)
+    def _():
+        for out in outs:
+            out[...] = jnp.zeros_like(out)
+
+    for i, ref in enumerate(x_refs):
+        x = flat(ref[...])
+        gate_out[0, span(i, ref), :] += dot(x, grad_gate_ref[...], TN)
+        up_out[0, span(i, ref), :] += dot(x, grad_up_ref[...], TN)
+    for i, ref in enumerate(g_refs):
+        grad_expert = (gate_ref[...] * flat(ref[...]).astype(F32)).astype(BF)
+        down_out[0, :, span(n_x + i, ref)] += dot(act_ref[...], grad_expert, TN)
+
+
+def owner_call(kernel, name, at, gate, given, x, g, weights, outs, steps):
+    dp, cap, _ = x[0].shape
+    rows = dp * cap // steps
+
+    def rowwise(a):
+        return pl.BlockSpec((rows, a.shape[1]), lambda i, m: (i, 0))
+
+    def piece(a):
+        return pl.BlockSpec((dp // steps, cap, a.shape[2]), lambda i, m: (i, 0, 0))
+
+    def weight(a):
+        return pl.BlockSpec((1,) + a.shape[1:], lambda i, m: (m[0], 0, 0))
+
+    out_specs = [rowwise(o) if len(o.shape) == 2 else whole_block(o.shape) for o in outs]
+    return pl.pallas_call(
+        functools.partial(kernel, len(x), len(g)),
+        grid_spec=pltpu.PrefetchScalarGridSpec(
+            num_scalar_prefetch=1,
+            grid=(steps,),
+            in_specs=[rowwise(gate)]
+            + [rowwise(a) for a in given]
+            + [weight(w) for w in weights]
+            + [piece(a) for a in list(x) + list(g)],
+            out_specs=out_specs,
+        ),
+        out_shape=outs,
+        compiler_params=pltpu.CompilerParams(vmem_limit_bytes=58 * 1024 * 1024),
+        cost_estimate=pl.CostEstimate(flops=10 << 30, bytes_accessed=24 << 20, transcendentals=1 << 20),
+        name=name,
+    )(at, gate, *given, *weights, *x, *g)
 
 
 def shards(
@@ -537,6 +611,7 @@
     first = tensor_at * part
     held = experts // dp
     cols = width // tensor_size
+    first_col = tensor_at * cols
 
     names = jnp.arange(experts, dtype=jnp.int32)
     named = jnp.any(routes[:, :, None] == names[None, None, :], axis=1)
@@ -550,9 +625,12 @@
         .reshape(rows, experts * CAP)
     )
 
-    def halves(x):
-        own = lax.dynamic_slice_in_dim(x, tensor_at * cols, cols, 2)
-        return own[..., : cols // 2], own[..., cols // 2 :]
+    def to_experts(x):
+        return dot(to_slots, x).astype(BF).reshape(experts, CAP, -1)
+
+    def half(x, i):
+        size = cols // 2
+        return to_experts(lax.dynamic_slice_in_dim(x, tensor_at * cols + i * size, size, 1))
 
     q_blocks = place ^ (jnp.arange(lines, dtype=jnp.int32) * stride)
     seg_query = jnp.stack(
@@ -580,8 +658,7 @@
     q = to_lines(q_mine)
     for bit in reversed(bits_of(stride)):
         kv = [piece for one in kv for piece in (one, across(one, "dp", bit))]
-    g_slots = dot(to_slots, out_grad).astype(BF).reshape(experts, CAP, width)
-    g_sent, (kv, q, starts, meta) = after(halves(g_slots), (kv, q, starts, meta))
+    g_sent, (kv, q, starts, meta) = after([half(out_grad, i) for i in range(2)], (kv, q, starts, meta))
     g_first = to_owner(g_sent[0])
     *mixed_far, raw, logs = attend(meta, q, kv, starts[:, None, :], group)
     mixed_far, g_first = after(mixed_far, g_first)
@@ -590,7 +667,7 @@
         return xor_blocks(to_lines(blocks), line)
 
     mixed = jnp.concatenate(from_lines(mixed_far), 1)
-    g_late, mixed = after(g_sent[1], mixed)
+    g_late, (mixed, g_slots) = after(g_sent[1], (mixed, to_experts(out_grad)))
     g_second = to_owner(g_late)
     attn = scatter_tensor(dot(mixed, w_out))
     hidden = lax.dynamic_slice_in_dim(layer_in, first, part, 0).astype(F32) + attn
@@ -604,16 +681,14 @@
     gates = expo / jnp.sum(expo, axis=1, keepdims=True)
     slot_gate = jnp.sum(jnp.where(in_slot, gates.T[:, None, :], 0.0), axis=-1)
 
-    x_slots = dot(to_slots, normed_mid).astype(BF).reshape(experts, CAP, width)
-    x_early, x_late = halves(x_slots)
+    x_slots = to_experts(normed_mid)
+    x_mine = lax.dynamic_slice_in_dim(x_slots, first_col, cols, 2)
+    x_early, x_late = x_mine[..., : cols // 2], x_mine[..., cols // 2 :]
     x_early, g_second = after(x_early, g_second)
     x_first = to_owner(x_early)
     gate_high = lax.reduce_precision(slot_gate, 8, 7)
     gate_mid = lax.reduce_precision(slot_gate - gate_high, 8, 7)
     gate_pieces = jnp.stack([gate_high, gate_mid, slot_gate - gate_high - gate_mid], 2)
-    x_late = jnp.concatenate(
-        [x_late, jnp.pad(gate_pieces.astype(BF), ((0, 0), (0, 0), (0, 125)))], 2
-    )
     g_first, x_slots = after(g_first, x_slots)
     g_first = swap_tensor(g_first, 2)
 
@@ -621,8 +696,6 @@
         x_slots, g_slots, slot_gate[:, :, None], w_gate, w_up, w_down
     )
     back_slots, (x_first, g_first) = after(back_slots, (x_first, g_first))
-    x_late, back_slots = after(x_late, back_slots)
-    x_second = to_owner(x_late)
     moe_part = dot(from_slots, out_slots.reshape(experts * CAP, width))
     grad_gates = jnp.sum(
         jnp.where(
@@ -633,13 +706,20 @@
         axis=-1,
     )
     grad_logits = gates * (grad_gates - jnp.sum(gates * grad_gates, axis=-1, keepdims=True))
-    router_part = lax.dot_general(
-        grad_logits, normed_mid.astype(F32), TN, precision=HIGH, preferred_element_type=F32
-    )
     grad_mid_part = dot(from_slots, back_slots.reshape(experts * CAP, width)) + lax.dot_general(
         grad_logits, router.astype(F32), NT, precision=HIGH, preferred_element_type=F32
     )
-    grad_mid = scatter_tensor(grad_mid_part)
+    (x_late, gate_pieces, router_part), grad_mid_part = after(
+        (x_late, gate_pieces, (grad_logits, normed_mid)), grad_mid_part
+    )
+    router_part = lax.dot_general(
+        router_part[0], router_part[1].astype(F32), TN, precision=HIGH, preferred_element_type=F32
+    )
+    x_late = jnp.concatenate(
+        [x_late, jnp.pad(gate_pieces.astype(BF), ((0, 0), (0, 0), (0, 125)))], 2
+    )
+    x_second = to_owner(x_late)
+    grad_mid, moe_part = after(scatter_tensor(grad_mid_part), moe_part)
     gain_two_part = jnp.sum(grad_mid * unit_two, axis=0)
     grad_rows = lax.dynamic_slice_in_dim(out_grad, first, part, 0).astype(F32)
     grad_hidden = grad_rows + norm_back(unit_two, factor_two, norm2_gain, grad_mid)
@@ -657,36 +737,73 @@
     for bit in bits_of(stride)[1:]:
         view = dkv.reshape((dkv.shape[0] // 2, 2) + dkv.shape[1:])
         dkv = view[:, 0] + across(view[:, 1], "dp", bit)
-    dkv, moe_part, x_owned, g_second = lax.optimization_barrier(
-        (dkv[0], moe_part, x_owned, g_second)
-    )
-    x_owned = assemble(x_owned, 2)
-    size = cols // 2
-    g_pieces = [assemble(g_first, 2), assemble(g_second, 2)]
-    g_owned = jnp.concatenate(
-        [g[..., t * size : (t + 1) * size] for t in range(tensor_size) for g in g_pieces], 2
-    )
+    dkv, (moe_part, x_owned) = after(dkv[0], (moe_part, x_owned))
     dq = from_lines(dq_far)
-    layer_out = (hidden + scatter_tensor(moe_part)).astype(BF)
+    moe_rows = scatter_tensor(moe_part)
     dkv = from_lines([dkv[s] for s in range(lines)])
-    owned = [
-        owner_forward(e, held, place, x_owned, g_owned, gate_owned, w_gate, w_up, w_down)
-        for e in range(held)
-    ]
     w_all = jnp.concatenate([w_query, w_key, w_value], 1)
     dqkv = jnp.concatenate(dq + [b[:, :HD] for b in dkv] + [b[:, HD:] for b in dkv], 1)
-    weight_part = jnp.concatenate(
-        [dot(normed_in, dqkv, TN).astype(BF), dot(hidden_low, mixed, TN).astype(BF)], 1
-    )
-    dqkv, weight_part, owned = lax.optimization_barrier((dqkv, weight_part, owned))
+    dqkv, x_owned, g_second = lax.optimization_barrier((dqkv, x_owned, g_second))
+    weight_keep, weight_send = weight_parts(place & 1, normed_in, dqkv, hidden_low, mixed, dp)
+    dqkv, weight_keep, weight_send = lax.optimization_barrier((dqkv, weight_keep, weight_send))
+    def mine(x, e):
+        return x.reshape((dp, held, CAP) + x.shape[2:])[:, e]
+
+    def pieces_of(parts, offset):
+        return [(parts[0], first_col + offset), (parts[1], cols - first_col + offset)]
+
+    def owner_work(given):
+        x_parts, g_parts = given
+        size = cols // 2
+        if tensor_size == 2:
+            x = pieces_of(x_parts, 0)
+            g = pieces_of(g_first, 0) + pieces_of(g_parts, size)
+        else:
+            x = [(assemble(x_parts, 2), 0)]
+            both = [assemble(g_first, 2), assemble(g_parts, 2)]
+            order = [each[..., t * size : (t + 1) * size] for t in range(tensor_size) for each in both]
+            g = [(jnp.concatenate(order, 2), 0)]
+        results = []
+        for e in range(held):
+            at = jnp.stack([jnp.int32(place * held + e)] + [jnp.int32(o) for _, o in x + g])
+            tokens = [mine(a, e) for a, _ in x], [mine(a, e) for a, _ in g]
+            gate = mine(gate_owned, e).reshape(dp * CAP, 1)
+            hidden_shape = jax.ShapeDtypeStruct((dp * CAP, w_gate.shape[2]), BF)
+            given_back = owner_call(
+                owner_forward_kernel,
+                "owner_forward",
+                at,
+                gate,
+                [],
+                *tokens,
+                [w_gate, w_up, w_down],
+                [hidden_shape] * 3,
+                4,
+            )
+            results.append((at, gate, given_back, *tokens))
+        return results
+
+    def owner_grads(owned):
+        shapes = [
+            jax.ShapeDtypeStruct((1,) + w.shape[1:], F32) for w in (w_gate, w_up, w_down)
+        ]
+        grad_outs = [
+            owner_call(owner_grads_kernel, "owner_grads", at, gate, given, x, g, [], shapes, 2)
+            for at, gate, given, x, g in owned
+        ]
+        return [jnp.concatenate(each, 0) for each in zip(*grad_outs)]
+
+    weight_grad, (owner_given, dqkv, small) = scatter_rows(
+        weight_keep, weight_send, ((x_owned, g_second), dqkv, (router_part, gain_two_part))
+    )
     grad_in_part = dot(dqkv, w_all, NT)
     in_float = layer_in.astype(F32)
     factor_one = norm_factor(in_float)
-    small_in = jnp.concatenate(
-        [router_part, gain_two_part[None], jnp.sum(grad_in_part * (in_float * factor_one), axis=0)[None]], 0
-    )
-    weight_grad, small_in = scatter_rows(weight_part, small_in)
+    gain_one_part = jnp.sum(grad_in_part * (in_float * factor_one), axis=0)
+    small = total(jnp.concatenate([small[0], small[1][None], gain_one_part[None]], 0))
+    gate_out, up_out, down_out = owner_grads(owner_work(owner_given))
     grad_in_rows = scatter_tensor(grad_in_part)
+    layer_out = (hidden + moe_rows).astype(BF)
     ends = [0]
     for size in (lines * q_cols, lines * HD, lines * HD, lines * q_cols):
         ends.append(ends[-1] + size)
@@ -698,16 +815,10 @@
     factor_rows = lax.dynamic_slice_in_dim(factor_one, first, part, 0)
     unit_rows = lax.dynamic_slice_in_dim(in_float, first, part, 0) * factor_rows
     input_grad = grad_hidden + norm_back(unit_rows, factor_rows, norm1_gain, grad_in_rows)
-    small = total(small_in)
     gain_one_grad = small[experts + 1]
     gain_two_grad = small[experts]
     router_grad = small[:experts].T
 
-    grad_outs = [
-        (dot(x, grad_gate, TN), dot(x, grad_up, TN), dot(act, grad_expert, TN))
-        for x, act, grad_expert, grad_gate, grad_up in owned
-    ]
-    gate_out, up_out, down_out = (jnp.stack(each) for each in zip(*grad_outs))
     return (
         layer_out,
         input_grad,

time: 590 us -> 598 us (1.014)
  Pallas kernels: 118 us -> 162 us
  matrix products: 88 us -> 49.2 us
  waiting for transfers between devices: 154 us -> 170 us
    pallas_call x1 -> x4, Pallas kernels: 45.4 us -> 85.2 us  [the longest x1 42.4 us: run_experts(): pl.pallas_call(experts_kernel, grid=(experts // at_once,), in_specs=[of(c...]
    dot_general x8 -> x2, matrix products: 44 us -> 7.18 us  [dot(): return lax.dot_general(a, b, dims, preferred_element_type=F32)]
    all_to_all x4, waiting for transfers between devices: 0.01 us -> 12.3 us  [to_owner(): return lax.all_to_all(x, 'dp', 0, 0, tiled=True)]
    select_n x5 -> x2, other arithmetic: 12.1 us -> 2.16 us  [assemble(): jnp.where(low, own, other)]
    optimization_barrier x1 -> x0, local copies, waits for them, and re-layouts: 8.61 us -> none  [shards(): lax.optimization_barrier((dqkv, weight_part, owned))]
    all_to_all x4, starting transfers between devices: 33.6 us -> 26.4 us  [to_owner(): return lax.all_to_all(x, 'dp', 0, 0, tiled=True)]
    add x10 -> x5, other arithmetic: 0.7 us -> 7.47 us  [the longest x1 6.04 us: scatter_rows(): x = keep + across(send, 'dp', 1)]
    convert_element_type x3 -> x0, other arithmetic: 6.36 us -> none  [the longest x1 3.91 us: owner_forward(): (mine(gate_owned)[:, None] * mine(g_owned).astype(F32)).astype(BF)]
  transfers between devices with their start and end apart: 48 -> 45, of which waited for: 20 -> 21; matrix products, arithmetic and copies ran while one was open for 24% -> 17% of each run, Pallas kernels for 19% -> 25%
where the time goes in v3:
time: 598 us; the launch traced here: 590 us
  waiting for transfers between devices  170 us (28%)
  Pallas kernels  162 us (27%)
  starting transfers between devices  112 us (19%)
  matrix products  49.2 us (8%)
  other arithmetic  49 us (8%)
  local copies, waits for them, and re-layouts  44.3 us (7%)
    ppermute x40, waiting for transfers between devices, across(): return lax.ppermute(x, axis, [(i, i ^ mask) for i in range(n)])  157 us
    ppermute x40, starting transfers between devices, across(): return lax.ppermute(x, axis, [(i, i ^ mask) for i in range(n)])  80.3 us
    pallas_call x1, Pallas kernels, run_experts(): pl.pallas_call(experts_kernel, grid=(experts // at_once,), in_specs=[of(c...  42.4 us
    pallas_call x1, Pallas kernels, attend_back(): pl.pallas_call(functools.partial(attend_back_kernel, heads, rows, lines,...  40.5 us
    dot_general x9, matrix products, dot(): return jnp.dot(a, b, preferred_element_type=F32)  38.2 us
    pallas_call x2, Pallas kernels, owner_call(): pl.pallas_call(functools.partial(kernel, len(x), len(g)), grid_spec=pltpu...  36.6 us
    pallas_call x1, Pallas kernels, attend(): pl.pallas_call(functools.partial(attend_kernel, heads, rows, lines, strid...  30.8 us
    all_to_all x4, starting transfers between devices, to_owner(): return lax.all_to_all(x, 'dp', 0, 0, tiled=True)  26.4 us
  transfers between devices with their start and end apart: 45, of which 21 were waited for; matrix products, arithmetic and copies ran while one was open for 17% of the time, Pallas kernels for 25%

profile of v3, /device:TPU:0, one launch (start us, length us, event | category | flops | bytes accessed | tf_op | source)
XLA Modules:
  0.0 590.1 jit_solution(17853217352350847961)
XLA Ops:
  3.8 5.7 project.1
  11.3 5.1 collective-permute-start.2
  18.4 2.9 collective-permute-start.7
  25.6 3.0 collective-permute-done.1
  32.4 9.3 %collective-permute-done.4.refs_6_.refs_10_ = bf16[4,512,128]{2,1,0:T(8,128)(2,1)} collective-permute-done((bf16[4,512,128]{2,1,0:T(8,128)(2,1)S(1)}, bf16[4,512,128]{2,1,0:T(8,128)(2,1)}, u32[]{:S(2)}, u32[]{:S(2)}) %collective-permute-start.4) | collective-permute-done | bytes 524320 | tf_op jit(solution)/shard_map/ppermute | solution.py:32
  41.9 3.5 convolution_convert_fusion.2
  45.5 3.7 convolution_convert_fusion.3
  49.3 4.9 all-to-all-start
  55.2 30.8 %attend.1 = (bf16[512,192]{1,0:T(8,128)(2,1)S(1)}, bf16[512,192]{1,0:T(8,128)(2,1)S(1)}, bf16[512,192]{1,0:T(8,128)(2,1)S(1)}, bf16[512,192]{1,0:T(8,128)(2,1)S(...) custom-call(s32[13]{0:T(128)S(1)} %pad_add_fusion.1.meta, bf16[512,192]{1,0:T(8,128)(2,1)S(1)} %copy-done.19, ...), custom_call_target="tpu_custom_call" | custom-call | flops 9663676416 | bytes 8388608 | tf_op jit(solution)/shard_map/attend/pallas_call | solution.py:274
  88.7 4.7 collective-permute-start.10
  94.9 7.8 %convolution_convert_fusion.1 = bf16[2048,1536]{1,0:T(8,128)(2,1)} fusion(pred[2048,512]{1,0:T(32,128)(4,1)} %copy-done.35, bf16[512,1536]{1,0:T(8,128)(2,1)} %param.27), kind=kOutput, calls=%fused_computation.1 | convolution fusion | flops 3224371200 | bytes 8912896 | tf_op jit(solution)/shard_map/dot_general | solution.py:26
  102.7 5.9 collective-permute-done.10
  108.6 5.0 collective-permute-done.11
  119.5 18.5 %collective-permute-done.12 = bf16[256,1536]{1,0:T(8,128)(2,1)} collective-permute-done((bf16[256,1536]{1,0:T(8,128)(2,1)}, bf16[256,1536]{1,0:T(8,128)(2,1)}, u32[]{:S(2)}, u32[]{:S(2)}) %collective-permute-start.12) | collective-permute-done | bytes 786464 | tf_op jit(solution)/shard_map/ppermute | solution.py:32
  138.0 2.2 multiply_reduce_fusion.5
  144.0 6.0 %all-to-all-start.1 = ((bf16[16,128,384]{2,1,0:T(8,128)(2,1)}), bf16[16,128,384]{2,1,0:T(8,128)(2,1)}, u32[]{:S(2)}, u32[]{:S(2)}) async-start(bf16[16,128,384]{2,1,0:T(8,128)(2,1)} %bitcast.111), calls=%async_computation.1 | async-start | bytes 3145728 | tf_op jit(solution)/shard_map/all_to_all | solution.py:44
  150.0 11.6 %collective-permute-done.13 = bf16[256,1536]{1,0:T(8,128)(2,1)} collective-permute-done((bf16[256,1536]{1,0:T(8,128)(2,1)}, bf16[256,1536]{1,0:T(8,128)(2,1)}, u32[]{:S(2)}, u32[]{:S(2)}) %collective-permute-start.13) | collective-permute-done | bytes 786464 | tf_op jit(solution)/shard_map/ppermute | solution.py:32
  161.6 2.1 broadcast_select_fusion.3
  167.6 5.1 convolution_convert_fusion
  175.3 2.0 constant_dynamic-slice_fusion
  177.3 4.7 all-to-all-done.1.refs_4_
  182.0 9.0 %all-to-all-start.2 = ((bf16[16,128,384]{2,1,0:T(8,128)(2,1)}), bf16[16,128,384]{2,1,0:T(8,128)(2,1)}, u32[]{:S(2)}, u32[]{:S(2)}) async-start(bf16[16,128,384]{2,1,0:T(8,128)(2,1)} %get-tuple-element.142), calls=%async_computation.2 | async-start | bytes 3145728 | tf_op jit(solution)/shard_map/all_to_all | solution.py:44
  191.0 42.4 %experts.1 = (bf16[16,128,1536]{2,1,0:T(8,128)(2,1)}, bf16[16,128,1536]{2,1,0:T(8,128)(2,1)}, f32[16,8,128]{2,1,0:T(8,128)}) custom-call(bf16[16,128,1536]{2,1,0:T(8,128)(2,1)} %bitcast.107, bf16[16,128,1536]{2,1,0:T(8,128)(2,1)} %bitcast.108, f32[16,128,1]{2,1,0:T(8,128)} %copy.42.gate_ref, bf16[16,1536,512]{2,1,0:T(8,128)(2,1)} %wg_ref.3, ...), custom_call_target="tpu_custom_call" | custom-call | flops 19327352832 | bytes 100663296 | tf_op jit(solution)/shard_map/experts/pallas_call | solution.py:431
  234.3 2.6 select_reduce_fusion
  237.0 3.1 fusion.47
  240.1 7.2 %fusion.11 = f32[512,1536]{1,0:T(8,128)S(1)} fusion(f32[512,1536]{1,0:T(8,128)} %fusion.47, bf16[16,128,1536]{2,1,0:T(8,128)(2,1)} %get-tuple-element.146, s32[512,16]{0,1:T(8,128)S(1)} %broadcast_select_fusion.34), kind=kOutput, calls=%fused_computation.20 | convolution fusion | flops 3223060480 | bytes 12615680 | tf_op jit(solution)/shard_map/dot_general | solution.py:26
  251.5 3.2 fusion.12
  254.7 6.4 %all-to-all-start.3 = ((bf16[16,128,512]{2,1,0:T(8,128)(2,1)}), bf16[16,128,512]{2,1,0:T(8,128)(2,1)}, u32[]{:S(2)}, u32[]{:S(2)}) async-start(bf16[16,128,512]{2,1,0:T(8,128)(2,1)} %fusion.12), calls=%async_computation.3 | async-start | bytes 4194304 | tf_op jit(solution)/shard_map/all_to_all | solution.py:44
  261.1 8.0 %fusion.10 = f32[512,1536]{1,0:T(8,128)} fusion(bf16[16,128,1536]{2,1,0:T(8,128)(2,1)} %get-tuple-element.151, s32[512,16]{0,1:T(8,128)S(1)} %broadcast_select_fusion.34), kind=kOutput, calls=%fused_computation.19 | convolution fusion | flops 3222274048 | bytes 9469952 | tf_op jit(solution)/shard_map/dot_general | solution.py:26
  274.9 18.4 %collective-permute-done.16 = bf16[256,1536]{1,0:T(8,128)(2,1)S(1)} collective-permute-done((bf16[256,1536]{1,0:T(8,128)(2,1)S(1)}, bf16[256,1536]{1,0:T(8,128)(2,1)S(1)}, u32[]{:S(2)}, u32[]{:S(2)}) %collective-permute-start.16) | collective-permute-done | bytes 786464 | tf_op jit(solution)/shard_map/ppermute | solution.py:32
  294.7 7.6 %all-to-all-done.3 = bf16[16,128,512]{2,1,0:T(8,128)(2,1)} async-done(((bf16[16,128,512]{2,1,0:T(8,128)(2,1)}), bf16[16,128,512]{2,1,0:T(8,128)(2,1)}, u32[]{:S(2)}, u32[]{:S(2)}) %all-to-all-start.3) | async-done | bytes 2097184 | tf_op jit(solution)/shard_map/all_to_all | solution.py:44
  302.3 2.8 convolution_convert_fusion.4
  306.0 6.6 %collective-permute-start.17 = (bf16[512,192]{1,0:T(8,128)(2,1)S(1)}, bf16[512,192]{1,0:T(8,128)(2,1)S(1)}, u32[]{:S(2)}, u32[]{:S(2)}) collective-permute-start(bf16[512,192]{1,0:T(8,128)(2,1)S(1)} %get-tuple-element.238), channel_id=1, source_target_pairs={{0,8},{2,10},{4,12},{6,14},{8,0},{10,2},{12,4},{14,6},{16,24},{18,... | collective-permute-start | bytes 589832 | tf_op jit(solution)/shard_map/ppermute | solution.py:32
  312.6 2.8 collective-permute-start.18
  318.5 3.4 pad_maximum_fusion.refs_0_
  325.1 8.9 %collective-permute-done.19.refs_7_ = bf16[512,192]{1,0:T(8,128)(2,1)S(1)} collective-permute-done((bf16[512,192]{1,0:T(8,128)(2,1)S(1)}, bf16[512,192]{1,0:T(8,128)(2,1)S(1)}, u32[]{:S(2)}, u32[]{:S(2)}) %collective-permute-start.19) | collective-permute-done | bytes 196640 | tf_op jit(solution)/shard_map/ppermute | solution.py:32
  334.7 40.5 %attend_back.1 = (bf16[512,192]{1,0:T(8,128)(2,1)}, bf16[512,192]{1,0:T(8,128)(2,1)}, bf16[512,192]{1,0:T(8,128)(2,1)}, bf16[512,192]{1,0:T(8,128)(2,1)}, bf16[8...) custom-call(s32[13]{0:T(128)} %copy-done.7, bf16[512,192]{1,0:T(8,128)(2,1)} %copy-done.18, ...), custom_call_target="tpu_custom_call" | custom-call | flops 24159191040 | bytes 10485760 | tf_op jit(solution)/shard_map/attend_back/pallas_call | solution.py:368
  375.3 3.3 collective-permute-start.20
  378.5 2.5 collective-permute-done.20
  382.6 12.1 %collective-permute-start.21 = (bf16[1,4,512,128]{3,2,1,0:T(8,128)(2,1)S(1)}, bf16[1,4,512,128]{3,2,1,0:T(8,128)(2,1)S(1)}, u32[]{:S(2)}, u32[]{:S(2)}) collective-permute-start(bf16[1,4,512,128]{3,2,1,0:T(8,128)(2,1)S(1)} %slice_bitcast_fusion), channel_id=1, source_target_pairs={{0,4},{2,6},{4,0},{6,2},{8,12},{10,14},{12,8},{14,10},{16,20},{18,... | collective-permute-start | bytes 1572872 | tf_op jit(solution)/shard_map/ppermute | solution.py:32
  397.1 5.7 collective-permute-start.25
  402.8 4.1 collective-permute-done.21
  406.9 5.1 collective-permute-start.26
  413.4 4.0 collective-permute-start.28
  417.4 11.3 %collective-permute-done.25 = bf16[512,192]{1,0:T(8,128)(2,1)S(1)} collective-permute-done((bf16[512,192]{1,0:T(8,128)(2,1)S(1)}, bf16[512,192]{1,0:T(8,128)(2,1)S(1)}, u32[]{:S(2)}, u32[]{:S(2)}) %collective-permute-start.25) | collective-permute-done | bytes 196640 | tf_op jit(solution)/shard_map/ppermute | solution.py:32
  430.5 3.8 collective-permute-done.28
  434.3 2.5 collective-permute-done.29
  438.4 4.0 concatenate.33.b_ref
  445.2 6.2 %weights.1 = (bf16[8,96,2048]{2,1,0:T(8,128)(2,1)}, bf16[8,96,2048]{2,1,0:T(8,128)(2,1)}) custom-call(s32[1]{0:T(128)} %bitcast.36.at, bf16[512,1536]{1,0:T(8,128)(2,1)S(1)} %copy-done.17, bf16[512,1280]{1,0:T(8,128)(2,1)S(1)} %copy-done.3, bf16[512,1536]{1,0:T(8,128)(2,1)S(1)} %copy-done.2, bf16[512,768]{1,0:T(8,128)(2,1)S(1)} %pad_maximum_fusion.3.d_ref), custom_call_target="tpu_custom_call" | custom-call | flops 3221225472 | bytes 12582912 | tf_op jit(solution)/shard_map/weights/pallas_call | solution.py:482
  451.4 3.6 convert_element_type.103
  455.0 1.9 multiply_reduce_fusion.1
  461.5 2.4 dynamic-slice_convert_fusion.1
  464.4 6.0 %add.169 = bf16[8,96,2048]{2,1,0:T(8,128)(2,1)} add(bf16[8,96,2048]{2,1,0:T(8,128)(2,1)} %get-tuple-element.179, bf16[8,96,2048]{2,1,0:T(8,128)(2,1)} %collective-permute-done.31) | non-fusion elementwise | flops 1572864 | bytes 9437184 | tf_op jit(solution)/shard_map/add | solution.py:113
  470.4 5.0 all-to-all-start.4
  475.4 4.4 multiply_reduce_fusion
  484.5 21.4 %collective-permute-done.34 = f32[18,1536]{1,0:T(8,128)S(1)} collective-permute-done((f32[18,1536]{1,0:T(8,128)S(1)}, f32[18,1536]{1,0:T(8,128)S(1)}, u32[]{:S(2)}, u32[]{:S(2)}) %collective-permute-start.34) | collective-permute-done | bytes 110624 | tf_op jit(solution)/shard_map/ppermute | solution.py:32
  505.9 2.9 collective-permute-done.35
  509.6 2.1 collective-permute-start.37
  513.3 18.0 %owner_forward.1 = (bf16[2048,512]{1,0:T(8,128)(2,1)}, bf16[2048,512]{1,0:T(8,128)(2,1)}, bf16[2048,512]{1,0:T(8,128)(2,1)}) custom-call(s32[7]{0:T(128)} %stack.69.at, f32[2048,1]{1,0:T(8,128)} %copy.45.gate_ref, bf16[16,1536,512]{2,1,0:T(8,128)(2,1)} %wg_ref.3, bf16[16,1536,512]{2,1,0:T(8,128)(2,1)} %wu_ref.3, bf16[16,512,1536]{2,1,0:T(8,128)(2,1)} %wd_ref.3, ...), custom_call_target="tpu_custom_call" | custom-call | flops 10737418240 | bytes 25165824 | tf_op jit(solution)/shard_map/owner_forward/pallas_call | solution.py:564
  531.5 25.4 %collective-permute-done.37 = f32[18,1536]{1,0:T(8,128)S(1)} collective-permute-done((f32[18,1536]{1,0:T(8,128)S(1)}, f32[18,1536]{1,0:T(8,128)S(1)}, u32[]{:S(2)}, u32[]{:S(2)}) %collective-permute-start.37) | collective-permute-done | bytes 110624 | tf_op jit(solution)/shard_map/ppermute | solution.py:32
  558.5 18.7 %owner_grads.1 = (f32[1,1536,512]{2,1,0:T(8,128)}, f32[1,1536,512]{2,1,0:T(8,128)}, f32[1,512,1536]{2,1,0:T(8,128)}) custom-call(s32[7]{0:T(128)} %stack.69.at, f32[2048,1]{1,0:T(8,128)} %copy.45.gate_ref, bf16[2048,512]{1,0:T(8,128)(2,1)} %get-tuple-element.198.act_ref, bf16[2048,512]{1,0:T(8,128)(2,1)} %get-tuple-element.199.grad_gate_ref, ...), custom_call_target="tpu_custom_call" | custom-call | flops 10737418240 | bytes 25165824 | tf_op jit(solution)/shard_map/owner_grads/pallas_call | solution.py:564
  578.5 2.0 multiply_reduce_fusion.2
  580.8 4.7 multiply_add_fusion
  585.6 2.7 convert_reduce_fusion
  (242 shorter events, 82.7 us)
Async XLA Ops:
  0.6 113.3 %copy-start = (bf16[768,1536]{1,0:T(8,128)(2,1)S(1)}, bf16[768,1536]{1,0:T(8,128)(2,1)}, u32[]{:S(2)}) copy-start(bf16[768,1536]{1,0:T(8,128)(2,1)} %param.19) | copy-start | bytes 7077892
  3.8 20.8 %copy-start.52 = (s32[512,2]{0,1:T(2,128)S(1)}, s32[512,2]{0,1:T(2,128)}, u32[]{:S(2)}) copy-start(s32[512,2]{0,1:T(2,128)} %param.26) | copy-start | bytes 12292
  11.3 14.3 %collective-permute-start.2 = (bf16[512,128]{1,0:T(8,128)(2,1)S(1)}, bf16[512,128]{1,0:T(8,128)(2,1)S(1)}, u32[]{:S(2)}, u32[]{:S(2)}) collective-permute-start(bf16[512,128]{1,0:T(8,128)(2,1)S(1)} %get-tuple-element.111), channel_id=1, source_target_pairs={{0,24},{2,26},{4,28},{6,30},{8,16},{10,18},{12,20},{14,22},{16,8},... | collective-permute-start | bytes 393224 | tf_op jit(solution)/shard_map/ppermute | solution.py:32
  16.3 9.2 %collective-permute-start = (bf16[512,128]{1,0:T(8,128)(2,1)S(1)}, bf16[512,128]{1,0:T(8,128)(2,1)S(1)}, u32[]{:S(2)}, u32[]{:S(2)}) collective-permute-start(bf16[512,128]{1,0:T(8,128)(2,1)S(1)} %get-tuple-element.109), channel_id=1, source_target_pairs={{0,8},{2,10},{4,12},{6,14},{8,0},{10,2},{12,4},{14,6},{16,24},{18,... | collective-permute-start | bytes 393224 | tf_op jit(solution)/shard_map/ppermute | solution.py:32
  16.3 12.2 %collective-permute-start.1 = (bf16[512,128]{1,0:T(8,128)(2,1)S(1)}, bf16[512,128]{1,0:T(8,128)(2,1)}, u32[]{:S(2)}, u32[]{:S(2)}) collective-permute-start(bf16[512,128]{1,0:T(8,128)(2,1)S(1)} %get-tuple-element.110), channel_id=1, source_target_pairs={{0,16},{2,18},{4,20},{6,22},{8,24},{10,26},{12,28},{14,30},{16,0},... | collective-permute-start | bytes 393224 | tf_op jit(solution)/shard_map/ppermute | solution.py:32
  16.9 32.3 %collective-permute-start.6 = (bf16[512,192]{1,0:T(8,128)(2,1)}, bf16[512,192]{1,0:T(8,128)(2,1)S(1)}, u32[]{:S(2)}, u32[]{:S(2)}) collective-permute-start(bf16[512,192]{1,0:T(8,128)(2,1)} %get-tuple-element.113), channel_id=1, source_target_pairs={{0,8},{2,10},{4,12},{6,14},{8,0},{10,2},{12,4},{14,6},{16,24},{18,... | collective-permute-start | bytes 589832 | tf_op jit(solution)/shard_map/ppermute | solution.py:32
  18.4 30.8 %collective-permute-start.7 = (bf16[512,192]{1,0:T(8,128)(2,1)}, bf16[512,192]{1,0:T(8,128)(2,1)}, u32[]{:S(2)}, u32[]{:S(2)}) collective-permute-start(bf16[512,192]{1,0:T(8,128)(2,1)} %get-tuple-element.114), channel_id=1, source_target_pairs={{0,16},{2,18},{4,20},{6,22},{8,24},{10,26},{12,28},{14,30},{16,0},... | collective-permute-start | bytes 589832 | tf_op jit(solution)/shard_map/ppermute | solution.py:32
  23.9 8.1 %copy-start.44 = (s32[8192]{0:T(1024)S(1)}, s32[8192]{0:T(1024)}, u32[]{:S(2)}) copy-start(s32[8192]{0:T(1024)} %param.25) | copy-start | bytes 98308
  25.6 19.9 %copy-start.40 = (s32[16,512]{1,0:T(8,128)}, s32[16,512]{1,0:T(8,128)S(1)}, u32[]{:S(2)}) copy-start(s32[16,512]{1,0:T(8,128)S(1)} %get-tuple-element.262) | copy-start | bytes 98308
  25.6 23.7 %collective-permute-start.8 = (bf16[512,192]{1,0:T(8,128)(2,1)}, bf16[512,192]{1,0:T(8,128)(2,1)}, u32[]{:S(2)}, u32[]{:S(2)}) collective-permute-start(bf16[512,192]{1,0:T(8,128)(2,1)} %get-tuple-element.115), channel_id=1, source_target_pairs={{0,24},{2,26},{4,28},{6,30},{8,16},{10,18},{12,20},{14,22},{16,8},... | collective-permute-start | bytes 589832 | tf_op jit(solution)/shard_map/ppermute | solution.py:32
  29.6 24.6 %copy-start.5 = (bf16[4,512,128]{2,1,0:T(8,128)(2,1)}, bf16[4,512,128]{2,1,0:T(8,128)(2,1)S(1)}, u32[]{:S(2)}) copy-start(bf16[4,512,128]{2,1,0:T(8,128)(2,1)S(1)} %pad_maximum_fusion.4.refs_4_.refs_8_) | copy-start | bytes 1572868
  29.6 12.1 %collective-permute-start.4 = (bf16[4,512,128]{2,1,0:T(8,128)(2,1)S(1)}, bf16[4,512,128]{2,1,0:T(8,128)(2,1)}, u32[]{:S(2)}, u32[]{:S(2)}) collective-permute-start(bf16[4,512,128]{2,1,0:T(8,128)(2,1)S(1)} %pad_maximum_fusion.4.refs_4_.refs_8_), channel_id=1, source_target_pairs={{0,4},{2,6},{4,0},{6,2},{8,12},{10,14},{12,8},{14,10},{16,20},{18,... | collective-permute-start | bytes 1572872 | tf_op jit(solution)/shard_map/ppermute | solution.py:32
  32.0 13.5 %copy-start.35 = (pred[2048,512]{1,0:T(32,128)(4,1)}, pred[2048,512]{1,0:T(32,128)(4,1)S(1)}, u32[]{:S(2)}) copy-start(pred[2048,512]{1,0:T(32,128)(4,1)S(1)} %bitcast_compare_fusion) | copy-start | bytes 3145732
  32.4 16.9 %collective-permute-start.3 = (bf16[4,512,128]{2,1,0:T(8,128)(2,1)S(1)}, bf16[4,512,128]{2,1,0:T(8,128)(2,1)}, u32[]{:S(2)}, u32[]{:S(2)}) collective-permute-start(bf16[4,512,128]{2,1,0:T(8,128)(2,1)S(1)} %pad_maximum_fusion.4.refs_4_.refs_8_), channel_id=1, source_target_pairs={{0,2},{2,0},{4,6},{6,4},{8,10},{10,8},{12,14},{14,12},{16,18},{18,... | collective-permute-start | bytes 1572872 | tf_op jit(solution)/shard_map/ppermute | solution.py:32
  41.7 7.5 %collective-permute-start.5 = (bf16[4,512,128]{2,1,0:T(8,128)(2,1)}, bf16[4,512,128]{2,1,0:T(8,128)(2,1)}, u32[]{:S(2)}, u32[]{:S(2)}) collective-permute-start(bf16[4,512,128]{2,1,0:T(8,128)(2,1)} %collective-permute-done.4.refs_6_.refs_10_), channel_id=1, source_target_pairs={{0,2},{2,0},{4,6},{6,4},{8,10},{10,8},{12,14},{14,12},{16,18},{18,... | collective-permute-start | bytes 1572872 | tf_op jit(solution)/shard_map/ppermute | solution.py:32
  45.5 8.7 %copy-start.7 = (s32[13]{0:T(128)}, s32[13]{0:T(128)S(1)}, u32[]{:S(2)}) copy-start(s32[13]{0:T(128)S(1)} %pad_add_fusion.1.meta) | copy-start | bytes 160
  49.3 39.5 %all-to-all-start = ((bf16[16,128,384]{2,1,0:T(8,128)(2,1)}), bf16[16,128,384]{2,1,0:T(8,128)(2,1)}, u32[]{:S(2)}, u32[]{:S(2)}) async-start(bf16[16,128,384]{2,1,0:T(8,128)(2,1)} %bitcast.112), calls=%async_computation | async-start | bytes 3145728 | tf_op jit(solution)/shard_map/all_to_all | solution.py:44
  55.2 30.8 %copy-start.6 = (s32[4,1,512]{2,1,0:T(1,128)}, s32[4,1,512]{2,1,0:T(1,128)S(1)}, u32[]{:S(2)}) copy-start(s32[4,1,512]{2,1,0:T(1,128)S(1)} %broadcast_in_dim.118.refs_8_.refs_14_) | copy-start | bytes 24580
  88.7 19.8 %collective-permute-start.10 = (bf16[512,192]{1,0:T(8,128)(2,1)}, bf16[512,192]{1,0:T(8,128)(2,1)S(1)}, u32[]{:S(2)}, u32[]{:S(2)}) collective-permute-start(bf16[512,192]{1,0:T(8,128)(2,1)} %copy-done.15), channel_id=1, source_target_pairs={{0,16},{2,18},{4,20},{6,22},{8,24},{10,26},{12,28},{14,30},{16,0},... | collective-permute-start | bytes 589832 | tf_op jit(solution)/shard_map/ppermute | solution.py:32
  93.4 20.1 %collective-permute-start.11 = (bf16[512,192]{1,0:T(8,128)(2,1)}, bf16[512,192]{1,0:T(8,128)(2,1)S(1)}, u32[]{:S(2)}, u32[]{:S(2)}) collective-permute-start(bf16[512,192]{1,0:T(8,128)(2,1)} %copy-done.14), channel_id=1, source_target_pairs={{0,8},{2,10},{4,12},{6,14},{8,0},{10,2},{12,4},{14,6},{16,24},{18,... | collective-permute-start | bytes 589832 | tf_op jit(solution)/shard_map/ppermute | solution.py:32
  93.4 20.1 %collective-permute-start.9 = (bf16[512,192]{1,0:T(8,128)(2,1)}, bf16[512,192]{1,0:T(8,128)(2,1)S(1)}, u32[]{:S(2)}, u32[]{:S(2)}) collective-permute-start(bf16[512,192]{1,0:T(8,128)(2,1)} %copy-done.13), channel_id=1, source_target_pairs={{0,24},{2,26},{4,28},{6,30},{8,16},{10,18},{12,20},{14,22},{16,8},... | collective-permute-start | bytes 589832 | tf_op jit(solution)/shard_map/ppermute | solution.py:32
  118.0 20.0 %collective-permute-start.12 = (bf16[256,1536]{1,0:T(8,128)(2,1)}, bf16[256,1536]{1,0:T(8,128)(2,1)}, u32[]{:S(2)}, u32[]{:S(2)}) collective-permute-start(bf16[256,1536]{1,0:T(8,128)(2,1)} %dynamic-slice_convert_fusion.3), channel_id=1, source_target_pairs={{0,1},{1,0},{2,3},{3,2},{4,5},{5,4},{6,7},{7,6},{8,9},{9,8},{10,11... | collective-permute-start | bytes 2359304 | tf_op jit(solution)/shard_map/ppermute | solution.py:32
  119.5 21.8 %copy-start.38 = (f32[1536]{0:T(1024)S(1)}, f32[1536]{0:T(1024)}, u32[]{:S(2)}) copy-start(f32[1536]{0:T(1024)} %param.20) | copy-start | bytes 18436
  140.2 132.2 %copy-start.45 = (f32[256]{0:T(256)}, f32[256]{0:T(256)S(1)}, u32[]{:S(2)}) copy-start(f32[256]{0:T(256)S(1)} %add_rsqrt_fusion.1) | copy-start | bytes 3076
  142.4 7.6 %copy-start.48 = (s32[512,16]{0,1:T(8,128)S(1)}, s32[512,16]{0,1:T(8,128)}, u32[]{:S(2)}) copy-start(s32[512,16]{0,1:T(8,128)} %get-tuple-element.263) | copy-start | bytes 98308
  142.5 19.2 %collective-permute-start.13 = (bf16[256,1536]{1,0:T(8,128)(2,1)}, bf16[256,1536]{1,0:T(8,128)(2,1)}, u32[]{:S(2)}, u32[]{:S(2)}) collective-permute-start(bf16[256,1536]{1,0:T(8,128)(2,1)} %multiply_convert_fusion), channel_id=1, source_target_pairs={{0,1},{1,0},{2,3},{3,2},{4,5},{5,4},{6,7},{7,6},{8,9},{9,8},{10,11... | collective-permute-start | bytes 2359304 | tf_op jit(solution)/shard_map/ppermute | solution.py:32
  144.0 38.1 %all-to-all-start.1 = ((bf16[16,128,384]{2,1,0:T(8,128)(2,1)}), bf16[16,128,384]{2,1,0:T(8,128)(2,1)}, u32[]{:S(2)}, u32[]{:S(2)}) async-start(bf16[16,128,384]{2,1,0:T(8,128)(2,1)} %bitcast.111), calls=%async_computation.1 | async-start | bytes 3145728 | tf_op jit(solution)/shard_map/all_to_all | solution.py:44
  172.7 67.4 %collective-permute-start.14 = (bf16[16,128,384]{2,1,0:T(8,128)(2,1)}, bf16[16,128,384]{2,1,0:T(8,128)(2,1)}, u32[]{:S(2)}, u32[]{:S(2)}) collective-permute-start(bf16[16,128,384]{2,1,0:T(8,128)(2,1)} %all-to-all-done.refs_2_), channel_id=1, source_target_pairs={{0,1},{1,0},{2,3},{3,2},{4,5},{5,4},{6,7},{7,6},{8,9},{9,8},{10,11... | collective-permute-start | bytes 4718600 | tf_op jit(solution)/shard_map/ppermute | solution.py:32
  182.0 58.1 %all-to-all-start.2 = ((bf16[16,128,384]{2,1,0:T(8,128)(2,1)}), bf16[16,128,384]{2,1,0:T(8,128)(2,1)}, u32[]{:S(2)}, u32[]{:S(2)}) async-start(bf16[16,128,384]{2,1,0:T(8,128)(2,1)} %get-tuple-element.142), calls=%async_computation.2 | async-start | bytes 3145728 | tf_op jit(solution)/shard_map/all_to_all | solution.py:44
  249.9 20.1 %collective-permute-start.15 = (bf16[256,1536]{1,0:T(8,128)(2,1)}, bf16[256,1536]{1,0:T(8,128)(2,1)}, u32[]{:S(2)}, u32[]{:S(2)}) collective-permute-start(bf16[256,1536]{1,0:T(8,128)(2,1)} %dynamic-slice_convert_fusion.2), channel_id=1, source_target_pairs={{0,1},{1,0},{2,3},{3,2},{4,5},{5,4},{6,7},{7,6},{8,9},{9,8},{10,11... | collective-permute-start | bytes 2359304 | tf_op jit(solution)/shard_map/ppermute | solution.py:32
  254.7 47.6 %all-to-all-start.3 = ((bf16[16,128,512]{2,1,0:T(8,128)(2,1)}), bf16[16,128,512]{2,1,0:T(8,128)(2,1)}, u32[]{:S(2)}, u32[]{:S(2)}) async-start(bf16[16,128,512]{2,1,0:T(8,128)(2,1)} %fusion.12), calls=%async_computation.3 | async-start | bytes 4194304 | tf_op jit(solution)/shard_map/all_to_all | solution.py:44
  261.1 8.9 %copy-start.32 = (f32[512,1536]{1,0:T(8,128)S(1)}, f32[512,1536]{1,0:T(8,128)}, u32[]{:S(2)}) copy-start(f32[512,1536]{1,0:T(8,128)} %copy-done.31) | copy-start | bytes 9437188
  273.9 19.4 %collective-permute-start.16 = (bf16[256,1536]{1,0:T(8,128)(2,1)S(1)}, bf16[256,1536]{1,0:T(8,128)(2,1)S(1)}, u32[]{:S(2)}, u32[]{:S(2)}) collective-permute-start(bf16[256,1536]{1,0:T(8,128)(2,1)S(1)} %fusion.38), channel_id=1, source_target_pairs={{0,1},{1,0},{2,3},{3,2},{4,5},{5,4},{6,7},{7,6},{8,9},{9,8},{10,11... | collective-permute-start | bytes 2359304 | tf_op jit(solution)/shard_map/ppermute | solution.py:32
  306.0 19.0 %collective-permute-start.17 = (bf16[512,192]{1,0:T(8,128)(2,1)S(1)}, bf16[512,192]{1,0:T(8,128)(2,1)S(1)}, u32[]{:S(2)}, u32[]{:S(2)}) collective-permute-start(bf16[512,192]{1,0:T(8,128)(2,1)S(1)} %get-tuple-element.238), channel_id=1, source_target_pairs={{0,8},{2,10},{4,12},{6,14},{8,0},{10,2},{12,4},{14,6},{16,24},{18,... | collective-permute-start | bytes 589832 | tf_op jit(solution)/shard_map/ppermute | solution.py:32
  312.6 12.4 %collective-permute-start.18 = (bf16[512,192]{1,0:T(8,128)(2,1)S(1)}, bf16[512,192]{1,0:T(8,128)(2,1)S(1)}, u32[]{:S(2)}, u32[]{:S(2)}) collective-permute-start(bf16[512,192]{1,0:T(8,128)(2,1)S(1)} %get-tuple-element.239), channel_id=1, source_target_pairs={{0,16},{2,18},{4,20},{6,22},{8,24},{10,26},{12,28},{14,30},{16,0},... | collective-permute-start | bytes 589832 | tf_op jit(solution)/shard_map/ppermute | solution.py:32
  315.4 18.6 %collective-permute-start.19 = (bf16[512,192]{1,0:T(8,128)(2,1)S(1)}, bf16[512,192]{1,0:T(8,128)(2,1)S(1)}, u32[]{:S(2)}, u32[]{:S(2)}) collective-permute-start(bf16[512,192]{1,0:T(8,128)(2,1)S(1)} %get-tuple-element.236), channel_id=1, source_target_pairs={{0,24},{2,26},{4,28},{6,30},{8,16},{10,18},{12,20},{14,22},{16,8},... | collective-permute-start | bytes 589832 | tf_op jit(solution)/shard_map/ppermute | solution.py:32
  321.9 90.2 %collective-permute-start.22 = (bf16[16,128,768]{2,1,0:T(8,128)(2,1)}, bf16[16,128,768]{2,1,0:T(8,128)(2,1)}, u32[]{:S(2)}, u32[]{:S(2)}) collective-permute-start(bf16[16,128,768]{2,1,0:T(8,128)(2,1)} %pad_maximum_fusion.refs_0_), channel_id=1, source_target_pairs={{0,1},{1,0},{2,3},{3,2},{4,5},{5,4},{6,7},{7,6},{8,9},{9,8},{10,11... | collective-permute-start | bytes 9437192 | tf_op jit(solution)/shard_map/ppermute | solution.py:32
  325.1 9.0 %copy-start.55 = (bf16[512,192]{1,0:T(8,128)(2,1)}, bf16[512,192]{1,0:T(8,128)(2,1)S(1)}, u32[]{:S(2)}) copy-start(bf16[512,192]{1,0:T(8,128)(2,1)S(1)} %collective-permute-done.17.refs_5_) | copy-start | bytes 589828
  325.1 9.0 %copy-start.56 = (bf16[512,192]{1,0:T(8,128)(2,1)}, bf16[512,192]{1,0:T(8,128)(2,1)S(1)}, u32[]{:S(2)}) copy-start(bf16[512,192]{1,0:T(8,128)(2,1)S(1)} %collective-permute-done.18.refs_6_) | copy-start | bytes 589828
  375.3 5.8 collective-permute-start.20
  381.0 16.1 %copy-start.54 = (bf16[512,192]{1,0:T(8,128)(2,1)S(1)}, bf16[512,192]{1,0:T(8,128)(2,1)}, u32[]{:S(2)}) copy-start(bf16[512,192]{1,0:T(8,128)(2,1)} %get-tuple-element.168) | copy-start | bytes 589828
  381.0 25.9 %copy-start.53 = (bf16[512,192]{1,0:T(8,128)(2,1)S(1)}, bf16[512,192]{1,0:T(8,128)(2,1)}, u32[]{:S(2)}) copy-start(bf16[512,192]{1,0:T(8,128)(2,1)} %get-tuple-element.169) | copy-start | bytes 589828
  382.6 24.3 %collective-permute-start.21 = (bf16[1,4,512,128]{3,2,1,0:T(8,128)(2,1)S(1)}, bf16[1,4,512,128]{3,2,1,0:T(8,128)(2,1)S(1)}, u32[]{:S(2)}, u32[]{:S(2)}) collective-permute-start(bf16[1,4,512,128]{3,2,1,0:T(8,128)(2,1)S(1)} %slice_bitcast_fusion), channel_id=1, source_target_pairs={{0,4},{2,6},{4,0},{6,2},{8,12},{10,14},{12,8},{14,10},{16,20},{18,... | collective-permute-start | bytes 1572872 | tf_op jit(solution)/shard_map/ppermute | solution.py:32
  394.7 47.7 %collective-permute-start.30 = (bf16[16,128,384]{2,1,0:T(8,128)(2,1)}, bf16[16,128,384]{2,1,0:T(8,128)(2,1)}, u32[]{:S(2)}, u32[]{:S(2)}) collective-permute-start(bf16[16,128,384]{2,1,0:T(8,128)(2,1)} %all-to-all-done.1.refs_4_), channel_id=1, source_target_pairs={{0,1},{1,0},{2,3},{3,2},{4,5},{5,4},{6,7},{7,6},{8,9},{9,8},{10,11... | collective-permute-start | bytes 4718600 | tf_op jit(solution)/shard_map/ppermute | solution.py:32
  396.2 17.2 %collective-permute-start.24 = (bf16[512,192]{1,0:T(8,128)(2,1)}, bf16[512,192]{1,0:T(8,128)(2,1)S(1)}, u32[]{:S(2)}, u32[]{:S(2)}) collective-permute-start(bf16[512,192]{1,0:T(8,128)(2,1)} %get-tuple-element.167), channel_id=1, source_target_pairs={{0,24},{2,26},{4,28},{6,30},{8,16},{10,18},{12,20},{14,22},{16,8},... | collective-permute-start | bytes 589832 | tf_op jit(solution)/shard_map/ppermute | solution.py:32
  397.1 31.5 %collective-permute-start.25 = (bf16[512,192]{1,0:T(8,128)(2,1)S(1)}, bf16[512,192]{1,0:T(8,128)(2,1)S(1)}, u32[]{:S(2)}, u32[]{:S(2)}) collective-permute-start(bf16[512,192]{1,0:T(8,128)(2,1)S(1)} %copy-done.54), channel_id=1, source_target_pairs={{0,16},{2,18},{4,20},{6,22},{8,24},{10,26},{12,28},{14,30},{16,0},... | collective-permute-start | bytes 589832 | tf_op jit(solution)/shard_map/ppermute | solution.py:32
  406.9 21.7 %collective-permute-start.26 = (bf16[512,192]{1,0:T(8,128)(2,1)S(1)}, bf16[512,192]{1,0:T(8,128)(2,1)S(1)}, u32[]{:S(2)}, u32[]{:S(2)}) collective-permute-start(bf16[512,192]{1,0:T(8,128)(2,1)S(1)} %copy-done.53), channel_id=1, source_target_pairs={{0,8},{2,10},{4,12},{6,14},{8,0},{10,2},{12,4},{14,6},{16,24},{18,... | collective-permute-start | bytes 589832 | tf_op jit(solution)/shard_map/ppermute | solution.py:32
  412.2 18.3 %collective-permute-start.27 = (bf16[512,128]{1,0:T(8,128)(2,1)S(1)}, bf16[512,128]{1,0:T(8,128)(2,1)S(1)}, u32[]{:S(2)}, u32[]{:S(2)}) collective-permute-start(bf16[512,128]{1,0:T(8,128)(2,1)S(1)} %get-tuple-element.242), channel_id=1, source_target_pairs={{0,24},{2,26},{4,28},{6,30},{8,16},{10,18},{12,20},{14,22},{16,8},... | collective-permute-start | bytes 393224 | tf_op jit(solution)/shard_map/ppermute | solution.py:32
  413.4 20.9 %collective-permute-start.28 = (bf16[512,128]{1,0:T(8,128)(2,1)S(1)}, bf16[512,128]{1,0:T(8,128)(2,1)S(1)}, u32[]{:S(2)}, u32[]{:S(2)}) collective-permute-start(bf16[512,128]{1,0:T(8,128)(2,1)S(1)} %get-tuple-element.241), channel_id=1, source_target_pairs={{0,16},{2,18},{4,20},{6,22},{8,24},{10,26},{12,28},{14,30},{16,0},... | collective-permute-start | bytes 393224 | tf_op jit(solution)/shard_map/ppermute | solution.py:32
  428.6 8.1 %collective-permute-start.29 = (bf16[512,128]{1,0:T(8,128)(2,1)S(1)}, bf16[512,128]{1,0:T(8,128)(2,1)S(1)}, u32[]{:S(2)}, u32[]{:S(2)}) collective-permute-start(bf16[512,128]{1,0:T(8,128)(2,1)S(1)} %get-tuple-element.240), channel_id=1, source_target_pairs={{0,8},{2,10},{4,12},{6,14},{8,0},{10,2},{12,4},{14,6},{16,24},{18,... | collective-permute-start | bytes 393224 | tf_op jit(solution)/shard_map/ppermute | solution.py:32
  451.3 13.0 %collective-permute-start.31 = (bf16[8,96,2048]{2,1,0:T(8,128)(2,1)}, bf16[8,96,2048]{2,1,0:T(8,128)(2,1)}, u32[]{:S(2)}, u32[]{:S(2)}) collective-permute-start(bf16[8,96,2048]{2,1,0:T(8,128)(2,1)} %get-tuple-element.180), channel_id=1, source_target_pairs={{0,2},{2,0},{4,6},{6,4},{8,10},{10,8},{12,14},{14,12},{16,18},{18,... | collective-permute-start | bytes 9437192 | tf_op jit(solution)/shard_map/ppermute | solution.py:32
  463.8 116.6 %collective-permute-start.23 = (bf16[256,1536]{1,0:T(8,128)(2,1)}, bf16[256,1536]{1,0:T(8,128)(2,1)}, u32[]{:S(2)}, u32[]{:S(2)}) collective-permute-start(bf16[256,1536]{1,0:T(8,128)(2,1)} %dynamic-slice_convert_fusion.1), channel_id=1, source_target_pairs={{0,1},{1,0},{2,3},{3,2},{4,5},{5,4},{6,7},{7,6},{8,9},{9,8},{10,11... | collective-permute-start | bytes 2359304 | tf_op jit(solution)/shard_map/ppermute | solution.py:32
  470.4 115.2 %all-to-all-start.4 = ((bf16[8,96,2048]{2,1,0:T(8,128)(2,1)}), bf16[8,96,2048]{2,1,0:T(8,128)(2,1)}, u32[]{:S(2)}, u32[]{:S(2)}) async-start(bf16[8,96,2048]{2,1,0:T(8,128)(2,1)} %add.169), calls=%async_computation.4 | async-start | bytes 6291456 | tf_op jit(solution)/shard_map/all_to_all | solution.py:116
  479.9 4.7 collective-permute-start.33
  480.1 25.8 %collective-permute-start.34 = (f32[18,1536]{1,0:T(8,128)S(1)}, f32[18,1536]{1,0:T(8,128)S(1)}, u32[]{:S(2)}, u32[]{:S(2)}) collective-permute-start(f32[18,1536]{1,0:T(8,128)S(1)} %pad_maximum_fusion.5), channel_id=1, source_target_pairs={{0,4},{2,6},{4,0},{6,2},{8,12},{10,14},{12,8},{14,10},{16,20},{18,... | collective-permute-start | bytes 331784 | tf_op jit(solution)/shard_map/ppermute | solution.py:32
  481.9 26.9 %collective-permute-start.35 = (f32[18,1536]{1,0:T(8,128)S(1)}, f32[18,1536]{1,0:T(8,128)S(1)}, u32[]{:S(2)}, u32[]{:S(2)}) collective-permute-start(f32[18,1536]{1,0:T(8,128)S(1)} %pad_maximum_fusion.5), channel_id=1, source_target_pairs={{0,6},{2,4},{4,2},{6,0},{8,14},{10,12},{12,10},{14,8},{16,22},{18,... | collective-permute-start | bytes 331784 | tf_op jit(solution)/shard_map/ppermute | solution.py:32
  483.0 95.5 %collective-permute-start.32 = (bf16[256,1536]{1,0:T(8,128)(2,1)}, bf16[256,1536]{1,0:T(8,128)(2,1)S(1)}, u32[]{:S(2)}, u32[]{:S(2)}) collective-permute-start(bf16[256,1536]{1,0:T(8,128)(2,1)} %dynamic-slice_convert_fusion), channel_id=1, source_target_pairs={{0,1},{1,0},{2,3},{3,2},{4,5},{5,4},{6,7},{7,6},{8,9},{9,8},{10,11... | collective-permute-start | bytes 2359304 | tf_op jit(solution)/shard_map/ppermute | solution.py:32
  508.9 22.6 %collective-permute-start.36 = (f32[18,1536]{1,0:T(8,128)S(1)}, f32[18,1536]{1,0:T(8,128)S(1)}, u32[]{:S(2)}, u32[]{:S(2)}) collective-permute-start(f32[18,1536]{1,0:T(8,128)S(1)} %add_add_fusion.2), channel_id=1, source_target_pairs={{0,8},{2,10},{4,12},{6,14},{8,0},{10,2},{12,4},{14,6},{16,24},{18,... | collective-permute-start | bytes 331784 | tf_op jit(solution)/shard_map/ppermute | solution.py:32
  509.6 47.3 %collective-permute-start.37 = (f32[18,1536]{1,0:T(8,128)S(1)}, f32[18,1536]{1,0:T(8,128)S(1)}, u32[]{:S(2)}, u32[]{:S(2)}) collective-permute-start(f32[18,1536]{1,0:T(8,128)S(1)} %add_add_fusion.2), channel_id=1, source_target_pairs={{0,16},{2,18},{4,20},{6,22},{8,24},{10,26},{12,28},{14,30},{16,0},... | collective-permute-start | bytes 331784 | tf_op jit(solution)/shard_map/ppermute | solution.py:32
  511.7 45.2 %collective-permute-start.38 = (f32[18,1536]{1,0:T(8,128)S(1)}, f32[18,1536]{1,0:T(8,128)S(1)}, u32[]{:S(2)}, u32[]{:S(2)}) collective-permute-start(f32[18,1536]{1,0:T(8,128)S(1)} %add_add_fusion.2), channel_id=1, source_target_pairs={{0,24},{2,26},{4,28},{6,30},{8,16},{10,18},{12,20},{14,22},{16,8},... | collective-permute-start | bytes 331784 | tf_op jit(solution)/shard_map/ppermute | solution.py:32
  556.9 20.3 %collective-permute-start.39 = (f32[18,1536]{1,0:T(8,128)S(1)}, f32[18,1536]{1,0:T(8,128)S(1)}, u32[]{:S(2)}, u32[]{:S(2)}) collective-permute-start(f32[18,1536]{1,0:T(8,128)S(1)} %add_add_fusion.1), channel_id=1, source_target_pairs={{0,1},{1,0},{2,3},{3,2},{4,5},{5,4},{6,7},{7,6},{8,9},{9,8},{10,11... | collective-permute-start | bytes 331784 | tf_op jit(solution)/shard_map/ppermute | solution.py:32
  558.5 20.0 %copy-start.29 = (f32[512,1536]{1,0:T(8,128)S(1)}, f32[512,1536]{1,0:T(8,128)}, u32[]{:S(2)}) copy-start(f32[512,1536]{1,0:T(8,128)} %convert_element_type.103) | copy-start | bytes 9437188
  558.5 20.0 %copy-start.43 = (f32[1536]{0:T(1024)S(1)}, f32[1536]{0:T(1024)}, u32[]{:S(2)}) copy-start(f32[1536]{0:T(1024)} %param.15) | copy-start | bytes 18436
  558.5 20.0 %copy-start.51 = (f32[256]{0:T(256)S(1)}, f32[256]{0:T(256)}, u32[]{:S(2)}) copy-start(f32[256]{0:T(256)} %dynamic-slice.3) | copy-start | bytes 3076
  (39 other events, 87.4 us)

commit v4 on v3

--- a/solution.py
+++ b/solution.py
@@ -53,17 +53,21 @@
     return factor * (inner - unit * jnp.mean(unit * inner, axis=-1, keepdims=True))
 
 
-def total(x):
-    for axis in ("dp", "tensor"):
-        bits = bits_of(lax.axis_size(axis))
-        while bits:
-            one, *bits = bits
-            if bits:
-                two, *bits = bits
-                far, both = across(x, axis, two), across(x, axis, one | two)
-                x = (x + across(x, axis, one)) + (far + both)
-            else:
-                x = x + across(x, axis, one)
+def total(x, axis):
+    bits = bits_of(lax.axis_size(axis))
+
+    def met(low, bit):
+        return across(low, axis, bit).astype(F32)
+
+    while bits:
+        one, *bits = bits
+        low = x.astype(BF)
+        if bits:
+            two, *bits = bits
+            far, both = met(low, two), met(low, one | two)
+            x = (low.astype(F32) + met(low, one)) + (far + both)
+        else:
+            x = low.astype(F32) + met(low, one)
     return x
 
 
@@ -108,13 +112,14 @@
     return [x[:, s * size : (s + 1) * size] for s in range(count)]
 
 
-def scatter_rows(keep, send, later):
+def pair_sum(keep, send):
+    return keep + across(send, "dp", 1)
+
+
+def send_rows(x):
     n = lax.axis_size("dp")
-    x = keep + across(send, "dp", 1)
-    x, later = after(x, later)
     groups = [list(range(first, n, 2)) for first in range(2)]
-    x = lax.all_to_all(x, "dp", 0, 0, tiled=True, axis_index_groups=groups)
-    return jnp.sum(x.astype(F32), axis=0), later
+    return lax.all_to_all(x, "dp", 0, 0, tiled=True, axis_index_groups=groups)
 
 
 def project_kernel(lines, q_cols, at, x_ref, gain_ref, wq_ref, wk_ref, wv_ref, normed_ref, *rest):
@@ -306,16 +311,16 @@
 
 
 def attend_back_kernel(heads, rows, lines, stride, meta, *refs):
-    q_refs, g_refs, kv_refs = refs[:lines], refs[lines : 2 * lines], refs[2 * lines : 2 * lines + stride]
-    raw_ref, log_ref, start_ref = refs[2 * lines + stride : 2 * lines + stride + 3]
-    outs = refs[2 * lines + stride + 3 :]
+    q_refs, g_ref, kv_refs = refs[:lines], refs[lines], refs[lines + 1 : lines + 1 + stride]
+    raw_ref, log_ref, start_ref = refs[lines + 1 + stride : lines + stride + 4]
+    outs = refs[lines + stride + 4 :]
     dq_refs, (keep_ref, send_ref, q_s, g_s, kv_s, dq_s, dkv_s, delta_s) = outs[:lines], outs[lines:]
     slot, place, own, low, clear = position(meta, lines)
 
     @pl.when(slot == 0)
     def _():
         spread_heads(q_refs, q_s, heads, False)
-        spread_heads(g_refs, g_s, heads, True)
+        spread_heads([g_ref.at[s ^ (place // stride)] for s in range(lines)], g_s, heads, True)
         gather_blocks(kv_refs, kv_s, lines)
         dkv_s[...] = jnp.zeros_like(dkv_s)
 
@@ -370,7 +375,8 @@
         grid_spec=pltpu.PrefetchScalarGridSpec(
             num_scalar_prefetch=1,
             grid=(lines,),
-            in_specs=[narrow] * (2 * lines)
+            in_specs=[narrow] * lines
+            + [whole_block((lines, rows, q_cols))]
             + [whole_block((lines, rows, PAIR))] * stride
             + [
                 pl.BlockSpec((1, heads, rows, PAIR), lambda i, m: (i, 0, 0, 0)),
@@ -394,7 +400,7 @@
             flops=36 * 10 * rows * rows * PAIR * 2, bytes_accessed=10 << 20, transcendentals=36 * rows * rows
         ),
         name="attend_back",
-    )(meta, *q, *g, *kv, raw, logs, start_row)
+    )(meta, *q, g, *kv, raw, logs, start_row)
 
 
 def experts_kernel(x_ref, g_ref, gate_ref, wg_ref, wu_ref, wd_ref, out_ref, back_ref, inner_ref):
@@ -455,45 +461,40 @@
     )(x, g, gate, w_gate, w_up, w_down)
 
 
-def weights_kernel(dp, at, a_ref, b_ref, c_ref, d_ref, keep_ref, send_ref):
+def weights_kernel(dp, at, a_ref, b_ref, keep_ref, send_ref):
     size = a_ref.shape[1] // dp
     chunk = 4
-    split = b_ref.shape[1]
     odd = at[0] != 0
     for part in range(dp // chunk):
         span = slice(part * chunk * size, (part + 1) * chunk * size)
-        for left, right, lanes in (
-            (a_ref, b_ref, slice(0, split)),
-            (c_ref, d_ref, slice(split, split + d_ref.shape[1])),
-        ):
-            block = dot(left[:, span], right[...], TN).astype(BF)
-            for pair in range(chunk // 2):
-                one = block[2 * pair * size : (2 * pair + 1) * size]
-                two = block[(2 * pair + 1) * size : (2 * pair + 2) * size]
-                at_pair = part * (chunk // 2) + pair
-                keep_ref[at_pair, :, lanes] = jnp.where(odd, two, one)
-                send_ref[at_pair, :, lanes] = jnp.where(odd, one, two)
-
-
-def weight_parts(bit, a, b, c, d, dp):
+        block = dot(a_ref[:, span], b_ref[...], TN).astype(BF)
+        for pair in range(chunk // 2):
+            one = block[2 * pair * size : (2 * pair + 1) * size]
+            two = block[(2 * pair + 1) * size : (2 * pair + 2) * size]
+            at_pair = part * (chunk // 2) + pair
+            keep_ref[at_pair] = jnp.where(odd, two, one)
+            send_ref[at_pair] = jnp.where(odd, one, two)
+
+
+def weight_parts(bit, a, b, dp):
     rows, width = a.shape
-    columns = b.shape[1] + d.shape[1]
+    columns = b.shape[1]
     out = (dp // 2, width // dp, columns)
     return pl.pallas_call(
         functools.partial(weights_kernel, dp),
         grid_spec=pltpu.PrefetchScalarGridSpec(
             num_scalar_prefetch=1,
             grid=(1,),
-            in_specs=[whole_block(x.shape) for x in (a, b, c, d)],
+            in_specs=[whole_block(x.shape) for x in (a, b)],
             out_specs=[whole_block(out)] * 2,
         ),
         out_shape=[jax.ShapeDtypeStruct(out, BF)] * 2,
         compiler_params=pltpu.CompilerParams(vmem_limit_bytes=48 * 1024 * 1024),
         cost_estimate=pl.CostEstimate(
-            flops=2 * rows * width * columns, bytes_accessed=12 << 20, transcendentals=0
+            flops=2 * rows * width * columns, bytes_accessed=8 << 20, transcendentals=0
         ),
         name="weights",
-    )(bit[None], a, b, c, d)
+    )(bit[None], a, b)
 
 
 def flat(x):
@@ -674,6 +675,7 @@
     factor_two = norm_factor(hidden)
     unit_two = hidden * factor_two
     normed_mid = gather_tensor((unit_two * norm2_gain).astype(BF), 0)
+    normed_mid, g_second = after(normed_mid, g_second)
 
     logits = dot(normed_mid, router)
     peak = jnp.max(jnp.where(named, logits, -jnp.inf), axis=1, keepdims=True)
@@ -682,20 +684,19 @@
     slot_gate = jnp.sum(jnp.where(in_slot, gates.T[:, None, :], 0.0), axis=-1)
 
     x_slots = to_experts(normed_mid)
-    x_mine = lax.dynamic_slice_in_dim(x_slots, first_col, cols, 2)
-    x_early, x_late = x_mine[..., : cols // 2], x_mine[..., cols // 2 :]
-    x_early, g_second = after(x_early, g_second)
-    x_first = to_owner(x_early)
     gate_high = lax.reduce_precision(slot_gate, 8, 7)
     gate_mid = lax.reduce_precision(slot_gate - gate_high, 8, 7)
     gate_pieces = jnp.stack([gate_high, gate_mid, slot_gate - gate_high - gate_mid], 2)
-    g_first, x_slots = after(g_first, x_slots)
-    g_first = swap_tensor(g_first, 2)
+    x_mine = lax.dynamic_slice_in_dim(x_slots, first_col, cols, 2)
+    early = cols // 2
+    x_late = x_mine[..., early:]
+    x_first = to_owner(x_mine[..., :early])
+    g_owned = swap_tensor(jnp.concatenate([g_first, g_second], 2), 2)
 
     out_slots, back_slots, inner_slots = run_experts(
         x_slots, g_slots, slot_gate[:, :, None], w_gate, w_up, w_down
     )
-    back_slots, (x_first, g_first) = after(back_slots, (x_first, g_first))
+    back_slots, (x_first, g_owned) = after(back_slots, (x_first, g_owned))
     moe_part = dot(from_slots, out_slots.reshape(experts * CAP, width))
     grad_gates = jnp.sum(
         jnp.where(
@@ -712,57 +713,53 @@
     (x_late, gate_pieces, router_part), grad_mid_part = after(
         (x_late, gate_pieces, (grad_logits, normed_mid)), grad_mid_part
     )
+    x_second = to_owner(
+        jnp.concatenate([x_late, jnp.pad(gate_pieces.astype(BF), ((0, 0), (0, 0), (0, 125)))], 2)
+    )
     router_part = lax.dot_general(
         router_part[0], router_part[1].astype(F32), TN, precision=HIGH, preferred_element_type=F32
     )
-    x_late = jnp.concatenate(
-        [x_late, jnp.pad(gate_pieces.astype(BF), ((0, 0), (0, 0), (0, 125)))], 2
-    )
-    x_second = to_owner(x_late)
     grad_mid, moe_part = after(scatter_tensor(grad_mid_part), moe_part)
     gain_two_part = jnp.sum(grad_mid * unit_two, axis=0)
     grad_rows = lax.dynamic_slice_in_dim(out_grad, first, part, 0).astype(F32)
     grad_hidden = grad_rows + norm_back(unit_two, factor_two, norm2_gain, grad_mid)
     hidden_low = gather_tensor(grad_hidden.astype(BF), 0)
-    (x_first, x_second, g_second), hidden_low = after((x_first, x_second, g_second), hidden_low)
-    g_second = swap_tensor(g_second, 2)
-    gate_owned = jnp.sum(x_second[..., cols // 2 : cols // 2 + 3].astype(F32), axis=2)
-    x_owned = swap_tensor(jnp.concatenate([x_first, x_second[..., : cols // 2]], 2), 2)
     grad_mixed = dot(hidden_low, w_out, NT).astype(BF)
-    g = to_lines(xor_blocks(columns_of(grad_mixed, lines), line))
+    g = jnp.stack(columns_of(grad_mixed, lines))
+    g, (x_first, x_second, hidden_late) = after(g, (x_first, x_second, hidden_low))
+    if lines > 1:
+        groups = [[first_of + j * stride for j in range(lines)] for first_of in range(stride)]
+        g = lax.all_to_all(g, "dp", 0, 0, tiled=True, axis_index_groups=groups)
+    gate_owned = jnp.sum(x_second[..., cols - early : cols - early + 3].astype(F32), axis=2)
+    x_owned = swap_tensor(jnp.concatenate([x_first, x_second[..., : cols - early]], 2), 2)
+    proj_part = dot(hidden_late, mixed, TN).astype(BF).reshape(dp // 2, 2, width // dp, -1)
+    proj_keep, proj_send = (
+        lax.dynamic_index_in_dim(proj_part, (place & 1) ^ other, 1, keepdims=False)
+        for other in (0, 1)
+    )
+    proj_got = send_rows(pair_sum(proj_keep, proj_send))
     *dq_far, keep, send = attend_back(meta, q, g, kv, raw, logs, starts[:, None, :], group)
 
     dkv = (keep + across(send, "dp", 1)).reshape(stride // 2, lines, rows, PAIR)
-    dkv, dq_far = after(dkv, dq_far)
+    dkv, dq_far, proj_got = lax.optimization_barrier((dkv, dq_far, proj_got))
+    proj_out = jnp.sum(proj_got.astype(F32), axis=0).T
     for bit in bits_of(stride)[1:]:
         view = dkv.reshape((dkv.shape[0] // 2, 2) + dkv.shape[1:])
         dkv = view[:, 0] + across(view[:, 1], "dp", bit)
-    dkv, (moe_part, x_owned) = after(dkv[0], (moe_part, x_owned))
+    dkv, (moe_part, x_owned, g_owned) = after(dkv[0], (moe_part, x_owned, g_owned))
     dq = from_lines(dq_far)
-    moe_rows = scatter_tensor(moe_part)
     dkv = from_lines([dkv[s] for s in range(lines)])
-    w_all = jnp.concatenate([w_query, w_key, w_value], 1)
-    dqkv = jnp.concatenate(dq + [b[:, :HD] for b in dkv] + [b[:, HD:] for b in dkv], 1)
-    dqkv, x_owned, g_second = lax.optimization_barrier((dqkv, x_owned, g_second))
-    weight_keep, weight_send = weight_parts(place & 1, normed_in, dqkv, hidden_low, mixed, dp)
-    dqkv, weight_keep, weight_send = lax.optimization_barrier((dqkv, weight_keep, weight_send))
     def mine(x, e):
         return x.reshape((dp, held, CAP) + x.shape[2:])[:, e]
 
-    def pieces_of(parts, offset):
-        return [(parts[0], first_col + offset), (parts[1], cols - first_col + offset)]
-
-    def owner_work(given):
-        x_parts, g_parts = given
-        size = cols // 2
+    def pieces_of(parts):
+        return [(parts[0], first_col), (parts[1], cols - first_col)]
+
+    def owner_work(x_parts, g_parts):
         if tensor_size == 2:
-            x = pieces_of(x_parts, 0)
-            g = pieces_of(g_first, 0) + pieces_of(g_parts, size)
+            x, g = pieces_of(x_parts), pieces_of(g_parts)
         else:
-            x = [(assemble(x_parts, 2), 0)]
-            both = [assemble(g_first, 2), assemble(g_parts, 2)]
-            order = [each[..., t * size : (t + 1) * size] for t in range(tensor_size) for each in both]
-            g = [(jnp.concatenate(order, 2), 0)]
+            x, g = [(assemble(x_parts, 2), 0)], [(assemble(g_parts, 2), 0)]
         results = []
         for e in range(held):
             at = jnp.stack([jnp.int32(place * held + e)] + [jnp.int32(o) for _, o in x + g])
@@ -793,28 +790,36 @@
         ]
         return [jnp.concatenate(each, 0) for each in zip(*grad_outs)]
 
-    weight_grad, (owner_given, dqkv, small) = scatter_rows(
-        weight_keep, weight_send, ((x_owned, g_second), dqkv, (router_part, gain_two_part))
-    )
-    grad_in_part = dot(dqkv, w_all, NT)
+    owned = owner_work(x_owned, g_owned)
+    w_all = jnp.concatenate([w_query, w_key, w_value], 1)
+    dqkv = jnp.concatenate(dq + [b[:, :HD] for b in dkv] + [b[:, HD:] for b in dkv], 1)
     in_float = layer_in.astype(F32)
     factor_one = norm_factor(in_float)
-    gain_one_part = jnp.sum(grad_in_part * (in_float * factor_one), axis=0)
-    small = total(jnp.concatenate([small[0], small[1][None], gain_one_part[None]], 0))
-    gate_out, up_out, down_out = owner_grads(owner_work(owner_given))
-    grad_in_rows = scatter_tensor(grad_in_part)
+    unit_one = in_float * factor_one
+    dqkv, (owned, moe_rows, unit_one) = after(dqkv, (owned, scatter_tensor(moe_part), unit_one))
+    grad_in_part = dot(dqkv, w_all, NT)
+    gain_one_part = jnp.sum(grad_in_part * unit_one, axis=0)
+    small = jnp.concatenate([router_part, gain_two_part[None], gain_one_part[None]], 0)
+    small = total(small.reshape(-1, 128), "dp")
+    weight_keep, weight_send = weight_parts(place & 1, normed_in, dqkv, dp)
+    weight_pair, (owned, small, grad_in_part) = after(
+        pair_sum(weight_keep, weight_send), (owned, small, grad_in_part)
+    )
+    small = total(small, "tensor")
+    (gate_out, up_out, down_out), small, weight_got, grad_in_rows = lax.optimization_barrier(
+        (owner_grads(owned), small, send_rows(weight_pair), scatter_tensor(grad_in_part))
+    )
+    weight_grad = jnp.sum(weight_got.astype(F32), axis=0)
     layer_out = (hidden + moe_rows).astype(BF)
     ends = [0]
-    for size in (lines * q_cols, lines * HD, lines * HD, lines * q_cols):
+    for size in (lines * q_cols, lines * HD, lines * HD):
         ends.append(ends[-1] + size)
-    query_out, key_out, value_out, proj_out = (
-        weight_grad[:, a:b] for a, b in zip(ends[:-1], ends[1:])
-    )
-    proj_out = proj_out.T
+    query_out, key_out, value_out = (weight_grad[:, a:b] for a, b in zip(ends[:-1], ends[1:]))
 
     factor_rows = lax.dynamic_slice_in_dim(factor_one, first, part, 0)
     unit_rows = lax.dynamic_slice_in_dim(in_float, first, part, 0) * factor_rows
     input_grad = grad_hidden + norm_back(unit_rows, factor_rows, norm1_gain, grad_in_rows)
+    small = small.reshape(-1, width)
     gain_one_grad = small[experts + 1]
     gain_two_grad = small[experts]
     router_grad = small[:experts].T

time: 598 us -> 559 us (0.935)
  waiting for transfers between devices: 170 us -> 116 us
  other arithmetic: 49 us -> 61 us
  local copies, waits for them, and re-layouts: 44.3 us -> 51.4 us
    ppermute x40 -> x37, waiting for transfers between devices: 157 us -> 78.6 us  [across(): return lax.ppermute(x, axis, [(i, i ^ mask) for i in range(n)])]
    ppermute x40 -> x37, starting transfers between devices: 80.3 us -> 49.2 us  [across(): return lax.ppermute(x, axis, [(i, i ^ mask) for i in range(n)])]
    all_to_all x1 -> x3, waiting for transfers between devices: 0.01 us -> 26 us  [the longest x2 13.5 us: send_rows(): return lax.all_to_all(x, 'dp', 0, 0, tiled=True, axis_index_groups=groups)]
    all_to_all x4, starting transfers between devices: 26.4 us -> 43 us  [to_owner(): return lax.all_to_all(x, 'dp', 0, 0, tiled=True)]
    all_to_all x1 -> x3, starting transfers between devices: 4.95 us -> 17.4 us  [the longest x1 9.87 us: shards(): g = lax.all_to_all(g, 'dp', 0, 0, tiled=True, axis_index_groups=groups)]
    unnamed x116 -> x125, local copies, waits for them, and re-layouts: 19.4 us -> 16.4 us
  transfers between devices with their start and end apart: 45 -> 44, of which waited for: 21 -> 18; matrix products, arithmetic and copies ran while one was open for 17% -> 20% of each run, Pallas kernels for 25% -> 28%
where the time goes in v4:
time: 559 us; the launch traced here: 551 us
  Pallas kernels  162 us (29%)
  waiting for transfers between devices  116 us (21%)
  starting transfers between devices  110 us (20%)
  other arithmetic  61 us (11%)
  local copies, waits for them, and re-layouts  51.4 us (9%)
  matrix products  45.8 us (8%)
    ppermute x37, waiting for transfers between devices, across(): return lax.ppermute(x, axis, [(i, i ^ mask) for i in range(n)])  78.6 us
    ppermute x37, starting transfers between devices, across(): return lax.ppermute(x, axis, [(i, i ^ mask) for i in range(n)])  49.2 us
    all_to_all x4, starting transfers between devices, to_owner(): return lax.all_to_all(x, 'dp', 0, 0, tiled=True)  43 us
    pallas_call x1, Pallas kernels, attend_back(): pl.pallas_call(functools.partial(attend_back_kernel, heads, rows, lines,...  42.7 us
    pallas_call x1, Pallas kernels, run_experts(): pl.pallas_call(experts_kernel, grid=(experts // at_once,), in_specs=[of(c...  42.4 us
    pallas_call x2, Pallas kernels, owner_call(): pl.pallas_call(functools.partial(kernel, len(x), len(g)), grid_spec=pltpu...  35.7 us
    dot_general x9, matrix products, dot(): return jnp.dot(a, b, preferred_element_type=F32)  35.3 us
    pallas_call x1, Pallas kernels, attend(): pl.pallas_call(functools.partial(attend_kernel, heads, rows, lines, strid...  32.3 us
  transfers between devices with their start and end apart: 44, of which 18 were waited for; matrix products, arithmetic and copies ran while one was open for 20% of the time, Pallas kernels for 28%

profile of v4, /device:TPU:0, one launch (start us, length us, event | category | flops | bytes accessed | tf_op | source)
XLA Modules:
  0.0 550.9 jit_solution(15473998116833918684)
XLA Ops:
  3.8 5.7 %project.1 = (bf16[512,1536]{1,0:T(8,128)(2,1)S(1)}, bf16[512,128]{1,0:T(8,128)(2,1)S(1)}, bf16[512,128]{1,0:T(8,128)(2,1)S(1)}, bf16[512,128]{1,0:T(8,128)(2,1)...) custom-call(s32[1]{0:T(128)} %bitcast.6.at, ...), custom_call_target="tpu_custom_call" | custom-call | flops 2013265920 | bytes 8388608 | tf_op jit(solution)/shard_map/project/pallas_call | solution.py:152
  11.3 5.0 collective-permute-start.2
  18.4 2.9 collective-permute-start.7
  25.6 3.0 collective-permute-done.1
  32.5 9.3 %collective-permute-done.4.refs_6_.refs_7_ = bf16[4,512,128]{2,1,0:T(8,128)(2,1)} collective-permute-done((bf16[4,512,128]{2,1,0:T(8,128)(2,1)S(1)}, bf16[4,512,128]{2,1,0:T(8,128)(2,1)}, u32[]{:S(2)}, u32[]{:S(2)}) %collective-permute-start.4) | collective-permute-done | bytes 524320 | tf_op jit(solution)/shard_map/ppermute | solution.py:32
  42.0 3.4 convolution_convert_fusion.3
  45.5 3.7 convolution_convert_fusion.4
  49.3 5.0 all-to-all-start
  55.3 32.3 %attend.1 = (bf16[512,192]{1,0:T(8,128)(2,1)S(1)}, bf16[512,192]{1,0:T(8,128)(2,1)S(1)}, bf16[512,192]{1,0:T(8,128)(2,1)S(1)}, bf16[512,192]{1,0:T(8,128)(2,1)S(...) custom-call(s32[13]{0:T(128)S(1)} %pad_add_fusion.1.meta, bf16[512,192]{1,0:T(8,128)(2,1)S(1)} %copy-done.16, ...), custom_call_target="tpu_custom_call" | custom-call | flops 9663676416 | bytes 8388608 | tf_op jit(solution)/shard_map/attend/pallas_call | solution.py:279
  90.3 3.3 collective-permute-start.10
  95.0 7.8 %convolution_convert_fusion.1 = bf16[2048,1536]{1,0:T(8,128)(2,1)} fusion(pred[2048,512]{1,0:T(32,128)(4,1)} %copy-done.34, bf16[512,1536]{1,0:T(8,128)(2,1)} %param.27), kind=kOutput, calls=%fused_computation.1 | convolution fusion | flops 3224371200 | bytes 8912896 | tf_op jit(solution)/shard_map/dot_general | solution.py:26
  103.5 2.0 collective-permute-done.9
  111.6 15.6 %all-to-all-start.1 = ((bf16[16,128,384]{2,1,0:T(8,128)(2,1)}), bf16[16,128,384]{2,1,0:T(8,128)(2,1)}, u32[]{:S(2)}, u32[]{:S(2)}) async-start(bf16[16,128,384]{2,1,0:T(8,128)(2,1)} %bitcast.127), calls=%async_computation.1 | async-start | bytes 3145728 | tf_op jit(solution)/shard_map/all_to_all | solution.py:44
  127.3 3.3 multiply_reduce_fusion.5
  130.6 2.5 multiply_convert_fusion
  134.2 2.9 constant_dynamic-update-slice_fusion.1
  137.1 13.4 %collective-permute-done.13 = bf16[256,1536]{1,0:T(8,128)(2,1)S(1)} collective-permute-done((bf16[256,1536]{1,0:T(8,128)(2,1)}, bf16[256,1536]{1,0:T(8,128)(2,1)S(1)}, u32[]{:S(2)}, u32[]{:S(2)}) %collective-permute-start.13) | collective-permute-done | bytes 786464 | tf_op jit(solution)/shard_map/ppermute | solution.py:32
  153.6 5.7 %all-to-all-done.1 = bf16[16,128,384]{2,1,0:T(8,128)(2,1)} async-done(((bf16[16,128,384]{2,1,0:T(8,128)(2,1)}), bf16[16,128,384]{2,1,0:T(8,128)(2,1)}, u32[]{:S(2)}, u32[]{:S(2)}) %all-to-all-start.1) | async-done | bytes 1572896 | tf_op jit(solution)/shard_map/all_to_all | solution.py:44
  159.3 3.0 constant_dynamic-update-slice_fusion.refs_2_
  162.8 5.4 convolution_convert_fusion
  170.6 4.1 constant_dynamic-slice_fusion
  174.7 15.4 %all-to-all-start.2 = ((bf16[16,128,384]{2,1,0:T(8,128)(2,1)}), bf16[16,128,384]{2,1,0:T(8,128)(2,1)}, u32[]{:S(2)}, u32[]{:S(2)}) async-start(bf16[16,128,384]{2,1,0:T(8,128)(2,1)} %get-tuple-element.240), calls=%async_computation.2 | async-start | bytes 3145728 | tf_op jit(solution)/shard_map/all_to_all | solution.py:44
  190.1 42.4 %experts.1 = (bf16[16,128,1536]{2,1,0:T(8,128)(2,1)}, bf16[16,128,1536]{2,1,0:T(8,128)(2,1)}, f32[16,8,128]{2,1,0:T(8,128)}) custom-call(bf16[16,128,1536]{2,1,0:T(8,128)(2,1)} %bitcast.121, bf16[16,128,1536]{2,1,0:T(8,128)(2,1)} %bitcast.122, f32[16,128,1]{2,1,0:T(8,128)} %copy.46.gate_ref, bf16[16,1536,512]{2,1,0:T(8,128)(2,1)} %wg_ref.3, ...), custom_call_target="tpu_custom_call" | custom-call | flops 19327352832 | bytes 100663296 | tf_op jit(solution)/shard_map/experts/pallas_call | solution.py:437
  233.4 2.6 select_reduce_fusion
  236.1 3.1 fusion.47
  239.2 7.3 %fusion.11 = f32[512,1536]{1,0:T(8,128)S(1)} fusion(f32[512,1536]{1,0:T(8,128)} %fusion.47, bf16[16,128,1536]{2,1,0:T(8,128)(2,1)} %get-tuple-element.159, s32[512,16]{0,1:T(8,128)S(1)} %copy-done.46), kind=kOutput, calls=%fused_computation.21 | convolution fusion | flops 3223060480 | bytes 12615680 | tf_op jit(solution)/shard_map/dot_general | solution.py:26
  249.6 4.8 fusion.10
  254.8 3.0 fusion.12
  257.8 6.9 %all-to-all-start.3 = ((bf16[16,128,512]{2,1,0:T(8,128)(2,1)}), bf16[16,128,512]{2,1,0:T(8,128)(2,1)}, u32[]{:S(2)}, u32[]{:S(2)}) async-start(bf16[16,128,512]{2,1,0:T(8,128)(2,1)} %fusion.12), calls=%async_computation.3 | async-start | bytes 4194304 | tf_op jit(solution)/shard_map/all_to_all | solution.py:44
  264.8 4.6 collective-permute-done.15
  271.3 3.1 multiply_reduce_fusion.3
  274.4 1.9 fusion.38
  276.8 18.8 %collective-permute-done.16 = bf16[256,1536]{1,0:T(8,128)(2,1)} collective-permute-done((bf16[256,1536]{1,0:T(8,128)(2,1)S(1)}, bf16[256,1536]{1,0:T(8,128)(2,1)}, u32[]{:S(2)}, u32[]{:S(2)}) %collective-permute-start.16) | collective-permute-done | bytes 786464 | tf_op jit(solution)/shard_map/ppermute | solution.py:32
  300.0 5.9 %all-to-all-done.3 = bf16[16,128,512]{2,1,0:T(8,128)(2,1)} async-done(((bf16[16,128,512]{2,1,0:T(8,128)(2,1)}), bf16[16,128,512]{2,1,0:T(8,128)(2,1)}, u32[]{:S(2)}, u32[]{:S(2)}) %all-to-all-start.3) | async-done | bytes 2097184 | tf_op jit(solution)/shard_map/all_to_all | solution.py:44
  305.9 3.0 convolution_convert_fusion.2
  312.1 9.9 %all-to-all-start.4 = ((bf16[4,512,192]{1,2,0:T(8,128)(2,1)}), bf16[4,512,192]{1,2,0:T(8,128)(2,1)S(1)}, u32[]{:S(2)}, u32[]{:S(2)}) async-start(bf16[4,512,192]{1,2,0:T(8,128)(2,1)} %copy.48), calls=%async_computation.4 | async-start | bytes 1572864 | tf_op jit(solution)/shard_map/all_to_all | solution.py:732
  323.5 3.4 pad_maximum_fusion.refs_0_
  327.8 2.4 bitcast_add_fusion
  330.2 12.5 %all-to-all-done.4 = bf16[4,512,192]{1,2,0:T(8,128)(2,1)S(1)} async-done(((bf16[4,512,192]{1,2,0:T(8,128)(2,1)}), bf16[4,512,192]{1,2,0:T(8,128)(2,1)S(1)}, u32[]{:S(2)}, u32[]{:S(2)}) %all-to-all-start.4) | async-done | bytes 786464 | tf_op jit(solution)/shard_map/all_to_all | solution.py:732
  342.7 3.6 all-to-all-start.5
  347.6 42.7 %attend_back.1 = (bf16[512,192]{1,0:T(8,128)(2,1)}, bf16[512,192]{1,0:T(8,128)(2,1)}, bf16[512,192]{1,0:T(8,128)(2,1)}, bf16[512,192]{1,0:T(8,128)(2,1)}, bf16[8...) custom-call(s32[13]{0:T(128)} %copy-done.4, bf16[512,192]{1,0:T(8,128)(2,1)} %copy-done.15, ...), custom_call_target="tpu_custom_call" | custom-call | flops 24159191040 | bytes 10485760 | tf_op jit(solution)/shard_map/attend_back/pallas_call | solution.py:373
  390.3 9.2 %collective-permute-start.17 = (bf16[8,512,128]{2,1,0:T(8,128)(2,1)}, bf16[8,512,128]{2,1,0:T(8,128)(2,1)S(1)}, u32[]{:S(2)}, u32[]{:S(2)}) collective-permute-start(bf16[8,512,128]{2,1,0:T(8,128)(2,1)} %get-tuple-element.170), channel_id=1, source_target_pairs={{0,2},{2,0},{4,6},{6,4},{8,10},{10,8},{12,14},{14,12},{16,18},{18,... | collective-permute-start | bytes 3145736 | tf_op jit(solution)/shard_map/ppermute | solution.py:32
  399.8 2.1 collective-permute-done.17
  403.2 2.2 slice_bitcast_fusion
  405.4 3.5 collective-permute-start.19
  409.8 1.9 broadcast_multiply_fusion
  416.7 15.5 %collective-permute-done.20 = bf16[512,192]{1,0:T(8,128)(2,1)} collective-permute-done((bf16[512,192]{1,0:T(8,128)(2,1)}, bf16[512,192]{1,0:T(8,128)(2,1)}, u32[]{:S(2)}, u32[]{:S(2)}) %collective-permute-start.20) | collective-permute-done | bytes 196640 | tf_op jit(solution)/shard_map/ppermute | solution.py:32
  436.1 2.4 collective-permute-start.24
  438.5 2.0 collective-permute-start.26
  440.5 16.8 %owner_forward.1 = (bf16[2048,512]{1,0:T(8,128)(2,1)}, bf16[2048,512]{1,0:T(8,128)(2,1)}, bf16[2048,512]{1,0:T(8,128)(2,1)}) custom-call(s32[5]{0:T(128)} %stack.81.at, f32[2048,1]{1,0:T(8,128)} %copy.50.gate_ref, bf16[16,1536,512]{2,1,0:T(8,128)(2,1)} %wg_ref.3, bf16[16,1536,512]{2,1,0:T(8,128)(2,1)} %wu_ref.3, bf16[16,512,1536]{2,1,0:T(8,128)(2,1)} %wd_ref.3, ...), custom_call_target="tpu_custom_call" | custom-call | flops 10737418240 | bytes 25165824 | tf_op jit(solution)/shard_map/owner_forward/pallas_call | solution.py:565
  459.1 2.5 concatenate.38.b_ref
  461.6 3.1 convert_add_fusion.1
  464.7 3.5 weights.1
  469.6 2.2 fusion.3
  475.7 2.4 collective-permute-done.30
  479.6 2.9 collective-permute-start.33
  486.2 2.3 collective-permute-done.34
  489.1 3.3 add.177
  492.5 4.0 all-to-all-start.6
  497.8 2.1 convert_element_type.150
  505.9 18.9 %owner_grads.1 = (f32[1,1536,512]{2,1,0:T(8,128)}, f32[1,1536,512]{2,1,0:T(8,128)}, f32[1,512,1536]{2,1,0:T(8,128)}) custom-call(s32[5]{0:T(128)} %stack.81.at, f32[2048,1]{1,0:T(8,128)} %copy.51.gate_ref, bf16[2048,512]{1,0:T(8,128)(2,1)} %get-tuple-element.214.act_ref, bf16[2048,512]{1,0:T(8,128)(2,1)} %get-tuple-element.215.grad_gate_ref, ...), custom_call_target="tpu_custom_call" | custom-call | flops 10737418240 | bytes 25165824 | tf_op jit(solution)/shard_map/owner_grads/pallas_call | solution.py:565
  525.5 1.8 convert_add_fusion
  527.3 13.5 %all-to-all-done.6 = bf16[8,96,1280]{2,1,0:T(8,128)(2,1)S(1)} async-done(((bf16[8,96,1280]{2,1,0:T(8,128)(2,1)}), bf16[8,96,1280]{2,1,0:T(8,128)(2,1)S(1)}, u32[]{:S(2)}, u32[]{:S(2)}) %all-to-all-start.6) | async-done | bytes 1966112 | tf_op jit(solution)/shard_map/all_to_all | solution.py:122
  544.7 5.8 %multiply_add_fusion = (f32[256,1536]{1,0:T(8,128)}, bf16[256,1536]{1,0:T(8,128)(2,1)}) fusion(f32[256,1536]{1,0:T(8,128)} %copy-done.23, f32[512,1536]{1,0:T(8,128)} %convert_element_type.150, s32[]{:T(128)S(6)} %select_n.209, f32[256]{0:T(256)S(1)} %broadcast_multiply_fusion.1, f32[1536]{0:T(1024)S(1)} %copy-done.48, f32[256]{0:T(256)S(1)} %copy-done.58, ...), kind=kLoop, calls=%fused_computation.34 | loop fusion | flops 5898240 | bytes 11026436 | tf_op jit(solution)/shard_map/add | solution.py:821
  (265 shorter events, 85.7 us)
Async XLA Ops:
  0.6 106.3 %copy-start = (bf16[768,1536]{1,0:T(8,128)(2,1)S(1)}, bf16[768,1536]{1,0:T(8,128)(2,1)}, u32[]{:S(2)}) copy-start(bf16[768,1536]{1,0:T(8,128)(2,1)} %param.19) | copy-start | bytes 7077892
  3.8 20.8 %copy-start.59 = (s32[512,2]{0,1:T(2,128)S(1)}, s32[512,2]{0,1:T(2,128)}, u32[]{:S(2)}) copy-start(s32[512,2]{0,1:T(2,128)} %param.26) | copy-start | bytes 12292
  11.3 14.3 %collective-permute-start.2 = (bf16[512,128]{1,0:T(8,128)(2,1)S(1)}, bf16[512,128]{1,0:T(8,128)(2,1)S(1)}, u32[]{:S(2)}, u32[]{:S(2)}) collective-permute-start(bf16[512,128]{1,0:T(8,128)(2,1)S(1)} %get-tuple-element.126), channel_id=1, source_target_pairs={{0,24},{2,26},{4,28},{6,30},{8,16},{10,18},{12,20},{14,22},{16,8},... | collective-permute-start | bytes 393224 | tf_op jit(solution)/shard_map/ppermute | solution.py:32
  16.4 9.2 %collective-permute-start = (bf16[512,128]{1,0:T(8,128)(2,1)S(1)}, bf16[512,128]{1,0:T(8,128)(2,1)}, u32[]{:S(2)}, u32[]{:S(2)}) collective-permute-start(bf16[512,128]{1,0:T(8,128)(2,1)S(1)} %get-tuple-element.124), channel_id=1, source_target_pairs={{0,8},{2,10},{4,12},{6,14},{8,0},{10,2},{12,4},{14,6},{16,24},{18,... | collective-permute-start | bytes 393224 | tf_op jit(solution)/shard_map/ppermute | solution.py:32
  16.4 12.2 %collective-permute-start.1 = (bf16[512,128]{1,0:T(8,128)(2,1)S(1)}, bf16[512,128]{1,0:T(8,128)(2,1)}, u32[]{:S(2)}, u32[]{:S(2)}) collective-permute-start(bf16[512,128]{1,0:T(8,128)(2,1)S(1)} %get-tuple-element.125), channel_id=1, source_target_pairs={{0,16},{2,18},{4,20},{6,22},{8,24},{10,26},{12,28},{14,30},{16,0},... | collective-permute-start | bytes 393224 | tf_op jit(solution)/shard_map/ppermute | solution.py:32
  17.0 32.3 %collective-permute-start.6 = (bf16[512,192]{1,0:T(8,128)(2,1)}, bf16[512,192]{1,0:T(8,128)(2,1)S(1)}, u32[]{:S(2)}, u32[]{:S(2)}) collective-permute-start(bf16[512,192]{1,0:T(8,128)(2,1)} %get-tuple-element.128), channel_id=1, source_target_pairs={{0,8},{2,10},{4,12},{6,14},{8,0},{10,2},{12,4},{14,6},{16,24},{18,... | collective-permute-start | bytes 589832 | tf_op jit(solution)/shard_map/ppermute | solution.py:32
  18.4 30.8 %collective-permute-start.7 = (bf16[512,192]{1,0:T(8,128)(2,1)}, bf16[512,192]{1,0:T(8,128)(2,1)}, u32[]{:S(2)}, u32[]{:S(2)}) collective-permute-start(bf16[512,192]{1,0:T(8,128)(2,1)} %get-tuple-element.129), channel_id=1, source_target_pairs={{0,16},{2,18},{4,20},{6,22},{8,24},{10,26},{12,28},{14,30},{16,0},... | collective-permute-start | bytes 589832 | tf_op jit(solution)/shard_map/ppermute | solution.py:32
  23.9 8.2 %copy-start.49 = (s32[8192]{0:T(1024)S(1)}, s32[8192]{0:T(1024)}, u32[]{:S(2)}) copy-start(s32[8192]{0:T(1024)} %param.25) | copy-start | bytes 98308
  25.6 23.6 %collective-permute-start.8 = (bf16[512,192]{1,0:T(8,128)(2,1)}, bf16[512,192]{1,0:T(8,128)(2,1)}, u32[]{:S(2)}, u32[]{:S(2)}) collective-permute-start(bf16[512,192]{1,0:T(8,128)(2,1)} %get-tuple-element.130), channel_id=1, source_target_pairs={{0,24},{2,26},{4,28},{6,30},{8,16},{10,18},{12,20},{14,22},{16,8},... | collective-permute-start | bytes 589832 | tf_op jit(solution)/shard_map/ppermute | solution.py:32
  29.7 24.5 %copy-start.2 = (bf16[4,512,128]{2,1,0:T(8,128)(2,1)}, bf16[4,512,128]{2,1,0:T(8,128)(2,1)S(1)}, u32[]{:S(2)}) copy-start(bf16[4,512,128]{2,1,0:T(8,128)(2,1)S(1)} %pad_maximum_fusion.5.refs_4_.refs_5_) | copy-start | bytes 1572868
  29.7 12.1 %collective-permute-start.4 = (bf16[4,512,128]{2,1,0:T(8,128)(2,1)S(1)}, bf16[4,512,128]{2,1,0:T(8,128)(2,1)}, u32[]{:S(2)}, u32[]{:S(2)}) collective-permute-start(bf16[4,512,128]{2,1,0:T(8,128)(2,1)S(1)} %pad_maximum_fusion.5.refs_4_.refs_5_), channel_id=1, source_target_pairs={{0,4},{2,6},{4,0},{6,2},{8,12},{10,14},{12,8},{14,10},{16,20},{18,... | collective-permute-start | bytes 1572872 | tf_op jit(solution)/shard_map/ppermute | solution.py:32
  32.1 13.4 %copy-start.34 = (pred[2048,512]{1,0:T(32,128)(4,1)}, pred[2048,512]{1,0:T(32,128)(4,1)S(1)}, u32[]{:S(2)}) copy-start(pred[2048,512]{1,0:T(32,128)(4,1)S(1)} %bitcast_compare_fusion) | copy-start | bytes 3145732
  32.5 16.8 %collective-permute-start.3 = (bf16[4,512,128]{2,1,0:T(8,128)(2,1)S(1)}, bf16[4,512,128]{2,1,0:T(8,128)(2,1)}, u32[]{:S(2)}, u32[]{:S(2)}) collective-permute-start(bf16[4,512,128]{2,1,0:T(8,128)(2,1)S(1)} %pad_maximum_fusion.5.refs_4_.refs_5_), channel_id=1, source_target_pairs={{0,2},{2,0},{4,6},{6,4},{8,10},{10,8},{12,14},{14,12},{16,18},{18,... | collective-permute-start | bytes 1572872 | tf_op jit(solution)/shard_map/ppermute | solution.py:32
  41.8 7.4 %collective-permute-start.5 = (bf16[4,512,128]{2,1,0:T(8,128)(2,1)}, bf16[4,512,128]{2,1,0:T(8,128)(2,1)}, u32[]{:S(2)}, u32[]{:S(2)}) collective-permute-start(bf16[4,512,128]{2,1,0:T(8,128)(2,1)} %collective-permute-done.4.refs_6_.refs_7_), channel_id=1, source_target_pairs={{0,2},{2,0},{4,6},{6,4},{8,10},{10,8},{12,14},{14,12},{16,18},{18,... | collective-permute-start | bytes 1572872 | tf_op jit(solution)/shard_map/ppermute | solution.py:32
  45.5 8.8 %copy-start.4 = (s32[13]{0:T(128)}, s32[13]{0:T(128)S(1)}, u32[]{:S(2)}) copy-start(s32[13]{0:T(128)S(1)} %pad_add_fusion.1.meta) | copy-start | bytes 160
  49.3 41.0 %all-to-all-start = ((bf16[16,128,384]{2,1,0:T(8,128)(2,1)}), bf16[16,128,384]{2,1,0:T(8,128)(2,1)}, u32[]{:S(2)}, u32[]{:S(2)}) async-start(bf16[16,128,384]{2,1,0:T(8,128)(2,1)} %bitcast.128), calls=%async_computation | async-start | bytes 3145728 | tf_op jit(solution)/shard_map/all_to_all | solution.py:44
  55.3 32.3 %copy-start.3 = (s32[4,1,512]{2,1,0:T(1,128)}, s32[4,1,512]{2,1,0:T(1,128)S(1)}, u32[]{:S(2)}) copy-start(s32[4,1,512]{2,1,0:T(1,128)S(1)} %broadcast_in_dim.118.refs_8_.refs_11_) | copy-start | bytes 24580
  90.3 12.5 %collective-permute-start.10 = (bf16[512,192]{1,0:T(8,128)(2,1)}, bf16[512,192]{1,0:T(8,128)(2,1)S(1)}, u32[]{:S(2)}, u32[]{:S(2)}) collective-permute-start(bf16[512,192]{1,0:T(8,128)(2,1)} %copy-done.12), channel_id=1, source_target_pairs={{0,16},{2,18},{4,20},{6,22},{8,24},{10,26},{12,28},{14,30},{16,0},... | collective-permute-start | bytes 589832 | tf_op jit(solution)/shard_map/ppermute | solution.py:32
  93.5 9.3 %collective-permute-start.11 = (bf16[512,192]{1,0:T(8,128)(2,1)}, bf16[512,192]{1,0:T(8,128)(2,1)S(1)}, u32[]{:S(2)}, u32[]{:S(2)}) collective-permute-start(bf16[512,192]{1,0:T(8,128)(2,1)} %copy-done.11), channel_id=1, source_target_pairs={{0,8},{2,10},{4,12},{6,14},{8,0},{10,2},{12,4},{14,6},{16,24},{18,... | collective-permute-start | bytes 589832 | tf_op jit(solution)/shard_map/ppermute | solution.py:32
  94.6 10.8 %collective-permute-start.9 = (bf16[512,192]{1,0:T(8,128)(2,1)}, bf16[512,192]{1,0:T(8,128)(2,1)}, u32[]{:S(2)}, u32[]{:S(2)}) collective-permute-start(bf16[512,192]{1,0:T(8,128)(2,1)} %copy-done.10), channel_id=1, source_target_pairs={{0,24},{2,26},{4,28},{6,30},{8,16},{10,18},{12,20},{14,22},{16,8},... | collective-permute-start | bytes 589832 | tf_op jit(solution)/shard_map/ppermute | solution.py:32
  110.1 17.2 %collective-permute-start.12 = (bf16[256,1536]{1,0:T(8,128)(2,1)S(1)}, bf16[256,1536]{1,0:T(8,128)(2,1)}, u32[]{:S(2)}, u32[]{:S(2)}) collective-permute-start(bf16[256,1536]{1,0:T(8,128)(2,1)S(1)} %dynamic-slice_convert_fusion.3), channel_id=1, source_target_pairs={{0,1},{1,0},{2,3},{3,2},{4,5},{5,4},{6,7},{7,6},{8,9},{9,8},{10,11... | collective-permute-start | bytes 2359304 | tf_op jit(solution)/shard_map/ppermute | solution.py:32
  111.6 47.7 %all-to-all-start.1 = ((bf16[16,128,384]{2,1,0:T(8,128)(2,1)}), bf16[16,128,384]{2,1,0:T(8,128)(2,1)}, u32[]{:S(2)}, u32[]{:S(2)}) async-start(bf16[16,128,384]{2,1,0:T(8,128)(2,1)} %bitcast.127), calls=%async_computation.1 | async-start | bytes 3145728 | tf_op jit(solution)/shard_map/all_to_all | solution.py:44
  130.6 143.7 %copy-start.50 = (f32[256]{0:T(256)}, f32[256]{0:T(256)S(1)}, u32[]{:S(2)}) copy-start(f32[256]{0:T(256)S(1)} %add_rsqrt_fusion.1) | copy-start | bytes 3076
  133.1 17.4 %collective-permute-start.13 = (bf16[256,1536]{1,0:T(8,128)(2,1)}, bf16[256,1536]{1,0:T(8,128)(2,1)S(1)}, u32[]{:S(2)}, u32[]{:S(2)}) collective-permute-start(bf16[256,1536]{1,0:T(8,128)(2,1)} %multiply_convert_fusion), channel_id=1, source_target_pairs={{0,1},{1,0},{2,3},{3,2},{4,5},{5,4},{6,7},{7,6},{8,9},{9,8},{10,11... | collective-permute-start | bytes 2359304 | tf_op jit(solution)/shard_map/ppermute | solution.py:32
  153.6 9.2 %copy-start.35 = (pred[2048,512]{1,0:T(32,128)(4,1)S(1)}, pred[2048,512]{1,0:T(32,128)(4,1)}, u32[]{:S(2)}) copy-start(pred[2048,512]{1,0:T(32,128)(4,1)} %copy-done.34) | copy-start | bytes 3145732
  162.3 5.9 %copy-start.45 = (bf16[1536,16]{0,1:T(8,128)(2,1)S(1)}, bf16[1536,16]{0,1:T(8,128)(2,1)}, u32[]{:S(2)}) copy-start(bf16[1536,16]{0,1:T(8,128)(2,1)} %param.21) | copy-start | bytes 147460
  162.3 76.9 %collective-permute-start.14 = (bf16[16,128,768]{2,1,0:T(8,128)(2,1)}, bf16[16,128,768]{2,1,0:T(8,128)(2,1)}, u32[]{:S(2)}, u32[]{:S(2)}) collective-permute-start(bf16[16,128,768]{2,1,0:T(8,128)(2,1)} %constant_dynamic-update-slice_fusion.refs_2_), channel_id=1, source_target_pairs={{0,1},{1,0},{2,3},{3,2},{4,5},{5,4},{6,7},{7,6},{8,9},{9,8},{10,11... | collective-permute-start | bytes 9437192 | tf_op jit(solution)/shard_map/ppermute | solution.py:32
  174.7 64.5 %all-to-all-start.2 = ((bf16[16,128,384]{2,1,0:T(8,128)(2,1)}), bf16[16,128,384]{2,1,0:T(8,128)(2,1)}, u32[]{:S(2)}, u32[]{:S(2)}) async-start(bf16[16,128,384]{2,1,0:T(8,128)(2,1)} %get-tuple-element.240), calls=%async_computation.2 | async-start | bytes 3145728 | tf_op jit(solution)/shard_map/all_to_all | solution.py:44
  190.1 43.3 %copy-start.46 = (s32[512,16]{0,1:T(8,128)S(1)}, s32[512,16]{0,1:T(8,128)}, u32[]{:S(2)}) copy-start(s32[512,16]{0,1:T(8,128)} %broadcast_select_fusion.26) | copy-start | bytes 98308
  239.2 10.5 %copy-start.60 = (bf16[16,128,1536]{2,1,0:T(8,128)(2,1)S(1)}, bf16[16,128,1536]{2,1,0:T(8,128)(2,1)}, u32[]{:S(2)}) copy-start(bf16[16,128,1536]{2,1,0:T(8,128)(2,1)} %get-tuple-element.161) | copy-start | bytes 18874372
  249.1 20.3 %collective-permute-start.15 = (bf16[256,1536]{1,0:T(8,128)(2,1)}, bf16[256,1536]{1,0:T(8,128)(2,1)}, u32[]{:S(2)}, u32[]{:S(2)}) collective-permute-start(bf16[256,1536]{1,0:T(8,128)(2,1)} %dynamic-slice_convert_fusion.2), channel_id=1, source_target_pairs={{0,1},{1,0},{2,3},{3,2},{4,5},{5,4},{6,7},{7,6},{8,9},{9,8},{10,11... | collective-permute-start | bytes 2359304 | tf_op jit(solution)/shard_map/ppermute | solution.py:32
  257.8 48.1 %all-to-all-start.3 = ((bf16[16,128,512]{2,1,0:T(8,128)(2,1)}), bf16[16,128,512]{2,1,0:T(8,128)(2,1)}, u32[]{:S(2)}, u32[]{:S(2)}) async-start(bf16[16,128,512]{2,1,0:T(8,128)(2,1)} %fusion.12), calls=%async_computation.3 | async-start | bytes 4194304 | tf_op jit(solution)/shard_map/all_to_all | solution.py:44
  276.3 19.3 %collective-permute-start.16 = (bf16[256,1536]{1,0:T(8,128)(2,1)S(1)}, bf16[256,1536]{1,0:T(8,128)(2,1)}, u32[]{:S(2)}, u32[]{:S(2)}) collective-permute-start(bf16[256,1536]{1,0:T(8,128)(2,1)S(1)} %fusion.38), channel_id=1, source_target_pairs={{0,1},{1,0},{2,3},{3,2},{4,5},{5,4},{6,7},{7,6},{8,9},{9,8},{10,11... | collective-permute-start | bytes 2359304 | tf_op jit(solution)/shard_map/ppermute | solution.py:32
  310.1 17.8 %collective-permute-start.18 = (bf16[8,96,768]{2,1,0:T(8,128)(2,1)}, bf16[8,96,768]{2,1,0:T(8,128)(2,1)}, u32[]{:S(2)}, u32[]{:S(2)}) collective-permute-start(bf16[8,96,768]{2,1,0:T(8,128)(2,1)} %dynamic-slice_bitcast_fusion), channel_id=1, source_target_pairs={{0,2},{2,0},{4,6},{6,4},{8,10},{10,8},{12,14},{14,12},{16,18},{18,... | collective-permute-start | bytes 3538952 | tf_op jit(solution)/shard_map/ppermute | solution.py:32
  312.1 30.7 %all-to-all-start.4 = ((bf16[4,512,192]{1,2,0:T(8,128)(2,1)}), bf16[4,512,192]{1,2,0:T(8,128)(2,1)S(1)}, u32[]{:S(2)}, u32[]{:S(2)}) async-start(bf16[4,512,192]{1,2,0:T(8,128)(2,1)} %copy.48), calls=%async_computation.4 | async-start | bytes 1572864 | tf_op jit(solution)/shard_map/all_to_all | solution.py:732
  326.9 106.6 %collective-permute-start.23 = (bf16[16,128,768]{2,1,0:T(8,128)(2,1)}, bf16[16,128,768]{2,1,0:T(8,128)(2,1)}, u32[]{:S(2)}, u32[]{:S(2)}) collective-permute-start(bf16[16,128,768]{2,1,0:T(8,128)(2,1)} %pad_maximum_fusion.refs_0_), channel_id=1, source_target_pairs={{0,1},{1,0},{2,3},{3,2},{4,5},{5,4},{6,7},{7,6},{8,9},{9,8},{10,11... | collective-permute-start | bytes 9437192 | tf_op jit(solution)/shard_map/ppermute | solution.py:32
  342.7 60.5 %all-to-all-start.5 = ((bf16[8,96,768]{2,1,0:T(8,128)(2,1)}), bf16[8,96,768]{2,1,0:T(8,128)(2,1)S(1)}, u32[]{:S(2)}, u32[]{:S(2)}) async-start(bf16[8,96,768]{2,1,0:T(8,128)(2,1)} %bitcast_add_fusion), calls=%async_computation.5 | async-start | bytes 2359296 | tf_op jit(solution)/shard_map/all_to_all | solution.py:122
  347.6 51.8 %copy-start.19 = (bf16[512,1536]{1,0:T(8,128)(2,1)S(1)}, bf16[512,1536]{1,0:T(8,128)(2,1)}, u32[]{:S(2)}) copy-start(bf16[512,1536]{1,0:T(8,128)(2,1)} %x_ref.1) | copy-start | bytes 4718596
  390.3 11.7 %copy-start.33 = (bf16[8,512,128]{2,1,0:T(8,128)(2,1)S(1)}, bf16[8,512,128]{2,1,0:T(8,128)(2,1)}, u32[]{:S(2)}) copy-start(bf16[8,512,128]{2,1,0:T(8,128)(2,1)} %get-tuple-element.169) | copy-start | bytes 3145732
  390.3 11.7 %collective-permute-start.17 = (bf16[8,512,128]{2,1,0:T(8,128)(2,1)}, bf16[8,512,128]{2,1,0:T(8,128)(2,1)S(1)}, u32[]{:S(2)}, u32[]{:S(2)}) collective-permute-start(bf16[8,512,128]{2,1,0:T(8,128)(2,1)} %get-tuple-element.170), channel_id=1, source_target_pairs={{0,2},{2,0},{4,6},{6,4},{8,10},{10,8},{12,14},{14,12},{16,18},{18,... | collective-permute-start | bytes 3145736 | tf_op jit(solution)/shard_map/ppermute | solution.py:32
  399.8 10.0 %copy-start.54 = (f32[512]{0:T(512)}, f32[512]{0:T(512)S(1)}, u32[]{:S(2)}) copy-start(f32[512]{0:T(512)S(1)} %add_rsqrt_fusion) | copy-start | bytes 6148
  403.2 8.6 %copy-start.27 = (bf16[8,96,768]{2,1,0:T(8,128)(2,1)}, bf16[8,96,768]{2,1,0:T(8,128)(2,1)S(1)}, u32[]{:S(2)}) copy-start(bf16[8,96,768]{2,1,0:T(8,128)(2,1)S(1)} %all-to-all-done.5) | copy-start | bytes 3538948
  405.4 28.1 %collective-permute-start.22 = (bf16[1,4,512,128]{3,2,1,0:T(8,128)(2,1)}, bf16[1,4,512,128]{3,2,1,0:T(8,128)(2,1)S(1)}, u32[]{:S(2)}, u32[]{:S(2)}) collective-permute-start(bf16[1,4,512,128]{3,2,1,0:T(8,128)(2,1)} %slice_bitcast_fusion), channel_id=1, source_target_pairs={{0,4},{2,6},{4,0},{6,2},{8,12},{10,14},{12,8},{14,10},{16,20},{18,... | collective-permute-start | bytes 1572872 | tf_op jit(solution)/shard_map/ppermute | solution.py:32
  405.4 11.3 %collective-permute-start.19 = (bf16[512,192]{1,0:T(8,128)(2,1)}, bf16[512,192]{1,0:T(8,128)(2,1)S(1)}, u32[]{:S(2)}, u32[]{:S(2)}) collective-permute-start(bf16[512,192]{1,0:T(8,128)(2,1)} %get-tuple-element.176), channel_id=1, source_target_pairs={{0,24},{2,26},{4,28},{6,30},{8,16},{10,18},{12,20},{14,22},{16,8},... | collective-permute-start | bytes 589832 | tf_op jit(solution)/shard_map/ppermute | solution.py:32
  408.9 23.3 %collective-permute-start.20 = (bf16[512,192]{1,0:T(8,128)(2,1)}, bf16[512,192]{1,0:T(8,128)(2,1)}, u32[]{:S(2)}, u32[]{:S(2)}) collective-permute-start(bf16[512,192]{1,0:T(8,128)(2,1)} %get-tuple-element.177), channel_id=1, source_target_pairs={{0,16},{2,18},{4,20},{6,22},{8,24},{10,26},{12,28},{14,30},{16,0},... | collective-permute-start | bytes 589832 | tf_op jit(solution)/shard_map/ppermute | solution.py:32
  408.9 23.4 %collective-permute-start.21 = (bf16[512,192]{1,0:T(8,128)(2,1)}, bf16[512,192]{1,0:T(8,128)(2,1)}, u32[]{:S(2)}, u32[]{:S(2)}) collective-permute-start(bf16[512,192]{1,0:T(8,128)(2,1)} %get-tuple-element.178), channel_id=1, source_target_pairs={{0,8},{2,10},{4,12},{6,14},{8,0},{10,2},{12,4},{14,6},{16,24},{18,... | collective-permute-start | bytes 589832 | tf_op jit(solution)/shard_map/ppermute | solution.py:32
  411.7 20.5 %copy-start.40 = (bf16[512,192]{1,0:T(8,128)(2,1)S(1)}, bf16[512,192]{1,0:T(8,128)(2,1)}, u32[]{:S(2)}) copy-start(bf16[512,192]{1,0:T(8,128)(2,1)} %get-tuple-element.179) | copy-start | bytes 589828
  413.7 19.8 %copy-start.29 = (bf16[8,512,128]{2,1,0:T(8,128)(2,1)S(1)}, bf16[8,512,128]{2,1,0:T(8,128)(2,1)}, u32[]{:S(2)}) copy-start(bf16[8,512,128]{2,1,0:T(8,128)(2,1)} %add.168) | copy-start | bytes 3145732
  416.7 15.5 %copy-start.42 = (bf16[512,192]{1,0:T(8,128)(2,1)}, bf16[512,192]{1,0:T(8,128)(2,1)S(1)}, u32[]{:S(2)}) copy-start(bf16[512,192]{1,0:T(8,128)(2,1)S(1)} %collective-permute-done.19) | copy-start | bytes 589828
  435.0 26.5 %collective-permute-start.27 = (bf16[256,1536]{1,0:T(8,128)(2,1)S(1)}, bf16[256,1536]{1,0:T(8,128)(2,1)}, u32[]{:S(2)}, u32[]{:S(2)}) collective-permute-start(bf16[256,1536]{1,0:T(8,128)(2,1)S(1)} %dynamic-slice_convert_fusion.1), channel_id=1, source_target_pairs={{0,1},{1,0},{2,3},{3,2},{4,5},{5,4},{6,7},{7,6},{8,9},{9,8},{10,11... | collective-permute-start | bytes 2359304 | tf_op jit(solution)/shard_map/ppermute | solution.py:32
  436.1 21.3 %collective-permute-start.24 = (bf16[512,128]{1,0:T(8,128)(2,1)S(1)}, bf16[512,128]{1,0:T(8,128)(2,1)S(1)}, u32[]{:S(2)}, u32[]{:S(2)}) collective-permute-start(bf16[512,128]{1,0:T(8,128)(2,1)S(1)} %get-tuple-element.266), channel_id=1, source_target_pairs={{0,24},{2,26},{4,28},{6,30},{8,16},{10,18},{12,20},{14,22},{16,8},... | collective-permute-start | bytes 393224 | tf_op jit(solution)/shard_map/ppermute | solution.py:32
  438.5 18.9 %collective-permute-start.25 = (bf16[512,128]{1,0:T(8,128)(2,1)S(1)}, bf16[512,128]{1,0:T(8,128)(2,1)S(1)}, u32[]{:S(2)}, u32[]{:S(2)}) collective-permute-start(bf16[512,128]{1,0:T(8,128)(2,1)S(1)} %get-tuple-element.265), channel_id=1, source_target_pairs={{0,16},{2,18},{4,20},{6,22},{8,24},{10,26},{12,28},{14,30},{16,0},... | collective-permute-start | bytes 393224 | tf_op jit(solution)/shard_map/ppermute | solution.py:32
  438.5 18.9 %collective-permute-start.26 = (bf16[512,128]{1,0:T(8,128)(2,1)S(1)}, bf16[512,128]{1,0:T(8,128)(2,1)S(1)}, u32[]{:S(2)}, u32[]{:S(2)}) collective-permute-start(bf16[512,128]{1,0:T(8,128)(2,1)S(1)} %get-tuple-element.264), channel_id=1, source_target_pairs={{0,8},{2,10},{4,12},{6,14},{8,0},{10,2},{12,4},{14,6},{16,24},{18,... | collective-permute-start | bytes 393224 | tf_op jit(solution)/shard_map/ppermute | solution.py:32
  468.2 20.9 %collective-permute-start.28 = (bf16[8,96,1280]{2,1,0:T(8,128)(2,1)}, bf16[8,96,1280]{2,1,0:T(8,128)(2,1)}, u32[]{:S(2)}, u32[]{:S(2)}) collective-permute-start(bf16[8,96,1280]{2,1,0:T(8,128)(2,1)} %get-tuple-element.199), channel_id=1, source_target_pairs={{0,2},{2,0},{4,6},{6,4},{8,10},{10,8},{12,14},{14,12},{16,18},{18,... | collective-permute-start | bytes 5898248 | tf_op jit(solution)/shard_map/ppermute | solution.py:32
  473.8 2.0 collective-permute-start.29
  473.9 4.3 collective-permute-start.30
  475.7 3.8 collective-permute-start.31
  479.5 5.2 collective-permute-start.32
  479.6 6.6 %collective-permute-start.33 = (bf16[216,128]{1,0:T(8,128)(2,1)S(1)}, bf16[216,128]{1,0:T(8,128)(2,1)S(1)}, u32[]{:S(2)}, u32[]{:S(2)}) collective-permute-start(bf16[216,128]{1,0:T(8,128)(2,1)S(1)} %add_convert_fusion.1), channel_id=1, source_target_pairs={{0,16},{2,18},{4,20},{6,22},{8,24},{10,26},{12,28},{14,30},{16,0},... | collective-permute-start | bytes 165896 | tf_op jit(solution)/shard_map/ppermute | solution.py:32
  482.5 6.0 %collective-permute-start.34 = (bf16[216,128]{1,0:T(8,128)(2,1)S(1)}, bf16[216,128]{1,0:T(8,128)(2,1)S(1)}, u32[]{:S(2)}, u32[]{:S(2)}) collective-permute-start(bf16[216,128]{1,0:T(8,128)(2,1)S(1)} %add_convert_fusion.1), channel_id=1, source_target_pairs={{0,24},{2,26},{4,28},{6,30},{8,16},{10,18},{12,20},{14,22},{16,8},... | collective-permute-start | bytes 165896 | tf_op jit(solution)/shard_map/ppermute | solution.py:32
  492.5 48.3 %all-to-all-start.6 = ((bf16[8,96,1280]{2,1,0:T(8,128)(2,1)}), bf16[8,96,1280]{2,1,0:T(8,128)(2,1)S(1)}, u32[]{:S(2)}, u32[]{:S(2)}) async-start(bf16[8,96,1280]{2,1,0:T(8,128)(2,1)} %add.177), calls=%async_computation.6 | async-start | bytes 3932160 | tf_op jit(solution)/shard_map/all_to_all | solution.py:122
  502.3 23.1 %collective-permute-start.36 = (bf16[256,1536]{1,0:T(8,128)(2,1)S(1)}, bf16[256,1536]{1,0:T(8,128)(2,1)}, u32[]{:S(2)}, u32[]{:S(2)}) collective-permute-start(bf16[256,1536]{1,0:T(8,128)(2,1)S(1)} %dynamic-slice_convert_fusion), channel_id=1, source_target_pairs={{0,1},{1,0},{2,3},{3,2},{4,5},{5,4},{6,7},{7,6},{8,9},{9,8},{10,11... | collective-permute-start | bytes 2359304 | tf_op jit(solution)/shard_map/ppermute | solution.py:32
  503.5 21.3 %collective-permute-start.35 = (bf16[216,128]{1,0:T(8,128)(2,1)S(1)}, bf16[216,128]{1,0:T(8,128)(2,1)S(1)}, u32[]{:S(2)}, u32[]{:S(2)}) collective-permute-start(bf16[216,128]{1,0:T(8,128)(2,1)S(1)} %copy-done.43), channel_id=1, source_target_pairs={{0,1},{1,0},{2,3},{3,2},{4,5},{5,4},{6,7},{7,6},{8,9},{9,8},{10,11... | collective-permute-start | bytes 165896 | tf_op jit(solution)/shard_map/ppermute | solution.py:32
  527.3 15.8 %copy-start.23 = (f32[256,1536]{1,0:T(8,128)}, f32[256,1536]{1,0:T(8,128)S(1)}, u32[]{:S(2)}) copy-start(f32[256,1536]{1,0:T(8,128)S(1)} %convert_add_fusion) | copy-start | bytes 4718596
  (43 other events, 95.3 us)

commit v5 on v4

--- a/solution.py
+++ b/solution.py
@@ -238,20 +238,23 @@
 
     def step(blk, masked):
         x = blk ^ place
-        kv = kv_s[(x % stride) * lines + x // stride]
+        index = (x % stride) * lines + x // stride
+        kv = kv_s[index]
         if masked:
             seen = visible(blk, own, rows, start_ref[0])
-        for h in range(heads):
-            s = dot(kv, q_s[slot, h], NT)
-            if masked:
-                s = jnp.where(seen, s, NEG)
-            m_old = m_s[h : h + 1, :]
-            m_new = jnp.maximum(m_old, jnp.max(s, axis=0, keepdims=True))
-            p = jnp.exp(s - m_new)
-            alpha = jnp.exp(m_old - m_new)
-            l_s[h : h + 1, :] = l_s[h : h + 1, :] * alpha + jnp.sum(p, axis=0, keepdims=True)
-            acc_s[h] = acc_s[h] * alpha + dot(kv, p.astype(BF), TN)
-            m_s[h : h + 1, :] = m_new
+        each = range(heads)
+        scores = [dot(kv, q_s[slot, h], NT) for h in each]
+        if masked:
+            scores = [jnp.where(seen, s, NEG) for s in scores]
+        m_old = [m_s[h : h + 1, :] for h in each]
+        m_new = [jnp.maximum(m_old[h], jnp.max(scores[h], axis=0, keepdims=True)) for h in each]
+        p = [jnp.exp(scores[h] - m_new[h]) for h in each]
+        alpha = [jnp.exp(m_old[h] - m_new[h]) for h in each]
+        added = [dot(kv, p[h].astype(BF), TN) for h in each]
+        for h in each:
+            l_s[h : h + 1, :] = l_s[h : h + 1, :] * alpha[h] + jnp.sum(p[h], axis=0, keepdims=True)
+            acc_s[h] = acc_s[h] * alpha[h] + added[h]
+            m_s[h : h + 1, :] = m_new[h]
 
     walk(low, clear, own, step)
     parts = []
@@ -335,18 +338,17 @@
         kv = kv_s[index]
         if masked:
             seen = visible(blk, own, rows, start_ref[0])
-        for h in range(heads):
-            q = q_s[slot, h]
-            g = g_s[slot, h]
-            s = dot(kv, q, NT)
-            if masked:
-                s = jnp.where(seen, s, NEG)
-            p = jnp.exp(s - log_ref[0, h : h + 1, :])
-            gp = dot(kv, g, NT)
-            gs = (p * (gp - delta_s[h : h + 1, :])).astype(BF)
-            part = dot(gs, q) + dot(p.astype(BF), g)
-            dkv_s[index] += part
-            dq_s[h] += dot(gs, kv, TN)
+        each = range(heads)
+        scores = [dot(kv, q_s[slot, h], NT) for h in each]
+        grad_probs = [dot(kv, g_s[slot, h], NT) for h in each]
+        if masked:
+            scores = [jnp.where(seen, s, NEG) for s in scores]
+        p = [jnp.exp(scores[h] - log_ref[0, h : h + 1, :]) for h in each]
+        grad_scores = [(p[h] * (grad_probs[h] - delta_s[h : h + 1, :])).astype(BF) for h in each]
+        parts = [dot(grad_scores[h], q_s[slot, h]) + dot(p[h].astype(BF), g_s[slot, h]) for h in each]
+        dkv_s[index] += sum(parts[1:], parts[0])
+        for h in each:
+            dq_s[h] += dot(grad_scores[h], kv, TN)
 
     walk(low, clear, own, step)
     dq = jnp.concatenate([dq_s[h][:, :HD] * 0.125 for h in range(heads)], 1).astype(BF)
@@ -657,9 +659,12 @@
 
     kv = [jnp.stack(to_lines(kv_mine))]
     q = to_lines(q_mine)
-    for bit in reversed(bits_of(stride)):
+    g_sent = [half(out_grad, i) for i in range(2)]
+    for turn, bit in enumerate(reversed(bits_of(stride))):
         kv = [piece for one in kv for piece in (one, across(one, "dp", bit))]
-    g_sent, (kv, q, starts, meta) = after([half(out_grad, i) for i in range(2)], (kv, q, starts, meta))
+        if turn == 0:
+            kv[1], g_sent = after(kv[1], g_sent)
+    g_sent, (kv, q, starts, meta) = after(g_sent, (kv, q, starts, meta))
     g_first = to_owner(g_sent[0])
     *mixed_far, raw, logs = attend(meta, q, kv, starts[:, None, :], group)
     mixed_far, g_first = after(mixed_far, g_first)
@@ -806,9 +811,10 @@
         pair_sum(weight_keep, weight_send), (owned, small, grad_in_part)
     )
     small = total(small, "tensor")
-    (gate_out, up_out, down_out), small, weight_got, grad_in_rows = lax.optimization_barrier(
-        (owner_grads(owned), small, send_rows(weight_pair), scatter_tensor(grad_in_part))
-    )
+    owner_outs, small, grad_in_rows = lax.optimization_barrier(
+        (owner_grads(owned), small, scatter_tensor(grad_in_part))
+    )
+    (gate_out, up_out, down_out), weight_got = after(owner_outs, send_rows(weight_pair))
     weight_grad = jnp.sum(weight_got.astype(F32), axis=0)
     layer_out = (hidden + moe_rows).astype(BF)
     ends = [0]

time: 559 us -> 557 us (level)
  starting transfers between devices: 110 us -> 101 us
  local copies, waits for them, and re-layouts: 51.4 us -> 59.6 us
  Pallas kernels: 162 us -> 170 us
    pallas_call x1, Pallas kernels: 42.7 us -> 51.1 us  [attend_back(): pl.pallas_call(functools.partial(attend_back_kernel, heads, rows, lines,...]
    ppermute x37, waiting for transfers between devices: 78.6 us -> 86.3 us  [across(): return lax.ppermute(x, axis, [(i, i ^ mask) for i in range(n)])]
    unnamed x125 -> x135, local copies, waits for them, and re-layouts: 16.4 us -> 23.5 us
    all_to_all x4, starting transfers between devices: 43 us -> 37 us  [to_owner(): return lax.all_to_all(x, 'dp', 0, 0, tiled=True)]
  transfers between devices with their start and end apart: 44 -> 44, of which waited for: 18 -> 18; matrix products, arithmetic and copies ran while one was open for 20% -> 20% of each run, Pallas kernels for 28% -> 29%
where the time goes in v5:
time: 557 us; the launch traced here: 554 us
  Pallas kernels  170 us (31%)
  waiting for transfers between devices  116 us (21%)
  starting transfers between devices  101 us (18%)
  local copies, waits for them, and re-layouts  59.6 us (11%)
  other arithmetic  56.7 us (10%)
  matrix products  45.9 us (8%)
    ppermute x37, waiting for transfers between devices, across(): return lax.ppermute(x, axis, [(i, i ^ mask) for i in range(n)])  86.3 us
    pallas_call x1, Pallas kernels, attend_back(): pl.pallas_call(functools.partial(attend_back_kernel, heads, rows, lines,...  51.1 us
    ppermute x37, starting transfers between devices, across(): return lax.ppermute(x, axis, [(i, i ^ mask) for i in range(n)])  45.7 us
    pallas_call x1, Pallas kernels, run_experts(): pl.pallas_call(experts_kernel, grid=(experts // at_once,), in_specs=[of(c...  42.4 us
    all_to_all x4, starting transfers between devices, to_owner(): return lax.all_to_all(x, 'dp', 0, 0, tiled=True)  37 us
    pallas_call x2, Pallas kernels, owner_call(): pl.pallas_call(functools.partial(kernel, len(x), len(g)), grid_spec=pltpu...  35.7 us
    dot_general x9, matrix products, dot(): return jnp.dot(a, b, preferred_element_type=F32)  35.4 us
    pallas_call x1, Pallas kernels, attend(): pl.pallas_call(functools.partial(attend_kernel, heads, rows, lines, strid...  31.6 us
  transfers between devices with their start and end apart: 44, of which 18 were waited for; matrix products, arithmetic and copies ran while one was open for 20% of the time, Pallas kernels for 29%

profile of v5, /device:TPU:0, one launch (start us, length us, event | category | flops | bytes accessed | tf_op | source)
XLA Modules:
  0.0 554.0 jit_solution(10061624649199368312)
XLA Ops:
  3.8 5.7 %project.1 = (bf16[512,1536]{1,0:T(8,128)(2,1)S(1)}, bf16[512,128]{1,0:T(8,128)(2,1)S(1)}, bf16[512,128]{1,0:T(8,128)(2,1)S(1)}, bf16[512,128]{1,0:T(8,128)(2,1)...) custom-call(s32[1]{0:T(128)} %bitcast.at, ...), custom_call_target="tpu_custom_call" | custom-call | flops 2013265920 | bytes 8388608 | tf_op jit(solution)/shard_map/project/pallas_call | solution.py:152
  11.3 3.0 collective-permute-start
  14.4 2.6 collective-permute-start.1
  17.9 3.5 collective-permute-start.7
  25.6 1.8 collective-permute-done.1
  31.7 3.8 convolution_convert_fusion.3
  35.5 3.4 convolution_convert_fusion.4
  40.5 6.6 %collective-permute-done.7.refs_2_ = bf16[512,192]{1,0:T(8,128)(2,1)} collective-permute-done((bf16[512,192]{1,0:T(8,128)(2,1)}, bf16[512,192]{1,0:T(8,128)(2,1)}, u32[]{:S(2)}, u32[]{:S(2)}) %collective-permute-start.7) | collective-permute-done | bytes 196640 | tf_op jit(solution)/shard_map/ppermute | solution.py:32
  48.7 8.4 %all-to-all-start = ((bf16[16,128,384]{2,1,0:T(8,128)(2,1)}), bf16[16,128,384]{2,1,0:T(8,128)(2,1)}, u32[]{:S(2)}, u32[]{:S(2)}) async-start(bf16[16,128,384]{2,1,0:T(8,128)(2,1)} %bitcast.128), calls=%async_computation | async-start | bytes 3145728 | tf_op jit(solution)/shard_map/all_to_all | solution.py:44
  60.2 31.6 %attend.1 = (bf16[512,192]{1,0:T(8,128)(2,1)S(1)}, bf16[512,192]{1,0:T(8,128)(2,1)S(1)}, bf16[512,192]{1,0:T(8,128)(2,1)S(1)}, bf16[512,192]{1,0:T(8,128)(2,1)S(...) custom-call(s32[13]{0:T(128)S(1)} %pad_add_fusion.1.meta, bf16[512,192]{1,0:T(8,128)(2,1)S(1)} %copy-done.20, ...), custom_call_target="tpu_custom_call" | custom-call | flops 9663676416 | bytes 8388608 | tf_op jit(solution)/shard_map/attend/pallas_call | solution.py:282
  95.2 2.9 collective-permute-start.10
  99.6 7.8 %convolution_convert_fusion.1 = bf16[2048,1536]{1,0:T(8,128)(2,1)} fusion(pred[2048,512]{1,0:T(32,128)(4,1)} %bitcast_compare_fusion, bf16[512,1536]{1,0:T(8,128)(2,1)} %param.27), kind=kOutput, calls=%fused_computation.1 | convolution fusion | flops 3224371200 | bytes 8912896 | tf_op jit(solution)/shard_map/dot_general | solution.py:26
  107.4 2.2 collective-permute-done.10
  110.3 5.9 %collective-permute-done.9 = bf16[512,192]{1,0:T(8,128)(2,1)} collective-permute-done((bf16[512,192]{1,0:T(8,128)(2,1)}, bf16[512,192]{1,0:T(8,128)(2,1)}, u32[]{:S(2)}, u32[]{:S(2)}) %collective-permute-start.9) | collective-permute-done | bytes 196640 | tf_op jit(solution)/shard_map/ppermute | solution.py:32
  122.4 10.5 %all-to-all-start.1 = ((bf16[16,128,384]{2,1,0:T(8,128)(2,1)}), bf16[16,128,384]{2,1,0:T(8,128)(2,1)}, u32[]{:S(2)}, u32[]{:S(2)}) async-start(bf16[16,128,384]{2,1,0:T(8,128)(2,1)} %bitcast.127), calls=%async_computation.1 | async-start | bytes 3145728 | tf_op jit(solution)/shard_map/all_to_all | solution.py:44
  133.0 6.7 %collective-permute-done.12 = bf16[256,1536]{1,0:T(8,128)(2,1)} collective-permute-done((bf16[256,1536]{1,0:T(8,128)(2,1)S(1)}, bf16[256,1536]{1,0:T(8,128)(2,1)}, u32[]{:S(2)}, u32[]{:S(2)}) %collective-permute-start.12) | collective-permute-done | bytes 786464 | tf_op jit(solution)/shard_map/ppermute | solution.py:32
  139.6 2.2 multiply_reduce_fusion.5
  146.2 3.0 constant_dynamic-update-slice_fusion.1
  149.2 14.5 %collective-permute-done.13 = bf16[256,1536]{1,0:T(8,128)(2,1)S(1)} collective-permute-done((bf16[256,1536]{1,0:T(8,128)(2,1)}, bf16[256,1536]{1,0:T(8,128)(2,1)S(1)}, u32[]{:S(2)}, u32[]{:S(2)}) %collective-permute-start.13) | collective-permute-done | bytes 786464 | tf_op jit(solution)/shard_map/ppermute | solution.py:32
  165.5 3.0 constant_dynamic-update-slice_fusion.refs_2_
  170.0 5.4 convolution_convert_fusion
  177.8 4.1 constant_dynamic-slice_fusion
  181.9 11.1 %all-to-all-start.2 = ((bf16[16,128,384]{2,1,0:T(8,128)(2,1)}), bf16[16,128,384]{2,1,0:T(8,128)(2,1)}, u32[]{:S(2)}, u32[]{:S(2)}) async-start(bf16[16,128,384]{2,1,0:T(8,128)(2,1)} %get-tuple-element.252), calls=%async_computation.2 | async-start | bytes 3145728 | tf_op jit(solution)/shard_map/all_to_all | solution.py:44
  193.1 42.4 %experts.1 = (bf16[16,128,1536]{2,1,0:T(8,128)(2,1)}, bf16[16,128,1536]{2,1,0:T(8,128)(2,1)}, f32[16,8,128]{2,1,0:T(8,128)}) custom-call(bf16[16,128,1536]{2,1,0:T(8,128)(2,1)} %bitcast.121, bf16[16,128,1536]{2,1,0:T(8,128)(2,1)} %bitcast.122, f32[16,128,1]{2,1,0:T(8,128)} %copy.46.gate_ref, bf16[16,1536,512]{2,1,0:T(8,128)(2,1)} %wg_ref.3, ...), custom_call_target="tpu_custom_call" | custom-call | flops 19327352832 | bytes 100663296 | tf_op jit(solution)/shard_map/experts/pallas_call | solution.py:439
  236.3 2.6 select_reduce_fusion
  239.0 3.1 fusion.47
  242.1 7.3 %fusion.11 = f32[512,1536]{1,0:T(8,128)S(1)} fusion(f32[512,1536]{1,0:T(8,128)} %fusion.47, bf16[16,128,1536]{2,1,0:T(8,128)(2,1)} %get-tuple-element.168, s32[512,16]{0,1:T(8,128)S(1)} %copy-done.52), kind=kOutput, calls=%fused_computation.21 | convolution fusion | flops 3223060480 | bytes 12615680 | tf_op jit(solution)/shard_map/dot_general | solution.py:26
  252.5 4.8 fusion.10
  257.7 3.0 fusion.12
  260.8 6.9 %all-to-all-start.3 = ((bf16[16,128,512]{2,1,0:T(8,128)(2,1)}), bf16[16,128,512]{2,1,0:T(8,128)(2,1)}, u32[]{:S(2)}, u32[]{:S(2)}) async-start(bf16[16,128,512]{2,1,0:T(8,128)(2,1)} %fusion.12), calls=%async_computation.3 | async-start | bytes 4194304 | tf_op jit(solution)/shard_map/all_to_all | solution.py:44
  267.7 4.6 collective-permute-done.15
  272.3 1.8 convert_add_fusion.2
  277.2 18.8 %collective-permute-done.16 = bf16[256,1536]{1,0:T(8,128)(2,1)} collective-permute-done((bf16[256,1536]{1,0:T(8,128)(2,1)S(1)}, bf16[256,1536]{1,0:T(8,128)(2,1)}, u32[]{:S(2)}, u32[]{:S(2)}) %collective-permute-start.16) | collective-permute-done | bytes 786464 | tf_op jit(solution)/shard_map/ppermute | solution.py:32
  300.4 8.4 %all-to-all-done.3 = bf16[16,128,512]{2,1,0:T(8,128)(2,1)} async-done(((bf16[16,128,512]{2,1,0:T(8,128)(2,1)}), bf16[16,128,512]{2,1,0:T(8,128)(2,1)}, u32[]{:S(2)}, u32[]{:S(2)}) %all-to-all-start.3) | async-done | bytes 2097184 | tf_op jit(solution)/shard_map/all_to_all | solution.py:44
  308.8 3.0 convolution_convert_fusion.2
  315.0 9.9 %all-to-all-start.4 = ((bf16[4,512,192]{1,2,0:T(8,128)(2,1)}), bf16[4,512,192]{1,2,0:T(8,128)(2,1)S(1)}, u32[]{:S(2)}, u32[]{:S(2)}) async-start(bf16[4,512,192]{1,2,0:T(8,128)(2,1)} %copy.48), calls=%async_computation.4 | async-start | bytes 1572864 | tf_op jit(solution)/shard_map/all_to_all | solution.py:737
  326.4 3.4 pad_maximum_fusion.refs_0_
  330.7 2.4 bitcast_add_fusion
  333.1 12.5 %all-to-all-done.4 = bf16[4,512,192]{1,2,0:T(8,128)(2,1)S(1)} async-done(((bf16[4,512,192]{1,2,0:T(8,128)(2,1)}), bf16[4,512,192]{1,2,0:T(8,128)(2,1)S(1)}, u32[]{:S(2)}, u32[]{:S(2)}) %all-to-all-start.4) | async-done | bytes 786464 | tf_op jit(solution)/shard_map/all_to_all | solution.py:737
  345.6 3.6 all-to-all-start.5
  350.5 51.1 %attend_back.1 = (bf16[512,192]{1,0:T(8,128)(2,1)}, bf16[512,192]{1,0:T(8,128)(2,1)}, bf16[512,192]{1,0:T(8,128)(2,1)}, bf16[512,192]{1,0:T(8,128)(2,1)}, bf16[8...) custom-call(s32[13]{0:T(128)} %copy-done.4, bf16[512,192]{1,0:T(8,128)(2,1)} %copy-done.19, ...), custom_call_target="tpu_custom_call" | custom-call | flops 24159191040 | bytes 10485760 | tf_op jit(solution)/shard_map/attend_back/pallas_call | solution.py:375
  401.6 4.1 collective-permute-start.17
  406.1 2.1 collective-permute-done.17
  409.5 2.2 slice_bitcast_fusion
  411.7 3.5 collective-permute-start.19
  416.1 1.9 broadcast_multiply_fusion
  423.0 15.5 %collective-permute-done.20 = bf16[512,192]{1,0:T(8,128)(2,1)} collective-permute-done((bf16[512,192]{1,0:T(8,128)(2,1)}, bf16[512,192]{1,0:T(8,128)(2,1)}, u32[]{:S(2)}, u32[]{:S(2)}) %collective-permute-start.20) | collective-permute-done | bytes 196640 | tf_op jit(solution)/shard_map/ppermute | solution.py:32
  442.4 2.4 collective-permute-start.24
  444.8 2.0 collective-permute-start.26
  446.8 16.8 %owner_forward.1 = (bf16[2048,512]{1,0:T(8,128)(2,1)}, bf16[2048,512]{1,0:T(8,128)(2,1)}, bf16[2048,512]{1,0:T(8,128)(2,1)}) custom-call(s32[5]{0:T(128)} %stack.81.at, f32[2048,1]{1,0:T(8,128)} %copy.50.gate_ref, bf16[16,1536,512]{2,1,0:T(8,128)(2,1)} %wg_ref.3, bf16[16,1536,512]{2,1,0:T(8,128)(2,1)} %wu_ref.3, bf16[16,512,1536]{2,1,0:T(8,128)(2,1)} %wd_ref.3, ...), custom_call_target="tpu_custom_call" | custom-call | flops 10737418240 | bytes 25165824 | tf_op jit(solution)/shard_map/owner_forward/pallas_call | solution.py:567
  465.4 2.5 concatenate.38.b_ref
  467.9 3.2 convert_add_fusion.1
  471.0 3.5 weights.1
  475.9 2.2 fusion.3
  484.1 2.6 collective-permute-done.30
  489.0 2.9 collective-permute-start.33
  494.6 2.2 convert_element_type.150
  497.9 3.3 add.177
  501.2 4.7 all-to-all-start.6
  511.8 18.9 %owner_grads.1 = (f32[1,1536,512]{2,1,0:T(8,128)}, f32[1,1536,512]{2,1,0:T(8,128)}, f32[1,512,1536]{2,1,0:T(8,128)}) custom-call(s32[5]{0:T(128)} %stack.81.at, f32[2048,1]{1,0:T(8,128)} %copy.51.gate_ref, bf16[2048,512]{1,0:T(8,128)(2,1)} %get-tuple-element.223.act_ref, bf16[2048,512]{1,0:T(8,128)(2,1)} %get-tuple-element.224.grad_gate_ref, ...), custom_call_target="tpu_custom_call" | custom-call | flops 10737418240 | bytes 25165824 | tf_op jit(solution)/shard_map/owner_grads/pallas_call | solution.py:567
  533.6 1.9 multiply_reduce_fusion.2
  536.1 5.0 multiply_add_fusion
  541.2 9.1 %all-to-all-done.6 = bf16[8,96,1280]{2,1,0:T(8,128)(2,1)} async-done(((bf16[8,96,1280]{2,1,0:T(8,128)(2,1)}), bf16[8,96,1280]{2,1,0:T(8,128)(2,1)}, u32[]{:S(2)}, u32[]{:S(2)}) %all-to-all-start.6) | async-done | bytes 1966112 | tf_op jit(solution)/shard_map/all_to_all | solution.py:122
  550.3 1.9 convert_reduce_fusion
  (274 shorter events, 95.5 us)
Async XLA Ops:
  0.6 117.0 %copy-start = (bf16[768,1536]{1,0:T(8,128)(2,1)S(1)}, bf16[768,1536]{1,0:T(8,128)(2,1)}, u32[]{:S(2)}) copy-start(bf16[768,1536]{1,0:T(8,128)(2,1)} %param.19) | copy-start | bytes 7077892
  3.8 20.8 %copy-start.64 = (s32[512,2]{0,1:T(2,128)S(1)}, s32[512,2]{0,1:T(2,128)}, u32[]{:S(2)}) copy-start(s32[512,2]{0,1:T(2,128)} %param.26) | copy-start | bytes 12292
  11.3 14.2 %collective-permute-start = (bf16[512,128]{1,0:T(8,128)(2,1)S(1)}, bf16[512,128]{1,0:T(8,128)(2,1)S(1)}, u32[]{:S(2)}, u32[]{:S(2)}) collective-permute-start(bf16[512,128]{1,0:T(8,128)(2,1)S(1)} %get-tuple-element.130), channel_id=1, source_target_pairs={{0,8},{2,10},{4,12},{6,14},{8,0},{10,2},{12,4},{14,6},{16,24},{18,... | collective-permute-start | bytes 393224 | tf_op jit(solution)/shard_map/ppermute | solution.py:32
  14.4 13.0 %collective-permute-start.1 = (bf16[512,128]{1,0:T(8,128)(2,1)S(1)}, bf16[512,128]{1,0:T(8,128)(2,1)}, u32[]{:S(2)}, u32[]{:S(2)}) collective-permute-start(bf16[512,128]{1,0:T(8,128)(2,1)S(1)} %get-tuple-element.131), channel_id=1, source_target_pairs={{0,16},{2,18},{4,20},{6,22},{8,24},{10,26},{12,28},{14,30},{16,0},... | collective-permute-start | bytes 393224 | tf_op jit(solution)/shard_map/ppermute | solution.py:32
  17.0 10.5 %collective-permute-start.2 = (bf16[512,128]{1,0:T(8,128)(2,1)S(1)}, bf16[512,128]{1,0:T(8,128)(2,1)}, u32[]{:S(2)}, u32[]{:S(2)}) collective-permute-start(bf16[512,128]{1,0:T(8,128)(2,1)S(1)} %get-tuple-element.132), channel_id=1, source_target_pairs={{0,24},{2,26},{4,28},{6,30},{8,16},{10,18},{12,20},{14,22},{16,8},... | collective-permute-start | bytes 393224 | tf_op jit(solution)/shard_map/ppermute | solution.py:32
  17.0 23.5 %collective-permute-start.6 = (bf16[512,192]{1,0:T(8,128)(2,1)}, bf16[512,192]{1,0:T(8,128)(2,1)S(1)}, u32[]{:S(2)}, u32[]{:S(2)}) collective-permute-start(bf16[512,192]{1,0:T(8,128)(2,1)} %get-tuple-element.137), channel_id=1, source_target_pairs={{0,8},{2,10},{4,12},{6,14},{8,0},{10,2},{12,4},{14,6},{16,24},{18,... | collective-permute-start | bytes 589832 | tf_op jit(solution)/shard_map/ppermute | solution.py:32
  17.9 29.2 %collective-permute-start.7 = (bf16[512,192]{1,0:T(8,128)(2,1)}, bf16[512,192]{1,0:T(8,128)(2,1)}, u32[]{:S(2)}, u32[]{:S(2)}) collective-permute-start(bf16[512,192]{1,0:T(8,128)(2,1)} %get-tuple-element.138), channel_id=1, source_target_pairs={{0,16},{2,18},{4,20},{6,22},{8,24},{10,26},{12,28},{14,30},{16,0},... | collective-permute-start | bytes 589832 | tf_op jit(solution)/shard_map/ppermute | solution.py:32
  24.5 7.1 %copy-start.55 = (s32[8192]{0:T(1024)S(1)}, s32[8192]{0:T(1024)}, u32[]{:S(2)}) copy-start(s32[8192]{0:T(1024)} %param.25) | copy-start | bytes 98308
  25.6 21.5 %collective-permute-start.8 = (bf16[512,192]{1,0:T(8,128)(2,1)}, bf16[512,192]{1,0:T(8,128)(2,1)}, u32[]{:S(2)}, u32[]{:S(2)}) collective-permute-start(bf16[512,192]{1,0:T(8,128)(2,1)} %get-tuple-element.139), channel_id=1, source_target_pairs={{0,24},{2,26},{4,28},{6,30},{8,16},{10,18},{12,20},{14,22},{16,8},... | collective-permute-start | bytes 589832 | tf_op jit(solution)/shard_map/ppermute | solution.py:32
  28.5 28.6 %copy-start.2 = (bf16[4,512,128]{2,1,0:T(8,128)(2,1)}, bf16[4,512,128]{2,1,0:T(8,128)(2,1)S(1)}, u32[]{:S(2)}) copy-start(bf16[4,512,128]{2,1,0:T(8,128)(2,1)S(1)} %pad_maximum_fusion.5.refs_4_.refs_5_) | copy-start | bytes 1572868
  28.5 11.4 %collective-permute-start.3 = (bf16[4,512,128]{2,1,0:T(8,128)(2,1)S(1)}, bf16[4,512,128]{2,1,0:T(8,128)(2,1)}, u32[]{:S(2)}, u32[]{:S(2)}) collective-permute-start(bf16[4,512,128]{2,1,0:T(8,128)(2,1)S(1)} %pad_maximum_fusion.5.refs_4_.refs_5_), channel_id=1, source_target_pairs={{0,4},{2,6},{4,0},{6,2},{8,12},{10,14},{12,8},{14,10},{16,20},{18,... | collective-permute-start | bytes 1572872 | tf_op jit(solution)/shard_map/ppermute | solution.py:32
  38.9 8.2 %collective-permute-start.4 = (bf16[4,512,128]{2,1,0:T(8,128)(2,1)S(1)}, bf16[4,512,128]{2,1,0:T(8,128)(2,1)S(1)}, u32[]{:S(2)}, u32[]{:S(2)}) collective-permute-start(bf16[4,512,128]{2,1,0:T(8,128)(2,1)S(1)} %pad_maximum_fusion.5.refs_4_.refs_5_), channel_id=1, source_target_pairs={{0,2},{2,0},{4,6},{6,4},{8,10},{10,8},{12,14},{14,12},{16,18},{18,... | collective-permute-start | bytes 1572872 | tf_op jit(solution)/shard_map/ppermute | solution.py:32
  39.9 8.0 %collective-permute-start.5 = (bf16[4,512,128]{2,1,0:T(8,128)(2,1)}, bf16[4,512,128]{2,1,0:T(8,128)(2,1)S(1)}, u32[]{:S(2)}, u32[]{:S(2)}) collective-permute-start(bf16[4,512,128]{2,1,0:T(8,128)(2,1)} %collective-permute-done.3.refs_6_.refs_7_), channel_id=1, source_target_pairs={{0,2},{2,0},{4,6},{6,4},{8,10},{10,8},{12,14},{14,12},{16,18},{18,... | collective-permute-start | bytes 1572872 | tf_op jit(solution)/shard_map/ppermute | solution.py:32
  40.5 16.7 %copy-start.4 = (s32[13]{0:T(128)}, s32[13]{0:T(128)S(1)}, u32[]{:S(2)}) copy-start(s32[13]{0:T(128)S(1)} %pad_add_fusion.1.meta) | copy-start | bytes 160
  48.7 46.5 %all-to-all-start = ((bf16[16,128,384]{2,1,0:T(8,128)(2,1)}), bf16[16,128,384]{2,1,0:T(8,128)(2,1)}, u32[]{:S(2)}, u32[]{:S(2)}) async-start(bf16[16,128,384]{2,1,0:T(8,128)(2,1)} %bitcast.128), calls=%async_computation | async-start | bytes 3145728 | tf_op jit(solution)/shard_map/all_to_all | solution.py:44
  60.2 31.6 %copy-start.3 = (s32[4,1,512]{2,1,0:T(1,128)}, s32[4,1,512]{2,1,0:T(1,128)S(1)}, u32[]{:S(2)}) copy-start(s32[4,1,512]{2,1,0:T(1,128)S(1)} %broadcast_in_dim.118.refs_8_.refs_11_) | copy-start | bytes 24580
  95.2 14.4 %collective-permute-start.10 = (bf16[512,192]{1,0:T(8,128)(2,1)}, bf16[512,192]{1,0:T(8,128)(2,1)S(1)}, u32[]{:S(2)}, u32[]{:S(2)}) collective-permute-start(bf16[512,192]{1,0:T(8,128)(2,1)} %copy-done.16), channel_id=1, source_target_pairs={{0,16},{2,18},{4,20},{6,22},{8,24},{10,26},{12,28},{14,30},{16,0},... | collective-permute-start | bytes 589832 | tf_op jit(solution)/shard_map/ppermute | solution.py:32
  98.2 11.5 %collective-permute-start.11 = (bf16[512,192]{1,0:T(8,128)(2,1)}, bf16[512,192]{1,0:T(8,128)(2,1)S(1)}, u32[]{:S(2)}, u32[]{:S(2)}) collective-permute-start(bf16[512,192]{1,0:T(8,128)(2,1)} %copy-done.15), channel_id=1, source_target_pairs={{0,8},{2,10},{4,12},{6,14},{8,0},{10,2},{12,4},{14,6},{16,24},{18,... | collective-permute-start | bytes 589832 | tf_op jit(solution)/shard_map/ppermute | solution.py:32
  99.6 16.6 %collective-permute-start.9 = (bf16[512,192]{1,0:T(8,128)(2,1)}, bf16[512,192]{1,0:T(8,128)(2,1)}, u32[]{:S(2)}, u32[]{:S(2)}) collective-permute-start(bf16[512,192]{1,0:T(8,128)(2,1)} %copy-done.14), channel_id=1, source_target_pairs={{0,24},{2,26},{4,28},{6,30},{8,16},{10,18},{12,20},{14,22},{16,8},... | collective-permute-start | bytes 589832 | tf_op jit(solution)/shard_map/ppermute | solution.py:32
  120.8 18.8 %collective-permute-start.12 = (bf16[256,1536]{1,0:T(8,128)(2,1)S(1)}, bf16[256,1536]{1,0:T(8,128)(2,1)}, u32[]{:S(2)}, u32[]{:S(2)}) collective-permute-start(bf16[256,1536]{1,0:T(8,128)(2,1)S(1)} %dynamic-slice_convert_fusion.3), channel_id=1, source_target_pairs={{0,1},{1,0},{2,3},{3,2},{4,5},{5,4},{6,7},{7,6},{8,9},{9,8},{10,11... | collective-permute-start | bytes 2359304 | tf_op jit(solution)/shard_map/ppermute | solution.py:32
  122.4 43.0 %all-to-all-start.1 = ((bf16[16,128,384]{2,1,0:T(8,128)(2,1)}), bf16[16,128,384]{2,1,0:T(8,128)(2,1)}, u32[]{:S(2)}, u32[]{:S(2)}) async-start(bf16[16,128,384]{2,1,0:T(8,128)(2,1)} %bitcast.127), calls=%async_computation.1 | async-start | bytes 3145728 | tf_op jit(solution)/shard_map/all_to_all | solution.py:44
  132.9 10.1 %copy-start.50 = (f32[1536]{0:T(1024)S(1)}, f32[1536]{0:T(1024)}, u32[]{:S(2)}) copy-start(f32[1536]{0:T(1024)} %param.20) | copy-start | bytes 18436
  141.9 133.3 %copy-start.56 = (f32[256]{0:T(256)}, f32[256]{0:T(256)S(1)}, u32[]{:S(2)}) copy-start(f32[256]{0:T(256)S(1)} %add_rsqrt_fusion.1) | copy-start | bytes 3076
  144.1 19.7 %collective-permute-start.13 = (bf16[256,1536]{1,0:T(8,128)(2,1)}, bf16[256,1536]{1,0:T(8,128)(2,1)S(1)}, u32[]{:S(2)}, u32[]{:S(2)}) collective-permute-start(bf16[256,1536]{1,0:T(8,128)(2,1)} %multiply_convert_fusion), channel_id=1, source_target_pairs={{0,1},{1,0},{2,3},{3,2},{4,5},{5,4},{6,7},{7,6},{8,9},{9,8},{10,11... | collective-permute-start | bytes 2359304 | tf_op jit(solution)/shard_map/ppermute | solution.py:32
  146.2 17.5 %copy-start.23 = (f32[256,1536]{1,0:T(8,128)S(1)}, f32[256,1536]{1,0:T(8,128)}, u32[]{:S(2)}) copy-start(f32[256,1536]{1,0:T(8,128)} %copy-done.22) | copy-start | bytes 4718596
  168.4 6.9 %copy-start.51 = (bf16[1536,16]{0,1:T(8,128)(2,1)S(1)}, bf16[1536,16]{0,1:T(8,128)(2,1)}, u32[]{:S(2)}) copy-start(bf16[1536,16]{0,1:T(8,128)(2,1)} %param.21) | copy-start | bytes 147460
  168.4 73.6 %collective-permute-start.14 = (bf16[16,128,768]{2,1,0:T(8,128)(2,1)}, bf16[16,128,768]{2,1,0:T(8,128)(2,1)}, u32[]{:S(2)}, u32[]{:S(2)}) collective-permute-start(bf16[16,128,768]{2,1,0:T(8,128)(2,1)} %constant_dynamic-update-slice_fusion.refs_2_), channel_id=1, source_target_pairs={{0,1},{1,0},{2,3},{3,2},{4,5},{5,4},{6,7},{7,6},{8,9},{9,8},{10,11... | collective-permute-start | bytes 9437192 | tf_op jit(solution)/shard_map/ppermute | solution.py:32
  181.9 60.2 %all-to-all-start.2 = ((bf16[16,128,384]{2,1,0:T(8,128)(2,1)}), bf16[16,128,384]{2,1,0:T(8,128)(2,1)}, u32[]{:S(2)}, u32[]{:S(2)}) async-start(bf16[16,128,384]{2,1,0:T(8,128)(2,1)} %get-tuple-element.252), calls=%async_computation.2 | async-start | bytes 3145728 | tf_op jit(solution)/shard_map/all_to_all | solution.py:44
  193.0 43.3 %copy-start.52 = (s32[512,16]{0,1:T(8,128)S(1)}, s32[512,16]{0,1:T(8,128)}, u32[]{:S(2)}) copy-start(s32[512,16]{0,1:T(8,128)} %broadcast_select_fusion.26) | copy-start | bytes 98308
  242.1 10.5 %copy-start.65 = (bf16[16,128,1536]{2,1,0:T(8,128)(2,1)S(1)}, bf16[16,128,1536]{2,1,0:T(8,128)(2,1)}, u32[]{:S(2)}) copy-start(bf16[16,128,1536]{2,1,0:T(8,128)(2,1)} %get-tuple-element.170) | copy-start | bytes 18874372
  252.0 20.3 %collective-permute-start.15 = (bf16[256,1536]{1,0:T(8,128)(2,1)}, bf16[256,1536]{1,0:T(8,128)(2,1)}, u32[]{:S(2)}, u32[]{:S(2)}) collective-permute-start(bf16[256,1536]{1,0:T(8,128)(2,1)} %dynamic-slice_convert_fusion.2), channel_id=1, source_target_pairs={{0,1},{1,0},{2,3},{3,2},{4,5},{5,4},{6,7},{7,6},{8,9},{9,8},{10,11... | collective-permute-start | bytes 2359304 | tf_op jit(solution)/shard_map/ppermute | solution.py:32
  260.8 48.1 %all-to-all-start.3 = ((bf16[16,128,512]{2,1,0:T(8,128)(2,1)}), bf16[16,128,512]{2,1,0:T(8,128)(2,1)}, u32[]{:S(2)}, u32[]{:S(2)}) async-start(bf16[16,128,512]{2,1,0:T(8,128)(2,1)} %fusion.12), calls=%async_computation.3 | async-start | bytes 4194304 | tf_op jit(solution)/shard_map/all_to_all | solution.py:44
  276.7 19.3 %collective-permute-start.16 = (bf16[256,1536]{1,0:T(8,128)(2,1)S(1)}, bf16[256,1536]{1,0:T(8,128)(2,1)}, u32[]{:S(2)}, u32[]{:S(2)}) collective-permute-start(bf16[256,1536]{1,0:T(8,128)(2,1)S(1)} %fusion.38), channel_id=1, source_target_pairs={{0,1},{1,0},{2,3},{3,2},{4,5},{5,4},{6,7},{7,6},{8,9},{9,8},{10,11... | collective-permute-start | bytes 2359304 | tf_op jit(solution)/shard_map/ppermute | solution.py:32
  313.0 17.8 %collective-permute-start.18 = (bf16[8,96,768]{2,1,0:T(8,128)(2,1)}, bf16[8,96,768]{2,1,0:T(8,128)(2,1)}, u32[]{:S(2)}, u32[]{:S(2)}) collective-permute-start(bf16[8,96,768]{2,1,0:T(8,128)(2,1)} %dynamic-slice_bitcast_fusion), channel_id=1, source_target_pairs={{0,2},{2,0},{4,6},{6,4},{8,10},{10,8},{12,14},{14,12},{16,18},{18,... | collective-permute-start | bytes 3538952 | tf_op jit(solution)/shard_map/ppermute | solution.py:32
  315.0 30.6 %all-to-all-start.4 = ((bf16[4,512,192]{1,2,0:T(8,128)(2,1)}), bf16[4,512,192]{1,2,0:T(8,128)(2,1)S(1)}, u32[]{:S(2)}, u32[]{:S(2)}) async-start(bf16[4,512,192]{1,2,0:T(8,128)(2,1)} %copy.48), calls=%async_computation.4 | async-start | bytes 1572864 | tf_op jit(solution)/shard_map/all_to_all | solution.py:737
  329.8 110.0 %collective-permute-start.23 = (bf16[16,128,768]{2,1,0:T(8,128)(2,1)}, bf16[16,128,768]{2,1,0:T(8,128)(2,1)}, u32[]{:S(2)}, u32[]{:S(2)}) collective-permute-start(bf16[16,128,768]{2,1,0:T(8,128)(2,1)} %pad_maximum_fusion.refs_0_), channel_id=1, source_target_pairs={{0,1},{1,0},{2,3},{3,2},{4,5},{5,4},{6,7},{7,6},{8,9},{9,8},{10,11... | collective-permute-start | bytes 9437192 | tf_op jit(solution)/shard_map/ppermute | solution.py:32
  345.6 63.8 %all-to-all-start.5 = ((bf16[8,96,768]{2,1,0:T(8,128)(2,1)}), bf16[8,96,768]{2,1,0:T(8,128)(2,1)S(1)}, u32[]{:S(2)}, u32[]{:S(2)}) async-start(bf16[8,96,768]{2,1,0:T(8,128)(2,1)} %bitcast_add_fusion), calls=%async_computation.5 | async-start | bytes 2359296 | tf_op jit(solution)/shard_map/all_to_all | solution.py:122
  350.5 55.2 %copy-start.28 = (bf16[512,1536]{1,0:T(8,128)(2,1)S(1)}, bf16[512,1536]{1,0:T(8,128)(2,1)}, u32[]{:S(2)}) copy-start(bf16[512,1536]{1,0:T(8,128)(2,1)} %x_ref.1) | copy-start | bytes 4718596
  401.6 6.6 %collective-permute-start.17 = (bf16[8,512,128]{2,1,0:T(8,128)(2,1)}, bf16[8,512,128]{2,1,0:T(8,128)(2,1)S(1)}, u32[]{:S(2)}, u32[]{:S(2)}) collective-permute-start(bf16[8,512,128]{2,1,0:T(8,128)(2,1)} %get-tuple-element.179), channel_id=1, source_target_pairs={{0,2},{2,0},{4,6},{6,4},{8,10},{10,8},{12,14},{14,12},{16,18},{18,... | collective-permute-start | bytes 3145736 | tf_op jit(solution)/shard_map/ppermute | solution.py:32
  406.1 10.0 %copy-start.60 = (f32[512]{0:T(512)}, f32[512]{0:T(512)S(1)}, u32[]{:S(2)}) copy-start(f32[512]{0:T(512)S(1)} %add_rsqrt_fusion) | copy-start | bytes 6148
  409.5 8.6 %copy-start.35 = (bf16[8,96,768]{2,1,0:T(8,128)(2,1)}, bf16[8,96,768]{2,1,0:T(8,128)(2,1)S(1)}, u32[]{:S(2)}) copy-start(bf16[8,96,768]{2,1,0:T(8,128)(2,1)S(1)} %all-to-all-done.5) | copy-start | bytes 3538948
  411.7 28.0 %collective-permute-start.22 = (bf16[1,4,512,128]{3,2,1,0:T(8,128)(2,1)}, bf16[1,4,512,128]{3,2,1,0:T(8,128)(2,1)S(1)}, u32[]{:S(2)}, u32[]{:S(2)}) collective-permute-start(bf16[1,4,512,128]{3,2,1,0:T(8,128)(2,1)} %slice_bitcast_fusion), channel_id=1, source_target_pairs={{0,4},{2,6},{4,0},{6,2},{8,12},{10,14},{12,8},{14,10},{16,20},{18,... | collective-permute-start | bytes 1572872 | tf_op jit(solution)/shard_map/ppermute | solution.py:32
  411.7 11.3 %collective-permute-start.19 = (bf16[512,192]{1,0:T(8,128)(2,1)}, bf16[512,192]{1,0:T(8,128)(2,1)S(1)}, u32[]{:S(2)}, u32[]{:S(2)}) collective-permute-start(bf16[512,192]{1,0:T(8,128)(2,1)} %get-tuple-element.185), channel_id=1, source_target_pairs={{0,24},{2,26},{4,28},{6,30},{8,16},{10,18},{12,20},{14,22},{16,8},... | collective-permute-start | bytes 589832 | tf_op jit(solution)/shard_map/ppermute | solution.py:32
  415.2 23.3 %collective-permute-start.20 = (bf16[512,192]{1,0:T(8,128)(2,1)}, bf16[512,192]{1,0:T(8,128)(2,1)}, u32[]{:S(2)}, u32[]{:S(2)}) collective-permute-start(bf16[512,192]{1,0:T(8,128)(2,1)} %get-tuple-element.186), channel_id=1, source_target_pairs={{0,16},{2,18},{4,20},{6,22},{8,24},{10,26},{12,28},{14,30},{16,0},... | collective-permute-start | bytes 589832 | tf_op jit(solution)/shard_map/ppermute | solution.py:32
  415.2 23.4 %collective-permute-start.21 = (bf16[512,192]{1,0:T(8,128)(2,1)}, bf16[512,192]{1,0:T(8,128)(2,1)}, u32[]{:S(2)}, u32[]{:S(2)}) collective-permute-start(bf16[512,192]{1,0:T(8,128)(2,1)} %get-tuple-element.187), channel_id=1, source_target_pairs={{0,8},{2,10},{4,12},{6,14},{8,0},{10,2},{12,4},{14,6},{16,24},{18,... | collective-permute-start | bytes 589832 | tf_op jit(solution)/shard_map/ppermute | solution.py:32
  418.0 20.5 %copy-start.47 = (bf16[512,192]{1,0:T(8,128)(2,1)S(1)}, bf16[512,192]{1,0:T(8,128)(2,1)}, u32[]{:S(2)}) copy-start(bf16[512,192]{1,0:T(8,128)(2,1)} %get-tuple-element.188) | copy-start | bytes 589828
  420.0 19.8 %copy-start.37 = (bf16[8,512,128]{2,1,0:T(8,128)(2,1)S(1)}, bf16[8,512,128]{2,1,0:T(8,128)(2,1)}, u32[]{:S(2)}) copy-start(bf16[8,512,128]{2,1,0:T(8,128)(2,1)} %add.168) | copy-start | bytes 3145732
  423.0 15.5 %copy-start.49 = (bf16[512,192]{1,0:T(8,128)(2,1)}, bf16[512,192]{1,0:T(8,128)(2,1)S(1)}, u32[]{:S(2)}) copy-start(bf16[512,192]{1,0:T(8,128)(2,1)S(1)} %collective-permute-done.19) | copy-start | bytes 589828
  441.3 26.5 %collective-permute-start.27 = (bf16[256,1536]{1,0:T(8,128)(2,1)S(1)}, bf16[256,1536]{1,0:T(8,128)(2,1)}, u32[]{:S(2)}, u32[]{:S(2)}) collective-permute-start(bf16[256,1536]{1,0:T(8,128)(2,1)S(1)} %dynamic-slice_convert_fusion.1), channel_id=1, source_target_pairs={{0,1},{1,0},{2,3},{3,2},{4,5},{5,4},{6,7},{7,6},{8,9},{9,8},{10,11... | collective-permute-start | bytes 2359304 | tf_op jit(solution)/shard_map/ppermute | solution.py:32
  442.4 21.3 %collective-permute-start.24 = (bf16[512,128]{1,0:T(8,128)(2,1)S(1)}, bf16[512,128]{1,0:T(8,128)(2,1)S(1)}, u32[]{:S(2)}, u32[]{:S(2)}) collective-permute-start(bf16[512,128]{1,0:T(8,128)(2,1)S(1)} %get-tuple-element.278), channel_id=1, source_target_pairs={{0,24},{2,26},{4,28},{6,30},{8,16},{10,18},{12,20},{14,22},{16,8},... | collective-permute-start | bytes 393224 | tf_op jit(solution)/shard_map/ppermute | solution.py:32
  444.8 18.9 %collective-permute-start.25 = (bf16[512,128]{1,0:T(8,128)(2,1)S(1)}, bf16[512,128]{1,0:T(8,128)(2,1)S(1)}, u32[]{:S(2)}, u32[]{:S(2)}) collective-permute-start(bf16[512,128]{1,0:T(8,128)(2,1)S(1)} %get-tuple-element.277), channel_id=1, source_target_pairs={{0,16},{2,18},{4,20},{6,22},{8,24},{10,26},{12,28},{14,30},{16,0},... | collective-permute-start | bytes 393224 | tf_op jit(solution)/shard_map/ppermute | solution.py:32
  444.8 18.9 %collective-permute-start.26 = (bf16[512,128]{1,0:T(8,128)(2,1)S(1)}, bf16[512,128]{1,0:T(8,128)(2,1)S(1)}, u32[]{:S(2)}, u32[]{:S(2)}) collective-permute-start(bf16[512,128]{1,0:T(8,128)(2,1)S(1)} %get-tuple-element.276), channel_id=1, source_target_pairs={{0,8},{2,10},{4,12},{6,14},{8,0},{10,2},{12,4},{14,6},{16,24},{18,... | collective-permute-start | bytes 393224 | tf_op jit(solution)/shard_map/ppermute | solution.py:32
  474.6 23.3 %collective-permute-start.28 = (bf16[8,96,1280]{2,1,0:T(8,128)(2,1)}, bf16[8,96,1280]{2,1,0:T(8,128)(2,1)}, u32[]{:S(2)}, u32[]{:S(2)}) collective-permute-start(bf16[8,96,1280]{2,1,0:T(8,128)(2,1)} %get-tuple-element.208), channel_id=1, source_target_pairs={{0,2},{2,0},{4,6},{6,4},{8,10},{10,8},{12,14},{14,12},{16,18},{18,... | collective-permute-start | bytes 5898248 | tf_op jit(solution)/shard_map/ppermute | solution.py:32
  478.2 16.5 %copy-start.29 = (bf16[512,1536]{1,0:T(8,128)(2,1)S(1)}, bf16[512,1536]{1,0:T(8,128)(2,1)}, u32[]{:S(2)}) copy-start(bf16[512,1536]{1,0:T(8,128)(2,1)} %x_ref.1) | copy-start | bytes 4718596
  482.2 1.9 collective-permute-start.29
  482.2 4.5 collective-permute-start.30
  484.0 4.1 collective-permute-start.31
  488.9 7.9 %collective-permute-start.32 = (bf16[216,128]{1,0:T(8,128)(2,1)S(1)}, bf16[216,128]{1,0:T(8,128)(2,1)S(1)}, u32[]{:S(2)}, u32[]{:S(2)}) collective-permute-start(bf16[216,128]{1,0:T(8,128)(2,1)S(1)} %add_convert_fusion.1), channel_id=1, source_target_pairs={{0,8},{2,10},{4,12},{6,14},{8,0},{10,2},{12,4},{14,6},{16,24},{18,... | collective-permute-start | bytes 165896 | tf_op jit(solution)/shard_map/ppermute | solution.py:32
  489.0 7.9 %collective-permute-start.33 = (bf16[216,128]{1,0:T(8,128)(2,1)S(1)}, bf16[216,128]{1,0:T(8,128)(2,1)S(1)}, u32[]{:S(2)}, u32[]{:S(2)}) collective-permute-start(bf16[216,128]{1,0:T(8,128)(2,1)S(1)} %add_convert_fusion.1), channel_id=1, source_target_pairs={{0,16},{2,18},{4,20},{6,22},{8,24},{10,26},{12,28},{14,30},{16,0},... | collective-permute-start | bytes 165896 | tf_op jit(solution)/shard_map/ppermute | solution.py:32
  491.9 6.0 %collective-permute-start.34 = (bf16[216,128]{1,0:T(8,128)(2,1)S(1)}, bf16[216,128]{1,0:T(8,128)(2,1)S(1)}, u32[]{:S(2)}, u32[]{:S(2)}) collective-permute-start(bf16[216,128]{1,0:T(8,128)(2,1)S(1)} %add_convert_fusion.1), channel_id=1, source_target_pairs={{0,24},{2,26},{4,28},{6,30},{8,16},{10,18},{12,20},{14,22},{16,8},... | collective-permute-start | bytes 165896 | tf_op jit(solution)/shard_map/ppermute | solution.py:32
  501.2 49.1 %all-to-all-start.6 = ((bf16[8,96,1280]{2,1,0:T(8,128)(2,1)}), bf16[8,96,1280]{2,1,0:T(8,128)(2,1)}, u32[]{:S(2)}, u32[]{:S(2)}) async-start(bf16[8,96,1280]{2,1,0:T(8,128)(2,1)} %add.177), calls=%async_computation.6 | async-start | bytes 3932160 | tf_op jit(solution)/shard_map/all_to_all | solution.py:122
  508.3 22.4 %collective-permute-start.36 = (bf16[256,1536]{1,0:T(8,128)(2,1)S(1)}, bf16[256,1536]{1,0:T(8,128)(2,1)S(1)}, u32[]{:S(2)}, u32[]{:S(2)}) collective-permute-start(bf16[256,1536]{1,0:T(8,128)(2,1)S(1)} %dynamic-slice_convert_fusion), channel_id=1, source_target_pairs={{0,1},{1,0},{2,3},{3,2},{4,5},{5,4},{6,7},{7,6},{8,9},{9,8},{10,11... | collective-permute-start | bytes 2359304 | tf_op jit(solution)/shard_map/ppermute | solution.py:32
  509.4 21.2 %collective-permute-start.35 = (bf16[216,128]{1,0:T(8,128)(2,1)S(1)}, bf16[216,128]{1,0:T(8,128)(2,1)S(1)}, u32[]{:S(2)}, u32[]{:S(2)}) collective-permute-start(bf16[216,128]{1,0:T(8,128)(2,1)S(1)} %add_add_fusion.1), channel_id=1, source_target_pairs={{0,1},{1,0},{2,3},{3,2},{4,5},{5,4},{6,7},{7,6},{8,9},{9,8},{10,11... | collective-permute-start | bytes 165896 | tf_op jit(solution)/shard_map/ppermute | solution.py:32
  536.1 17.5 %copy-start.1 = (bf16[768,1536]{1,0:T(8,128)(2,1)S(1)}, bf16[768,1536]{1,0:T(8,128)(2,1)}, u32[]{:S(2)}) copy-start(bf16[768,1536]{1,0:T(8,128)(2,1)} %param.19) | copy-start | bytes 7077892
  (47 other events, 100.9 us)

commit v6 on v5

--- a/solution.py
+++ b/solution.py
@@ -338,17 +338,18 @@
         kv = kv_s[index]
         if masked:
             seen = visible(blk, own, rows, start_ref[0])
-        each = range(heads)
-        scores = [dot(kv, q_s[slot, h], NT) for h in each]
-        grad_probs = [dot(kv, g_s[slot, h], NT) for h in each]
-        if masked:
-            scores = [jnp.where(seen, s, NEG) for s in scores]
-        p = [jnp.exp(scores[h] - log_ref[0, h : h + 1, :]) for h in each]
-        grad_scores = [(p[h] * (grad_probs[h] - delta_s[h : h + 1, :])).astype(BF) for h in each]
-        parts = [dot(grad_scores[h], q_s[slot, h]) + dot(p[h].astype(BF), g_s[slot, h]) for h in each]
-        dkv_s[index] += sum(parts[1:], parts[0])
-        for h in each:
-            dq_s[h] += dot(grad_scores[h], kv, TN)
+        for h in range(heads):
+            q = q_s[slot, h]
+            g = g_s[slot, h]
+            s = dot(kv, q, NT)
+            if masked:
+                s = jnp.where(seen, s, NEG)
+            p = jnp.exp(s - log_ref[0, h : h + 1, :])
+            gp = dot(kv, g, NT)
+            gs = (p * (gp - delta_s[h : h + 1, :])).astype(BF)
+            part = dot(gs, q) + dot(p.astype(BF), g)
+            dkv_s[index] += part
+            dq_s[h] += dot(gs, kv, TN)
 
     walk(low, clear, own, step)
     dq = jnp.concatenate([dq_s[h][:, :HD] * 0.125 for h in range(heads)], 1).astype(BF)
@@ -659,12 +660,9 @@
 
     kv = [jnp.stack(to_lines(kv_mine))]
     q = to_lines(q_mine)
-    g_sent = [half(out_grad, i) for i in range(2)]
-    for turn, bit in enumerate(reversed(bits_of(stride))):
+    for bit in reversed(bits_of(stride)):
         kv = [piece for one in kv for piece in (one, across(one, "dp", bit))]
-        if turn == 0:
-            kv[1], g_sent = after(kv[1], g_sent)
-    g_sent, (kv, q, starts, meta) = after(g_sent, (kv, q, starts, meta))
+    g_sent, (kv, q, starts, meta) = after([half(out_grad, i) for i in range(2)], (kv, q, starts, meta))
     g_first = to_owner(g_sent[0])
     *mixed_far, raw, logs = attend(meta, q, kv, starts[:, None, :], group)
     mixed_far, g_first = after(mixed_far, g_first)

time: 557 us -> 550 us (0.987)
  starting transfers between devices: 101 us -> 92 us
    all_to_all x4, waiting for transfers between devices: 8.45 us -> 14.2 us  [to_owner(): return lax.all_to_all(x, 'dp', 0, 0, tiled=True)]
    unnamed x135 -> x127, local copies, waits for them, and re-layouts: 23.5 us -> 19.1 us
  transfers between devices with their start and end apart: 44 -> 44, of which waited for: 18 -> 17; matrix products, arithmetic and copies ran while one was open for 20% -> 20% of each run, Pallas kernels for 29% -> 30%
where the time goes in v6:
time: 550 us; the launch traced here: 544 us
  Pallas kernels  172 us (31%)
  waiting for transfers between devices  118 us (21%)
  starting transfers between devices  92 us (17%)
  other arithmetic  55.9 us (10%)
  local copies, waits for them, and re-layouts  55.1 us (10%)
  matrix products  45.8 us (8%)
    ppermute x37, waiting for transfers between devices, across(): return lax.ppermute(x, axis, [(i, i ^ mask) for i in range(n)])  82.1 us
    pallas_call x1, Pallas kernels, attend_back(): pl.pallas_call(functools.partial(attend_back_kernel, heads, rows, lines,...  50 us
    pallas_call x1, Pallas kernels, run_experts(): pl.pallas_call(experts_kernel, grid=(experts // at_once,), in_specs=[of(c...  42.4 us
    ppermute x37, starting transfers between devices, across(): return lax.ppermute(x, axis, [(i, i ^ mask) for i in range(n)])  40.8 us
    pallas_call x2, Pallas kernels, owner_call(): pl.pallas_call(functools.partial(kernel, len(x), len(g)), grid_spec=pltpu...  35.7 us
    dot_general x9, matrix products, dot(): return jnp.dot(a, b, preferred_element_type=F32)  35.3 us
    pallas_call x1, Pallas kernels, attend(): pl.pallas_call(functools.partial(attend_kernel, heads, rows, lines, strid...  35 us
    all_to_all x4, starting transfers between devices, to_owner(): return lax.all_to_all(x, 'dp', 0, 0, tiled=True)  33.1 us
  transfers between devices with their start and end apart: 44, of which 17 were waited for; matrix products, arithmetic and copies ran while one was open for 20% of the time, Pallas kernels for 30%

profile of v6, /device:TPU:0, one launch (start us, length us, event | category | flops | bytes accessed | tf_op | source)
XLA Modules:
  0.0 543.9 jit_solution(17427942499136762723)
XLA Ops:
  3.8 5.7 %project.1 = (bf16[512,1536]{1,0:T(8,128)(2,1)S(1)}, bf16[512,128]{1,0:T(8,128)(2,1)S(1)}, bf16[512,128]{1,0:T(8,128)(2,1)S(1)}, bf16[512,128]{1,0:T(8,128)(2,1)...) custom-call(s32[1]{0:T(128)} %bitcast.6.at, ...), custom_call_target="tpu_custom_call" | custom-call | flops 2013265920 | bytes 8388608 | tf_op jit(solution)/shard_map/project/pallas_call | solution.py:152
  11.3 5.0 collective-permute-start.2
  18.4 2.9 collective-permute-start.7
  25.6 3.0 collective-permute-done.1
  32.6 9.3 %collective-permute-done.4.refs_6_.refs_7_ = bf16[4,512,128]{2,1,0:T(8,128)(2,1)} collective-permute-done((bf16[4,512,128]{2,1,0:T(8,128)(2,1)S(1)}, bf16[4,512,128]{2,1,0:T(8,128)(2,1)}, u32[]{:S(2)}, u32[]{:S(2)}) %collective-permute-start.4) | collective-permute-done | bytes 524320 | tf_op jit(solution)/shard_map/ppermute | solution.py:32
  42.0 3.4 convolution_convert_fusion.3
  45.5 3.7 convolution_convert_fusion.4
  49.3 5.0 all-to-all-start
  55.3 35.0 %attend.1 = (bf16[512,192]{1,0:T(8,128)(2,1)S(1)}, bf16[512,192]{1,0:T(8,128)(2,1)S(1)}, bf16[512,192]{1,0:T(8,128)(2,1)S(1)}, bf16[512,192]{1,0:T(8,128)(2,1)S(...) custom-call(s32[13]{0:T(128)S(1)} %pad_add_fusion.1.meta, bf16[512,192]{1,0:T(8,128)(2,1)S(1)} %copy-done.16, ...), custom_call_target="tpu_custom_call" | custom-call | flops 9663676416 | bytes 8388608 | tf_op jit(solution)/shard_map/attend/pallas_call | solution.py:282
  93.0 2.9 collective-permute-start.10
  97.4 7.8 %convolution_convert_fusion.1 = bf16[2048,1536]{1,0:T(8,128)(2,1)} fusion(pred[2048,512]{1,0:T(32,128)(4,1)} %copy-done.38, bf16[512,1536]{1,0:T(8,128)(2,1)} %param.27), kind=kOutput, calls=%fused_computation.1 | convolution fusion | flops 3224371200 | bytes 8912896 | tf_op jit(solution)/shard_map/dot_general | solution.py:26
  105.2 6.8 %collective-permute-done.10 = bf16[512,192]{1,0:T(8,128)(2,1)S(1)} collective-permute-done((bf16[512,192]{1,0:T(8,128)(2,1)}, bf16[512,192]{1,0:T(8,128)(2,1)S(1)}, u32[]{:S(2)}, u32[]{:S(2)}) %collective-permute-start.10) | collective-permute-done | bytes 196640 | tf_op jit(solution)/shard_map/ppermute | solution.py:32
  115.6 1.7 copy-done.35
  118.9 8.6 %all-to-all-start.1 = ((bf16[16,128,384]{2,1,0:T(8,128)(2,1)}), bf16[16,128,384]{2,1,0:T(8,128)(2,1)}, u32[]{:S(2)}, u32[]{:S(2)}) async-start(bf16[16,128,384]{2,1,0:T(8,128)(2,1)} %bitcast.127), calls=%async_computation.1 | async-start | bytes 3145728 | tf_op jit(solution)/shard_map/all_to_all | solution.py:44
  127.6 4.6 collective-permute-done.12
  132.2 2.2 multiply_reduce_fusion.5
  138.8 3.0 constant_dynamic-update-slice_fusion.1
  141.8 10.3 %collective-permute-done.13 = bf16[256,1536]{1,0:T(8,128)(2,1)S(1)} collective-permute-done((bf16[256,1536]{1,0:T(8,128)(2,1)}, bf16[256,1536]{1,0:T(8,128)(2,1)S(1)}, u32[]{:S(2)}, u32[]{:S(2)}) %collective-permute-start.13) | collective-permute-done | bytes 786464 | tf_op jit(solution)/shard_map/ppermute | solution.py:32
  153.7 5.9 %all-to-all-done.1 = bf16[16,128,384]{2,1,0:T(8,128)(2,1)} async-done(((bf16[16,128,384]{2,1,0:T(8,128)(2,1)}), bf16[16,128,384]{2,1,0:T(8,128)(2,1)}, u32[]{:S(2)}, u32[]{:S(2)}) %all-to-all-start.1) | async-done | bytes 1572896 | tf_op jit(solution)/shard_map/all_to_all | solution.py:44
  159.6 2.9 constant_dynamic-update-slice_fusion.refs_2_
  163.1 5.4 convolution_convert_fusion
  170.9 4.1 constant_dynamic-slice_fusion
  175.0 12.6 %all-to-all-start.2 = ((bf16[16,128,384]{2,1,0:T(8,128)(2,1)}), bf16[16,128,384]{2,1,0:T(8,128)(2,1)}, u32[]{:S(2)}, u32[]{:S(2)}) async-start(bf16[16,128,384]{2,1,0:T(8,128)(2,1)} %get-tuple-element.246), calls=%async_computation.2 | async-start | bytes 3145728 | tf_op jit(solution)/shard_map/all_to_all | solution.py:44
  187.6 42.4 %experts.1 = (bf16[16,128,1536]{2,1,0:T(8,128)(2,1)}, bf16[16,128,1536]{2,1,0:T(8,128)(2,1)}, f32[16,8,128]{2,1,0:T(8,128)}) custom-call(bf16[16,128,1536]{2,1,0:T(8,128)(2,1)} %bitcast.121, bf16[16,128,1536]{2,1,0:T(8,128)(2,1)} %bitcast.122, f32[16,128,1]{2,1,0:T(8,128)} %copy.46.gate_ref, bf16[16,1536,512]{2,1,0:T(8,128)(2,1)} %wg_ref.3, ...), custom_call_target="tpu_custom_call" | custom-call | flops 19327352832 | bytes 100663296 | tf_op jit(solution)/shard_map/experts/pallas_call | solution.py:440
  230.8 2.6 select_reduce_fusion
  233.5 3.1 fusion.47
  236.6 7.3 %fusion.11 = f32[512,1536]{1,0:T(8,128)S(1)} fusion(f32[512,1536]{1,0:T(8,128)} %fusion.47, bf16[16,128,1536]{2,1,0:T(8,128)(2,1)} %get-tuple-element.162, s32[512,16]{0,1:T(8,128)S(1)} %copy-done.48), kind=kOutput, calls=%fused_computation.21 | convolution fusion | flops 3223060480 | bytes 12615680 | tf_op jit(solution)/shard_map/dot_general | solution.py:26
  247.1 4.8 fusion.10
  252.3 3.0 fusion.12
  255.3 6.9 %all-to-all-start.3 = ((bf16[16,128,512]{2,1,0:T(8,128)(2,1)}), bf16[16,128,512]{2,1,0:T(8,128)(2,1)}, u32[]{:S(2)}, u32[]{:S(2)}) async-start(bf16[16,128,512]{2,1,0:T(8,128)(2,1)} %fusion.12), calls=%async_computation.3 | async-start | bytes 4194304 | tf_op jit(solution)/shard_map/all_to_all | solution.py:44
  262.2 4.6 collective-permute-done.15
  266.8 1.8 convert_add_fusion.2
  271.8 18.8 %collective-permute-done.16 = bf16[256,1536]{1,0:T(8,128)(2,1)} collective-permute-done((bf16[256,1536]{1,0:T(8,128)(2,1)S(1)}, bf16[256,1536]{1,0:T(8,128)(2,1)}, u32[]{:S(2)}, u32[]{:S(2)}) %collective-permute-start.16) | collective-permute-done | bytes 786464 | tf_op jit(solution)/shard_map/ppermute | solution.py:32
  295.0 8.4 %all-to-all-done.3 = bf16[16,128,512]{2,1,0:T(8,128)(2,1)} async-done(((bf16[16,128,512]{2,1,0:T(8,128)(2,1)}), bf16[16,128,512]{2,1,0:T(8,128)(2,1)}, u32[]{:S(2)}, u32[]{:S(2)}) %all-to-all-start.3) | async-done | bytes 2097184 | tf_op jit(solution)/shard_map/all_to_all | solution.py:44
  303.3 3.0 convolution_convert_fusion.2
  309.5 9.9 %all-to-all-start.4 = ((bf16[4,512,192]{1,2,0:T(8,128)(2,1)}), bf16[4,512,192]{1,2,0:T(8,128)(2,1)S(1)}, u32[]{:S(2)}, u32[]{:S(2)}) async-start(bf16[4,512,192]{1,2,0:T(8,128)(2,1)} %copy.48), calls=%async_computation.4 | async-start | bytes 1572864 | tf_op jit(solution)/shard_map/all_to_all | solution.py:735
  320.9 3.4 pad_maximum_fusion.refs_0_
  325.3 2.4 bitcast_add_fusion
  327.7 12.4 %all-to-all-done.4 = bf16[4,512,192]{1,2,0:T(8,128)(2,1)S(1)} async-done(((bf16[4,512,192]{1,2,0:T(8,128)(2,1)}), bf16[4,512,192]{1,2,0:T(8,128)(2,1)S(1)}, u32[]{:S(2)}, u32[]{:S(2)}) %all-to-all-start.4) | async-done | bytes 786464 | tf_op jit(solution)/shard_map/all_to_all | solution.py:735
  340.1 3.6 all-to-all-start.5
  345.0 50.0 %attend_back.1 = (bf16[512,192]{1,0:T(8,128)(2,1)}, bf16[512,192]{1,0:T(8,128)(2,1)}, bf16[512,192]{1,0:T(8,128)(2,1)}, bf16[512,192]{1,0:T(8,128)(2,1)}, bf16[8...) custom-call(s32[13]{0:T(128)} %copy-done.4, bf16[512,192]{1,0:T(8,128)(2,1)} %copy-done.15, ...), custom_call_target="tpu_custom_call" | custom-call | flops 24159191040 | bytes 10485760 | tf_op jit(solution)/shard_map/attend_back/pallas_call | solution.py:376
  395.5 2.4 collective-permute-done.17
  399.2 2.2 slice_bitcast_fusion
  401.5 3.7 collective-permute-start.19
  405.9 1.9 broadcast_multiply_fusion
  412.7 15.6 %collective-permute-done.20 = bf16[512,192]{1,0:T(8,128)(2,1)} collective-permute-done((bf16[512,192]{1,0:T(8,128)(2,1)}, bf16[512,192]{1,0:T(8,128)(2,1)}, u32[]{:S(2)}, u32[]{:S(2)}) %collective-permute-start.20) | collective-permute-done | bytes 196640 | tf_op jit(solution)/shard_map/ppermute | solution.py:32
  432.2 2.4 collective-permute-start.24
  434.7 2.0 collective-permute-start.26
  436.7 16.8 %owner_forward.1 = (bf16[2048,512]{1,0:T(8,128)(2,1)}, bf16[2048,512]{1,0:T(8,128)(2,1)}, bf16[2048,512]{1,0:T(8,128)(2,1)}) custom-call(s32[5]{0:T(128)} %stack.81.at, f32[2048,1]{1,0:T(8,128)} %copy.50.gate_ref, bf16[16,1536,512]{2,1,0:T(8,128)(2,1)} %wg_ref.3, bf16[16,1536,512]{2,1,0:T(8,128)(2,1)} %wu_ref.3, bf16[16,512,1536]{2,1,0:T(8,128)(2,1)} %wd_ref.3, ...), custom_call_target="tpu_custom_call" | custom-call | flops 10737418240 | bytes 25165824 | tf_op jit(solution)/shard_map/owner_forward/pallas_call | solution.py:568
  455.2 2.5 concatenate.38.b_ref
  457.7 3.1 convert_add_fusion.1
  460.9 3.5 weights.1
  465.8 2.2 fusion.3
  472.1 1.7 collective-permute-start.30
  474.0 2.6 collective-permute-done.30
  478.8 2.9 collective-permute-start.33
  484.5 2.2 convert_element_type.150
  487.7 3.3 add.177
  491.1 4.7 all-to-all-start.6
  501.6 18.9 %owner_grads.1 = (f32[1,1536,512]{2,1,0:T(8,128)}, f32[1,1536,512]{2,1,0:T(8,128)}, f32[1,512,1536]{2,1,0:T(8,128)}) custom-call(s32[5]{0:T(128)} %stack.81.at, f32[2048,1]{1,0:T(8,128)} %copy.51.gate_ref, bf16[2048,512]{1,0:T(8,128)(2,1)} %get-tuple-element.217.act_ref, bf16[2048,512]{1,0:T(8,128)(2,1)} %get-tuple-element.218.grad_gate_ref, ...), custom_call_target="tpu_custom_call" | custom-call | flops 10737418240 | bytes 25165824 | tf_op jit(solution)/shard_map/owner_grads/pallas_call | solution.py:568
  523.4 1.9 multiply_reduce_fusion.2
  526.0 5.0 multiply_add_fusion
  531.0 9.2 %all-to-all-done.6 = bf16[8,96,1280]{2,1,0:T(8,128)(2,1)} async-done(((bf16[8,96,1280]{2,1,0:T(8,128)(2,1)}), bf16[8,96,1280]{2,1,0:T(8,128)(2,1)}, u32[]{:S(2)}, u32[]{:S(2)}) %all-to-all-start.6) | async-done | bytes 1966112 | tf_op jit(solution)/shard_map/all_to_all | solution.py:122
  540.2 1.9 convert_reduce_fusion
  (266 shorter events, 86.0 us)
Async XLA Ops:
  0.6 113.6 %copy-start = (bf16[768,1536]{1,0:T(8,128)(2,1)S(1)}, bf16[768,1536]{1,0:T(8,128)(2,1)}, u32[]{:S(2)}) copy-start(bf16[768,1536]{1,0:T(8,128)(2,1)} %param.19) | copy-start | bytes 7077892
  3.8 20.8 %copy-start.60 = (s32[512,2]{0,1:T(2,128)S(1)}, s32[512,2]{0,1:T(2,128)}, u32[]{:S(2)}) copy-start(s32[512,2]{0,1:T(2,128)} %param.26) | copy-start | bytes 12292
  11.3 14.3 %collective-permute-start.2 = (bf16[512,128]{1,0:T(8,128)(2,1)S(1)}, bf16[512,128]{1,0:T(8,128)(2,1)S(1)}, u32[]{:S(2)}, u32[]{:S(2)}) collective-permute-start(bf16[512,128]{1,0:T(8,128)(2,1)S(1)} %get-tuple-element.129), channel_id=1, source_target_pairs={{0,24},{2,26},{4,28},{6,30},{8,16},{10,18},{12,20},{14,22},{16,8},... | collective-permute-start | bytes 393224 | tf_op jit(solution)/shard_map/ppermute | solution.py:32
  16.4 9.2 %collective-permute-start = (bf16[512,128]{1,0:T(8,128)(2,1)S(1)}, bf16[512,128]{1,0:T(8,128)(2,1)}, u32[]{:S(2)}, u32[]{:S(2)}) collective-permute-start(bf16[512,128]{1,0:T(8,128)(2,1)S(1)} %get-tuple-element.127), channel_id=1, source_target_pairs={{0,8},{2,10},{4,12},{6,14},{8,0},{10,2},{12,4},{14,6},{16,24},{18,... | collective-permute-start | bytes 393224 | tf_op jit(solution)/shard_map/ppermute | solution.py:32
  16.4 12.2 %collective-permute-start.1 = (bf16[512,128]{1,0:T(8,128)(2,1)S(1)}, bf16[512,128]{1,0:T(8,128)(2,1)}, u32[]{:S(2)}, u32[]{:S(2)}) collective-permute-start(bf16[512,128]{1,0:T(8,128)(2,1)S(1)} %get-tuple-element.128), channel_id=1, source_target_pairs={{0,16},{2,18},{4,20},{6,22},{8,24},{10,26},{12,28},{14,30},{16,0},... | collective-permute-start | bytes 393224 | tf_op jit(solution)/shard_map/ppermute | solution.py:32
  17.0 32.3 %collective-permute-start.6 = (bf16[512,192]{1,0:T(8,128)(2,1)}, bf16[512,192]{1,0:T(8,128)(2,1)S(1)}, u32[]{:S(2)}, u32[]{:S(2)}) collective-permute-start(bf16[512,192]{1,0:T(8,128)(2,1)} %get-tuple-element.131), channel_id=1, source_target_pairs={{0,8},{2,10},{4,12},{6,14},{8,0},{10,2},{12,4},{14,6},{16,24},{18,... | collective-permute-start | bytes 589832 | tf_op jit(solution)/shard_map/ppermute | solution.py:32
  18.4 30.8 %collective-permute-start.7 = (bf16[512,192]{1,0:T(8,128)(2,1)}, bf16[512,192]{1,0:T(8,128)(2,1)}, u32[]{:S(2)}, u32[]{:S(2)}) collective-permute-start(bf16[512,192]{1,0:T(8,128)(2,1)} %get-tuple-element.132), channel_id=1, source_target_pairs={{0,16},{2,18},{4,20},{6,22},{8,24},{10,26},{12,28},{14,30},{16,0},... | collective-permute-start | bytes 589832 | tf_op jit(solution)/shard_map/ppermute | solution.py:32
  23.9 8.2 %copy-start.51 = (s32[8192]{0:T(1024)S(1)}, s32[8192]{0:T(1024)}, u32[]{:S(2)}) copy-start(s32[8192]{0:T(1024)} %param.25) | copy-start | bytes 98308
  25.6 23.6 %collective-permute-start.8 = (bf16[512,192]{1,0:T(8,128)(2,1)}, bf16[512,192]{1,0:T(8,128)(2,1)}, u32[]{:S(2)}, u32[]{:S(2)}) collective-permute-start(bf16[512,192]{1,0:T(8,128)(2,1)} %get-tuple-element.133), channel_id=1, source_target_pairs={{0,24},{2,26},{4,28},{6,30},{8,16},{10,18},{12,20},{14,22},{16,8},... | collective-permute-start | bytes 589832 | tf_op jit(solution)/shard_map/ppermute | solution.py:32
  29.7 24.5 %copy-start.2 = (bf16[4,512,128]{2,1,0:T(8,128)(2,1)}, bf16[4,512,128]{2,1,0:T(8,128)(2,1)S(1)}, u32[]{:S(2)}) copy-start(bf16[4,512,128]{2,1,0:T(8,128)(2,1)S(1)} %pad_maximum_fusion.5.refs_4_.refs_5_) | copy-start | bytes 1572868
  29.7 12.1 %collective-permute-start.4 = (bf16[4,512,128]{2,1,0:T(8,128)(2,1)S(1)}, bf16[4,512,128]{2,1,0:T(8,128)(2,1)}, u32[]{:S(2)}, u32[]{:S(2)}) collective-permute-start(bf16[4,512,128]{2,1,0:T(8,128)(2,1)S(1)} %pad_maximum_fusion.5.refs_4_.refs_5_), channel_id=1, source_target_pairs={{0,4},{2,6},{4,0},{6,2},{8,12},{10,14},{12,8},{14,10},{16,20},{18,... | collective-permute-start | bytes 1572872 | tf_op jit(solution)/shard_map/ppermute | solution.py:32
  32.1 13.4 %copy-start.38 = (pred[2048,512]{1,0:T(32,128)(4,1)}, pred[2048,512]{1,0:T(32,128)(4,1)S(1)}, u32[]{:S(2)}) copy-start(pred[2048,512]{1,0:T(32,128)(4,1)S(1)} %bitcast_compare_fusion) | copy-start | bytes 3145732
  32.5 16.8 %collective-permute-start.3 = (bf16[4,512,128]{2,1,0:T(8,128)(2,1)S(1)}, bf16[4,512,128]{2,1,0:T(8,128)(2,1)}, u32[]{:S(2)}, u32[]{:S(2)}) collective-permute-start(bf16[4,512,128]{2,1,0:T(8,128)(2,1)S(1)} %pad_maximum_fusion.5.refs_4_.refs_5_), channel_id=1, source_target_pairs={{0,2},{2,0},{4,6},{6,4},{8,10},{10,8},{12,14},{14,12},{16,18},{18,... | collective-permute-start | bytes 1572872 | tf_op jit(solution)/shard_map/ppermute | solution.py:32
  41.8 7.4 %collective-permute-start.5 = (bf16[4,512,128]{2,1,0:T(8,128)(2,1)}, bf16[4,512,128]{2,1,0:T(8,128)(2,1)}, u32[]{:S(2)}, u32[]{:S(2)}) collective-permute-start(bf16[4,512,128]{2,1,0:T(8,128)(2,1)} %collective-permute-done.4.refs_6_.refs_7_), channel_id=1, source_target_pairs={{0,2},{2,0},{4,6},{6,4},{8,10},{10,8},{12,14},{14,12},{16,18},{18,... | collective-permute-start | bytes 1572872 | tf_op jit(solution)/shard_map/ppermute | solution.py:32
  45.5 8.8 %copy-start.4 = (s32[13]{0:T(128)}, s32[13]{0:T(128)S(1)}, u32[]{:S(2)}) copy-start(s32[13]{0:T(128)S(1)} %pad_add_fusion.1.meta) | copy-start | bytes 160
  49.3 43.8 %all-to-all-start = ((bf16[16,128,384]{2,1,0:T(8,128)(2,1)}), bf16[16,128,384]{2,1,0:T(8,128)(2,1)}, u32[]{:S(2)}, u32[]{:S(2)}) async-start(bf16[16,128,384]{2,1,0:T(8,128)(2,1)} %bitcast.128), calls=%async_computation | async-start | bytes 3145728 | tf_op jit(solution)/shard_map/all_to_all | solution.py:44
  55.3 35.0 %copy-start.3 = (s32[4,1,512]{2,1,0:T(1,128)}, s32[4,1,512]{2,1,0:T(1,128)S(1)}, u32[]{:S(2)}) copy-start(s32[4,1,512]{2,1,0:T(1,128)S(1)} %broadcast_in_dim.118.refs_8_.refs_11_) | copy-start | bytes 24580
  93.0 19.0 %collective-permute-start.10 = (bf16[512,192]{1,0:T(8,128)(2,1)}, bf16[512,192]{1,0:T(8,128)(2,1)S(1)}, u32[]{:S(2)}, u32[]{:S(2)}) collective-permute-start(bf16[512,192]{1,0:T(8,128)(2,1)} %copy-done.12), channel_id=1, source_target_pairs={{0,16},{2,18},{4,20},{6,22},{8,24},{10,26},{12,28},{14,30},{16,0},... | collective-permute-start | bytes 589832 | tf_op jit(solution)/shard_map/ppermute | solution.py:32
  96.0 16.1 %collective-permute-start.11 = (bf16[512,192]{1,0:T(8,128)(2,1)}, bf16[512,192]{1,0:T(8,128)(2,1)S(1)}, u32[]{:S(2)}, u32[]{:S(2)}) collective-permute-start(bf16[512,192]{1,0:T(8,128)(2,1)} %copy-done.11), channel_id=1, source_target_pairs={{0,8},{2,10},{4,12},{6,14},{8,0},{10,2},{12,4},{14,6},{16,24},{18,... | collective-permute-start | bytes 589832 | tf_op jit(solution)/shard_map/ppermute | solution.py:32
  97.4 15.3 %collective-permute-start.9 = (bf16[512,192]{1,0:T(8,128)(2,1)}, bf16[512,192]{1,0:T(8,128)(2,1)}, u32[]{:S(2)}, u32[]{:S(2)}) collective-permute-start(bf16[512,192]{1,0:T(8,128)(2,1)} %copy-done.10), channel_id=1, source_target_pairs={{0,24},{2,26},{4,28},{6,30},{8,16},{10,18},{12,20},{14,22},{16,8},... | collective-permute-start | bytes 589832 | tf_op jit(solution)/shard_map/ppermute | solution.py:32
  117.4 14.8 %collective-permute-start.12 = (bf16[256,1536]{1,0:T(8,128)(2,1)S(1)}, bf16[256,1536]{1,0:T(8,128)(2,1)}, u32[]{:S(2)}, u32[]{:S(2)}) collective-permute-start(bf16[256,1536]{1,0:T(8,128)(2,1)S(1)} %dynamic-slice_convert_fusion.3), channel_id=1, source_target_pairs={{0,1},{1,0},{2,3},{3,2},{4,5},{5,4},{6,7},{7,6},{8,9},{9,8},{10,11... | collective-permute-start | bytes 2359304 | tf_op jit(solution)/shard_map/ppermute | solution.py:32
  118.9 40.6 %all-to-all-start.1 = ((bf16[16,128,384]{2,1,0:T(8,128)(2,1)}), bf16[16,128,384]{2,1,0:T(8,128)(2,1)}, u32[]{:S(2)}, u32[]{:S(2)}) async-start(bf16[16,128,384]{2,1,0:T(8,128)(2,1)} %bitcast.127), calls=%async_computation.1 | async-start | bytes 3145728 | tf_op jit(solution)/shard_map/all_to_all | solution.py:44
  134.5 135.3 %copy-start.52 = (f32[256]{0:T(256)}, f32[256]{0:T(256)S(1)}, u32[]{:S(2)}) copy-start(f32[256]{0:T(256)S(1)} %add_rsqrt_fusion.1) | copy-start | bytes 3076
  136.6 15.4 %collective-permute-start.13 = (bf16[256,1536]{1,0:T(8,128)(2,1)}, bf16[256,1536]{1,0:T(8,128)(2,1)S(1)}, u32[]{:S(2)}, u32[]{:S(2)}) collective-permute-start(bf16[256,1536]{1,0:T(8,128)(2,1)} %multiply_convert_fusion), channel_id=1, source_target_pairs={{0,1},{1,0},{2,3},{3,2},{4,5},{5,4},{6,7},{7,6},{8,9},{9,8},{10,11... | collective-permute-start | bytes 2359304 | tf_op jit(solution)/shard_map/ppermute | solution.py:32
  138.8 13.3 %copy-start.19 = (f32[256,1536]{1,0:T(8,128)S(1)}, f32[256,1536]{1,0:T(8,128)}, u32[]{:S(2)}) copy-start(f32[256,1536]{1,0:T(8,128)} %copy-done.18) | copy-start | bytes 4718596
  153.7 9.3 %copy-start.39 = (pred[2048,512]{1,0:T(32,128)(4,1)S(1)}, pred[2048,512]{1,0:T(32,128)(4,1)}, u32[]{:S(2)}) copy-start(pred[2048,512]{1,0:T(32,128)(4,1)} %copy-done.38) | copy-start | bytes 3145732
  162.5 74.1 %collective-permute-start.14 = (bf16[16,128,768]{2,1,0:T(8,128)(2,1)}, bf16[16,128,768]{2,1,0:T(8,128)(2,1)}, u32[]{:S(2)}, u32[]{:S(2)}) collective-permute-start(bf16[16,128,768]{2,1,0:T(8,128)(2,1)} %constant_dynamic-update-slice_fusion.refs_2_), channel_id=1, source_target_pairs={{0,1},{1,0},{2,3},{3,2},{4,5},{5,4},{6,7},{7,6},{8,9},{9,8},{10,11... | collective-permute-start | bytes 9437192 | tf_op jit(solution)/shard_map/ppermute | solution.py:32
  175.0 61.7 %all-to-all-start.2 = ((bf16[16,128,384]{2,1,0:T(8,128)(2,1)}), bf16[16,128,384]{2,1,0:T(8,128)(2,1)}, u32[]{:S(2)}, u32[]{:S(2)}) async-start(bf16[16,128,384]{2,1,0:T(8,128)(2,1)} %get-tuple-element.246), calls=%async_computation.2 | async-start | bytes 3145728 | tf_op jit(solution)/shard_map/all_to_all | solution.py:44
  187.6 43.3 %copy-start.48 = (s32[512,16]{0,1:T(8,128)S(1)}, s32[512,16]{0,1:T(8,128)}, u32[]{:S(2)}) copy-start(s32[512,16]{0,1:T(8,128)} %broadcast_select_fusion.26) | copy-start | bytes 98308
  236.6 10.5 %copy-start.61 = (bf16[16,128,1536]{2,1,0:T(8,128)(2,1)S(1)}, bf16[16,128,1536]{2,1,0:T(8,128)(2,1)}, u32[]{:S(2)}) copy-start(bf16[16,128,1536]{2,1,0:T(8,128)(2,1)} %get-tuple-element.164) | copy-start | bytes 18874372
  246.6 20.3 %collective-permute-start.15 = (bf16[256,1536]{1,0:T(8,128)(2,1)}, bf16[256,1536]{1,0:T(8,128)(2,1)}, u32[]{:S(2)}, u32[]{:S(2)}) collective-permute-start(bf16[256,1536]{1,0:T(8,128)(2,1)} %dynamic-slice_convert_fusion.2), channel_id=1, source_target_pairs={{0,1},{1,0},{2,3},{3,2},{4,5},{5,4},{6,7},{7,6},{8,9},{9,8},{10,11... | collective-permute-start | bytes 2359304 | tf_op jit(solution)/shard_map/ppermute | solution.py:32
  255.3 48.0 %all-to-all-start.3 = ((bf16[16,128,512]{2,1,0:T(8,128)(2,1)}), bf16[16,128,512]{2,1,0:T(8,128)(2,1)}, u32[]{:S(2)}, u32[]{:S(2)}) async-start(bf16[16,128,512]{2,1,0:T(8,128)(2,1)} %fusion.12), calls=%async_computation.3 | async-start | bytes 4194304 | tf_op jit(solution)/shard_map/all_to_all | solution.py:44
  271.3 19.3 %collective-permute-start.16 = (bf16[256,1536]{1,0:T(8,128)(2,1)S(1)}, bf16[256,1536]{1,0:T(8,128)(2,1)}, u32[]{:S(2)}, u32[]{:S(2)}) collective-permute-start(bf16[256,1536]{1,0:T(8,128)(2,1)S(1)} %fusion.38), channel_id=1, source_target_pairs={{0,1},{1,0},{2,3},{3,2},{4,5},{5,4},{6,7},{7,6},{8,9},{9,8},{10,11... | collective-permute-start | bytes 2359304 | tf_op jit(solution)/shard_map/ppermute | solution.py:32
  307.5 17.8 %collective-permute-start.18 = (bf16[8,96,768]{2,1,0:T(8,128)(2,1)}, bf16[8,96,768]{2,1,0:T(8,128)(2,1)}, u32[]{:S(2)}, u32[]{:S(2)}) collective-permute-start(bf16[8,96,768]{2,1,0:T(8,128)(2,1)} %dynamic-slice_bitcast_fusion), channel_id=1, source_target_pairs={{0,2},{2,0},{4,6},{6,4},{8,10},{10,8},{12,14},{14,12},{16,18},{18,... | collective-permute-start | bytes 3538952 | tf_op jit(solution)/shard_map/ppermute | solution.py:32
  309.5 30.6 %all-to-all-start.4 = ((bf16[4,512,192]{1,2,0:T(8,128)(2,1)}), bf16[4,512,192]{1,2,0:T(8,128)(2,1)S(1)}, u32[]{:S(2)}, u32[]{:S(2)}) async-start(bf16[4,512,192]{1,2,0:T(8,128)(2,1)} %copy.48), calls=%async_computation.4 | async-start | bytes 1572864 | tf_op jit(solution)/shard_map/all_to_all | solution.py:735
  324.3 105.3 %collective-permute-start.23 = (bf16[16,128,768]{2,1,0:T(8,128)(2,1)}, bf16[16,128,768]{2,1,0:T(8,128)(2,1)}, u32[]{:S(2)}, u32[]{:S(2)}) collective-permute-start(bf16[16,128,768]{2,1,0:T(8,128)(2,1)} %pad_maximum_fusion.refs_0_), channel_id=1, source_target_pairs={{0,1},{1,0},{2,3},{3,2},{4,5},{5,4},{6,7},{7,6},{8,9},{9,8},{10,11... | collective-permute-start | bytes 9437192 | tf_op jit(solution)/shard_map/ppermute | solution.py:32
  340.1 59.1 %all-to-all-start.5 = ((bf16[8,96,768]{2,1,0:T(8,128)(2,1)}), bf16[8,96,768]{2,1,0:T(8,128)(2,1)S(1)}, u32[]{:S(2)}, u32[]{:S(2)}) async-start(bf16[8,96,768]{2,1,0:T(8,128)(2,1)} %bitcast_add_fusion), calls=%async_computation.5 | async-start | bytes 2359296 | tf_op jit(solution)/shard_map/all_to_all | solution.py:122
  345.0 50.1 %copy-start.24 = (bf16[512,1536]{1,0:T(8,128)(2,1)S(1)}, bf16[512,1536]{1,0:T(8,128)(2,1)}, u32[]{:S(2)}) copy-start(bf16[512,1536]{1,0:T(8,128)(2,1)} %x_ref.1) | copy-start | bytes 4718596
  395.0 2.9 collective-permute-start.17
  395.5 10.3 %copy-start.56 = (f32[512]{0:T(512)}, f32[512]{0:T(512)S(1)}, u32[]{:S(2)}) copy-start(f32[512]{0:T(512)S(1)} %add_rsqrt_fusion) | copy-start | bytes 6148
  399.2 8.6 %copy-start.31 = (bf16[8,96,768]{2,1,0:T(8,128)(2,1)}, bf16[8,96,768]{2,1,0:T(8,128)(2,1)S(1)}, u32[]{:S(2)}) copy-start(bf16[8,96,768]{2,1,0:T(8,128)(2,1)S(1)} %all-to-all-done.5) | copy-start | bytes 3538948
  401.5 28.1 %collective-permute-start.22 = (bf16[1,4,512,128]{3,2,1,0:T(8,128)(2,1)}, bf16[1,4,512,128]{3,2,1,0:T(8,128)(2,1)S(1)}, u32[]{:S(2)}, u32[]{:S(2)}) collective-permute-start(bf16[1,4,512,128]{3,2,1,0:T(8,128)(2,1)} %slice_bitcast_fusion), channel_id=1, source_target_pairs={{0,4},{2,6},{4,0},{6,2},{8,12},{10,14},{12,8},{14,10},{16,20},{18,... | collective-permute-start | bytes 1572872 | tf_op jit(solution)/shard_map/ppermute | solution.py:32
  401.5 11.3 %collective-permute-start.19 = (bf16[512,192]{1,0:T(8,128)(2,1)}, bf16[512,192]{1,0:T(8,128)(2,1)S(1)}, u32[]{:S(2)}, u32[]{:S(2)}) collective-permute-start(bf16[512,192]{1,0:T(8,128)(2,1)} %get-tuple-element.179), channel_id=1, source_target_pairs={{0,24},{2,26},{4,28},{6,30},{8,16},{10,18},{12,20},{14,22},{16,8},... | collective-permute-start | bytes 589832 | tf_op jit(solution)/shard_map/ppermute | solution.py:32
  405.2 23.1 %collective-permute-start.20 = (bf16[512,192]{1,0:T(8,128)(2,1)}, bf16[512,192]{1,0:T(8,128)(2,1)}, u32[]{:S(2)}, u32[]{:S(2)}) collective-permute-start(bf16[512,192]{1,0:T(8,128)(2,1)} %get-tuple-element.180), channel_id=1, source_target_pairs={{0,16},{2,18},{4,20},{6,22},{8,24},{10,26},{12,28},{14,30},{16,0},... | collective-permute-start | bytes 589832 | tf_op jit(solution)/shard_map/ppermute | solution.py:32
  405.2 23.1 %collective-permute-start.21 = (bf16[512,192]{1,0:T(8,128)(2,1)}, bf16[512,192]{1,0:T(8,128)(2,1)}, u32[]{:S(2)}, u32[]{:S(2)}) collective-permute-start(bf16[512,192]{1,0:T(8,128)(2,1)} %get-tuple-element.181), channel_id=1, source_target_pairs={{0,8},{2,10},{4,12},{6,14},{8,0},{10,2},{12,4},{14,6},{16,24},{18,... | collective-permute-start | bytes 589832 | tf_op jit(solution)/shard_map/ppermute | solution.py:32
  407.8 20.6 %copy-start.43 = (bf16[512,192]{1,0:T(8,128)(2,1)S(1)}, bf16[512,192]{1,0:T(8,128)(2,1)}, u32[]{:S(2)}) copy-start(bf16[512,192]{1,0:T(8,128)(2,1)} %get-tuple-element.182) | copy-start | bytes 589828
  409.7 19.8 %copy-start.33 = (bf16[8,512,128]{2,1,0:T(8,128)(2,1)S(1)}, bf16[8,512,128]{2,1,0:T(8,128)(2,1)}, u32[]{:S(2)}) copy-start(bf16[8,512,128]{2,1,0:T(8,128)(2,1)} %add.168) | copy-start | bytes 3145732
  412.7 15.6 %copy-start.45 = (bf16[512,192]{1,0:T(8,128)(2,1)}, bf16[512,192]{1,0:T(8,128)(2,1)S(1)}, u32[]{:S(2)}) copy-start(bf16[512,192]{1,0:T(8,128)(2,1)S(1)} %collective-permute-done.19) | copy-start | bytes 589828
  431.1 26.6 %collective-permute-start.27 = (bf16[256,1536]{1,0:T(8,128)(2,1)S(1)}, bf16[256,1536]{1,0:T(8,128)(2,1)}, u32[]{:S(2)}, u32[]{:S(2)}) collective-permute-start(bf16[256,1536]{1,0:T(8,128)(2,1)S(1)} %dynamic-slice_convert_fusion.1), channel_id=1, source_target_pairs={{0,1},{1,0},{2,3},{3,2},{4,5},{5,4},{6,7},{7,6},{8,9},{9,8},{10,11... | collective-permute-start | bytes 2359304 | tf_op jit(solution)/shard_map/ppermute | solution.py:32
  432.2 21.3 %collective-permute-start.24 = (bf16[512,128]{1,0:T(8,128)(2,1)S(1)}, bf16[512,128]{1,0:T(8,128)(2,1)S(1)}, u32[]{:S(2)}, u32[]{:S(2)}) collective-permute-start(bf16[512,128]{1,0:T(8,128)(2,1)S(1)} %get-tuple-element.272), channel_id=1, source_target_pairs={{0,24},{2,26},{4,28},{6,30},{8,16},{10,18},{12,20},{14,22},{16,8},... | collective-permute-start | bytes 393224 | tf_op jit(solution)/shard_map/ppermute | solution.py:32
  434.7 18.8 %collective-permute-start.25 = (bf16[512,128]{1,0:T(8,128)(2,1)S(1)}, bf16[512,128]{1,0:T(8,128)(2,1)S(1)}, u32[]{:S(2)}, u32[]{:S(2)}) collective-permute-start(bf16[512,128]{1,0:T(8,128)(2,1)S(1)} %get-tuple-element.271), channel_id=1, source_target_pairs={{0,16},{2,18},{4,20},{6,22},{8,24},{10,26},{12,28},{14,30},{16,0},... | collective-permute-start | bytes 393224 | tf_op jit(solution)/shard_map/ppermute | solution.py:32
  434.7 18.8 %collective-permute-start.26 = (bf16[512,128]{1,0:T(8,128)(2,1)S(1)}, bf16[512,128]{1,0:T(8,128)(2,1)S(1)}, u32[]{:S(2)}, u32[]{:S(2)}) collective-permute-start(bf16[512,128]{1,0:T(8,128)(2,1)S(1)} %get-tuple-element.270), channel_id=1, source_target_pairs={{0,8},{2,10},{4,12},{6,14},{8,0},{10,2},{12,4},{14,6},{16,24},{18,... | collective-permute-start | bytes 393224 | tf_op jit(solution)/shard_map/ppermute | solution.py:32
  464.4 23.3 %collective-permute-start.28 = (bf16[8,96,1280]{2,1,0:T(8,128)(2,1)}, bf16[8,96,1280]{2,1,0:T(8,128)(2,1)}, u32[]{:S(2)}, u32[]{:S(2)}) collective-permute-start(bf16[8,96,1280]{2,1,0:T(8,128)(2,1)} %get-tuple-element.202), channel_id=1, source_target_pairs={{0,2},{2,0},{4,6},{6,4},{8,10},{10,8},{12,14},{14,12},{16,18},{18,... | collective-permute-start | bytes 5898248 | tf_op jit(solution)/shard_map/ppermute | solution.py:32
  468.0 16.5 %copy-start.25 = (bf16[512,1536]{1,0:T(8,128)(2,1)S(1)}, bf16[512,1536]{1,0:T(8,128)(2,1)}, u32[]{:S(2)}) copy-start(bf16[512,1536]{1,0:T(8,128)(2,1)} %x_ref.1) | copy-start | bytes 4718596
  472.1 1.9 collective-permute-start.29
  472.1 4.5 collective-permute-start.30
  473.8 4.1 collective-permute-start.31
  478.7 7.9 %collective-permute-start.32 = (bf16[216,128]{1,0:T(8,128)(2,1)S(1)}, bf16[216,128]{1,0:T(8,128)(2,1)S(1)}, u32[]{:S(2)}, u32[]{:S(2)}) collective-permute-start(bf16[216,128]{1,0:T(8,128)(2,1)S(1)} %add_convert_fusion.1), channel_id=1, source_target_pairs={{0,8},{2,10},{4,12},{6,14},{8,0},{10,2},{12,4},{14,6},{16,24},{18,... | collective-permute-start | bytes 165896 | tf_op jit(solution)/shard_map/ppermute | solution.py:32
  478.8 7.8 %collective-permute-start.33 = (bf16[216,128]{1,0:T(8,128)(2,1)S(1)}, bf16[216,128]{1,0:T(8,128)(2,1)S(1)}, u32[]{:S(2)}, u32[]{:S(2)}) collective-permute-start(bf16[216,128]{1,0:T(8,128)(2,1)S(1)} %add_convert_fusion.1), channel_id=1, source_target_pairs={{0,16},{2,18},{4,20},{6,22},{8,24},{10,26},{12,28},{14,30},{16,0},... | collective-permute-start | bytes 165896 | tf_op jit(solution)/shard_map/ppermute | solution.py:32
  481.7 6.0 %collective-permute-start.34 = (bf16[216,128]{1,0:T(8,128)(2,1)S(1)}, bf16[216,128]{1,0:T(8,128)(2,1)S(1)}, u32[]{:S(2)}, u32[]{:S(2)}) collective-permute-start(bf16[216,128]{1,0:T(8,128)(2,1)S(1)} %add_convert_fusion.1), channel_id=1, source_target_pairs={{0,24},{2,26},{4,28},{6,30},{8,16},{10,18},{12,20},{14,22},{16,8},... | collective-permute-start | bytes 165896 | tf_op jit(solution)/shard_map/ppermute | solution.py:32
  491.1 49.1 %all-to-all-start.6 = ((bf16[8,96,1280]{2,1,0:T(8,128)(2,1)}), bf16[8,96,1280]{2,1,0:T(8,128)(2,1)}, u32[]{:S(2)}, u32[]{:S(2)}) async-start(bf16[8,96,1280]{2,1,0:T(8,128)(2,1)} %add.177), calls=%async_computation.6 | async-start | bytes 3932160 | tf_op jit(solution)/shard_map/all_to_all | solution.py:122
  498.2 22.4 %collective-permute-start.36 = (bf16[256,1536]{1,0:T(8,128)(2,1)S(1)}, bf16[256,1536]{1,0:T(8,128)(2,1)S(1)}, u32[]{:S(2)}, u32[]{:S(2)}) collective-permute-start(bf16[256,1536]{1,0:T(8,128)(2,1)S(1)} %dynamic-slice_convert_fusion), channel_id=1, source_target_pairs={{0,1},{1,0},{2,3},{3,2},{4,5},{5,4},{6,7},{7,6},{8,9},{9,8},{10,11... | collective-permute-start | bytes 2359304 | tf_op jit(solution)/shard_map/ppermute | solution.py:32
  499.3 21.3 %collective-permute-start.35 = (bf16[216,128]{1,0:T(8,128)(2,1)S(1)}, bf16[216,128]{1,0:T(8,128)(2,1)S(1)}, u32[]{:S(2)}, u32[]{:S(2)}) collective-permute-start(bf16[216,128]{1,0:T(8,128)(2,1)S(1)} %add_add_fusion.1), channel_id=1, source_target_pairs={{0,1},{1,0},{2,3},{3,2},{4,5},{5,4},{6,7},{7,6},{8,9},{9,8},{10,11... | collective-permute-start | bytes 165896 | tf_op jit(solution)/shard_map/ppermute | solution.py:32
  526.0 17.5 %copy-start.1 = (bf16[768,1536]{1,0:T(8,128)(2,1)S(1)}, bf16[768,1536]{1,0:T(8,128)(2,1)}, u32[]{:S(2)}) copy-start(bf16[768,1536]{1,0:T(8,128)(2,1)} %param.19) | copy-start | bytes 7077892
  (43 other events, 103.6 us)
